TPU v7x, 1024 devices: a whole 4x4x32 slice. The times are simulated.
1024 devices in a mesh: row: 16 (over y_lo, x, core), col: 32 (over z), seq: 2 (over y_hi).
Axes of the slice: x: 4, y: 4 (y_hi: 2, y_lo: 2; y = y_hi * 2 + y_lo), z: 32, core: 2. Of those that a mesh axis runs over, the one named last changes fastest.
Arguments:
- ffn_input: bfloat16 [1024, 6144], P('seq', 'row'), may hold values from -6 to 6
- attn_mix: bfloat16 [1024, 6144], P('seq', 'col'), may hold values from -6 to 6
- out_grad: bfloat16 [1024, 6144], P('seq', 'row'), may hold values from -6 to 6
- w_gate: bfloat16 [6144, 16384], P('row', 'col'), may hold values from -0.078125 to 0.078125
- w_up: bfloat16 [6144, 16384], P('row', 'col'), may hold values from -0.078125 to 0.078125
- w_down: bfloat16 [6144, 16384], P('row', 'col'), may hold values from -0.046875 to 0.046875
- w_out: bfloat16 [6144, 6144], P('row', 'col'), may hold values from -0.078125 to 0.078125
Outputs:
- resid_grad: bfloat16 [1024, 6144], P('seq', 'row')
- attn_grad: bfloat16 [1024, 6144], P('seq', 'col')
- gate_wgrad: float32 [6144, 16384], P('row', ('col', 'seq'))
- up_wgrad: float32 [6144, 16384], P('row', ('col', 'seq'))
- down_wgrad: float32 [6144, 16384], P('row', ('col', 'seq'))
- out_wgrad: float32 [6144, 6144], P('row', ('col', 'seq'))
All inputs are finite; a program needn't handle non-finite values.
Results may differ from a plain program's by a relative error of at most 0.01.
Values may be sent and summed in bfloat16 or wider, within the bound.
No kernel may reach another device: no remote copies, remote signals or barrier semaphores. Data moves between devices by JAX's collectives and lax.ppermute only.
A program may use at most 32 MiB of HBM per device.

v0:
```python
import jax
import jax.numpy as jnp
from jax import lax
from jax.sharding import PartitionSpec as P


def swiglu_grads(gate_pre, up_pre, hidden_grad):
    sigmoid_gate = jax.nn.sigmoid(gate_pre)
    activated = gate_pre * sigmoid_gate
    hidden = (activated * up_pre).astype(jnp.bfloat16)
    up_grad = (hidden_grad * activated).astype(jnp.bfloat16)
    slope = sigmoid_gate * (1.0 + gate_pre * (1.0 - sigmoid_gate))
    gate_grad = (hidden_grad * up_pre * slope).astype(jnp.bfloat16)
    return (gate_grad, up_grad, hidden)


def contract_rows(first, second):
    return lax.dot_general(
        first, second, (((0,), (0,)), ((), ())), preferred_element_type=jnp.float32
    )


def contract_cols(first, second):
    return lax.dot_general(
        first, second, (((1,), (1,)), ((), ())), preferred_element_type=jnp.float32
    )


def per_device(ffn_input, attn_mix, out_grad, w_gate, w_up, w_down, w_out):
    gate_part = jnp.dot(ffn_input, w_gate, preferred_element_type=jnp.float32)
    up_part = jnp.dot(ffn_input, w_up, preferred_element_type=jnp.float32)
    grad_part = jnp.dot(out_grad, w_down, preferred_element_type=jnp.float32)
    gate_pre, up_pre, hidden_grad = (
        lax.psum_scatter(gate_part, "row", scatter_dimension=0, tiled=True),
        lax.psum_scatter(up_part, "row", scatter_dimension=0, tiled=True),
        lax.psum_scatter(grad_part, "row", scatter_dimension=0, tiled=True),
    )
    gate_share, up_share, hidden_share = swiglu_grads(gate_pre, up_pre, hidden_grad)
    gate_grad, up_grad, hidden = (
        lax.all_gather(gate_share, "row", axis=0, tiled=True),
        lax.all_gather(up_share, "row", axis=0, tiled=True),
        lax.all_gather(hidden_share, "row", axis=0, tiled=True),
    )
    back_part = contract_cols(gate_grad, w_gate) + contract_cols(up_grad, w_up)
    back_sum = lax.psum(back_part, "col")
    resid_grad = (out_grad.astype(jnp.float32) + back_sum).astype(jnp.bfloat16)
    mix_part = jnp.dot(resid_grad, w_out, preferred_element_type=jnp.float32)
    attn_grad = lax.psum(mix_part, "row").astype(jnp.bfloat16)
    seq_count = lax.axis_size("seq")
    norm_factor = (ffn_input.shape[0] * seq_count) ** (-0.5)
    gate_term = contract_rows(ffn_input, gate_grad) * norm_factor
    up_term = contract_rows(ffn_input, up_grad) * norm_factor
    down_term = contract_rows(out_grad, hidden) * norm_factor
    out_term = contract_rows(resid_grad, attn_mix) * norm_factor
    gate_wgrad, up_wgrad, down_wgrad, out_wgrad = (
        lax.psum_scatter(
            gate_term.astype(jnp.bfloat16), "seq", scatter_dimension=1, tiled=True
        ).astype(jnp.float32),
        lax.psum_scatter(
            up_term.astype(jnp.bfloat16), "seq", scatter_dimension=1, tiled=True
        ).astype(jnp.float32),
        lax.psum_scatter(
            down_term.astype(jnp.bfloat16), "seq", scatter_dimension=1, tiled=True
        ).astype(jnp.float32),
        lax.psum_scatter(
            out_term.astype(jnp.bfloat16), "seq", scatter_dimension=1, tiled=True
        ).astype(jnp.float32),
    )
    return (resid_grad, attn_grad, gate_wgrad, up_wgrad, down_wgrad, out_wgrad)


def solution(mesh):
    return jax.shard_map(
        per_device,
        mesh=mesh,
        in_specs=(
            P("seq", "row"),
            P("seq", "col"),
            P("seq", "row"),
            P("row", "col"),
            P("row", "col"),
            P("row", "col"),
            P("row", "col"),
        ),
        out_specs=(
            P("seq", "row"),
            P("seq", "col"),
            P("row", ("col", "seq")),
            P("row", ("col", "seq")),
            P("row", ("col", "seq")),
            P("row", ("col", "seq")),
        ),
        check_vma=False,
    )
```

profile of v0, /device:TPU:1, one launch (start us, length us, event | category | flops | bytes accessed | tf_op | source)
XLA Modules:
  0.0 738.9 jit_solution(7670060461911109162)
XLA Ops:
  7.2 0.0 copy-start
  7.2 0.0 reduce-scatter.8.cloned.1.call-start
  7.2 2.6 fusion.8
  9.8 0.0 copy-start.4
  9.8 0.0 reduce-scatter.8.cloned.1.call-update
  9.8 0.0 reduce-scatter.12.cloned.1.call-start
  9.9 0.0 copy-done
  9.9 0.9 copy-done.4
  10.8 1.5 fusion.10
  12.2 0.0 copy-start.2
  12.2 0.0 reduce-scatter.12.cloned.1.call-update
  12.3 0.0 reduce-scatter.10.cloned.1.call-start
  12.3 0.9 copy-done.2
  13.2 1.4 fusion.9
  14.7 0.0 reduce-scatter.10.cloned.1.call-update
  14.7 0.0 all-reduce.3.cloned.1.call-start
  14.7 83.4 %reduce-scatter.8.cloned.1.call-done = f32[32,512]{1,0:T(8,128)} async-done(((f32[512,512]{1,0:T(8,128)}), f32[32,512]{1,0:T(8,128)}) %reduce-scatter.8.cloned.1.call-update) | async-done | bytes 65552 | tf_op jit(solution)/shard_map/reduce_scatter | solution.py:36
  98.1 81.8 %reduce-scatter.12.cloned.1.call-done = f32[32,512]{1,0:T(8,128)} async-done(((f32[512,512]{1,0:T(8,128)}), f32[32,512]{1,0:T(8,128)}) %reduce-scatter.12.cloned.1.call-update) | async-done | bytes 65552 | tf_op jit(solution)/shard_map/reduce_scatter | solution.py:34
  179.9 81.5 %reduce-scatter.10.cloned.1.call-done = f32[32,512]{1,0:T(8,128)} async-done(((f32[512,512]{1,0:T(8,128)}), f32[32,512]{1,0:T(8,128)}) %reduce-scatter.10.cloned.1.call-update) | async-done | bytes 65552 | tf_op jit(solution)/shard_map/reduce_scatter | solution.py:35
  261.4 0.9 multiply_convert_fusion
  262.4 19.0 %all_gather.9 = bf16[512,512]{1,0:T(8,128)(2,1)S(1)} all-gather(bf16[32,512]{1,0:T(8,128)(2,1)S(1)} %get-tuple-element.13), channel_id=1, replica_groups=mesh['row'=16,'col'=32,'seq'=2] {'row'}, dimensions={0}, use_global_device_ids=true | all-gather | bytes 557056 | tf_op jit(solution)/shard_map/all_gather | solution.py:40
  281.3 0.5 fusion.11
  281.8 19.3 %all_gather.10 = bf16[512,512]{1,0:T(8,128)(2,1)S(1)} all-gather(bf16[32,512]{1,0:T(8,128)(2,1)S(1)} %get-tuple-element.14), channel_id=1, replica_groups=mesh['row'=16,'col'=32,'seq'=2] {'row'}, dimensions={0}, use_global_device_ids=true | all-gather | bytes 557056 | tf_op jit(solution)/shard_map/all_gather | solution.py:41
  301.1 1.4 convolution_add_fusion
  302.5 0.0 all-reduce.3.cloned.1.call-update
  302.5 0.0 copy-start.3
  302.5 0.0 reduce-scatter.18.cloned.1.call-start
  302.5 17.8 %all_gather.11 = bf16[512,512]{1,0:T(8,128)(2,1)S(1)} all-gather(bf16[32,512]{1,0:T(8,128)(2,1)S(1)} %get-tuple-element.12), channel_id=1, replica_groups=mesh['row'=16,'col'=32,'seq'=2] {'row'}, dimensions={0}, use_global_device_ids=true | all-gather | bytes 557056 | tf_op jit(solution)/shard_map/all_gather | solution.py:42
  320.4 0.0 copy-done.3
  320.4 1.2 fusion.3
  321.6 0.0 reduce-scatter.18.cloned.1.call-update
  321.6 0.0 reduce-scatter.14.cloned.1.call-start
  321.7 1.2 fusion.5
  322.9 0.0 reduce-scatter.14.cloned.1.call-update
  322.9 0.0 reduce-scatter.16.cloned.1.call-start
  323.0 1.2 fusion.4
  324.2 0.0 reduce-scatter.16.cloned.1.call-update
  324.2 0.0 copy-start.6
  324.2 0.0 reduce-scatter.20.cloned.1.call-start
  324.3 221.3 %all-reduce.3.cloned.1.call-done = f32[512,384]{1,0:T(8,128)} async-done(((f32[512,384]{1,0:T(8,128)}), f32[512,384]{1,0:T(8,128)}) %all-reduce.3.cloned.1.call-update) | async-done | bytes 786448 | tf_op jit(solution)/shard_map/psum | solution.py:45
  545.6 1.2 add_convert_fusion
  546.8 0.0 copy-done.6
  546.8 0.0 copy-start.1
  546.8 0.0 copy-start.5
  546.8 0.3 fusion.12
  547.1 0.4 copy-done.1
  547.5 0.3 copy-done.5
  547.9 0.9 fusion.6
  548.8 0.0 reduce-scatter.20.cloned.1.call-update
  548.8 47.4 %reduce-scatter.18.cloned.1.call-done = bf16[384,256]{0,1:T(8,128)(2,1)} async-done(((bf16[384,512]{0,1:T(8,128)(2,1)}), bf16[384,256]{0,1:T(8,128)(2,1)}) %reduce-scatter.18.cloned.1.call-update) | async-done | bytes 196624 | tf_op jit(solution)/shard_map/reduce_scatter | solution.py:62
  596.2 1.8 copy.15
  598.0 37.1 %reduce-scatter.14.cloned.1.call-done = bf16[384,256]{0,1:T(8,128)(2,1)} async-done(((bf16[384,512]{0,1:T(8,128)(2,1)}), bf16[384,256]{0,1:T(8,128)(2,1)}) %reduce-scatter.14.cloned.1.call-update) | async-done | bytes 196624 | tf_op jit(solution)/shard_map/reduce_scatter | solution.py:56
  635.1 1.8 copy.13
  636.9 36.2 %reduce-scatter.16.cloned.1.call-done = bf16[384,256]{0,1:T(8,128)(2,1)} async-done(((bf16[384,512]{0,1:T(8,128)(2,1)}), bf16[384,256]{0,1:T(8,128)(2,1)}) %reduce-scatter.16.cloned.1.call-update) | async-done | bytes 196624 | tf_op jit(solution)/shard_map/reduce_scatter | solution.py:59
  673.2 1.8 copy.14
  675.0 55.5 %all-reduce.4 = bf16[512,192]{0,1:T(8,128)(2,1)} all-reduce(f32[512,192]{0,1:T(8,128)S(1)} %fusion.12), channel_id=1, replica_groups=mesh['row'=16,'col'=32,'seq'=2] {'row'}, use_global_device_ids=true, to_apply=%region_4.0 | all-reduce | flops 98304 | bytes 589824 | tf_op jit(solution)/shard_map/psum | solution.py:48
  730.5 0.0 reduce-scatter.20.cloned.1.call-done
  730.5 1.6 convert_element_type.67
Async XLA Ops:
  7.2 2.7 copy-start
  7.2 90.9 %reduce-scatter.8.cloned.1.call-start = ((), (), s32[]{:S(2)}) async-start(), calls=%async_computation.7 | async-start | bytes 1114112 | tf_op jit(solution)/shard_map/reduce_scatter | solution.py:36
  9.8 1.0 copy-start.4
  9.8 170.1 %reduce-scatter.12.cloned.1.call-start = ((), (), s32[]{:S(2)}) async-start(), calls=%async_computation.9 | async-start | bytes 1114112 | tf_op jit(solution)/shard_map/reduce_scatter | solution.py:34
  12.2 1.0 copy-start.2
  12.3 249.1 %reduce-scatter.10.cloned.1.call-start = ((), (), s32[]{:S(2)}) async-start(), calls=%async_computation.8 | async-start | bytes 1114112 | tf_op jit(solution)/shard_map/reduce_scatter | solution.py:35
  14.7 530.9 %all-reduce.3.cloned.1.call-start = ((), (), s32[]{:S(2)}) async-start(), calls=%async_computation.10 | async-start | bytes 1572864 | tf_op jit(solution)/shard_map/psum | solution.py:45
  302.5 17.9 %copy-start.3 = (bf16[512,384]{1,0:T(8,128)(2,1)S(1)}, bf16[512,384]{1,0:T(8,128)(2,1)}, u32[]{:S(2)}) copy-start(bf16[512,384]{1,0:T(8,128)(2,1)} %param.9) | copy-start | bytes 1179652
  302.5 293.7 %reduce-scatter.18.cloned.1.call-start = ((), (), s32[]{:S(2)}) async-start(), calls=%async_computation.13 | async-start | bytes 589824 | tf_op jit(solution)/shard_map/reduce_scatter | solution.py:62
  321.6 313.5 %reduce-scatter.14.cloned.1.call-start = ((), (), s32[]{:S(2)}) async-start(), calls=%async_computation.11 | async-start | bytes 589824 | tf_op jit(solution)/shard_map/reduce_scatter | solution.py:56
  322.9 350.2 %reduce-scatter.16.cloned.1.call-start = ((), (), s32[]{:S(2)}) async-start(), calls=%async_computation.12 | async-start | bytes 589824 | tf_op jit(solution)/shard_map/reduce_scatter | solution.py:59
  324.2 222.6 %copy-start.6 = (bf16[384,192]{0,1:T(8,128)(2,1)S(1)}, bf16[384,192]{0,1:T(8,128)(2,1)}, u32[]{:S(2)}) copy-start(bf16[384,192]{0,1:T(8,128)(2,1)} %param.13) | copy-start | bytes 442372
  324.2 406.3 %reduce-scatter.20.cloned.1.call-start = ((), (), s32[]{:S(2)}) async-start(), calls=%async_computation.14 | async-start | bytes 221184 | tf_op jit(solution)/shard_map/reduce_scatter | solution.py:65
  546.8 0.7 copy-start.1
  546.8 1.1 copy-start.5
Sparse Core Ops, SparseCore 0:
  11.4 86.6 reduce-scatter.7
  101.9 78.0 reduce-scatter.11
  183.3 78.0 reduce-scatter.9
  302.6 242.9 all-reduce.2
  549.4 46.8 reduce-scatter.17
  600.4 34.6 reduce-scatter.13
  638.5 34.6 reduce-scatter.15
  677.5 32.3 reduce-scatter.19
where the time goes:
time: 742 us; the launch traced here: 739 us
  waiting for transfers between devices  589 us (79%)
  blocking collectives  112 us (15%)
  between operations  14.2 us (2%)
  matrix products  12.1 us (2%)
  local copies, waits for them, and re-layouts  8.05 us (1%)
    psum x1, waiting for transfers between devices, per_device(): back_sum = lax.psum(back_part, 'col')  221 us
    reduce_scatter x1, waiting for transfers between devices, per_device(): lax.psum_scatter(grad_part, 'row', scatter_dimension=0, tiled=True)  83.4 us
    reduce_scatter x1, waiting for transfers between devices, per_device(): lax.psum_scatter(gate_part, 'row', scatter_dimension=0, tiled=True)  81.8 us
    reduce_scatter x1, waiting for transfers between devices, per_device(): lax.psum_scatter(up_part, 'row', scatter_dimension=0, tiled=True)  81.5 us
    psum x1, blocking collectives, per_device(): attn_grad = lax.psum(mix_part, 'row').astype(jnp.bfloat16)  55.5 us
    reduce_scatter x1, waiting for transfers between devices, per_device(): lax.psum_scatter(down_term.astype(jnp.bfloat16), 'seq', scatter_dimension...  47.4 us
    reduce_scatter x1, waiting for transfers between devices, per_device(): lax.psum_scatter(gate_term.astype(jnp.bfloat16), 'seq', scatter_dimension...  37.1 us
    reduce_scatter x1, waiting for transfers between devices, per_device(): lax.psum_scatter(up_term.astype(jnp.bfloat16), 'seq', scatter_dimension=1...  36.2 us
  transfers between devices with their start and end apart: 8, of which 7 were waited for; matrix products, arithmetic and copies ran while one was open for 2% of the time, Pallas kernels for 0%

commit v1 on v0

v1 whole, which is shorter than its diff:
```python
import jax
import jax.numpy as jnp
from jax import lax
from jax.sharding import PartitionSpec as P

BF16 = jnp.bfloat16
F32 = jnp.float32


def swiglu_grads(gate_pre, up_pre, hidden_grad):
    sigmoid_gate = jax.nn.sigmoid(gate_pre)
    activated = gate_pre * sigmoid_gate
    hidden = (activated * up_pre).astype(BF16)
    up_grad = (hidden_grad * activated).astype(BF16)
    slope = sigmoid_gate * (1.0 + gate_pre * (1.0 - sigmoid_gate))
    gate_grad = (hidden_grad * up_pre * slope).astype(BF16)
    return (gate_grad, up_grad, hidden)


def dot(first, second):
    return jnp.dot(first, second, preferred_element_type=F32)


def contract_rows(first, second):
    return lax.dot_general(
        first, second, (((0,), (0,)), ((), ())), preferred_element_type=F32
    )


def contract_cols(first, second):
    return lax.dot_general(
        first, second, (((1,), (1,)), ((), ())), preferred_element_type=F32
    )


def scatter_sum(parts, axis, groups):
    got = lax.all_to_all(parts, axis, 0, 0, tiled=True, axis_index_groups=groups)
    return jnp.sum(got.astype(F32), axis=0)


def gather(block, count, axis, groups):
    copies = jnp.broadcast_to(block[None], (count,) + block.shape)
    return lax.all_to_all(copies, axis, 0, 0, tiled=True, axis_index_groups=groups)


def per_device(ffn_input, attn_mix, out_grad, w_gate, w_up, w_down, w_out):
    rows, cols = lax.axis_size("row"), lax.axis_size("col")
    core = lax.axis_index("row") % 2
    seq = lax.axis_index("seq")
    tokens, width = ffn_input.shape
    hidden_width = w_gate.shape[1]
    half = tokens // 2
    chips = rows // 2
    share = half // chips
    core_swap = [(i, i ^ 1) for i in range(rows)]
    seq_swap = [(0, 1), (1, 0)]
    chip_groups = [list(range(c, rows, 2)) for c in range(2)]
    tie = lax.optimization_barrier

    def halves(x):
        mine = lax.dynamic_slice_in_dim(x, core * half, half, 0)
        other = lax.dynamic_slice_in_dim(x, (1 - core) * half, half, 0)
        return mine, other

    in_mine, in_other = halves(ffn_input)
    out_mine, out_other = halves(out_grad)
    acts = lax.ppermute(jnp.concatenate([in_other, out_other]), "row", core_swap)
    weights = lax.ppermute(jnp.concatenate([w_gate, w_up, w_down]), "row", core_swap)
    in_far, out_far = acts[:half], acts[half:]
    gate_far, up_far, down_far = (weights[i * width : (i + 1) * width] for i in range(3))

    def product(x, w, x_far, w_far):
        whole = dot(x, w) + dot(x_far, w_far)
        return whole.astype(BF16).reshape(chips, share, hidden_width)

    parts = jnp.concatenate(
        [
            product(in_mine, w_gate, in_far, gate_far),
            product(in_mine, w_up, in_far, up_far),
            product(out_mine, w_down, out_far, down_far),
        ],
        axis=1,
    )
    parts, w_out_sent = tie((parts, w_out))
    w_out_far = lax.ppermute(w_out_sent, "row", core_swap)
    total = scatter_sum(parts, "row", chip_groups)
    total, w_out_far = tie((total, w_out_far))
    grads = swiglu_grads(total[:share], total[share : 2 * share], total[2 * share :])
    mine = gather(jnp.concatenate(grads, axis=0), chips, "row", chip_groups)

    def split(x):
        return [
            x[:, i * share : (i + 1) * share].reshape(half, hidden_width)
            for i in range(3)
        ]

    gate_mine, up_mine, hid_mine = split(mine)

    near, far = 4, cols // 4

    def place(r, k, j):
        return r * cols + (k * near + j + 2 * (r % 2)) % cols

    near_groups = [[place(r, k, j) for j in range(near)] for r in range(rows) for k in range(far)]
    far_groups = [[place(r, k, j) for k in range(far)] for r in range(rows) for j in range(near)]
    both = ("row", "col")
    spot = (lax.axis_index("col") + cols - 2 * core) % cols
    piece = tokens // cols

    def pair_blocks(own, away):
        return jnp.concatenate([x.reshape(near, half // near, width) for x in (own, away)], axis=1)

    def back(wg, wu):
        return (contract_cols(gate_mine, wg) + contract_cols(up_mine, wu)).astype(BF16)

    back_part = pair_blocks(back(w_gate, w_up), back(gate_far, up_far))
    back_part, mine = tie((back_part, mine))
    other = lax.ppermute(mine, "row", core_swap)
    near_sum = scatter_sum(back_part, both, near_groups).astype(BF16)
    near_sum, other = tie((near_sum, other))
    gate_other, up_other, hid_other = split(other)

    norm_factor = (tokens * lax.axis_size("seq")) ** (-0.5)

    def wgrad(pairs, which):
        size = pairs[0][1].shape[1] // 2
        terms = [
            contract_rows(a, lax.dynamic_slice_in_dim(b, which * size, size, 1))
            for a, b in pairs
        ]
        return sum(terms) * norm_factor

    operands = (
        ((in_mine, gate_mine), (in_other, gate_other)),
        ((in_mine, up_mine), (in_other, up_other)),
        ((out_mine, hid_mine), (out_other, hid_other)),
    )
    sent = jnp.concatenate([wgrad(p, 1 - seq).astype(BF16) for p in operands])
    received = lax.ppermute(sent, "seq", seq_swap)

    far_sum = scatter_sum(near_sum.reshape(far, piece, width), both, far_groups)
    out_all = pair_blocks(out_mine, out_far).reshape(cols, piece, width)
    out_piece = lax.dynamic_index_in_dim(out_all, (spot % near) * far + spot // near, 0, False)
    resid_piece = (out_piece.astype(F32) + far_sum).astype(BF16)
    resid_near = gather(resid_piece, far, both, far_groups).reshape(tokens // near, width)
    resid_near, received = tie((resid_near, received))
    received = received.astype(F32).reshape(3, width, -1)
    wgrads = [wgrad(p, seq) + received[i] for i, p in enumerate(operands)]

    resid_all = gather(resid_near, near, both, near_groups)
    resid_all = resid_all.reshape(near, 2, half // near, width)
    resid_mine, resid_far = (resid_all[:, i].reshape(half, width) for i in range(2))
    mix_part = (dot(resid_mine, w_out) + dot(resid_far, w_out_far)).astype(BF16)
    mix_share = scatter_sum(mix_part.reshape(chips, share, -1), "row", chip_groups)
    mix_all = gather(mix_share.astype(BF16), rows, "row", None)
    attn_grad = mix_all.reshape(chips, 2, share, -1).swapaxes(0, 1).reshape(tokens, -1)

    resid_other = lax.ppermute(resid_far, "row", core_swap)
    resid_grad = jnp.where(
        core == 0,
        jnp.concatenate([resid_mine, resid_other]),
        jnp.concatenate([resid_other, resid_mine]),
    )
    out_pairs = ((resid_grad, attn_mix),)
    out_sent = wgrad(out_pairs, 1 - seq).astype(BF16)
    out_wgrad = wgrad(out_pairs, seq) + lax.ppermute(out_sent, "seq", seq_swap).astype(F32)
    return (resid_grad, attn_grad, *wgrads, out_wgrad)


def solution(mesh):
    return jax.shard_map(
        per_device,
        mesh=mesh,
        in_specs=(
            P("seq", "row"),
            P("seq", "col"),
            P("seq", "row"),
            P("row", "col"),
            P("row", "col"),
            P("row", "col"),
            P("row", "col"),
        ),
        out_specs=(
            P("seq", "row"),
            P("seq", "col"),
            P("row", ("col", "seq")),
            P("row", ("col", "seq")),
            P("row", ("col", "seq")),
            P("row", ("col", "seq")),
        ),
        check_vma=False,
    )
```

time: 742 us -> 196 us (0.26)
  waiting for transfers between devices: 589 us -> 52 us
  blocking collectives: 112 us -> 14.4 us
  starting transfers between devices: 0.33 us -> 94.6 us
  between operations: 14.2 us -> 1.3 us
    reduce_scatter x7 -> x0, waiting for transfers between devices: 367 us -> none  [the longest x1 83.4 us: per_device(): lax.psum_scatter(grad_part, 'row', scatter_dimension=0, tiled=True)]
    psum x1 -> x0, waiting for transfers between devices: 221 us -> none  [per_device(): back_sum = lax.psum(back_part, 'col')]
    all_gather x3 -> x0, blocking collectives: 56.1 us -> none  [the longest x1 19.3 us: per_device(): lax.all_gather(up_share, 'row', axis=0, tiled=True)]
    psum x1 -> x0, blocking collectives: 55.5 us -> none  [per_device(): attn_grad = lax.psum(mix_part, 'row').astype(jnp.bfloat16)]
    all_to_all x0 -> x7, starting transfers between devices: none -> 55.4 us  [the longest x4 33.7 us: scatter_sum(): lax.all_to_all(parts, axis, 0, 0, tiled=True, axis_index_groups=groups)]
    ppermute x0 -> x7, starting transfers between devices: none -> 39.1 us  [the longest x1 16.2 us: per_device(): lax.ppermute(jnp.concatenate([w_gate, w_up, w_down]), 'row', core_swap)]
    all_to_all x0 -> x7, waiting for transfers between devices: none -> 36 us  [the longest x4 32.1 us: scatter_sum(): lax.all_to_all(parts, axis, 0, 0, tiled=True, axis_index_groups=groups)]
    ppermute x0 -> x7, waiting for transfers between devices: none -> 16 us  [the longest x1 13.3 us: per_device(): received = lax.ppermute(sent, 'seq', seq_swap)]
  transfers between devices with their start and end apart: 8 -> 14, of which waited for: 7 -> 10; matrix products, arithmetic and copies ran while one was open for 2% -> 10% of each run, Pallas kernels for 0% -> 0%
where the time goes in v1:
time: 196 us; the launch traced here: 194 us
  starting transfers between devices  94.6 us (48%)
  waiting for transfers between devices  52 us (27%)
  matrix products  14.7 us (8%)
  blocking collectives  14.4 us (7%)
  other arithmetic  10.1 us (5%)
  local copies, waits for them, and re-layouts  7.35 us (4%)
    all_to_all x4, starting transfers between devices, scatter_sum(): lax.all_to_all(parts, axis, 0, 0, tiled=True, axis_index_groups=groups)  33.7 us
    all_to_all x4, waiting for transfers between devices, scatter_sum(): lax.all_to_all(parts, axis, 0, 0, tiled=True, axis_index_groups=groups)  32.1 us
    all_to_all x3, starting transfers between devices, gather(): lax.all_to_all(copies, axis, 0, 0, tiled=True, axis_index_groups=groups)  21.8 us
    ppermute x1, starting transfers between devices, per_device(): lax.ppermute(jnp.concatenate([w_gate, w_up, w_down]), 'row', core_swap)  16.2 us
    all_to_all x1, blocking collectives, gather(): lax.all_to_all(copies, axis, 0, 0, tiled=True, axis_index_groups=groups)  14.4 us
    ppermute x1, waiting for transfers between devices, per_device(): received = lax.ppermute(sent, 'seq', seq_swap)  13.3 us
    dot_general x14, matrix products, contract_rows(): lax.dot_general(first, second, (((0,), (0,)), ((), ())), preferred_elemen...  9.32 us
    ppermute x1, starting transfers between devices, per_device(): resid_other = lax.ppermute(resid_far, 'row', core_swap)  7.9 us
  transfers between devices with their start and end apart: 14, of which 10 were waited for; matrix products, arithmetic and copies ran while one was open for 10% of the time, Pallas kernels for 0%

profile of v1, /device:TPU:1, one launch (start us, length us, event | category | flops | bytes accessed | tf_op | source)
XLA Modules:
  0.0 194.4 jit_solution(11953485558348758609)
XLA Ops:
  0.7 2.4 %pad_maximum_fusion = bf16[1152,512]{1,0:T(8,128)(2,1)} fusion(bf16[384,512]{1,0:T(8,128)(2,1)} %param.12, bf16[384,512]{1,0:T(8,128)(2,1)} %param.11, bf16[384,512]{1,0:T(8,128)(2,1)} %param.10), kind=kLoop, calls=%fused_computation.21 | loop fusion | flops 3538944 | bytes 2359296 | tf_op jit(solution)/shard_map/concatenate | solution.py:68
  3.1 16.2 %collective-permute-start.1 = (bf16[1152,512]{1,0:T(8,128)(2,1)}, bf16[1152,512]{1,0:T(8,128)(2,1)S(1)}, u32[]{:S(2)}, u32[]{:S(2)}) collective-permute-start(bf16[1152,512]{1,0:T(8,128)(2,1)} %pad_maximum_fusion), channel_id=1, source_target_pairs={{0,64},{64,0},{128,192},{192,128},{256,320},{320,256},{384,448},{4... | collective-permute-start | bytes 3538952 | tf_op jit(solution)/shard_map/ppermute | solution.py:68
  19.5 2.1 %collective-permute-start = (bf16[512,384]{1,0:T(8,128)(2,1)S(1)}, bf16[512,384]{1,0:T(8,128)(2,1)S(1)}, u32[]{:S(2)}, u32[]{:S(2)}) collective-permute-start(bf16[512,384]{1,0:T(8,128)(2,1)S(1)} %pad_maximum_fusion.3), channel_id=1, source_target_pairs={{0,64},{64,0},{128,192},{192,128},{256,320},{320,256},{384,448},{4... | collective-permute-start | bytes 1179656 | tf_op jit(solution)/shard_map/ppermute | solution.py:67
  21.6 0.3 fusion.49
  21.9 0.3 fusion.51
  22.2 0.3 fusion.76
  22.5 0.8 collective-permute-done
  23.2 0.3 fusion.8
  23.5 0.3 fusion.7
  23.9 0.3 fusion.6
  24.2 1.0 pad_maximum_fusion.1
  25.1 4.2 %all-to-all-start = ((bf16[8,96,512]{2,1,0:T(8,128)(2,1)}), bf16[8,96,512]{2,1,0:T(8,128)(2,1)}, u32[]{:S(2)}, u32[]{:S(2)}) async-start(bf16[8,96,512]{2,1,0:T(8,128)(2,1)} %pad_maximum_fusion.1), calls=%async_computation | async-start | bytes 1572864 | tf_op jit(solution)/shard_map/all_to_all | solution.py:37
  29.3 2.0 %collective-permute-start.2 = (bf16[384,192]{0,1:T(8,128)(2,1)}, bf16[384,192]{0,1:T(8,128)(2,1)S(1)}, u32[]{:S(2)}, u32[]{:S(2)}) collective-permute-start(bf16[384,192]{0,1:T(8,128)(2,1)} %param.13), channel_id=1, source_target_pairs={{0,64},{64,0},{128,192},{192,128},{256,320},{320,256},{384,448},{4... | collective-permute-start | bytes 442376 | tf_op jit(solution)/shard_map/ppermute | solution.py:85
  31.4 11.1 %all-to-all-done = bf16[8,96,512]{2,1,0:T(8,128)(2,1)} async-done(((bf16[8,96,512]{2,1,0:T(8,128)(2,1)}), bf16[8,96,512]{2,1,0:T(8,128)(2,1)}, u32[]{:S(2)}, u32[]{:S(2)}) %all-to-all-start) | async-done | bytes 786464 | tf_op jit(solution)/shard_map/all_to_all | solution.py:37
  42.5 1.3 convert_reduce_fusion
  43.9 0.5 copy-done.25
  44.4 14.4 %all_to_all.40 = bf16[8,96,512]{2,1,0:T(8,128)(2,1)S(1)} all-to-all(bf16[8,96,512]{2,1,0:T(8,128)(2,1)S(1)} %broadcast_in_dim.10), channel_id=1, replica_groups={{0,128,256,384,512,640,768,896},{64,192,320,448,576,704,832,960},{1,129..., dimensions={0} | all-to-all | bytes 1572864 | tf_op jit(solution)/shard_map/all_to_all | solution.py:43
  58.8 0.8 fusion.74
  59.6 0.3 fusion.77
  60.0 0.3 fusion.9
  60.3 0.3 fusion.18
  60.6 0.3 fusion.10
  61.0 0.8 pad_maximum_fusion.5
  61.8 8.6 %all-to-all-start.2 = ((bf16[4,128,384]{2,1,0:T(8,128)(2,1)}), bf16[4,128,384]{2,1,0:T(8,128)(2,1)S(1)}, u32[]{:S(2)}, u32[]{:S(2)}) async-start(bf16[4,128,384]{2,1,0:T(8,128)(2,1)} %pad_maximum_fusion.5), calls=%async_computation.2 | async-start | bytes 786432 | tf_op jit(solution)/shard_map/all_to_all | solution.py:37
  70.4 1.9 collective-permute-start.3
  72.4 0.8 pad_maximum_fusion.4
  73.2 1.0 fusion.38
  74.2 1.0 fusion.41
  75.4 0.8 all-to-all-done.2
  76.2 0.7 reduce_sum.45
  77.0 17.5 %all-to-all-start.3 = ((bf16[8,16,384]{2,1,0:T(8,128)(2,1)}), bf16[8,16,384]{2,1,0:T(8,128)(2,1)S(1)}, u32[]{:S(2)}, u32[]{:S(2)}) async-start(bf16[8,16,384]{2,1,0:T(8,128)(2,1)} %bitcast.10), calls=%async_computation.3 | async-start | bytes 196608 | tf_op jit(solution)/shard_map/all_to_all | solution.py:37
  94.4 1.2 fusion.73
  95.7 0.9 fusion.11
  97.0 0.3 fusion.13
  97.3 15.9 %all-to-all-done.3 = bf16[8,16,384]{2,1,0:T(8,128)(2,1)S(1)} async-done(((bf16[8,16,384]{2,1,0:T(8,128)(2,1)}), bf16[8,16,384]{2,1,0:T(8,128)(2,1)S(1)}, u32[]{:S(2)}, u32[]{:S(2)}) %all-to-all-start.3) | async-done | bytes 98336 | tf_op jit(solution)/shard_map/all_to_all | solution.py:37
  113.2 0.7 fusion.55
  113.9 0.7 broadcast_in_dim.12
  114.5 12.1 %all-to-all-start.4 = ((bf16[8,16,384]{2,1,0:T(8,128)(2,1)}), bf16[8,16,384]{2,1,0:T(8,128)(2,1)S(1)}, u32[]{:S(2)}, u32[]{:S(2)}) async-start(bf16[8,16,384]{2,1,0:T(8,128)(2,1)} %broadcast_in_dim.12), calls=%async_computation.4 | async-start | bytes 196608 | tf_op jit(solution)/shard_map/all_to_all | solution.py:43
  126.7 4.5 %collective-permute-start.4 = (bf16[1152,256]{1,0:T(8,128)(2,1)S(1)}, bf16[1152,256]{1,0:T(8,128)(2,1)S(1)}, u32[]{:S(2)}, u32[]{:S(2)}) collective-permute-start(bf16[1152,256]{1,0:T(8,128)(2,1)S(1)} %pad_maximum_fusion.2), channel_id=1, source_target_pairs={{0,1},{1,0},{2,3},{3,2},{4,5},{5,4},{6,7},{7,6},{8,9},{9,8},{10,11... | collective-permute-start | bytes 1769480 | tf_op jit(solution)/shard_map/ppermute | solution.py:139
  131.2 13.3 %collective-permute-done.4 = bf16[1152,256]{1,0:T(8,128)(2,1)S(1)} collective-permute-done((bf16[1152,256]{1,0:T(8,128)(2,1)S(1)}, bf16[1152,256]{1,0:T(8,128)(2,1)S(1)}, u32[]{:S(2)}, u32[]{:S(2)}) %collective-permute-start.4) | collective-permute-done | bytes 589856 | tf_op jit(solution)/shard_map/ppermute | solution.py:139
  144.5 2.7 %all-to-all-done.4 = bf16[8,16,384]{2,1,0:T(8,128)(2,1)S(1)} async-done(((bf16[8,16,384]{2,1,0:T(8,128)(2,1)}), bf16[8,16,384]{2,1,0:T(8,128)(2,1)S(1)}, u32[]{:S(2)}, u32[]{:S(2)}) %all-to-all-start.4) | async-done | bytes 98336 | tf_op jit(solution)/shard_map/all_to_all | solution.py:43
  147.3 0.8 broadcast_in_dim.13
  148.0 5.0 %all-to-all-start.5 = ((bf16[4,128,384]{2,1,0:T(8,128)(2,1)}), bf16[4,128,384]{2,1,0:T(8,128)(2,1)S(1)}, u32[]{:S(2)}, u32[]{:S(2)}) async-start(bf16[4,128,384]{2,1,0:T(8,128)(2,1)} %broadcast_in_dim.13), calls=%async_computation.5 | async-start | bytes 786432 | tf_op jit(solution)/shard_map/all_to_all | solution.py:43
  153.3 1.0 fusion.29
  154.5 1.1 convert_element_type.79
  155.7 1.0 slice_add_fusion.2
  156.7 0.9 all-to-all-done.5
  157.6 0.7 fusion.75
  158.3 7.9 %collective-permute-start.5 = (bf16[256,384]{1,0:T(8,128)(2,1)}, bf16[256,384]{1,0:T(8,128)(2,1)}, u32[]{:S(2)}, u32[]{:S(2)}) collective-permute-start(bf16[256,384]{1,0:T(8,128)(2,1)} %bitcast.20), channel_id=1, source_target_pairs={{0,64},{64,0},{128,192},{192,128},{256,320},{320,256},{384,448},{4... | collective-permute-start | bytes 589832 | tf_op jit(solution)/shard_map/ppermute | solution.py:158
  166.2 1.1 fusion.78
  167.4 1.2 fusion.15
  168.6 0.8 copy.16
  169.3 3.4 %all-to-all-start.6 = ((bf16[8,32,192]{2,1,0:T(8,128)(2,1)}), bf16[8,32,192]{2,1,0:T(8,128)(2,1)S(1)}, u32[]{:S(2)}, u32[]{:S(2)}) async-start(bf16[8,32,192]{2,1,0:T(8,128)(2,1)} %bitcast.21), calls=%async_computation.6 | async-start | bytes 262144 | tf_op jit(solution)/shard_map/all_to_all | solution.py:37
  172.7 1.0 slice_add_fusion.1
  173.7 4.4 %all-to-all-done.6 = bf16[8,32,192]{2,1,0:T(8,128)(2,1)S(1)} async-done(((bf16[8,32,192]{2,1,0:T(8,128)(2,1)}), bf16[8,32,192]{2,1,0:T(8,128)(2,1)S(1)}, u32[]{:S(2)}, u32[]{:S(2)}) %all-to-all-start.6) | async-done | bytes 98336 | tf_op jit(solution)/shard_map/all_to_all | solution.py:37
  178.1 0.7 broadcast_in_dim.14
  178.9 4.7 %all-to-all-start.7 = ((bf16[16,32,192]{2,1,0:T(8,128)(2,1)}), bf16[16,32,192]{2,1,0:T(8,128)(2,1)S(1)}, u32[]{:S(2)}, u32[]{:S(2)}) async-start(bf16[16,32,192]{2,1,0:T(8,128)(2,1)} %broadcast_in_dim.14), calls=%async_computation.7 | async-start | bytes 524288 | tf_op jit(solution)/shard_map/all_to_all | solution.py:43
  183.6 1.1 maximum_select_fusion
  184.9 4.5 %collective-permute-start.6 = (bf16[384,96]{0,1:T(8,128)(2,1)S(1)}, bf16[384,96]{0,1:T(8,128)(2,1)S(1)}, u32[]{:S(2)}, u32[]{:S(2)}) collective-permute-start(bf16[384,96]{0,1:T(8,128)(2,1)S(1)} %fusion.16), channel_id=1, source_target_pairs={{0,1},{1,0},{2,3},{3,2},{4,5},{5,4},{6,7},{7,6},{8,9},{9,8},{10,11... | collective-permute-start | bytes 221192 | tf_op jit(solution)/shard_map/ppermute | solution.py:166
  189.5 1.0 slice_add_fusion
  190.5 0.3 all-to-all-done.7
  190.8 0.8 copy.18
  191.6 1.9 collective-permute-done.6
  193.5 0.9 fusion.14
  (73 shorter events, 1.7 us)
Async XLA Ops:
  0.6 184.1 %copy-start = (bf16[512,192]{0,1:T(8,128)(2,1)S(1)}, bf16[512,192]{0,1:T(8,128)(2,1)}, u32[]{:S(2)}) copy-start(bf16[512,192]{0,1:T(8,128)(2,1)} %param.8) | copy-start | bytes 589828
  0.6 18.7 %copy-start.24 = (bf16[512,384]{1,0:T(8,128)(2,1)S(1)}, bf16[512,384]{1,0:T(8,128)(2,1)}, u32[]{:S(2)}) copy-start(bf16[512,384]{1,0:T(8,128)(2,1)} %param.9) | copy-start | bytes 1179652
  0.7 18.7 %copy-start.1 = (bf16[512,384]{1,0:T(8,128)(2,1)S(1)}, bf16[512,384]{1,0:T(8,128)(2,1)}, u32[]{:S(2)}) copy-start(bf16[512,384]{1,0:T(8,128)(2,1)} %param.7) | copy-start | bytes 1179652
  3.1 18.5 %copy-start.2 = (bf16[384,512]{1,0:T(8,128)(2,1)S(1)}, bf16[384,512]{1,0:T(8,128)(2,1)}, u32[]{:S(2)}) copy-start(bf16[384,512]{1,0:T(8,128)(2,1)} %param.11) | copy-start | bytes 1179652
  3.1 20.1 %collective-permute-start.1 = (bf16[1152,512]{1,0:T(8,128)(2,1)}, bf16[1152,512]{1,0:T(8,128)(2,1)S(1)}, u32[]{:S(2)}, u32[]{:S(2)}) collective-permute-start(bf16[1152,512]{1,0:T(8,128)(2,1)} %pad_maximum_fusion), channel_id=1, source_target_pairs={{0,64},{64,0},{128,192},{192,128},{256,320},{320,256},{384,448},{4... | collective-permute-start | bytes 3538952 | tf_op jit(solution)/shard_map/ppermute | solution.py:68
  19.4 2.8 %copy-start.7 = (bf16[256,384]{1,0:T(8,128)(2,1)}, bf16[256,384]{1,0:T(8,128)(2,1)S(1)}, u32[]{:S(2)}) copy-start(bf16[256,384]{1,0:T(8,128)(2,1)S(1)} %get-tuple-element.46) | copy-start | bytes 589828
  19.4 2.4 %copy-start.3 = (bf16[384,512]{1,0:T(8,128)(2,1)S(1)}, bf16[384,512]{1,0:T(8,128)(2,1)}, u32[]{:S(2)}) copy-start(bf16[384,512]{1,0:T(8,128)(2,1)} %param.10) | copy-start | bytes 1179652
  19.5 2.7 %copy-start.9 = (bf16[384,512]{1,0:T(8,128)(2,1)S(1)}, bf16[384,512]{1,0:T(8,128)(2,1)}, u32[]{:S(2)}) copy-start(bf16[384,512]{1,0:T(8,128)(2,1)} %param.12) | copy-start | bytes 1179652
  19.5 3.7 %collective-permute-start = (bf16[512,384]{1,0:T(8,128)(2,1)S(1)}, bf16[512,384]{1,0:T(8,128)(2,1)S(1)}, u32[]{:S(2)}, u32[]{:S(2)}) collective-permute-start(bf16[512,384]{1,0:T(8,128)(2,1)S(1)} %pad_maximum_fusion.3), channel_id=1, source_target_pairs={{0,64},{64,0},{128,192},{192,128},{256,320},{320,256},{384,448},{4... | collective-permute-start | bytes 1179656 | tf_op jit(solution)/shard_map/ppermute | solution.py:67
  23.2 0.9 copy-start.13
  25.1 17.3 %all-to-all-start = ((bf16[8,96,512]{2,1,0:T(8,128)(2,1)}), bf16[8,96,512]{2,1,0:T(8,128)(2,1)}, u32[]{:S(2)}, u32[]{:S(2)}) async-start(bf16[8,96,512]{2,1,0:T(8,128)(2,1)} %pad_maximum_fusion.1), calls=%async_computation | async-start | bytes 1572864 | tf_op jit(solution)/shard_map/all_to_all | solution.py:37
  29.3 14.4 %collective-permute-start.2 = (bf16[384,192]{0,1:T(8,128)(2,1)}, bf16[384,192]{0,1:T(8,128)(2,1)S(1)}, u32[]{:S(2)}, u32[]{:S(2)}) collective-permute-start(bf16[384,192]{0,1:T(8,128)(2,1)} %param.13), channel_id=1, source_target_pairs={{0,64},{64,0},{128,192},{192,128},{256,320},{320,256},{384,448},{4... | collective-permute-start | bytes 442376 | tf_op jit(solution)/shard_map/ppermute | solution.py:85
  43.7 0.7 copy-start.25
  58.8 1.2 copy-start.5
  60.6 9.8 %copy-start.6 = (bf16[8,96,512]{2,1,0:T(8,128)(2,1)S(1)}, bf16[8,96,512]{2,1,0:T(8,128)(2,1)}, u32[]{:S(2)}) copy-start(bf16[8,96,512]{2,1,0:T(8,128)(2,1)} %copy-done.5) | copy-start | bytes 2359300
  61.0 11.4 %slice-start = ((bf16[512,384]{1,0:T(8,128)(2,1)}), bf16[256,384]{1,0:T(8,128)(2,1)S(1)}, s32[]{:S(2)}) async-start(bf16[512,384]{1,0:T(8,128)(2,1)} %copy-done.13), calls=%async_computation.8 | async-start | bytes 393216 | tf_op jit(solution)/shard_map/slice | solution.py:69
  61.8 14.5 %all-to-all-start.2 = ((bf16[4,128,384]{2,1,0:T(8,128)(2,1)}), bf16[4,128,384]{2,1,0:T(8,128)(2,1)S(1)}, u32[]{:S(2)}, u32[]{:S(2)}) async-start(bf16[4,128,384]{2,1,0:T(8,128)(2,1)} %pad_maximum_fusion.5), calls=%async_computation.2 | async-start | bytes 786432 | tf_op jit(solution)/shard_map/all_to_all | solution.py:37
  70.4 6.6 %collective-permute-start.3 = (bf16[8,96,512]{2,1,0:T(8,128)(2,1)S(1)}, bf16[8,96,512]{2,1,0:T(8,128)(2,1)}, u32[]{:S(2)}, u32[]{:S(2)}) collective-permute-start(bf16[8,96,512]{2,1,0:T(8,128)(2,1)S(1)} %copy-done.6), channel_id=1, source_target_pairs={{0,64},{64,0},{128,192},{192,128},{256,320},{320,256},{384,448},{4... | collective-permute-start | bytes 2359304 | tf_op jit(solution)/shard_map/ppermute | solution.py:118
  72.4 2.8 %copy-start.14 = (bf16[8,32,512]{2,1,0:T(8,128)(2,1)S(1)}, bf16[8,32,512]{2,1,0:T(8,128)(2,1)}, u32[]{:S(2)}) copy-start(bf16[8,32,512]{2,1,0:T(8,128)(2,1)} %get-tuple-element.41) | copy-start | bytes 786436
  75.4 20.3 %copy-start.8 = (bf16[256,384]{1,0:T(8,128)(2,1)S(1)}, bf16[256,384]{1,0:T(8,128)(2,1)}, u32[]{:S(2)}) copy-start(bf16[256,384]{1,0:T(8,128)(2,1)} %copy-done.7) | copy-start | bytes 589828
  77.0 36.2 %all-to-all-start.3 = ((bf16[8,16,384]{2,1,0:T(8,128)(2,1)}), bf16[8,16,384]{2,1,0:T(8,128)(2,1)S(1)}, u32[]{:S(2)}, u32[]{:S(2)}) async-start(bf16[8,16,384]{2,1,0:T(8,128)(2,1)} %bitcast.10), calls=%async_computation.3 | async-start | bytes 196608 | tf_op jit(solution)/shard_map/all_to_all | solution.py:37
  94.4 2.2 %copy-start.11 = (f32[384,256]{1,0:T(8,128)S(1)}, f32[384,256]{1,0:T(8,128)}, u32[]{:S(2)}) copy-start(f32[384,256]{1,0:T(8,128)} %fusion.38) | copy-start | bytes 1179652
  95.7 1.3 copy-start.20
  95.7 1.6 copy-start.16
  95.7 1.6 copy-start.18
  95.7 1.3 copy-start.10
  96.6 30.0 %copy-start.22 = (bf16[384,256]{1,0:T(8,128)(2,1)S(1)}, bf16[384,256]{1,0:T(8,128)(2,1)}, u32[]{:S(2)}) copy-start(bf16[384,256]{1,0:T(8,128)(2,1)} %fusion.11) | copy-start | bytes 589828
  114.5 32.7 %all-to-all-start.4 = ((bf16[8,16,384]{2,1,0:T(8,128)(2,1)}), bf16[8,16,384]{2,1,0:T(8,128)(2,1)S(1)}, u32[]{:S(2)}, u32[]{:S(2)}) async-start(bf16[8,16,384]{2,1,0:T(8,128)(2,1)} %broadcast_in_dim.12), calls=%async_computation.4 | async-start | bytes 196608 | tf_op jit(solution)/shard_map/all_to_all | solution.py:43
  126.7 17.9 %collective-permute-start.4 = (bf16[1152,256]{1,0:T(8,128)(2,1)S(1)}, bf16[1152,256]{1,0:T(8,128)(2,1)S(1)}, u32[]{:S(2)}, u32[]{:S(2)}) collective-permute-start(bf16[1152,256]{1,0:T(8,128)(2,1)S(1)} %pad_maximum_fusion.2), channel_id=1, source_target_pairs={{0,1},{1,0},{2,3},{3,2},{4,5},{5,4},{6,7},{7,6},{8,9},{9,8},{10,11... | collective-permute-start | bytes 1769480 | tf_op jit(solution)/shard_map/ppermute | solution.py:139
  144.5 2.7 %copy-start.23 = (bf16[1152,256]{1,0:T(8,128)(2,1)}, bf16[1152,256]{1,0:T(8,128)(2,1)S(1)}, u32[]{:S(2)}) copy-start(bf16[1152,256]{1,0:T(8,128)(2,1)S(1)} %collective-permute-done.4) | copy-start | bytes 1769476
  148.0 6.2 %copy-start.15 = (bf16[8,32,512]{2,1,0:T(8,128)(2,1)S(1)}, bf16[8,32,512]{2,1,0:T(8,128)(2,1)}, u32[]{:S(2)}) copy-start(bf16[8,32,512]{2,1,0:T(8,128)(2,1)} %get-tuple-element.41) | copy-start | bytes 786436
  148.0 9.6 %all-to-all-start.5 = ((bf16[4,128,384]{2,1,0:T(8,128)(2,1)}), bf16[4,128,384]{2,1,0:T(8,128)(2,1)S(1)}, u32[]{:S(2)}, u32[]{:S(2)}) async-start(bf16[4,128,384]{2,1,0:T(8,128)(2,1)} %broadcast_in_dim.13), calls=%async_computation.5 | async-start | bytes 786432 | tf_op jit(solution)/shard_map/all_to_all | solution.py:43
  154.3 1.4 copy-start.21
  155.7 11.7 %copy-start.26 = (bf16[384,192]{0,1:T(8,128)(2,1)S(1)}, bf16[384,192]{0,1:T(8,128)(2,1)}, u32[]{:S(2)}) copy-start(bf16[384,192]{0,1:T(8,128)(2,1)} %copy-done.25) | copy-start | bytes 442372
  157.6 15.1 %copy-start.12 = (f32[384,256]{1,0:T(8,128)S(1)}, f32[384,256]{1,0:T(8,128)}, u32[]{:S(2)}) copy-start(f32[384,256]{1,0:T(8,128)} %fusion.29) | copy-start | bytes 1179652
  157.6 15.1 %copy-start.19 = (bf16[8,32,512]{2,1,0:T(8,128)(2,1)S(1)}, bf16[8,32,512]{2,1,0:T(8,128)(2,1)}, u32[]{:S(2)}) copy-start(bf16[8,32,512]{2,1,0:T(8,128)(2,1)} %copy-done.18) | copy-start | bytes 786436
  158.3 25.2 %collective-permute-start.5 = (bf16[256,384]{1,0:T(8,128)(2,1)}, bf16[256,384]{1,0:T(8,128)(2,1)}, u32[]{:S(2)}, u32[]{:S(2)}) collective-permute-start(bf16[256,384]{1,0:T(8,128)(2,1)} %bitcast.20), channel_id=1, source_target_pairs={{0,64},{64,0},{128,192},{192,128},{256,320},{320,256},{384,448},{4... | collective-permute-start | bytes 589832 | tf_op jit(solution)/shard_map/ppermute | solution.py:158
  169.3 8.8 %all-to-all-start.6 = ((bf16[8,32,192]{2,1,0:T(8,128)(2,1)}), bf16[8,32,192]{2,1,0:T(8,128)(2,1)S(1)}, u32[]{:S(2)}, u32[]{:S(2)}) async-start(bf16[8,32,192]{2,1,0:T(8,128)(2,1)} %bitcast.21), calls=%async_computation.6 | async-start | bytes 262144 | tf_op jit(solution)/shard_map/all_to_all | solution.py:37
  173.7 15.7 %copy-start.17 = (bf16[8,32,512]{2,1,0:T(8,128)(2,1)S(1)}, bf16[8,32,512]{2,1,0:T(8,128)(2,1)}, u32[]{:S(2)}) copy-start(bf16[8,32,512]{2,1,0:T(8,128)(2,1)} %copy-done.16) | copy-start | bytes 786436
  178.9 11.9 %all-to-all-start.7 = ((bf16[16,32,192]{2,1,0:T(8,128)(2,1)}), bf16[16,32,192]{2,1,0:T(8,128)(2,1)S(1)}, u32[]{:S(2)}, u32[]{:S(2)}) async-start(bf16[16,32,192]{2,1,0:T(8,128)(2,1)} %broadcast_in_dim.14), calls=%async_computation.7 | async-start | bytes 524288 | tf_op jit(solution)/shard_map/all_to_all | solution.py:43
  184.7 8.8 %copy-start.4 = (bf16[512,384]{1,0:T(8,128)(2,1)}, bf16[512,384]{1,0:T(8,128)(2,1)S(1)}, u32[]{:S(2)}) copy-start(bf16[512,384]{1,0:T(8,128)(2,1)S(1)} %maximum_select_fusion) | copy-start | bytes 1179652
  184.9 8.5 %collective-permute-start.6 = (bf16[384,96]{0,1:T(8,128)(2,1)S(1)}, bf16[384,96]{0,1:T(8,128)(2,1)S(1)}, u32[]{:S(2)}, u32[]{:S(2)}) collective-permute-start(bf16[384,96]{0,1:T(8,128)(2,1)S(1)} %fusion.16), channel_id=1, source_target_pairs={{0,1},{1,0},{2,3},{3,2},{4,5},{5,4},{6,7},{7,6},{8,9},{9,8},{10,11... | collective-permute-start | bytes 221192 | tf_op jit(solution)/shard_map/ppermute | solution.py:166

commit v2 on v1

--- a/solution.py
+++ b/solution.py
@@ -57,6 +57,9 @@
     chip_groups = [list(range(c, rows, 2)) for c in range(2)]
     tie = lax.optimization_barrier
 
+    def swap(x):
+        return lax.ppermute(x, "row", core_swap)
+
     def halves(x):
         mine = lax.dynamic_slice_in_dim(x, core * half, half, 0)
         other = lax.dynamic_slice_in_dim(x, (1 - core) * half, half, 0)
@@ -64,37 +67,32 @@
 
     in_mine, in_other = halves(ffn_input)
     out_mine, out_other = halves(out_grad)
-    acts = lax.ppermute(jnp.concatenate([in_other, out_other]), "row", core_swap)
-    weights = lax.ppermute(jnp.concatenate([w_gate, w_up, w_down]), "row", core_swap)
-    in_far, out_far = acts[:half], acts[half:]
-    gate_far, up_far, down_far = (weights[i * width : (i + 1) * width] for i in range(3))
-
-    def product(x, w, x_far, w_far):
-        whole = dot(x, w) + dot(x_far, w_far)
-        return whole.astype(BF16).reshape(chips, share, hidden_width)
-
-    parts = jnp.concatenate(
-        [
-            product(in_mine, w_gate, in_far, gate_far),
-            product(in_mine, w_up, in_far, up_far),
-            product(out_mine, w_down, out_far, down_far),
-        ],
-        axis=1,
-    )
-    parts, w_out_sent = tie((parts, w_out))
-    w_out_far = lax.ppermute(w_out_sent, "row", core_swap)
+
+    def products(x, g):
+        blocks = [
+            dot(a, w).astype(BF16).reshape(chips, share, hidden_width)
+            for a, w in ((x, w_gate), (x, w_up), (g, w_down))
+        ]
+        return jnp.concatenate(blocks, axis=1)
+
+    away = swap(products(in_other, out_other))
+    parts = (products(in_mine, out_mine).astype(F32) + away.astype(F32)).astype(BF16)
+    parts, *to_swap = tie((parts, w_gate, w_up, w_out, out_other))
     total = scatter_sum(parts, "row", chip_groups)
-    total, w_out_far = tie((total, w_out_far))
-    grads = swiglu_grads(total[:share], total[share : 2 * share], total[2 * share :])
-    mine = gather(jnp.concatenate(grads, axis=0), chips, "row", chip_groups)
+    total, gate_far, up_far, w_out_far, out_far = tie((total, *(swap(x) for x in to_swap)))
+    gate_share, up_share, hid_share = swiglu_grads(
+        total[:share], total[share : 2 * share], total[2 * share :]
+    )
+    hid_all = lax.all_gather(hid_share.astype(F32), "row", axis=0, tiled=True)
+    mine = gather(jnp.concatenate([gate_share, up_share]), chips, "row", chip_groups)
 
     def split(x):
         return [
             x[:, i * share : (i + 1) * share].reshape(half, hidden_width)
-            for i in range(3)
+            for i in range(2)
         ]
 
-    gate_mine, up_mine, hid_mine = split(mine)
+    gate_mine, up_mine = split(mine)
 
     near, far = 4, cols // 4
 
@@ -115,10 +113,10 @@
 
     back_part = pair_blocks(back(w_gate, w_up), back(gate_far, up_far))
     back_part, mine = tie((back_part, mine))
-    other = lax.ppermute(mine, "row", core_swap)
+    other = swap(mine)
     near_sum = scatter_sum(back_part, both, near_groups).astype(BF16)
     near_sum, other = tie((near_sum, other))
-    gate_other, up_other, hid_other = split(other)
+    gate_other, up_other = split(other)
 
     norm_factor = (tokens * lax.axis_size("seq")) ** (-0.5)
 
@@ -130,32 +128,42 @@
         ]
         return sum(terms) * norm_factor
 
-    operands = (
-        ((in_mine, gate_mine), (in_other, gate_other)),
-        ((in_mine, up_mine), (in_other, up_other)),
-        ((out_mine, hid_mine), (out_other, hid_other)),
-    )
-    sent = jnp.concatenate([wgrad(p, 1 - seq).astype(BF16) for p in operands])
+    gate_pairs = ((in_mine, gate_mine), (in_other, gate_other))
+    up_pairs = ((in_mine, up_mine), (in_other, up_other))
+    sent = jnp.concatenate([wgrad(p, 1 - seq).astype(BF16) for p in (gate_pairs, up_pairs)])
     received = lax.ppermute(sent, "seq", seq_swap)
 
     far_sum = scatter_sum(near_sum.reshape(far, piece, width), both, far_groups)
+    far_sum, received, hid_all = tie((far_sum, received, hid_all))
     out_all = pair_blocks(out_mine, out_far).reshape(cols, piece, width)
     out_piece = lax.dynamic_index_in_dim(out_all, (spot % near) * far + spot // near, 0, False)
     resid_piece = (out_piece.astype(F32) + far_sum).astype(BF16)
+    out_rows = out_grad.reshape(2, chips, share, width).swapaxes(0, 1).reshape(tokens, width)
+    down_pairs = ((out_rows, hid_all.astype(BF16)),)
+    down_received = lax.ppermute(wgrad(down_pairs, 1 - seq).astype(BF16), "seq", seq_swap)
+    gate_wgrad = wgrad(gate_pairs, seq) + received[:width].astype(F32)
+    up_wgrad = wgrad(up_pairs, seq) + received[width:].astype(F32)
     resid_near = gather(resid_piece, far, both, far_groups).reshape(tokens // near, width)
-    resid_near, received = tie((resid_near, received))
-    received = received.astype(F32).reshape(3, width, -1)
-    wgrads = [wgrad(p, seq) + received[i] for i, p in enumerate(operands)]
+    resid_near, down_received, gate_wgrad, up_wgrad = tie(
+        (resid_near, down_received, gate_wgrad, up_wgrad)
+    )
+    down_wgrad = wgrad(down_pairs, seq) + down_received.astype(F32)
 
     resid_all = gather(resid_near, near, both, near_groups)
+    resid_all, down_wgrad = tie((resid_all, down_wgrad))
     resid_all = resid_all.reshape(near, 2, half // near, width)
     resid_mine, resid_far = (resid_all[:, i].reshape(half, width) for i in range(2))
-    mix_part = (dot(resid_mine, w_out) + dot(resid_far, w_out_far)).astype(BF16)
-    mix_share = scatter_sum(mix_part.reshape(chips, share, -1), "row", chip_groups)
+
+    def heads_by_tokens(w, x):
+        return lax.dot_general(w, x, (((0,), (1,)), ((), ())), preferred_element_type=F32)
+
+    mix_part = (heads_by_tokens(w_out, resid_mine) + heads_by_tokens(w_out_far, resid_far)).astype(BF16)
+    mix_part, resid_far = tie((mix_part, resid_far))
+    mix_share = scatter_sum(mix_part.reshape(chips, -1, half), "row", chip_groups)
     mix_all = gather(mix_share.astype(BF16), rows, "row", None)
-    attn_grad = mix_all.reshape(chips, 2, share, -1).swapaxes(0, 1).reshape(tokens, -1)
-
-    resid_other = lax.ppermute(resid_far, "row", core_swap)
+    attn_grad = mix_all.reshape(chips, 2, -1, half).transpose(1, 3, 0, 2).reshape(tokens, -1)
+
+    resid_other = swap(resid_far)
     resid_grad = jnp.where(
         core == 0,
         jnp.concatenate([resid_mine, resid_other]),
@@ -164,7 +172,7 @@
     out_pairs = ((resid_grad, attn_mix),)
     out_sent = wgrad(out_pairs, 1 - seq).astype(BF16)
     out_wgrad = wgrad(out_pairs, seq) + lax.ppermute(out_sent, "seq", seq_swap).astype(F32)
-    return (resid_grad, attn_grad, *wgrads, out_wgrad)
+    return (resid_grad, attn_grad, gate_wgrad, up_wgrad, down_wgrad, out_wgrad)
 
 
 def solution(mesh):

time: 196 us -> 209 us (1.066)
  blocking collectives: 14.4 us -> 32.1 us
  starting transfers between devices: 94.6 us -> 109 us
  waiting for transfers between devices: 52 us -> 38.7 us
  other arithmetic: 10.1 us -> 3.98 us
    all_gather x0 -> x1, blocking collectives: none -> 20.5 us  [per_device(): hid_all = lax.all_gather(hid_share.astype(F32), 'row', axis=0, tiled=True)]
    ppermute x1, waiting for transfers between devices: 13.3 us -> 0.01 us  [per_device(): received = lax.ppermute(sent, 'seq', seq_swap)]
    all_to_all x3, waiting for transfers between devices: 3.92 us -> 14.5 us  [gather(): lax.all_to_all(copies, axis, 0, 0, tiled=True, axis_index_groups=groups)]
    all_to_all x4, waiting for transfers between devices: 32.1 us -> 21.8 us  [scatter_sum(): lax.all_to_all(parts, axis, 0, 0, tiled=True, axis_index_groups=groups)]
    ppermute x5 -> x8, starting transfers between devices: 30.1 us -> 39.1 us  [the longest x7 34.6 us: swap(): return lax.ppermute(x, 'row', core_swap)]
    all_to_all x3, starting transfers between devices: 21.8 us -> 28.7 us  [gather(): lax.all_to_all(copies, axis, 0, 0, tiled=True, axis_index_groups=groups)]
    concatenate x5 -> x3, other arithmetic: 3.47 us -> 0.09 us  [the longest x1 0.05 us: products(): return jnp.concatenate(blocks, axis=1)]
    all_to_all x1, blocking collectives: 14.4 us -> 11.6 us  [gather(): lax.all_to_all(copies, axis, 0, 0, tiled=True, axis_index_groups=groups)]
  transfers between devices with their start and end apart: 14 -> 17, of which waited for: 10 -> 8; matrix products, arithmetic and copies ran while one was open for 10% -> 6% of each run, Pallas kernels for 0% -> 0%
where the time goes in v2:
time: 209 us; the launch traced here: 207 us
  starting transfers between devices  109 us (52%)
  waiting for transfers between devices  38.7 us (19%)
  blocking collectives  32.1 us (15%)
  matrix products  15.3 us (7%)
  local copies, waits for them, and re-layouts  7.44 us (4%)
  other arithmetic  3.98 us (2%)
    ppermute x7, starting transfers between devices, swap(): return lax.ppermute(x, 'row', core_swap)  34.6 us
    all_to_all x4, starting transfers between devices, scatter_sum(): lax.all_to_all(parts, axis, 0, 0, tiled=True, axis_index_groups=groups)  31.8 us
    all_to_all x3, starting transfers between devices, gather(): lax.all_to_all(copies, axis, 0, 0, tiled=True, axis_index_groups=groups)  28.7 us
    all_to_all x4, waiting for transfers between devices, scatter_sum(): lax.all_to_all(parts, axis, 0, 0, tiled=True, axis_index_groups=groups)  21.8 us
    all_gather x1, blocking collectives, per_device(): hid_all = lax.all_gather(hid_share.astype(F32), 'row', axis=0, tiled=True)  20.5 us
    all_to_all x3, waiting for transfers between devices, gather(): lax.all_to_all(copies, axis, 0, 0, tiled=True, axis_index_groups=groups)  14.5 us
    all_to_all x1, blocking collectives, gather(): lax.all_to_all(copies, axis, 0, 0, tiled=True, axis_index_groups=groups)  11.6 us
    dot_general x12, matrix products, contract_rows(): lax.dot_general(first, second, (((0,), (0,)), ((), ())), preferred_elemen...  7.17 us
  transfers between devices with their start and end apart: 17, of which 8 were waited for; matrix products, arithmetic and copies ran while one was open for 6% of the time, Pallas kernels for 0%

profile of v2, /device:TPU:1, one launch (start us, length us, event | category | flops | bytes accessed | tf_op | source)
XLA Modules:
  0.0 207.4 jit_solution(1816941492423693429)
XLA Ops:
  0.7 1.0 copy-done
  1.6 1.3 convolution_convert_fusion.2
  3.0 0.3 convolution_convert_fusion.1
  3.4 0.6 copy-done.5
  4.0 0.3 convolution_convert_fusion
  4.4 16.2 %collective-permute-start = (bf16[8,96,512]{2,1,0:T(8,128)(2,1)S(1)}, bf16[8,96,512]{2,1,0:T(8,128)(2,1)S(1)}, u32[]{:S(2)}, u32[]{:S(2)}) collective-permute-start(bf16[8,96,512]{2,1,0:T(8,128)(2,1)S(1)} %pad_maximum_fusion), channel_id=1, source_target_pairs={{0,64},{64,0},{128,192},{192,128},{256,320},{320,256},{384,448},{4... | collective-permute-start | bytes 2359304 | tf_op jit(solution)/shard_map/ppermute | solution.py:61
  20.6 0.3 convolution_convert_fusion.5
  20.9 0.3 convolution_convert_fusion.4
  21.2 0.3 convolution_convert_fusion.3
  21.5 1.0 collective-permute-done
  22.5 1.1 add_convert_fusion
  23.6 3.5 %all-to-all-start = ((bf16[8,96,512]{2,1,0:T(8,128)(2,1)}), bf16[8,96,512]{2,1,0:T(8,128)(2,1)S(1)}, u32[]{:S(2)}, u32[]{:S(2)}) async-start(bf16[8,96,512]{2,1,0:T(8,128)(2,1)} %add_convert_fusion), calls=%async_computation | async-start | bytes 1572864 | tf_op jit(solution)/shard_map/all_to_all | solution.py:37
  27.1 2.3 %collective-permute-start.1 = (bf16[384,512]{1,0:T(8,128)(2,1)S(1)}, bf16[384,512]{1,0:T(8,128)(2,1)}, u32[]{:S(2)}, u32[]{:S(2)}) collective-permute-start(bf16[384,512]{1,0:T(8,128)(2,1)S(1)} %copy-done.2), channel_id=1, source_target_pairs={{0,64},{64,0},{128,192},{192,128},{256,320},{320,256},{384,448},{4... | collective-permute-start | bytes 1179656 | tf_op jit(solution)/shard_map/ppermute | solution.py:61
  29.4 2.0 collective-permute-start.2
  31.5 2.3 %collective-permute-start.4 = (bf16[256,384]{1,0:T(8,128)(2,1)S(1)}, bf16[256,384]{1,0:T(8,128)(2,1)S(1)}, u32[]{:S(2)}, u32[]{:S(2)}) collective-permute-start(bf16[256,384]{1,0:T(8,128)(2,1)S(1)} %get-tuple-element.35), channel_id=1, source_target_pairs={{0,64},{64,0},{128,192},{192,128},{256,320},{320,256},{384,448},{4... | collective-permute-start | bytes 589832 | tf_op jit(solution)/shard_map/ppermute | solution.py:61
  33.8 2.0 collective-permute-start.3
  35.8 4.3 %all-to-all-done = bf16[8,96,512]{2,1,0:T(8,128)(2,1)S(1)} async-done(((bf16[8,96,512]{2,1,0:T(8,128)(2,1)}), bf16[8,96,512]{2,1,0:T(8,128)(2,1)S(1)}, u32[]{:S(2)}, u32[]{:S(2)}) %all-to-all-start) | async-done | bytes 786464 | tf_op jit(solution)/shard_map/all_to_all | solution.py:37
  40.4 0.6 copy-done.10
  41.1 11.6 %all_to_all.40 = bf16[8,64,512]{2,1,0:T(8,128)(2,1)S(1)} all-to-all(bf16[8,64,512]{2,1,0:T(8,128)(2,1)S(1)} %broadcast_in_dim.8), channel_id=1, replica_groups={{0,128,256,384,512,640,768,896},{64,192,320,448,576,704,832,960},{1,129..., dimensions={0} | all-to-all | bytes 1048576 | tf_op jit(solution)/shard_map/all_to_all | solution.py:43
  52.7 0.3 fusion.66
  53.0 0.3 fusion.5
  53.4 1.3 fusion.67
  54.7 1.3 fusion.6
  56.0 0.8 pad_maximum_fusion.2
  56.8 9.3 %all-to-all-start.2 = ((bf16[4,128,384]{2,1,0:T(8,128)(2,1)}), bf16[4,128,384]{2,1,0:T(8,128)(2,1)S(1)}, u32[]{:S(2)}, u32[]{:S(2)}) async-start(bf16[4,128,384]{2,1,0:T(8,128)(2,1)} %pad_maximum_fusion.2), calls=%async_computation.2 | async-start | bytes 786432 | tf_op jit(solution)/shard_map/all_to_all | solution.py:37
  66.1 1.9 collective-permute-start.5
  68.1 20.5 %all_gather.3 = bf16[512,512]{1,0:T(8,128)(2,1)} all-gather(bf16[32,512]{1,0:T(8,128)(2,1)S(1)} %get-tuple-element.88), channel_id=1, replica_groups=mesh['row'=16,'col'=32,'seq'=2] {'row'}, dimensions={0}, use_global_device_ids=true | all-gather | bytes 557056 | tf_op jit(solution)/shard_map/all_gather | solution.py:86
  88.6 0.3 fusion.28
  88.9 0.3 fusion.25
  89.2 0.7 reduce_sum.43
  89.9 1.1 fusion.63
  91.0 15.6 %all-to-all-start.3 = ((bf16[8,16,384]{2,1,0:T(8,128)(2,1)}), bf16[8,16,384]{2,1,0:T(8,128)(2,1)}, u32[]{:S(2)}, u32[]{:S(2)}) async-start(bf16[8,16,384]{2,1,0:T(8,128)(2,1)} %bitcast.14), calls=%async_computation.3 | async-start | bytes 196608 | tf_op jit(solution)/shard_map/all_to_all | solution.py:37
  106.6 0.3 fusion.9
  106.9 0.3 fusion.8
  107.2 4.5 %collective-permute-start.6 = (bf16[768,256]{1,0:T(8,128)(2,1)S(1)}, bf16[768,256]{1,0:T(8,128)(2,1)}, u32[]{:S(2)}, u32[]{:S(2)}) collective-permute-start(bf16[768,256]{1,0:T(8,128)(2,1)S(1)} %pad_maximum_fusion.3), channel_id=1, source_target_pairs={{0,1},{1,0},{2,3},{3,2},{4,5},{5,4},{6,7},{7,6},{8,9},{9,8},{10,11... | collective-permute-start | bytes 1179656 | tf_op jit(solution)/shard_map/ppermute | solution.py:134
  111.8 0.3 fusion.19
  112.0 0.3 fusion.22
  112.3 12.2 %all-to-all-done.3 = bf16[8,16,384]{2,1,0:T(8,128)(2,1)} async-done(((bf16[8,16,384]{2,1,0:T(8,128)(2,1)}), bf16[8,16,384]{2,1,0:T(8,128)(2,1)}, u32[]{:S(2)}, u32[]{:S(2)}) %all-to-all-start.3) | async-done | bytes 98336 | tf_op jit(solution)/shard_map/all_to_all | solution.py:37
  124.6 0.9 convert_reduce_fusion.1
  125.5 0.7 broadcast_in_dim.9
  126.2 15.9 %all-to-all-start.4 = ((bf16[8,16,384]{2,1,0:T(8,128)(2,1)}), bf16[8,16,384]{2,1,0:T(8,128)(2,1)S(1)}, u32[]{:S(2)}, u32[]{:S(2)}) async-start(bf16[8,16,384]{2,1,0:T(8,128)(2,1)} %broadcast_in_dim.9), calls=%async_computation.4 | async-start | bytes 196608 | tf_op jit(solution)/shard_map/all_to_all | solution.py:43
  142.1 0.3 fusion.10
  142.4 4.5 %collective-permute-start.7 = (bf16[384,256]{0,1:T(8,128)(2,1)S(1)}, bf16[384,256]{0,1:T(8,128)(2,1)S(1)}, u32[]{:S(2)}, u32[]{:S(2)}) collective-permute-start(bf16[384,256]{0,1:T(8,128)(2,1)S(1)} %fusion.10), channel_id=1, source_target_pairs={{0,1},{1,0},{2,3},{3,2},{4,5},{5,4},{6,7},{7,6},{8,9},{9,8},{10,11... | collective-permute-start | bytes 589832 | tf_op jit(solution)/shard_map/ppermute | solution.py:143
  147.0 1.9 convert_add_fusion.1
  148.9 1.9 convert_add_fusion.2
  150.8 9.3 %all-to-all-done.4 = bf16[8,16,384]{2,1,0:T(8,128)(2,1)S(1)} async-done(((bf16[8,16,384]{2,1,0:T(8,128)(2,1)}), bf16[8,16,384]{2,1,0:T(8,128)(2,1)S(1)}, u32[]{:S(2)}, u32[]{:S(2)}) %all-to-all-start.4) | async-done | bytes 98336 | tf_op jit(solution)/shard_map/all_to_all | solution.py:43
  160.1 0.8 broadcast_in_dim.10
  160.9 8.2 %all-to-all-start.5 = ((bf16[4,128,384]{2,1,0:T(8,128)(2,1)}), bf16[4,128,384]{2,1,0:T(8,128)(2,1)S(1)}, u32[]{:S(2)}, u32[]{:S(2)}) async-start(bf16[4,128,384]{2,1,0:T(8,128)(2,1)} %broadcast_in_dim.10), calls=%async_computation.5 | async-start | bytes 786432 | tf_op jit(solution)/shard_map/all_to_all | solution.py:43
  169.1 0.3 convert_add_fusion
  169.5 4.2 %all-to-all-done.5 = bf16[4,128,384]{2,1,0:T(8,128)(2,1)S(1)} async-done(((bf16[4,128,384]{2,1,0:T(8,128)(2,1)}), bf16[4,128,384]{2,1,0:T(8,128)(2,1)S(1)}, u32[]{:S(2)}, u32[]{:S(2)}) %all-to-all-start.5) | async-done | bytes 393248 | tf_op jit(solution)/shard_map/all_to_all | solution.py:43
  173.8 1.1 convolution_bitcast_fusion
  174.9 0.9 fusion.12
  175.8 7.8 %collective-permute-start.8 = (bf16[256,384]{1,0:T(8,128)(2,1)S(1)}, bf16[256,384]{1,0:T(8,128)(2,1)S(1)}, u32[]{:S(2)}, u32[]{:S(2)}) collective-permute-start(bf16[256,384]{1,0:T(8,128)(2,1)S(1)} %bitcast.98), channel_id=1, source_target_pairs={{0,64},{64,0},{128,192},{192,128},{256,320},{320,256},{384,448},{4... | collective-permute-start | bytes 589832 | tf_op jit(solution)/shard_map/ppermute | solution.py:61
  183.6 3.4 %all-to-all-start.6 = ((bf16[8,24,256]{2,1,0:T(8,128)(2,1)}), bf16[8,24,256]{2,1,0:T(8,128)(2,1)S(1)}, u32[]{:S(2)}, u32[]{:S(2)}) async-start(bf16[8,24,256]{2,1,0:T(8,128)(2,1)} %bitcast.27), calls=%async_computation.6 | async-start | bytes 196608 | tf_op jit(solution)/shard_map/all_to_all | solution.py:37
  187.0 5.2 %all-to-all-done.6 = bf16[8,24,256]{2,1,0:T(8,128)(2,1)S(1)} async-done(((bf16[8,24,256]{2,1,0:T(8,128)(2,1)}), bf16[8,24,256]{2,1,0:T(8,128)(2,1)S(1)}, u32[]{:S(2)}, u32[]{:S(2)}) %all-to-all-start.6) | async-done | bytes 98336 | tf_op jit(solution)/shard_map/all_to_all | solution.py:37
  192.2 0.7 broadcast_in_dim.11
  192.9 4.5 %all-to-all-start.7 = ((bf16[16,24,256]{2,1,0:T(8,128)(2,1)}), bf16[16,24,256]{2,1,0:T(8,128)(2,1)S(1)}, u32[]{:S(2)}, u32[]{:S(2)}) async-start(bf16[16,24,256]{2,1,0:T(8,128)(2,1)} %broadcast_in_dim.11), calls=%async_computation.7 | async-start | bytes 393216 | tf_op jit(solution)/shard_map/all_to_all | solution.py:43
  197.6 0.2 fusion.13
  197.9 4.5 %collective-permute-start.9 = (bf16[384,96]{0,1:T(8,128)(2,1)S(1)}, bf16[384,96]{0,1:T(8,128)(2,1)S(1)}, u32[]{:S(2)}, u32[]{:S(2)}) collective-permute-start(bf16[384,96]{0,1:T(8,128)(2,1)S(1)} %fusion.13), channel_id=1, source_target_pairs={{0,1},{1,0},{2,3},{3,2},{4,5},{5,4},{6,7},{7,6},{8,9},{9,8},{10,11... | collective-permute-start | bytes 221192 | tf_op jit(solution)/shard_map/ppermute | solution.py:174
  202.4 0.9 copy.20
  203.3 0.9 all-to-all-done.7
  204.4 0.7 copy.21
  205.1 1.4 collective-permute-done.9
  206.5 0.9 fusion.11
  (49 shorter events, 0.9 us)
Async XLA Ops:
  0.6 1.0 copy-start
  0.6 2.3 %copy-start.1 = (bf16[384,512]{1,0:T(8,128)(2,1)S(1)}, bf16[384,512]{1,0:T(8,128)(2,1)}, u32[]{:S(2)}) copy-start(bf16[384,512]{1,0:T(8,128)(2,1)} %param.11) | copy-start | bytes 1179652
  1.6 1.7 copy-start.4
  3.0 1.0 copy-start.5
  4.3 16.3 %copy-start.2 = (bf16[384,512]{1,0:T(8,128)(2,1)S(1)}, bf16[384,512]{1,0:T(8,128)(2,1)}, u32[]{:S(2)}) copy-start(bf16[384,512]{1,0:T(8,128)(2,1)} %param.10) | copy-start | bytes 1179652
  4.4 18.1 %collective-permute-start = (bf16[8,96,512]{2,1,0:T(8,128)(2,1)S(1)}, bf16[8,96,512]{2,1,0:T(8,128)(2,1)S(1)}, u32[]{:S(2)}, u32[]{:S(2)}) collective-permute-start(bf16[8,96,512]{2,1,0:T(8,128)(2,1)S(1)} %pad_maximum_fusion), channel_id=1, source_target_pairs={{0,64},{64,0},{128,192},{192,128},{256,320},{320,256},{384,448},{4... | collective-permute-start | bytes 2359304 | tf_op jit(solution)/shard_map/ppermute | solution.py:61
  23.6 16.6 %all-to-all-start = ((bf16[8,96,512]{2,1,0:T(8,128)(2,1)}), bf16[8,96,512]{2,1,0:T(8,128)(2,1)S(1)}, u32[]{:S(2)}, u32[]{:S(2)}) async-start(bf16[8,96,512]{2,1,0:T(8,128)(2,1)} %add_convert_fusion), calls=%async_computation | async-start | bytes 1572864 | tf_op jit(solution)/shard_map/all_to_all | solution.py:37
  27.1 13.2 %collective-permute-start.1 = (bf16[384,512]{1,0:T(8,128)(2,1)S(1)}, bf16[384,512]{1,0:T(8,128)(2,1)}, u32[]{:S(2)}, u32[]{:S(2)}) collective-permute-start(bf16[384,512]{1,0:T(8,128)(2,1)S(1)} %copy-done.2), channel_id=1, source_target_pairs={{0,64},{64,0},{128,192},{192,128},{256,320},{320,256},{384,448},{4... | collective-permute-start | bytes 1179656 | tf_op jit(solution)/shard_map/ppermute | solution.py:61
  29.4 10.9 %collective-permute-start.2 = (bf16[384,512]{1,0:T(8,128)(2,1)S(1)}, bf16[384,512]{1,0:T(8,128)(2,1)}, u32[]{:S(2)}, u32[]{:S(2)}) collective-permute-start(bf16[384,512]{1,0:T(8,128)(2,1)S(1)} %copy-done.1), channel_id=1, source_target_pairs={{0,64},{64,0},{128,192},{192,128},{256,320},{320,256},{384,448},{4... | collective-permute-start | bytes 1179656 | tf_op jit(solution)/shard_map/ppermute | solution.py:61
  31.5 8.8 %collective-permute-start.4 = (bf16[256,384]{1,0:T(8,128)(2,1)S(1)}, bf16[256,384]{1,0:T(8,128)(2,1)S(1)}, u32[]{:S(2)}, u32[]{:S(2)}) collective-permute-start(bf16[256,384]{1,0:T(8,128)(2,1)S(1)} %get-tuple-element.35), channel_id=1, source_target_pairs={{0,64},{64,0},{128,192},{192,128},{256,320},{320,256},{384,448},{4... | collective-permute-start | bytes 589832 | tf_op jit(solution)/shard_map/ppermute | solution.py:61
  33.8 6.5 %collective-permute-start.3 = (bf16[384,192]{0,1:T(8,128)(2,1)}, bf16[384,192]{0,1:T(8,128)(2,1)S(1)}, u32[]{:S(2)}, u32[]{:S(2)}) collective-permute-start(bf16[384,192]{0,1:T(8,128)(2,1)} %param.13), channel_id=1, source_target_pairs={{0,64},{64,0},{128,192},{192,128},{256,320},{320,256},{384,448},{4... | collective-permute-start | bytes 442376 | tf_op jit(solution)/shard_map/ppermute | solution.py:61
  40.3 13.1 %copy-start.12 = (bf16[384,192]{0,1:T(8,128)(2,1)}, bf16[384,192]{0,1:T(8,128)(2,1)S(1)}, u32[]{:S(2)}) copy-start(bf16[384,192]{0,1:T(8,128)(2,1)S(1)} %collective-permute-done.3) | copy-start | bytes 442372
  40.3 0.7 copy-start.10
  56.8 32.4 %all-to-all-start.2 = ((bf16[4,128,384]{2,1,0:T(8,128)(2,1)}), bf16[4,128,384]{2,1,0:T(8,128)(2,1)S(1)}, u32[]{:S(2)}, u32[]{:S(2)}) async-start(bf16[4,128,384]{2,1,0:T(8,128)(2,1)} %pad_maximum_fusion.2), calls=%async_computation.2 | async-start | bytes 786432 | tf_op jit(solution)/shard_map/all_to_all | solution.py:37
  66.1 23.8 %collective-permute-start.5 = (bf16[8,64,512]{2,1,0:T(8,128)(2,1)S(1)}, bf16[8,64,512]{2,1,0:T(8,128)(2,1)}, u32[]{:S(2)}, u32[]{:S(2)}) collective-permute-start(bf16[8,64,512]{2,1,0:T(8,128)(2,1)S(1)} %all_to_all.40), channel_id=1, source_target_pairs={{0,64},{64,0},{128,192},{192,128},{256,320},{320,256},{384,448},{4... | collective-permute-start | bytes 1572872 | tf_op jit(solution)/shard_map/ppermute | solution.py:61
  91.0 16.2 %copy-start.7 = (bf16[8,32,512]{2,1,0:T(8,128)(2,1)}, bf16[8,32,512]{2,1,0:T(8,128)(2,1)S(1)}, u32[]{:S(2)}) copy-start(bf16[8,32,512]{2,1,0:T(8,128)(2,1)S(1)} %get-tuple-element.81) | copy-start | bytes 786436
  91.0 33.6 %all-to-all-start.3 = ((bf16[8,16,384]{2,1,0:T(8,128)(2,1)}), bf16[8,16,384]{2,1,0:T(8,128)(2,1)}, u32[]{:S(2)}, u32[]{:S(2)}) async-start(bf16[8,16,384]{2,1,0:T(8,128)(2,1)} %bitcast.14), calls=%async_computation.3 | async-start | bytes 196608 | tf_op jit(solution)/shard_map/all_to_all | solution.py:37
  106.8 4.8 %copy-start.11 = (bf16[256,384]{1,0:T(8,128)(2,1)S(1)}, bf16[256,384]{1,0:T(8,128)(2,1)}, u32[]{:S(2)}) copy-start(bf16[256,384]{1,0:T(8,128)(2,1)} %copy-done.10) | copy-start | bytes 589828
  107.2 18.3 %collective-permute-start.6 = (bf16[768,256]{1,0:T(8,128)(2,1)S(1)}, bf16[768,256]{1,0:T(8,128)(2,1)}, u32[]{:S(2)}, u32[]{:S(2)}) collective-permute-start(bf16[768,256]{1,0:T(8,128)(2,1)S(1)} %pad_maximum_fusion.3), channel_id=1, source_target_pairs={{0,1},{1,0},{2,3},{3,2},{4,5},{5,4},{6,7},{7,6},{8,9},{9,8},{10,11... | collective-permute-start | bytes 1179656 | tf_op jit(solution)/shard_map/ppermute | solution.py:134
  111.8 30.3 %copy-start.6 = (bf16[512,512]{1,0:T(8,128)(2,1)S(1)}, bf16[512,512]{1,0:T(8,128)(2,1)}, u32[]{:S(2)}) copy-start(bf16[512,512]{1,0:T(8,128)(2,1)} %all_gather.3) | copy-start | bytes 1572868
  112.3 34.7 %copy-start.8 = (bf16[8,32,512]{2,1,0:T(8,128)(2,1)S(1)}, bf16[8,32,512]{2,1,0:T(8,128)(2,1)}, u32[]{:S(2)}) copy-start(bf16[8,32,512]{2,1,0:T(8,128)(2,1)} %copy-done.7) | copy-start | bytes 786436
  126.2 34.0 %all-to-all-start.4 = ((bf16[8,16,384]{2,1,0:T(8,128)(2,1)}), bf16[8,16,384]{2,1,0:T(8,128)(2,1)S(1)}, u32[]{:S(2)}, u32[]{:S(2)}) async-start(bf16[8,16,384]{2,1,0:T(8,128)(2,1)} %broadcast_in_dim.9), calls=%async_computation.4 | async-start | bytes 196608 | tf_op jit(solution)/shard_map/all_to_all | solution.py:43
  142.4 8.4 %collective-permute-start.7 = (bf16[384,256]{0,1:T(8,128)(2,1)S(1)}, bf16[384,256]{0,1:T(8,128)(2,1)S(1)}, u32[]{:S(2)}, u32[]{:S(2)}) collective-permute-start(bf16[384,256]{0,1:T(8,128)(2,1)S(1)} %fusion.10), channel_id=1, source_target_pairs={{0,1},{1,0},{2,3},{3,2},{4,5},{5,4},{6,7},{7,6},{8,9},{9,8},{10,11... | collective-permute-start | bytes 589832 | tf_op jit(solution)/shard_map/ppermute | solution.py:143
  160.9 12.8 %all-to-all-start.5 = ((bf16[4,128,384]{2,1,0:T(8,128)(2,1)}), bf16[4,128,384]{2,1,0:T(8,128)(2,1)S(1)}, u32[]{:S(2)}, u32[]{:S(2)}) async-start(bf16[4,128,384]{2,1,0:T(8,128)(2,1)} %broadcast_in_dim.10), calls=%async_computation.5 | async-start | bytes 786432 | tf_op jit(solution)/shard_map/all_to_all | solution.py:43
  169.4 5.5 %copy-start.13 = (bf16[384,192]{0,1:T(8,128)(2,1)S(1)}, bf16[384,192]{0,1:T(8,128)(2,1)}, u32[]{:S(2)}) copy-start(bf16[384,192]{0,1:T(8,128)(2,1)} %copy-done.12) | copy-start | bytes 442372
  175.8 21.7 %collective-permute-start.8 = (bf16[256,384]{1,0:T(8,128)(2,1)S(1)}, bf16[256,384]{1,0:T(8,128)(2,1)S(1)}, u32[]{:S(2)}, u32[]{:S(2)}) collective-permute-start(bf16[256,384]{1,0:T(8,128)(2,1)S(1)} %bitcast.98), channel_id=1, source_target_pairs={{0,64},{64,0},{128,192},{192,128},{256,320},{320,256},{384,448},{4... | collective-permute-start | bytes 589832 | tf_op jit(solution)/shard_map/ppermute | solution.py:61
  183.6 8.6 %all-to-all-start.6 = ((bf16[8,24,256]{2,1,0:T(8,128)(2,1)}), bf16[8,24,256]{2,1,0:T(8,128)(2,1)S(1)}, u32[]{:S(2)}, u32[]{:S(2)}) async-start(bf16[8,24,256]{2,1,0:T(8,128)(2,1)} %bitcast.27), calls=%async_computation.6 | async-start | bytes 196608 | tf_op jit(solution)/shard_map/all_to_all | solution.py:37
  187.0 10.6 %copy-start.9 = (bf16[512,192]{0,1:T(8,128)(2,1)S(1)}, bf16[512,192]{0,1:T(8,128)(2,1)}, u32[]{:S(2)}) copy-start(bf16[512,192]{0,1:T(8,128)(2,1)} %param.8) | copy-start | bytes 589828
  192.9 11.3 %all-to-all-start.7 = ((bf16[16,24,256]{2,1,0:T(8,128)(2,1)}), bf16[16,24,256]{2,1,0:T(8,128)(2,1)S(1)}, u32[]{:S(2)}, u32[]{:S(2)}) async-start(bf16[16,24,256]{2,1,0:T(8,128)(2,1)} %broadcast_in_dim.11), calls=%async_computation.7 | async-start | bytes 393216 | tf_op jit(solution)/shard_map/all_to_all | solution.py:43
  197.6 8.9 %copy-start.3 = (bf16[512,384]{1,0:T(8,128)(2,1)}, bf16[512,384]{1,0:T(8,128)(2,1)S(1)}, u32[]{:S(2)}) copy-start(bf16[512,384]{1,0:T(8,128)(2,1)S(1)} %maximum_select_fusion) | copy-start | bytes 1179652
  197.9 8.6 %collective-permute-start.9 = (bf16[384,96]{0,1:T(8,128)(2,1)S(1)}, bf16[384,96]{0,1:T(8,128)(2,1)S(1)}, u32[]{:S(2)}, u32[]{:S(2)}) collective-permute-start(bf16[384,96]{0,1:T(8,128)(2,1)S(1)} %fusion.13), channel_id=1, source_target_pairs={{0,1},{1,0},{2,3},{3,2},{4,5},{5,4},{6,7},{7,6},{8,9},{9,8},{10,11... | collective-permute-start | bytes 221192 | tf_op jit(solution)/shard_map/ppermute | solution.py:174

commit v3 on v2

--- a/solution.py
+++ b/solution.py
@@ -10,7 +10,7 @@
 def swiglu_grads(gate_pre, up_pre, hidden_grad):
     sigmoid_gate = jax.nn.sigmoid(gate_pre)
     activated = gate_pre * sigmoid_gate
-    hidden = (activated * up_pre).astype(BF16)
+    hidden = activated * up_pre
     up_grad = (hidden_grad * activated).astype(BF16)
     slope = sigmoid_gate * (1.0 + gate_pre * (1.0 - sigmoid_gate))
     gate_grad = (hidden_grad * up_pre * slope).astype(BF16)
@@ -83,8 +83,9 @@
     gate_share, up_share, hid_share = swiglu_grads(
         total[:share], total[share : 2 * share], total[2 * share :]
     )
-    hid_all = lax.all_gather(hid_share.astype(F32), "row", axis=0, tiled=True)
     mine = gather(jnp.concatenate([gate_share, up_share]), chips, "row", chip_groups)
+    mine, hid_share = tie((mine, hid_share))
+    hid_all = lax.all_gather(hid_share, "row", axis=0, tiled=True)
 
     def split(x):
         return [
@@ -94,16 +95,16 @@
 
     gate_mine, up_mine = split(mine)
 
-    near, far = 4, cols // 4
+    near, far = 8, cols // 8
 
     def place(r, k, j):
-        return r * cols + (k * near + j + 2 * (r % 2)) % cols
+        return r * cols + (k * near + j + 4 * (r % 2)) % cols
 
     near_groups = [[place(r, k, j) for j in range(near)] for r in range(rows) for k in range(far)]
     far_groups = [[place(r, k, j) for k in range(far)] for r in range(rows) for j in range(near)]
     both = ("row", "col")
-    spot = (lax.axis_index("col") + cols - 2 * core) % cols
-    piece = tokens // cols
+    spot = (lax.axis_index("col") + cols - 4 * core) % near
+    piece = tokens // near
 
     def pair_blocks(own, away):
         return jnp.concatenate([x.reshape(near, half // near, width) for x in (own, away)], axis=1)
@@ -120,37 +121,34 @@
 
     norm_factor = (tokens * lax.axis_size("seq")) ** (-0.5)
 
-    def wgrad(pairs, which):
+    def wgrad(pairs, which, factor=norm_factor):
         size = pairs[0][1].shape[1] // 2
         terms = [
             contract_rows(a, lax.dynamic_slice_in_dim(b, which * size, size, 1))
             for a, b in pairs
         ]
-        return sum(terms) * norm_factor
+        return sum(terms) * factor
 
     gate_pairs = ((in_mine, gate_mine), (in_other, gate_other))
     up_pairs = ((in_mine, up_mine), (in_other, up_other))
     sent = jnp.concatenate([wgrad(p, 1 - seq).astype(BF16) for p in (gate_pairs, up_pairs)])
     received = lax.ppermute(sent, "seq", seq_swap)
 
-    far_sum = scatter_sum(near_sum.reshape(far, piece, width), both, far_groups)
+    group_sums = gather(near_sum, far, both, far_groups)
+    far_sum = jnp.sum(group_sums.astype(F32), axis=0)
     far_sum, received, hid_all = tie((far_sum, received, hid_all))
-    out_all = pair_blocks(out_mine, out_far).reshape(cols, piece, width)
-    out_piece = lax.dynamic_index_in_dim(out_all, (spot % near) * far + spot // near, 0, False)
+    out_piece = lax.dynamic_index_in_dim(pair_blocks(out_mine, out_far), spot, 0, False)
     resid_piece = (out_piece.astype(F32) + far_sum).astype(BF16)
     out_rows = out_grad.reshape(2, chips, share, width).swapaxes(0, 1).reshape(tokens, width)
-    down_pairs = ((out_rows, hid_all.astype(BF16)),)
-    down_received = lax.ppermute(wgrad(down_pairs, 1 - seq).astype(BF16), "seq", seq_swap)
+    down_pairs = ((out_rows, (hid_all * norm_factor).astype(BF16)),)
+    down_received = lax.ppermute(wgrad(down_pairs, 1 - seq, 1.0).astype(BF16), "seq", seq_swap)
     gate_wgrad = wgrad(gate_pairs, seq) + received[:width].astype(F32)
     up_wgrad = wgrad(up_pairs, seq) + received[width:].astype(F32)
-    resid_near = gather(resid_piece, far, both, far_groups).reshape(tokens // near, width)
-    resid_near, down_received, gate_wgrad, up_wgrad = tie(
-        (resid_near, down_received, gate_wgrad, up_wgrad)
+    resid_all = gather(resid_piece, near, both, near_groups)
+    resid_all, down_received, gate_wgrad, up_wgrad = tie(
+        (resid_all, down_received, gate_wgrad, up_wgrad)
     )
-    down_wgrad = wgrad(down_pairs, seq) + down_received.astype(F32)
-
-    resid_all = gather(resid_near, near, both, near_groups)
-    resid_all, down_wgrad = tie((resid_all, down_wgrad))
+    down_wgrad = wgrad(down_pairs, seq, 1.0) + down_received.astype(F32)
     resid_all = resid_all.reshape(near, 2, half // near, width)
     resid_mine, resid_far = (resid_all[:, i].reshape(half, width) for i in range(2))
 

time: 209 us -> 196 us (0.938)
  blocking collectives: 32.1 us -> 11.6 us
  between operations: 1.31 us -> 14.7 us
  waiting for transfers between devices: 38.7 us -> 32.8 us
  starting transfers between devices: 109 us -> 112 us
    all_gather x1 -> x0, blocking collectives: 20.5 us -> none  [per_device(): hid_all = lax.all_gather(hid_share.astype(F32), 'row', axis=0, tiled=True)]
    all_to_all x4 -> x3, starting transfers between devices: 31.8 us -> 17 us  [scatter_sum(): lax.all_to_all(parts, axis, 0, 0, tiled=True, axis_index_groups=groups)]
    all_to_all x3, starting transfers between devices: 28.7 us -> 39.6 us  [gather(): lax.all_to_all(copies, axis, 0, 0, tiled=True, axis_index_groups=groups)]
    ppermute x7, starting transfers between devices: 34.6 us -> 41.5 us  [swap(): return lax.ppermute(x, 'row', core_swap)]
    all_to_all x3, waiting for transfers between devices: 14.5 us -> 8.52 us  [gather(): lax.all_to_all(copies, axis, 0, 0, tiled=True, axis_index_groups=groups)]
    all_to_all x4 -> x3, waiting for transfers between devices: 21.8 us -> 16.6 us  [scatter_sum(): lax.all_to_all(parts, axis, 0, 0, tiled=True, axis_index_groups=groups)]
    ppermute x1, waiting for transfers between devices: 0.01 us -> 2.61 us  [per_device(): received = lax.ppermute(sent, 'seq', seq_swap)]
  transfers between devices with their start and end apart: 17 -> 17, of which waited for: 8 -> 10; matrix products, arithmetic and copies ran while one was open for 6% -> 5% of each run, Pallas kernels for 0% -> 0%
where the time goes in v3:
time: 196 us; the launch traced here: 194 us
  starting transfers between devices  112 us (57%)
  waiting for transfers between devices  32.8 us (17%)
  between operations  14.7 us (8%)
  matrix products  13.4 us (7%)
  blocking collectives  11.6 us (6%)
  local copies, waits for them, and re-layouts  7.18 us (4%)
  other arithmetic  3.16 us (2%)
    ppermute x7, starting transfers between devices, swap(): return lax.ppermute(x, 'row', core_swap)  41.5 us
    all_to_all x3, starting transfers between devices, gather(): lax.all_to_all(copies, axis, 0, 0, tiled=True, axis_index_groups=groups)  39.6 us
    all_to_all x3, starting transfers between devices, scatter_sum(): lax.all_to_all(parts, axis, 0, 0, tiled=True, axis_index_groups=groups)  17 us
    all_to_all x3, waiting for transfers between devices, scatter_sum(): lax.all_to_all(parts, axis, 0, 0, tiled=True, axis_index_groups=groups)  16.6 us
    all_to_all x1, blocking collectives, gather(): lax.all_to_all(copies, axis, 0, 0, tiled=True, axis_index_groups=groups)  11.6 us
    all_to_all x3, waiting for transfers between devices, gather(): lax.all_to_all(copies, axis, 0, 0, tiled=True, axis_index_groups=groups)  8.52 us
    dot_general x12, matrix products, contract_rows(): lax.dot_general(first, second, (((0,), (0,)), ((), ())), preferred_elemen...  5.34 us
    ppermute x1, starting transfers between devices, per_device(): lax.ppermute(wgrad(down_pairs, 1 - seq, 1.0).astype(BF16), 'seq', seq_swap)  4.89 us
  transfers between devices with their start and end apart: 17, of which 10 were waited for; matrix products, arithmetic and copies ran while one was open for 5% of the time, Pallas kernels for 0%

profile of v3, /device:TPU:1, one launch (start us, length us, event | category | flops | bytes accessed | tf_op | source)
XLA Modules:
  0.0 194.4 jit_solution(5553676239687432855)
XLA Ops:
  7.2 0.9 copy-done
  8.2 1.3 convolution_convert_fusion.2
  9.5 0.3 convolution_convert_fusion.1
  9.9 0.3 convolution_convert_fusion
  10.3 16.1 %collective-permute-start = (bf16[8,96,512]{2,1,0:T(8,128)(2,1)S(1)}, bf16[8,96,512]{2,1,0:T(8,128)(2,1)S(1)}, u32[]{:S(2)}, u32[]{:S(2)}) collective-permute-start(bf16[8,96,512]{2,1,0:T(8,128)(2,1)S(1)} %pad_maximum_fusion), channel_id=1, source_target_pairs={{0,64},{64,0},{128,192},{192,128},{256,320},{320,256},{384,448},{4... | collective-permute-start | bytes 2359304 | tf_op jit(solution)/shard_map/ppermute | solution.py:61
  26.4 0.3 convolution_convert_fusion.5
  26.7 0.3 convolution_convert_fusion.4
  27.0 0.3 convolution_convert_fusion.3
  27.3 1.0 collective-permute-done
  28.2 1.1 add_convert_fusion
  29.4 3.5 %all-to-all-start = ((bf16[8,96,512]{2,1,0:T(8,128)(2,1)}), bf16[8,96,512]{2,1,0:T(8,128)(2,1)S(1)}, u32[]{:S(2)}, u32[]{:S(2)}) async-start(bf16[8,96,512]{2,1,0:T(8,128)(2,1)} %add_convert_fusion), calls=%async_computation | async-start | bytes 1572864 | tf_op jit(solution)/shard_map/all_to_all | solution.py:37
  32.9 2.3 %collective-permute-start.1 = (bf16[384,512]{1,0:T(8,128)(2,1)S(1)}, bf16[384,512]{1,0:T(8,128)(2,1)}, u32[]{:S(2)}, u32[]{:S(2)}) collective-permute-start(bf16[384,512]{1,0:T(8,128)(2,1)S(1)} %copy-done.2), channel_id=1, source_target_pairs={{0,64},{64,0},{128,192},{192,128},{256,320},{320,256},{384,448},{4... | collective-permute-start | bytes 1179656 | tf_op jit(solution)/shard_map/ppermute | solution.py:61
  35.2 2.0 %collective-permute-start.2 = (bf16[384,512]{1,0:T(8,128)(2,1)S(1)}, bf16[384,512]{1,0:T(8,128)(2,1)}, u32[]{:S(2)}, u32[]{:S(2)}) collective-permute-start(bf16[384,512]{1,0:T(8,128)(2,1)S(1)} %copy-done.1), channel_id=1, source_target_pairs={{0,64},{64,0},{128,192},{192,128},{256,320},{320,256},{384,448},{4... | collective-permute-start | bytes 1179656 | tf_op jit(solution)/shard_map/ppermute | solution.py:61
  37.3 2.3 %collective-permute-start.4 = (bf16[256,384]{1,0:T(8,128)(2,1)S(1)}, bf16[256,384]{1,0:T(8,128)(2,1)S(1)}, u32[]{:S(2)}, u32[]{:S(2)}) collective-permute-start(bf16[256,384]{1,0:T(8,128)(2,1)S(1)} %get-tuple-element.35), channel_id=1, source_target_pairs={{0,64},{64,0},{128,192},{192,128},{256,320},{320,256},{384,448},{4... | collective-permute-start | bytes 589832 | tf_op jit(solution)/shard_map/ppermute | solution.py:61
  39.5 2.0 %collective-permute-start.3 = (bf16[384,192]{0,1:T(8,128)(2,1)}, bf16[384,192]{0,1:T(8,128)(2,1)S(1)}, u32[]{:S(2)}, u32[]{:S(2)}) collective-permute-start(bf16[384,192]{0,1:T(8,128)(2,1)} %param.13), channel_id=1, source_target_pairs={{0,64},{64,0},{128,192},{192,128},{256,320},{320,256},{384,448},{4... | collective-permute-start | bytes 442376 | tf_op jit(solution)/shard_map/ppermute | solution.py:61
  41.6 4.3 %all-to-all-done = bf16[8,96,512]{2,1,0:T(8,128)(2,1)S(1)} async-done(((bf16[8,96,512]{2,1,0:T(8,128)(2,1)}), bf16[8,96,512]{2,1,0:T(8,128)(2,1)S(1)}, u32[]{:S(2)}, u32[]{:S(2)}) %all-to-all-start) | async-done | bytes 786464 | tf_op jit(solution)/shard_map/all_to_all | solution.py:37
  46.1 0.7 slice_multiply_fusion
  46.9 11.6 %all_to_all.35 = bf16[8,64,512]{2,1,0:T(8,128)(2,1)S(1)} all-to-all(bf16[8,64,512]{2,1,0:T(8,128)(2,1)S(1)} %broadcast_in_dim.8), channel_id=1, replica_groups={{0,128,256,384,512,640,768,896},{64,192,320,448,576,704,832,960},{1,129..., dimensions={0} | all-to-all | bytes 1048576 | tf_op jit(solution)/shard_map/all_to_all | solution.py:43
  58.5 0.3 fusion.64
  58.8 0.3 fusion.4
  59.2 1.3 fusion.65
  60.5 1.3 fusion.5
  61.8 0.8 pad_maximum_fusion.1
  62.6 10.1 %all-to-all-start.2 = ((bf16[8,64,384]{2,1,0:T(8,128)(2,1)}), bf16[8,64,384]{2,1,0:T(8,128)(2,1)S(1)}, u32[]{:S(2)}, u32[]{:S(2)}) async-start(bf16[8,64,384]{2,1,0:T(8,128)(2,1)} %pad_maximum_fusion.1), calls=%async_computation.2 | async-start | bytes 786432 | tf_op jit(solution)/shard_map/all_to_all | solution.py:37
  72.7 0.7 all-gather.2.cloned.1.call-update
  73.4 1.9 collective-permute-start.5
  75.4 0.3 fusion.26
  75.6 7.1 %all-to-all-done.2 = bf16[8,64,384]{2,1,0:T(8,128)(2,1)S(1)} async-done(((bf16[8,64,384]{2,1,0:T(8,128)(2,1)}), bf16[8,64,384]{2,1,0:T(8,128)(2,1)S(1)}, u32[]{:S(2)}, u32[]{:S(2)}) %all-to-all-start.2) | async-done | bytes 393248 | tf_op jit(solution)/shard_map/all_to_all | solution.py:37
  82.8 0.7 broadcast_in_dim.9
  83.5 21.8 %all-to-all-start.3 = ((bf16[4,64,384]{2,1,0:T(8,128)(2,1)}), bf16[4,64,384]{2,1,0:T(8,128)(2,1)S(1)}, u32[]{:S(2)}, u32[]{:S(2)}) async-start(bf16[4,64,384]{2,1,0:T(8,128)(2,1)} %broadcast_in_dim.9), calls=%async_computation.3 | async-start | bytes 393216 | tf_op jit(solution)/shard_map/all_to_all | solution.py:43
  105.3 0.2 fusion.23
  105.5 1.1 fusion.61
  106.6 0.3 fusion.7
  106.9 0.3 fusion.6
  107.4 4.6 %collective-permute-start.6 = (bf16[768,256]{1,0:T(8,128)(2,1)S(1)}, bf16[768,256]{1,0:T(8,128)(2,1)S(1)}, u32[]{:S(2)}, u32[]{:S(2)}) collective-permute-start(bf16[768,256]{1,0:T(8,128)(2,1)S(1)} %pad_maximum_fusion.2), channel_id=1, source_target_pairs={{0,1},{1,0},{2,3},{3,2},{4,5},{5,4},{6,7},{7,6},{8,9},{9,8},{10,11... | collective-permute-start | bytes 1179656 | tf_op jit(solution)/shard_map/ppermute | solution.py:135
  112.0 7.3 %all-to-all-done.3 = bf16[4,64,384]{2,1,0:T(8,128)(2,1)S(1)} async-done(((bf16[4,64,384]{2,1,0:T(8,128)(2,1)}), bf16[4,64,384]{2,1,0:T(8,128)(2,1)S(1)}, u32[]{:S(2)}, u32[]{:S(2)}) %all-to-all-start.3) | async-done | bytes 196640 | tf_op jit(solution)/shard_map/all_to_all | solution.py:43
  119.3 1.3 all-gather.2.cloned.1.call-done
  120.7 2.6 %collective-permute-done.6 = bf16[768,256]{1,0:T(8,128)(2,1)S(1)} collective-permute-done((bf16[768,256]{1,0:T(8,128)(2,1)S(1)}, bf16[768,256]{1,0:T(8,128)(2,1)S(1)}, u32[]{:S(2)}, u32[]{:S(2)}) %collective-permute-start.6) | collective-permute-done | bytes 393248 | tf_op jit(solution)/shard_map/ppermute | solution.py:135
  123.3 0.8 broadcast_in_dim.10
  124.2 13.3 %all-to-all-start.4 = ((bf16[8,64,384]{2,1,0:T(8,128)(2,1)}), bf16[8,64,384]{2,1,0:T(8,128)(2,1)S(1)}, u32[]{:S(2)}, u32[]{:S(2)}) async-start(bf16[8,64,384]{2,1,0:T(8,128)(2,1)} %broadcast_in_dim.10), calls=%async_computation.4 | async-start | bytes 786432 | tf_op jit(solution)/shard_map/all_to_all | solution.py:43
  137.5 0.3 fusion.17
  137.8 0.3 fusion.20
  138.1 0.7 copy-done.6
  138.9 0.3 fusion.8
  139.2 4.9 %collective-permute-start.7 = (bf16[384,256]{0,1:T(8,128)(2,1)S(1)}, bf16[384,256]{0,1:T(8,128)(2,1)S(1)}, u32[]{:S(2)}, u32[]{:S(2)}) collective-permute-start(bf16[384,256]{0,1:T(8,128)(2,1)S(1)} %fusion.8), channel_id=1, source_target_pairs={{0,1},{1,0},{2,3},{3,2},{4,5},{5,4},{6,7},{7,6},{8,9},{9,8},{10,11... | collective-permute-start | bytes 589832 | tf_op jit(solution)/shard_map/ppermute | solution.py:144
  144.1 1.0 convert_add_fusion.1
  145.2 1.0 convert_add_fusion.2
  146.2 1.0 collective-permute-done.7
  147.2 1.1 convolution_bitcast_fusion.1
  148.4 0.9 fusion.10
  149.3 14.9 %collective-permute-start.8 = (bf16[256,384]{1,0:T(8,128)(2,1)S(1)}, bf16[256,384]{1,0:T(8,128)(2,1)S(1)}, u32[]{:S(2)}, u32[]{:S(2)}) collective-permute-start(bf16[256,384]{1,0:T(8,128)(2,1)S(1)} %bitcast.95), channel_id=1, source_target_pairs={{0,64},{64,0},{128,192},{192,128},{256,320},{320,256},{384,448},{4... | collective-permute-start | bytes 589832 | tf_op jit(solution)/shard_map/ppermute | solution.py:61
  164.2 3.4 %all-to-all-start.5 = ((bf16[8,24,256]{2,1,0:T(8,128)(2,1)}), bf16[8,24,256]{2,1,0:T(8,128)(2,1)S(1)}, u32[]{:S(2)}, u32[]{:S(2)}) async-start(bf16[8,24,256]{2,1,0:T(8,128)(2,1)} %bitcast.23), calls=%async_computation.5 | async-start | bytes 196608 | tf_op jit(solution)/shard_map/all_to_all | solution.py:37
  167.6 5.2 %all-to-all-done.5 = bf16[8,24,256]{2,1,0:T(8,128)(2,1)S(1)} async-done(((bf16[8,24,256]{2,1,0:T(8,128)(2,1)}), bf16[8,24,256]{2,1,0:T(8,128)(2,1)S(1)}, u32[]{:S(2)}, u32[]{:S(2)}) %all-to-all-start.5) | async-done | bytes 98336 | tf_op jit(solution)/shard_map/all_to_all | solution.py:37
  172.8 0.7 broadcast_in_dim.11
  173.5 4.5 %all-to-all-start.6 = ((bf16[16,24,256]{2,1,0:T(8,128)(2,1)}), bf16[16,24,256]{2,1,0:T(8,128)(2,1)S(1)}, u32[]{:S(2)}, u32[]{:S(2)}) async-start(bf16[16,24,256]{2,1,0:T(8,128)(2,1)} %broadcast_in_dim.11), calls=%async_computation.6 | async-start | bytes 393216 | tf_op jit(solution)/shard_map/all_to_all | solution.py:43
  178.2 0.2 fusion.11
  178.4 3.9 %collective-permute-start.9 = (bf16[384,96]{0,1:T(8,128)(2,1)S(1)}, bf16[384,96]{0,1:T(8,128)(2,1)S(1)}, u32[]{:S(2)}, u32[]{:S(2)}) collective-permute-start(bf16[384,96]{0,1:T(8,128)(2,1)S(1)} %fusion.11), channel_id=1, source_target_pairs={{0,1},{1,0},{2,3},{3,2},{4,5},{5,4},{6,7},{7,6},{8,9},{9,8},{10,11... | collective-permute-start | bytes 221192 | tf_op jit(solution)/shard_map/ppermute | solution.py:172
  182.4 0.3 convert_add_fusion
  182.7 0.9 copy.20
  183.6 1.2 all-to-all-done.6
  184.8 0.2 copy.19
  185.0 0.7 copy.21
  185.7 1.0 collective-permute-done.9
  186.7 0.9 fusion.9
  (57 shorter events, 1.1 us)
Async XLA Ops:
  7.2 1.0 copy-start
  7.2 2.3 %copy-start.1 = (bf16[384,512]{1,0:T(8,128)(2,1)S(1)}, bf16[384,512]{1,0:T(8,128)(2,1)}, u32[]{:S(2)}) copy-start(bf16[384,512]{1,0:T(8,128)(2,1)} %param.11) | copy-start | bytes 1179652
  7.2 2.7 %copy-start.4 = (bf16[512,384]{1,0:T(8,128)(2,1)S(1)}, bf16[512,384]{1,0:T(8,128)(2,1)}, u32[]{:S(2)}) copy-start(bf16[512,384]{1,0:T(8,128)(2,1)} %param.9) | copy-start | bytes 1179652
  8.2 1.7 copy-start.5
  9.9 16.4 %copy-start.2 = (bf16[384,512]{1,0:T(8,128)(2,1)S(1)}, bf16[384,512]{1,0:T(8,128)(2,1)}, u32[]{:S(2)}) copy-start(bf16[384,512]{1,0:T(8,128)(2,1)} %param.10) | copy-start | bytes 1179652
  10.3 18.0 %collective-permute-start = (bf16[8,96,512]{2,1,0:T(8,128)(2,1)S(1)}, bf16[8,96,512]{2,1,0:T(8,128)(2,1)S(1)}, u32[]{:S(2)}, u32[]{:S(2)}) collective-permute-start(bf16[8,96,512]{2,1,0:T(8,128)(2,1)S(1)} %pad_maximum_fusion), channel_id=1, source_target_pairs={{0,64},{64,0},{128,192},{192,128},{256,320},{320,256},{384,448},{4... | collective-permute-start | bytes 2359304 | tf_op jit(solution)/shard_map/ppermute | solution.py:61
  29.4 16.6 %all-to-all-start = ((bf16[8,96,512]{2,1,0:T(8,128)(2,1)}), bf16[8,96,512]{2,1,0:T(8,128)(2,1)S(1)}, u32[]{:S(2)}, u32[]{:S(2)}) async-start(bf16[8,96,512]{2,1,0:T(8,128)(2,1)} %add_convert_fusion), calls=%async_computation | async-start | bytes 1572864 | tf_op jit(solution)/shard_map/all_to_all | solution.py:37
  32.9 13.2 %collective-permute-start.1 = (bf16[384,512]{1,0:T(8,128)(2,1)S(1)}, bf16[384,512]{1,0:T(8,128)(2,1)}, u32[]{:S(2)}, u32[]{:S(2)}) collective-permute-start(bf16[384,512]{1,0:T(8,128)(2,1)S(1)} %copy-done.2), channel_id=1, source_target_pairs={{0,64},{64,0},{128,192},{192,128},{256,320},{320,256},{384,448},{4... | collective-permute-start | bytes 1179656 | tf_op jit(solution)/shard_map/ppermute | solution.py:61
  35.2 10.9 %collective-permute-start.2 = (bf16[384,512]{1,0:T(8,128)(2,1)S(1)}, bf16[384,512]{1,0:T(8,128)(2,1)}, u32[]{:S(2)}, u32[]{:S(2)}) collective-permute-start(bf16[384,512]{1,0:T(8,128)(2,1)S(1)} %copy-done.1), channel_id=1, source_target_pairs={{0,64},{64,0},{128,192},{192,128},{256,320},{320,256},{384,448},{4... | collective-permute-start | bytes 1179656 | tf_op jit(solution)/shard_map/ppermute | solution.py:61
  37.3 8.8 %collective-permute-start.4 = (bf16[256,384]{1,0:T(8,128)(2,1)S(1)}, bf16[256,384]{1,0:T(8,128)(2,1)S(1)}, u32[]{:S(2)}, u32[]{:S(2)}) collective-permute-start(bf16[256,384]{1,0:T(8,128)(2,1)S(1)} %get-tuple-element.35), channel_id=1, source_target_pairs={{0,64},{64,0},{128,192},{192,128},{256,320},{320,256},{384,448},{4... | collective-permute-start | bytes 589832 | tf_op jit(solution)/shard_map/ppermute | solution.py:61
  39.5 6.5 %collective-permute-start.3 = (bf16[384,192]{0,1:T(8,128)(2,1)}, bf16[384,192]{0,1:T(8,128)(2,1)S(1)}, u32[]{:S(2)}, u32[]{:S(2)}) collective-permute-start(bf16[384,192]{0,1:T(8,128)(2,1)} %param.13), channel_id=1, source_target_pairs={{0,64},{64,0},{128,192},{192,128},{256,320},{320,256},{384,448},{4... | collective-permute-start | bytes 442376 | tf_op jit(solution)/shard_map/ppermute | solution.py:61
  46.1 14.4 %copy-start.16 = (bf16[384,192]{0,1:T(8,128)(2,1)}, bf16[384,192]{0,1:T(8,128)(2,1)S(1)}, u32[]{:S(2)}) copy-start(bf16[384,192]{0,1:T(8,128)(2,1)S(1)} %collective-permute-done.3) | copy-start | bytes 442372
  46.1 0.7 copy-start.14
  62.6 20.1 %all-to-all-start.2 = ((bf16[8,64,384]{2,1,0:T(8,128)(2,1)}), bf16[8,64,384]{2,1,0:T(8,128)(2,1)S(1)}, u32[]{:S(2)}, u32[]{:S(2)}) async-start(bf16[8,64,384]{2,1,0:T(8,128)(2,1)} %pad_maximum_fusion.1), calls=%async_computation.2 | async-start | bytes 786432 | tf_op jit(solution)/shard_map/all_to_all | solution.py:37
  72.7 48.0 %all-gather.2.cloned.1.call-start = ((), (), s32[]{:S(2)}) async-start(), calls=%async_computation.7 | async-start | bytes 1114112 | tf_op jit(solution)/shard_map/all_gather | solution.py:88
  73.4 9.4 %collective-permute-start.5 = (bf16[8,64,512]{2,1,0:T(8,128)(2,1)S(1)}, bf16[8,64,512]{2,1,0:T(8,128)(2,1)}, u32[]{:S(2)}, u32[]{:S(2)}) collective-permute-start(bf16[8,64,512]{2,1,0:T(8,128)(2,1)S(1)} %all_to_all.35), channel_id=1, source_target_pairs={{0,64},{64,0},{128,192},{192,128},{256,320},{320,256},{384,448},{4... | collective-permute-start | bytes 1572872 | tf_op jit(solution)/shard_map/ppermute | solution.py:61
  83.5 35.8 %all-to-all-start.3 = ((bf16[4,64,384]{2,1,0:T(8,128)(2,1)}), bf16[4,64,384]{2,1,0:T(8,128)(2,1)S(1)}, u32[]{:S(2)}, u32[]{:S(2)}) async-start(bf16[4,64,384]{2,1,0:T(8,128)(2,1)} %broadcast_in_dim.9), calls=%async_computation.3 | async-start | bytes 393216 | tf_op jit(solution)/shard_map/all_to_all | solution.py:43
  106.6 0.7 copy-start.7
  106.6 0.8 copy-start.9
  106.9 16.4 %copy-start.15 = (bf16[256,384]{1,0:T(8,128)(2,1)S(1)}, bf16[256,384]{1,0:T(8,128)(2,1)}, u32[]{:S(2)}) copy-start(bf16[256,384]{1,0:T(8,128)(2,1)} %copy-done.14) | copy-start | bytes 589828
  107.4 15.9 %collective-permute-start.6 = (bf16[768,256]{1,0:T(8,128)(2,1)S(1)}, bf16[768,256]{1,0:T(8,128)(2,1)S(1)}, u32[]{:S(2)}, u32[]{:S(2)}) collective-permute-start(bf16[768,256]{1,0:T(8,128)(2,1)S(1)} %pad_maximum_fusion.2), channel_id=1, source_target_pairs={{0,1},{1,0},{2,3},{3,2},{4,5},{5,4},{6,7},{7,6},{8,9},{9,8},{10,11... | collective-permute-start | bytes 1179656 | tf_op jit(solution)/shard_map/ppermute | solution.py:135
  123.3 14.2 %copy-start.11 = (bf16[768,256]{1,0:T(8,128)(2,1)}, bf16[768,256]{1,0:T(8,128)(2,1)S(1)}, u32[]{:S(2)}) copy-start(bf16[768,256]{1,0:T(8,128)(2,1)S(1)} %collective-permute-done.6) | copy-start | bytes 1179652
  124.2 23.0 %all-to-all-start.4 = ((bf16[8,64,384]{2,1,0:T(8,128)(2,1)}), bf16[8,64,384]{2,1,0:T(8,128)(2,1)S(1)}, u32[]{:S(2)}, u32[]{:S(2)}) async-start(bf16[8,64,384]{2,1,0:T(8,128)(2,1)} %broadcast_in_dim.10), calls=%async_computation.4 | async-start | bytes 786432 | tf_op jit(solution)/shard_map/all_to_all | solution.py:43
  137.5 1.2 copy-start.6
  138.7 5.4 %copy-start.10 = (bf16[8,32,512]{2,1,0:T(8,128)(2,1)S(1)}, bf16[8,32,512]{2,1,0:T(8,128)(2,1)}, u32[]{:S(2)}) copy-start(bf16[8,32,512]{2,1,0:T(8,128)(2,1)} %copy-done.9) | copy-start | bytes 786436
  138.7 5.4 %copy-start.12 = (bf16[768,256]{1,0:T(8,128)(2,1)S(1)}, bf16[768,256]{1,0:T(8,128)(2,1)}, u32[]{:S(2)}) copy-start(bf16[768,256]{1,0:T(8,128)(2,1)} %copy-done.11) | copy-start | bytes 1179652
  138.9 6.3 %copy-start.8 = (bf16[8,32,512]{2,1,0:T(8,128)(2,1)S(1)}, bf16[8,32,512]{2,1,0:T(8,128)(2,1)}, u32[]{:S(2)}) copy-start(bf16[8,32,512]{2,1,0:T(8,128)(2,1)} %copy-done.7) | copy-start | bytes 786436
  139.2 7.9 %collective-permute-start.7 = (bf16[384,256]{0,1:T(8,128)(2,1)S(1)}, bf16[384,256]{0,1:T(8,128)(2,1)S(1)}, u32[]{:S(2)}, u32[]{:S(2)}) collective-permute-start(bf16[384,256]{0,1:T(8,128)(2,1)S(1)} %fusion.8), channel_id=1, source_target_pairs={{0,1},{1,0},{2,3},{3,2},{4,5},{5,4},{6,7},{7,6},{8,9},{9,8},{10,11... | collective-permute-start | bytes 589832 | tf_op jit(solution)/shard_map/ppermute | solution.py:144
  145.2 3.2 %copy-start.17 = (bf16[384,192]{0,1:T(8,128)(2,1)S(1)}, bf16[384,192]{0,1:T(8,128)(2,1)}, u32[]{:S(2)}) copy-start(bf16[384,192]{0,1:T(8,128)(2,1)} %copy-done.16) | copy-start | bytes 442372
  148.4 29.8 %copy-start.13 = (bf16[512,192]{0,1:T(8,128)(2,1)S(1)}, bf16[512,192]{0,1:T(8,128)(2,1)}, u32[]{:S(2)}) copy-start(bf16[512,192]{0,1:T(8,128)(2,1)} %param.8) | copy-start | bytes 589828
  149.3 28.8 %collective-permute-start.8 = (bf16[256,384]{1,0:T(8,128)(2,1)S(1)}, bf16[256,384]{1,0:T(8,128)(2,1)S(1)}, u32[]{:S(2)}, u32[]{:S(2)}) collective-permute-start(bf16[256,384]{1,0:T(8,128)(2,1)S(1)} %bitcast.95), channel_id=1, source_target_pairs={{0,64},{64,0},{128,192},{192,128},{256,320},{320,256},{384,448},{4... | collective-permute-start | bytes 589832 | tf_op jit(solution)/shard_map/ppermute | solution.py:61
  164.2 8.6 %all-to-all-start.5 = ((bf16[8,24,256]{2,1,0:T(8,128)(2,1)}), bf16[8,24,256]{2,1,0:T(8,128)(2,1)S(1)}, u32[]{:S(2)}, u32[]{:S(2)}) async-start(bf16[8,24,256]{2,1,0:T(8,128)(2,1)} %bitcast.23), calls=%async_computation.5 | async-start | bytes 196608 | tf_op jit(solution)/shard_map/all_to_all | solution.py:37
  173.5 11.3 %all-to-all-start.6 = ((bf16[16,24,256]{2,1,0:T(8,128)(2,1)}), bf16[16,24,256]{2,1,0:T(8,128)(2,1)S(1)}, u32[]{:S(2)}, u32[]{:S(2)}) async-start(bf16[16,24,256]{2,1,0:T(8,128)(2,1)} %broadcast_in_dim.11), calls=%async_computation.6 | async-start | bytes 393216 | tf_op jit(solution)/shard_map/all_to_all | solution.py:43
  178.2 8.5 %copy-start.3 = (bf16[512,384]{1,0:T(8,128)(2,1)}, bf16[512,384]{1,0:T(8,128)(2,1)S(1)}, u32[]{:S(2)}) copy-start(bf16[512,384]{1,0:T(8,128)(2,1)S(1)} %maximum_select_fusion) | copy-start | bytes 1179652
  178.4 8.3 %collective-permute-start.9 = (bf16[384,96]{0,1:T(8,128)(2,1)S(1)}, bf16[384,96]{0,1:T(8,128)(2,1)S(1)}, u32[]{:S(2)}, u32[]{:S(2)}) collective-permute-start(bf16[384,96]{0,1:T(8,128)(2,1)S(1)} %fusion.11), channel_id=1, source_target_pairs={{0,1},{1,0},{2,3},{3,2},{4,5},{5,4},{6,7},{7,6},{8,9},{9,8},{10,11... | collective-permute-start | bytes 221192 | tf_op jit(solution)/shard_map/ppermute | solution.py:172
Sparse Core Ops, SparseCore 0:
  76.8 43.7 all-gather.1

commit v4 on v3

--- a/solution.py
+++ b/solution.py
@@ -10,7 +10,7 @@
 def swiglu_grads(gate_pre, up_pre, hidden_grad):
     sigmoid_gate = jax.nn.sigmoid(gate_pre)
     activated = gate_pre * sigmoid_gate
-    hidden = activated * up_pre
+    hidden = (activated * up_pre).astype(BF16)
     up_grad = (hidden_grad * activated).astype(BF16)
     slope = sigmoid_gate * (1.0 + gate_pre * (1.0 - sigmoid_gate))
     gate_grad = (hidden_grad * up_pre * slope).astype(BF16)
@@ -84,8 +84,6 @@
         total[:share], total[share : 2 * share], total[2 * share :]
     )
     mine = gather(jnp.concatenate([gate_share, up_share]), chips, "row", chip_groups)
-    mine, hid_share = tie((mine, hid_share))
-    hid_all = lax.all_gather(hid_share, "row", axis=0, tiled=True)
 
     def split(x):
         return [
@@ -113,42 +111,49 @@
         return (contract_cols(gate_mine, wg) + contract_cols(up_mine, wu)).astype(BF16)
 
     back_part = pair_blocks(back(w_gate, w_up), back(gate_far, up_far))
-    back_part, mine = tie((back_part, mine))
+    def double(x, bit):
+        got = lax.ppermute(x, "row", [(i, i ^ bit) for i in range(rows)])
+        low = (lax.axis_index("row") & bit) == 0
+        return jnp.where(low, jnp.concatenate([x, got]), jnp.concatenate([got, x]))
+
+    back_part, mine, hid_share = tie((back_part, mine, hid_share))
     other = swap(mine)
+    hid_row = double(double(hid_share, 2), 4)
     near_sum = scatter_sum(back_part, both, near_groups).astype(BF16)
-    near_sum, other = tie((near_sum, other))
+    near_sum, other, hid_row = tie((near_sum, other, hid_row))
     gate_other, up_other = split(other)
 
     norm_factor = (tokens * lax.axis_size("seq")) ** (-0.5)
 
-    def wgrad(pairs, which, factor=norm_factor):
+    def wgrad(pairs, which):
         size = pairs[0][1].shape[1] // 2
         terms = [
             contract_rows(a, lax.dynamic_slice_in_dim(b, which * size, size, 1))
             for a, b in pairs
         ]
-        return sum(terms) * factor
+        return sum(terms) * norm_factor
 
     gate_pairs = ((in_mine, gate_mine), (in_other, gate_other))
     up_pairs = ((in_mine, up_mine), (in_other, up_other))
     sent = jnp.concatenate([wgrad(p, 1 - seq).astype(BF16) for p in (gate_pairs, up_pairs)])
     received = lax.ppermute(sent, "seq", seq_swap)
+    hid_row, _ = tie((hid_row, sent))
+    hid_all = double(double(hid_row, 8), 1)
 
     group_sums = gather(near_sum, far, both, far_groups)
     far_sum = jnp.sum(group_sums.astype(F32), axis=0)
     far_sum, received, hid_all = tie((far_sum, received, hid_all))
     out_piece = lax.dynamic_index_in_dim(pair_blocks(out_mine, out_far), spot, 0, False)
     resid_piece = (out_piece.astype(F32) + far_sum).astype(BF16)
-    out_rows = out_grad.reshape(2, chips, share, width).swapaxes(0, 1).reshape(tokens, width)
-    down_pairs = ((out_rows, (hid_all * norm_factor).astype(BF16)),)
-    down_received = lax.ppermute(wgrad(down_pairs, 1 - seq, 1.0).astype(BF16), "seq", seq_swap)
+    down_pairs = ((out_grad, hid_all),)
+    down_received = lax.ppermute(wgrad(down_pairs, 1 - seq).astype(BF16), "seq", seq_swap)
     gate_wgrad = wgrad(gate_pairs, seq) + received[:width].astype(F32)
     up_wgrad = wgrad(up_pairs, seq) + received[width:].astype(F32)
     resid_all = gather(resid_piece, near, both, near_groups)
     resid_all, down_received, gate_wgrad, up_wgrad = tie(
         (resid_all, down_received, gate_wgrad, up_wgrad)
     )
-    down_wgrad = wgrad(down_pairs, seq, 1.0) + down_received.astype(F32)
+    down_wgrad = wgrad(down_pairs, seq) + down_received.astype(F32)
     resid_all = resid_all.reshape(near, 2, half // near, width)
     resid_mine, resid_far = (resid_all[:, i].reshape(half, width) for i in range(2))
 

time: 196 us -> 186 us (0.949)
  between operations: 14.7 us -> 1.36 us
  starting transfers between devices: 112 us -> 114 us
    ppermute x1 -> x5, waiting for transfers between devices: 1 us -> 12.6 us  [the longest x4 10.5 us: double(): got = lax.ppermute(x, 'row', [(i, i ^ bit) for i in range(rows)])]
    ppermute x1 -> x5, starting transfers between devices: 4.89 us -> 13.9 us  [the longest x4 9.2 us: double(): got = lax.ppermute(x, 'row', [(i, i ^ bit) for i in range(rows)])]
    all_to_all x3, waiting for transfers between devices: 8.52 us -> 0.88 us  [gather(): lax.all_to_all(copies, axis, 0, 0, tiled=True, axis_index_groups=groups)]
    all_to_all x3, waiting for transfers between devices: 16.6 us -> 9.54 us  [scatter_sum(): lax.all_to_all(parts, axis, 0, 0, tiled=True, axis_index_groups=groups)]
    ppermute x1, waiting for transfers between devices: 2.61 us -> 7.49 us  [per_device(): received = lax.ppermute(sent, 'seq', seq_swap)]
    ppermute x7, starting transfers between devices: 41.5 us -> 37.6 us  [swap(): return lax.ppermute(x, 'row', core_swap)]
    all_to_all x3, starting transfers between devices: 39.6 us -> 36.5 us  [gather(): lax.all_to_all(copies, axis, 0, 0, tiled=True, axis_index_groups=groups)]
  transfers between devices with their start and end apart: 17 -> 20, of which waited for: 10 -> 11; matrix products, arithmetic and copies ran while one was open for 5% -> 5% of each run, Pallas kernels for 0% -> 0%
where the time goes in v4:
time: 186 us; the launch traced here: 185 us
  starting transfers between devices  114 us (61%)
  waiting for transfers between devices  32.9 us (18%)
  matrix products  13.4 us (7%)
  blocking collectives  11.6 us (6%)
  local copies, waits for them, and re-layouts  8.08 us (4%)
  other arithmetic  3.49 us (2%)
    ppermute x7, starting transfers between devices, swap(): return lax.ppermute(x, 'row', core_swap)  37.6 us
    all_to_all x3, starting transfers between devices, gather(): lax.all_to_all(copies, axis, 0, 0, tiled=True, axis_index_groups=groups)  36.5 us
    all_to_all x3, starting transfers between devices, scatter_sum(): lax.all_to_all(parts, axis, 0, 0, tiled=True, axis_index_groups=groups)  17 us
    all_to_all x1, blocking collectives, gather(): lax.all_to_all(copies, axis, 0, 0, tiled=True, axis_index_groups=groups)  11.6 us
    ppermute x4, waiting for transfers between devices, double(): got = lax.ppermute(x, 'row', [(i, i ^ bit) for i in range(rows)])  10.5 us
    all_to_all x3, waiting for transfers between devices, scatter_sum(): lax.all_to_all(parts, axis, 0, 0, tiled=True, axis_index_groups=groups)  9.54 us
    ppermute x4, starting transfers between devices, double(): got = lax.ppermute(x, 'row', [(i, i ^ bit) for i in range(rows)])  9.2 us
    ppermute x1, waiting for transfers between devices, per_device(): received = lax.ppermute(sent, 'seq', seq_swap)  7.49 us
  transfers between devices with their start and end apart: 20, of which 11 were waited for; matrix products, arithmetic and copies ran while one was open for 5% of the time, Pallas kernels for 0%

profile of v4, /device:TPU:1, one launch (start us, length us, event | category | flops | bytes accessed | tf_op | source)
XLA Modules:
  0.0 184.9 jit_solution(13121469239604983752)
XLA Ops:
  0.7 1.0 copy-done
  1.6 1.3 convolution_convert_fusion.2
  3.0 0.3 convolution_convert_fusion.1
  3.4 0.6 copy-done.5
  4.0 0.3 convolution_convert_fusion
  4.4 16.2 %collective-permute-start = (bf16[8,96,512]{2,1,0:T(8,128)(2,1)S(1)}, bf16[8,96,512]{2,1,0:T(8,128)(2,1)S(1)}, u32[]{:S(2)}, u32[]{:S(2)}) collective-permute-start(bf16[8,96,512]{2,1,0:T(8,128)(2,1)S(1)} %pad_maximum_fusion), channel_id=1, source_target_pairs={{0,64},{64,0},{128,192},{192,128},{256,320},{320,256},{384,448},{4... | collective-permute-start | bytes 2359304 | tf_op jit(solution)/shard_map/ppermute | solution.py:61
  20.6 0.3 convolution_convert_fusion.5
  20.9 0.3 convolution_convert_fusion.4
  21.2 0.3 convolution_convert_fusion.3
  21.5 1.0 collective-permute-done
  22.5 1.1 add_convert_fusion
  23.6 3.5 %all-to-all-start = ((bf16[8,96,512]{2,1,0:T(8,128)(2,1)}), bf16[8,96,512]{2,1,0:T(8,128)(2,1)S(1)}, u32[]{:S(2)}, u32[]{:S(2)}) async-start(bf16[8,96,512]{2,1,0:T(8,128)(2,1)} %add_convert_fusion), calls=%async_computation | async-start | bytes 1572864 | tf_op jit(solution)/shard_map/all_to_all | solution.py:37
  27.1 2.3 %collective-permute-start.1 = (bf16[384,512]{1,0:T(8,128)(2,1)S(1)}, bf16[384,512]{1,0:T(8,128)(2,1)}, u32[]{:S(2)}, u32[]{:S(2)}) collective-permute-start(bf16[384,512]{1,0:T(8,128)(2,1)S(1)} %copy-done.2), channel_id=1, source_target_pairs={{0,64},{64,0},{128,192},{192,128},{256,320},{320,256},{384,448},{4... | collective-permute-start | bytes 1179656 | tf_op jit(solution)/shard_map/ppermute | solution.py:61
  29.4 2.0 %collective-permute-start.2 = (bf16[384,512]{1,0:T(8,128)(2,1)S(1)}, bf16[384,512]{1,0:T(8,128)(2,1)}, u32[]{:S(2)}, u32[]{:S(2)}) collective-permute-start(bf16[384,512]{1,0:T(8,128)(2,1)S(1)} %copy-done.1), channel_id=1, source_target_pairs={{0,64},{64,0},{128,192},{192,128},{256,320},{320,256},{384,448},{4... | collective-permute-start | bytes 1179656 | tf_op jit(solution)/shard_map/ppermute | solution.py:61
  31.5 2.3 %collective-permute-start.4 = (bf16[256,384]{1,0:T(8,128)(2,1)S(1)}, bf16[256,384]{1,0:T(8,128)(2,1)S(1)}, u32[]{:S(2)}, u32[]{:S(2)}) collective-permute-start(bf16[256,384]{1,0:T(8,128)(2,1)S(1)} %get-tuple-element.36), channel_id=1, source_target_pairs={{0,64},{64,0},{128,192},{192,128},{256,320},{320,256},{384,448},{4... | collective-permute-start | bytes 589832 | tf_op jit(solution)/shard_map/ppermute | solution.py:61
  33.8 2.0 %collective-permute-start.3 = (bf16[384,192]{0,1:T(8,128)(2,1)}, bf16[384,192]{0,1:T(8,128)(2,1)S(1)}, u32[]{:S(2)}, u32[]{:S(2)}) collective-permute-start(bf16[384,192]{0,1:T(8,128)(2,1)} %param.13), channel_id=1, source_target_pairs={{0,64},{64,0},{128,192},{192,128},{256,320},{320,256},{384,448},{4... | collective-permute-start | bytes 442376 | tf_op jit(solution)/shard_map/ppermute | solution.py:61
  35.8 4.3 %all-to-all-done = bf16[8,96,512]{2,1,0:T(8,128)(2,1)S(1)} async-done(((bf16[8,96,512]{2,1,0:T(8,128)(2,1)}), bf16[8,96,512]{2,1,0:T(8,128)(2,1)S(1)}, u32[]{:S(2)}, u32[]{:S(2)}) %all-to-all-start) | async-done | bytes 786464 | tf_op jit(solution)/shard_map/all_to_all | solution.py:37
  40.4 0.6 copy-done.14
  41.1 11.6 %all_to_all.35 = bf16[8,64,512]{2,1,0:T(8,128)(2,1)S(1)} all-to-all(bf16[8,64,512]{2,1,0:T(8,128)(2,1)S(1)} %broadcast_in_dim.8), channel_id=1, replica_groups={{0,128,256,384,512,640,768,896},{64,192,320,448,576,704,832,960},{1,129..., dimensions={0} | all-to-all | bytes 1048576 | tf_op jit(solution)/shard_map/all_to_all | solution.py:43
  52.7 0.3 fusion.65
  53.0 0.3 fusion.6
  53.4 1.3 fusion.66
  54.7 1.3 fusion.7
  56.0 0.8 pad_maximum_fusion.1
  56.8 10.1 %all-to-all-start.2 = ((bf16[8,64,384]{2,1,0:T(8,128)(2,1)}), bf16[8,64,384]{2,1,0:T(8,128)(2,1)S(1)}, u32[]{:S(2)}, u32[]{:S(2)}) async-start(bf16[8,64,384]{2,1,0:T(8,128)(2,1)} %pad_maximum_fusion.1), calls=%async_computation.2 | async-start | bytes 786432 | tf_op jit(solution)/shard_map/all_to_all | solution.py:37
  66.9 1.9 %collective-permute-start.5 = (bf16[8,64,512]{2,1,0:T(8,128)(2,1)S(1)}, bf16[8,64,512]{2,1,0:T(8,128)(2,1)}, u32[]{:S(2)}, u32[]{:S(2)}) collective-permute-start(bf16[8,64,512]{2,1,0:T(8,128)(2,1)S(1)} %all_to_all.35), channel_id=1, source_target_pairs={{0,64},{64,0},{128,192},{192,128},{256,320},{320,256},{384,448},{4... | collective-permute-start | bytes 1572872 | tf_op jit(solution)/shard_map/ppermute | solution.py:61
  68.8 2.5 %collective-permute-start.6 = (bf16[32,512]{1,0:T(8,128)(2,1)S(1)}, bf16[32,512]{1,0:T(8,128)(2,1)S(1)}, u32[]{:S(2)}, u32[]{:S(2)}) collective-permute-start(bf16[32,512]{1,0:T(8,128)(2,1)S(1)} %get-tuple-element.43), channel_id=1, source_target_pairs={{0,128},{64,192},{128,0},{192,64},{256,384},{320,448},{384,256},{4... | collective-permute-start | bytes 98312 | tf_op jit(solution)/shard_map/ppermute | solution.py:115
  71.6 2.2 %collective-permute-done.6 = bf16[32,512]{1,0:T(8,128)(2,1)S(1)} collective-permute-done((bf16[32,512]{1,0:T(8,128)(2,1)S(1)}, bf16[32,512]{1,0:T(8,128)(2,1)S(1)}, u32[]{:S(2)}, u32[]{:S(2)}) %collective-permute-start.6) | collective-permute-done | bytes 32800 | tf_op jit(solution)/shard_map/ppermute | solution.py:115
  73.8 2.4 %collective-permute-start.7 = (bf16[64,512]{1,0:T(8,128)(2,1)S(1)}, bf16[64,512]{1,0:T(8,128)(2,1)S(1)}, u32[]{:S(2)}, u32[]{:S(2)}) collective-permute-start(bf16[64,512]{1,0:T(8,128)(2,1)S(1)} %maximum_select_fusion.4), channel_id=1, source_target_pairs={{0,256},{64,320},{128,384},{192,448},{256,0},{320,64},{384,128},{4... | collective-permute-start | bytes 196616 | tf_op jit(solution)/shard_map/ppermute | solution.py:115
  76.5 4.1 %collective-permute-done.7 = bf16[64,512]{1,0:T(8,128)(2,1)S(1)} collective-permute-done((bf16[64,512]{1,0:T(8,128)(2,1)S(1)}, bf16[64,512]{1,0:T(8,128)(2,1)S(1)}, u32[]{:S(2)}, u32[]{:S(2)}) %collective-permute-start.7) | collective-permute-done | bytes 65568 | tf_op jit(solution)/shard_map/ppermute | solution.py:115
  80.7 1.1 fusion.62
  81.8 0.7 broadcast_in_dim.9
  82.5 18.8 %all-to-all-start.3 = ((bf16[4,64,384]{2,1,0:T(8,128)(2,1)}), bf16[4,64,384]{2,1,0:T(8,128)(2,1)S(1)}, u32[]{:S(2)}, u32[]{:S(2)}) async-start(bf16[4,64,384]{2,1,0:T(8,128)(2,1)} %broadcast_in_dim.9), calls=%async_computation.3 | async-start | bytes 393216 | tf_op jit(solution)/shard_map/all_to_all | solution.py:43
  101.3 0.3 fusion.10
  101.6 0.3 fusion.9
  101.9 2.2 %collective-permute-start.9 = (bf16[128,512]{1,0:T(8,128)(2,1)S(1)}, bf16[128,512]{1,0:T(8,128)(2,1)S(1)}, u32[]{:S(2)}, u32[]{:S(2)}) collective-permute-start(bf16[128,512]{1,0:T(8,128)(2,1)S(1)} %maximum_select_fusion.3), channel_id=1, source_target_pairs={{0,512},{64,576},{128,640},{192,704},{256,768},{320,832},{384,896}... | collective-permute-start | bytes 393224 | tf_op jit(solution)/shard_map/ppermute | solution.py:115
  104.1 4.2 %collective-permute-done.9 = bf16[128,512]{1,0:T(8,128)(2,1)S(1)} collective-permute-done((bf16[128,512]{1,0:T(8,128)(2,1)S(1)}, bf16[128,512]{1,0:T(8,128)(2,1)S(1)}, u32[]{:S(2)}, u32[]{:S(2)}) %collective-permute-start.9) | collective-permute-done | bytes 131104 | tf_op jit(solution)/shard_map/ppermute | solution.py:115
  108.4 2.1 %collective-permute-start.10 = (bf16[256,512]{1,0:T(8,128)(2,1)S(1)}, bf16[256,512]{1,0:T(8,128)(2,1)S(1)}, u32[]{:S(2)}, u32[]{:S(2)}) collective-permute-start(bf16[256,512]{1,0:T(8,128)(2,1)S(1)} %maximum_select_fusion.2), channel_id=1, source_target_pairs={{0,64},{64,0},{128,192},{192,128},{256,320},{320,256},{384,448},{4... | collective-permute-start | bytes 786440 | tf_op jit(solution)/shard_map/ppermute | solution.py:115
  110.5 4.7 %collective-permute-start.8 = (bf16[768,256]{1,0:T(8,128)(2,1)S(1)}, bf16[768,256]{1,0:T(8,128)(2,1)S(1)}, u32[]{:S(2)}, u32[]{:S(2)}) collective-permute-start(bf16[768,256]{1,0:T(8,128)(2,1)S(1)} %pad_maximum_fusion.2), channel_id=1, source_target_pairs={{0,1},{1,0},{2,3},{3,2},{4,5},{5,4},{6,7},{7,6},{8,9},{9,8},{10,11... | collective-permute-start | bytes 1179656 | tf_op jit(solution)/shard_map/ppermute | solution.py:139
  115.2 1.0 maximum_select_fusion
  116.2 0.3 all-to-all-done.3
  116.6 7.5 %collective-permute-done.8 = bf16[768,256]{1,0:T(8,128)(2,1)S(1)} collective-permute-done((bf16[768,256]{1,0:T(8,128)(2,1)S(1)}, bf16[768,256]{1,0:T(8,128)(2,1)S(1)}, u32[]{:S(2)}, u32[]{:S(2)}) %collective-permute-start.8) | collective-permute-done | bytes 393248 | tf_op jit(solution)/shard_map/ppermute | solution.py:139
  124.1 0.8 broadcast_in_dim.10
  124.9 13.1 %all-to-all-start.4 = ((bf16[8,64,384]{2,1,0:T(8,128)(2,1)}), bf16[8,64,384]{2,1,0:T(8,128)(2,1)S(1)}, u32[]{:S(2)}, u32[]{:S(2)}) async-start(bf16[8,64,384]{2,1,0:T(8,128)(2,1)} %broadcast_in_dim.10), calls=%async_computation.4 | async-start | bytes 786432 | tf_op jit(solution)/shard_map/all_to_all | solution.py:43
  138.6 0.5 copy-done.6
  139.1 0.3 fusion.11
  139.5 4.7 %collective-permute-start.11 = (bf16[384,256]{0,1:T(8,128)(2,1)S(1)}, bf16[384,256]{0,1:T(8,128)(2,1)S(1)}, u32[]{:S(2)}, u32[]{:S(2)}) collective-permute-start(bf16[384,256]{0,1:T(8,128)(2,1)S(1)} %fusion.11), channel_id=1, source_target_pairs={{0,1},{1,0},{2,3},{3,2},{4,5},{5,4},{6,7},{7,6},{8,9},{9,8},{10,11... | collective-permute-start | bytes 589832 | tf_op jit(solution)/shard_map/ppermute | solution.py:149
  144.2 1.0 convert_add_fusion
  145.2 1.0 convert_add_fusion.1
  146.2 2.1 %collective-permute-done.11 = bf16[384,256]{0,1:T(8,128)(2,1)S(1)} collective-permute-done((bf16[384,256]{0,1:T(8,128)(2,1)S(1)}, bf16[384,256]{0,1:T(8,128)(2,1)S(1)}, u32[]{:S(2)}, u32[]{:S(2)}) %collective-permute-start.11) | collective-permute-done | bytes 196640 | tf_op jit(solution)/shard_map/ppermute | solution.py:149
  148.4 1.1 convolution_bitcast_fusion
  149.5 0.9 fusion.13
  150.4 10.8 %collective-permute-start.12 = (bf16[256,384]{1,0:T(8,128)(2,1)S(1)}, bf16[256,384]{1,0:T(8,128)(2,1)S(1)}, u32[]{:S(2)}, u32[]{:S(2)}) collective-permute-start(bf16[256,384]{1,0:T(8,128)(2,1)S(1)} %bitcast.88), channel_id=1, source_target_pairs={{0,64},{64,0},{128,192},{192,128},{256,320},{320,256},{384,448},{4... | collective-permute-start | bytes 589832 | tf_op jit(solution)/shard_map/ppermute | solution.py:61
  161.2 3.4 %all-to-all-start.5 = ((bf16[8,24,256]{2,1,0:T(8,128)(2,1)}), bf16[8,24,256]{2,1,0:T(8,128)(2,1)S(1)}, u32[]{:S(2)}, u32[]{:S(2)}) async-start(bf16[8,24,256]{2,1,0:T(8,128)(2,1)} %bitcast.20), calls=%async_computation.5 | async-start | bytes 196608 | tf_op jit(solution)/shard_map/all_to_all | solution.py:37
  164.6 5.2 %all-to-all-done.5 = bf16[8,24,256]{2,1,0:T(8,128)(2,1)S(1)} async-done(((bf16[8,24,256]{2,1,0:T(8,128)(2,1)}), bf16[8,24,256]{2,1,0:T(8,128)(2,1)S(1)}, u32[]{:S(2)}, u32[]{:S(2)}) %all-to-all-start.5) | async-done | bytes 98336 | tf_op jit(solution)/shard_map/all_to_all | solution.py:37
  169.8 0.7 broadcast_in_dim.11
  170.5 4.5 %all-to-all-start.6 = ((bf16[16,24,256]{2,1,0:T(8,128)(2,1)}), bf16[16,24,256]{2,1,0:T(8,128)(2,1)S(1)}, u32[]{:S(2)}, u32[]{:S(2)}) async-start(bf16[16,24,256]{2,1,0:T(8,128)(2,1)} %broadcast_in_dim.11), calls=%async_computation.6 | async-start | bytes 393216 | tf_op jit(solution)/shard_map/all_to_all | solution.py:43
  175.4 4.5 %collective-permute-start.13 = (bf16[384,96]{0,1:T(8,128)(2,1)S(1)}, bf16[384,96]{0,1:T(8,128)(2,1)S(1)}, u32[]{:S(2)}, u32[]{:S(2)}) collective-permute-start(bf16[384,96]{0,1:T(8,128)(2,1)S(1)} %fusion.14), channel_id=1, source_target_pairs={{0,1},{1,0},{2,3},{3,2},{4,5},{5,4},{6,7},{7,6},{8,9},{9,8},{10,11... | collective-permute-start | bytes 221192 | tf_op jit(solution)/shard_map/ppermute | solution.py:177
  180.0 0.3 fusion.5
  180.3 0.9 copy.18
  181.2 0.6 all-to-all-done.6
  181.9 0.7 copy.19
  182.6 1.4 collective-permute-done.13
  184.1 0.9 fusion.12
  (64 shorter events, 2.3 us)
Async XLA Ops:
  0.6 1.0 copy-start
  0.6 2.3 %copy-start.1 = (bf16[384,512]{1,0:T(8,128)(2,1)S(1)}, bf16[384,512]{1,0:T(8,128)(2,1)}, u32[]{:S(2)}) copy-start(bf16[384,512]{1,0:T(8,128)(2,1)} %param.11) | copy-start | bytes 1179652
  1.6 1.7 copy-start.4
  3.0 1.0 copy-start.5
  4.3 16.3 %copy-start.2 = (bf16[384,512]{1,0:T(8,128)(2,1)S(1)}, bf16[384,512]{1,0:T(8,128)(2,1)}, u32[]{:S(2)}) copy-start(bf16[384,512]{1,0:T(8,128)(2,1)} %param.10) | copy-start | bytes 1179652
  4.4 18.1 %collective-permute-start = (bf16[8,96,512]{2,1,0:T(8,128)(2,1)S(1)}, bf16[8,96,512]{2,1,0:T(8,128)(2,1)S(1)}, u32[]{:S(2)}, u32[]{:S(2)}) collective-permute-start(bf16[8,96,512]{2,1,0:T(8,128)(2,1)S(1)} %pad_maximum_fusion), channel_id=1, source_target_pairs={{0,64},{64,0},{128,192},{192,128},{256,320},{320,256},{384,448},{4... | collective-permute-start | bytes 2359304 | tf_op jit(solution)/shard_map/ppermute | solution.py:61
  23.6 16.6 %all-to-all-start = ((bf16[8,96,512]{2,1,0:T(8,128)(2,1)}), bf16[8,96,512]{2,1,0:T(8,128)(2,1)S(1)}, u32[]{:S(2)}, u32[]{:S(2)}) async-start(bf16[8,96,512]{2,1,0:T(8,128)(2,1)} %add_convert_fusion), calls=%async_computation | async-start | bytes 1572864 | tf_op jit(solution)/shard_map/all_to_all | solution.py:37
  27.1 13.2 %collective-permute-start.1 = (bf16[384,512]{1,0:T(8,128)(2,1)S(1)}, bf16[384,512]{1,0:T(8,128)(2,1)}, u32[]{:S(2)}, u32[]{:S(2)}) collective-permute-start(bf16[384,512]{1,0:T(8,128)(2,1)S(1)} %copy-done.2), channel_id=1, source_target_pairs={{0,64},{64,0},{128,192},{192,128},{256,320},{320,256},{384,448},{4... | collective-permute-start | bytes 1179656 | tf_op jit(solution)/shard_map/ppermute | solution.py:61
  29.4 10.9 %collective-permute-start.2 = (bf16[384,512]{1,0:T(8,128)(2,1)S(1)}, bf16[384,512]{1,0:T(8,128)(2,1)}, u32[]{:S(2)}, u32[]{:S(2)}) collective-permute-start(bf16[384,512]{1,0:T(8,128)(2,1)S(1)} %copy-done.1), channel_id=1, source_target_pairs={{0,64},{64,0},{128,192},{192,128},{256,320},{320,256},{384,448},{4... | collective-permute-start | bytes 1179656 | tf_op jit(solution)/shard_map/ppermute | solution.py:61
  31.5 8.8 %collective-permute-start.4 = (bf16[256,384]{1,0:T(8,128)(2,1)S(1)}, bf16[256,384]{1,0:T(8,128)(2,1)S(1)}, u32[]{:S(2)}, u32[]{:S(2)}) collective-permute-start(bf16[256,384]{1,0:T(8,128)(2,1)S(1)} %get-tuple-element.36), channel_id=1, source_target_pairs={{0,64},{64,0},{128,192},{192,128},{256,320},{320,256},{384,448},{4... | collective-permute-start | bytes 589832 | tf_op jit(solution)/shard_map/ppermute | solution.py:61
  33.8 6.5 %collective-permute-start.3 = (bf16[384,192]{0,1:T(8,128)(2,1)}, bf16[384,192]{0,1:T(8,128)(2,1)S(1)}, u32[]{:S(2)}, u32[]{:S(2)}) collective-permute-start(bf16[384,192]{0,1:T(8,128)(2,1)} %param.13), channel_id=1, source_target_pairs={{0,64},{64,0},{128,192},{192,128},{256,320},{320,256},{384,448},{4... | collective-permute-start | bytes 442376 | tf_op jit(solution)/shard_map/ppermute | solution.py:61
  40.3 13.1 %copy-start.16 = (bf16[384,192]{0,1:T(8,128)(2,1)}, bf16[384,192]{0,1:T(8,128)(2,1)S(1)}, u32[]{:S(2)}) copy-start(bf16[384,192]{0,1:T(8,128)(2,1)S(1)} %collective-permute-done.3) | copy-start | bytes 442372
  40.3 0.7 copy-start.14
  56.8 23.8 %all-to-all-start.2 = ((bf16[8,64,384]{2,1,0:T(8,128)(2,1)}), bf16[8,64,384]{2,1,0:T(8,128)(2,1)S(1)}, u32[]{:S(2)}, u32[]{:S(2)}) async-start(bf16[8,64,384]{2,1,0:T(8,128)(2,1)} %pad_maximum_fusion.1), calls=%async_computation.2 | async-start | bytes 786432 | tf_op jit(solution)/shard_map/all_to_all | solution.py:37
  66.9 13.8 %collective-permute-start.5 = (bf16[8,64,512]{2,1,0:T(8,128)(2,1)S(1)}, bf16[8,64,512]{2,1,0:T(8,128)(2,1)}, u32[]{:S(2)}, u32[]{:S(2)}) collective-permute-start(bf16[8,64,512]{2,1,0:T(8,128)(2,1)S(1)} %all_to_all.35), channel_id=1, source_target_pairs={{0,64},{64,0},{128,192},{192,128},{256,320},{320,256},{384,448},{4... | collective-permute-start | bytes 1572872 | tf_op jit(solution)/shard_map/ppermute | solution.py:61
  68.8 5.0 %collective-permute-start.6 = (bf16[32,512]{1,0:T(8,128)(2,1)S(1)}, bf16[32,512]{1,0:T(8,128)(2,1)S(1)}, u32[]{:S(2)}, u32[]{:S(2)}) collective-permute-start(bf16[32,512]{1,0:T(8,128)(2,1)S(1)} %get-tuple-element.43), channel_id=1, source_target_pairs={{0,128},{64,192},{128,0},{192,64},{256,384},{320,448},{384,256},{4... | collective-permute-start | bytes 98312 | tf_op jit(solution)/shard_map/ppermute | solution.py:115
  73.8 6.8 %collective-permute-start.7 = (bf16[64,512]{1,0:T(8,128)(2,1)S(1)}, bf16[64,512]{1,0:T(8,128)(2,1)S(1)}, u32[]{:S(2)}, u32[]{:S(2)}) collective-permute-start(bf16[64,512]{1,0:T(8,128)(2,1)S(1)} %maximum_select_fusion.4), channel_id=1, source_target_pairs={{0,256},{64,320},{128,384},{192,448},{256,0},{320,64},{384,128},{4... | collective-permute-start | bytes 196616 | tf_op jit(solution)/shard_map/ppermute | solution.py:115
  81.8 20.1 %copy-start.7 = (bf16[8,32,512]{2,1,0:T(8,128)(2,1)}, bf16[8,32,512]{2,1,0:T(8,128)(2,1)S(1)}, u32[]{:S(2)}) copy-start(bf16[8,32,512]{2,1,0:T(8,128)(2,1)S(1)} %get-tuple-element.82) | copy-start | bytes 786436
  81.8 20.1 %copy-start.9 = (bf16[8,32,512]{2,1,0:T(8,128)(2,1)}, bf16[8,32,512]{2,1,0:T(8,128)(2,1)S(1)}, u32[]{:S(2)}) copy-start(bf16[8,32,512]{2,1,0:T(8,128)(2,1)S(1)} %get-tuple-element.83) | copy-start | bytes 786436
  82.5 34.0 %all-to-all-start.3 = ((bf16[4,64,384]{2,1,0:T(8,128)(2,1)}), bf16[4,64,384]{2,1,0:T(8,128)(2,1)S(1)}, u32[]{:S(2)}, u32[]{:S(2)}) async-start(bf16[4,64,384]{2,1,0:T(8,128)(2,1)} %broadcast_in_dim.9), calls=%async_computation.3 | async-start | bytes 393216 | tf_op jit(solution)/shard_map/all_to_all | solution.py:43
  101.9 6.4 %collective-permute-start.9 = (bf16[128,512]{1,0:T(8,128)(2,1)S(1)}, bf16[128,512]{1,0:T(8,128)(2,1)S(1)}, u32[]{:S(2)}, u32[]{:S(2)}) collective-permute-start(bf16[128,512]{1,0:T(8,128)(2,1)S(1)} %maximum_select_fusion.3), channel_id=1, source_target_pairs={{0,512},{64,576},{128,640},{192,704},{256,768},{320,832},{384,896}... | collective-permute-start | bytes 393224 | tf_op jit(solution)/shard_map/ppermute | solution.py:115
  108.4 15.7 %copy-start.15 = (bf16[256,384]{1,0:T(8,128)(2,1)S(1)}, bf16[256,384]{1,0:T(8,128)(2,1)}, u32[]{:S(2)}) copy-start(bf16[256,384]{1,0:T(8,128)(2,1)} %copy-done.14) | copy-start | bytes 589828
  108.4 6.8 %collective-permute-start.10 = (bf16[256,512]{1,0:T(8,128)(2,1)S(1)}, bf16[256,512]{1,0:T(8,128)(2,1)S(1)}, u32[]{:S(2)}, u32[]{:S(2)}) collective-permute-start(bf16[256,512]{1,0:T(8,128)(2,1)S(1)} %maximum_select_fusion.2), channel_id=1, source_target_pairs={{0,64},{64,0},{128,192},{192,128},{256,320},{320,256},{384,448},{4... | collective-permute-start | bytes 786440 | tf_op jit(solution)/shard_map/ppermute | solution.py:115
  110.5 13.6 %collective-permute-start.8 = (bf16[768,256]{1,0:T(8,128)(2,1)S(1)}, bf16[768,256]{1,0:T(8,128)(2,1)S(1)}, u32[]{:S(2)}, u32[]{:S(2)}) collective-permute-start(bf16[768,256]{1,0:T(8,128)(2,1)S(1)} %pad_maximum_fusion.2), channel_id=1, source_target_pairs={{0,1},{1,0},{2,3},{3,2},{4,5},{5,4},{6,7},{7,6},{8,9},{9,8},{10,11... | collective-permute-start | bytes 1179656 | tf_op jit(solution)/shard_map/ppermute | solution.py:139
  124.1 0.9 copy-start.11
  124.9 23.4 %all-to-all-start.4 = ((bf16[8,64,384]{2,1,0:T(8,128)(2,1)}), bf16[8,64,384]{2,1,0:T(8,128)(2,1)S(1)}, u32[]{:S(2)}, u32[]{:S(2)}) async-start(bf16[8,64,384]{2,1,0:T(8,128)(2,1)} %broadcast_in_dim.10), calls=%async_computation.4 | async-start | bytes 786432 | tf_op jit(solution)/shard_map/all_to_all | solution.py:43
  138.1 1.0 copy-start.6
  138.3 5.8 %copy-start.10 = (bf16[8,32,512]{2,1,0:T(8,128)(2,1)S(1)}, bf16[8,32,512]{2,1,0:T(8,128)(2,1)}, u32[]{:S(2)}) copy-start(bf16[8,32,512]{2,1,0:T(8,128)(2,1)} %copy-done.9) | copy-start | bytes 786436
  138.3 5.8 %copy-start.12 = (bf16[768,256]{1,0:T(8,128)(2,1)S(1)}, bf16[768,256]{1,0:T(8,128)(2,1)}, u32[]{:S(2)}) copy-start(bf16[768,256]{1,0:T(8,128)(2,1)} %copy-done.11) | copy-start | bytes 1179652
  139.5 5.7 %copy-start.8 = (bf16[8,32,512]{2,1,0:T(8,128)(2,1)S(1)}, bf16[8,32,512]{2,1,0:T(8,128)(2,1)}, u32[]{:S(2)}) copy-start(bf16[8,32,512]{2,1,0:T(8,128)(2,1)} %copy-done.7) | copy-start | bytes 786436
  139.5 8.8 %collective-permute-start.11 = (bf16[384,256]{0,1:T(8,128)(2,1)S(1)}, bf16[384,256]{0,1:T(8,128)(2,1)S(1)}, u32[]{:S(2)}, u32[]{:S(2)}) collective-permute-start(bf16[384,256]{0,1:T(8,128)(2,1)S(1)} %fusion.11), channel_id=1, source_target_pairs={{0,1},{1,0},{2,3},{3,2},{4,5},{5,4},{6,7},{7,6},{8,9},{9,8},{10,11... | collective-permute-start | bytes 589832 | tf_op jit(solution)/shard_map/ppermute | solution.py:149
  146.2 3.3 %copy-start.17 = (bf16[384,192]{0,1:T(8,128)(2,1)S(1)}, bf16[384,192]{0,1:T(8,128)(2,1)}, u32[]{:S(2)}) copy-start(bf16[384,192]{0,1:T(8,128)(2,1)} %copy-done.16) | copy-start | bytes 442372
  150.4 24.6 %collective-permute-start.12 = (bf16[256,384]{1,0:T(8,128)(2,1)S(1)}, bf16[256,384]{1,0:T(8,128)(2,1)S(1)}, u32[]{:S(2)}, u32[]{:S(2)}) collective-permute-start(bf16[256,384]{1,0:T(8,128)(2,1)S(1)} %bitcast.88), channel_id=1, source_target_pairs={{0,64},{64,0},{128,192},{192,128},{256,320},{320,256},{384,448},{4... | collective-permute-start | bytes 589832 | tf_op jit(solution)/shard_map/ppermute | solution.py:61
  161.2 8.6 %all-to-all-start.5 = ((bf16[8,24,256]{2,1,0:T(8,128)(2,1)}), bf16[8,24,256]{2,1,0:T(8,128)(2,1)S(1)}, u32[]{:S(2)}, u32[]{:S(2)}) async-start(bf16[8,24,256]{2,1,0:T(8,128)(2,1)} %bitcast.20), calls=%async_computation.5 | async-start | bytes 196608 | tf_op jit(solution)/shard_map/all_to_all | solution.py:37
  164.6 10.6 %copy-start.13 = (bf16[512,192]{0,1:T(8,128)(2,1)S(1)}, bf16[512,192]{0,1:T(8,128)(2,1)}, u32[]{:S(2)}) copy-start(bf16[512,192]{0,1:T(8,128)(2,1)} %param.8) | copy-start | bytes 589828
  170.5 11.2 %all-to-all-start.6 = ((bf16[16,24,256]{2,1,0:T(8,128)(2,1)}), bf16[16,24,256]{2,1,0:T(8,128)(2,1)S(1)}, u32[]{:S(2)}, u32[]{:S(2)}) async-start(bf16[16,24,256]{2,1,0:T(8,128)(2,1)} %broadcast_in_dim.11), calls=%async_computation.6 | async-start | bytes 393216 | tf_op jit(solution)/shard_map/all_to_all | solution.py:43
  175.2 8.9 %copy-start.3 = (bf16[512,384]{1,0:T(8,128)(2,1)}, bf16[512,384]{1,0:T(8,128)(2,1)S(1)}, u32[]{:S(2)}) copy-start(bf16[512,384]{1,0:T(8,128)(2,1)S(1)} %maximum_select_fusion.1) | copy-start | bytes 1179652
  175.4 8.6 %collective-permute-start.13 = (bf16[384,96]{0,1:T(8,128)(2,1)S(1)}, bf16[384,96]{0,1:T(8,128)(2,1)S(1)}, u32[]{:S(2)}, u32[]{:S(2)}) collective-permute-start(bf16[384,96]{0,1:T(8,128)(2,1)S(1)} %fusion.14), channel_id=1, source_target_pairs={{0,1},{1,0},{2,3},{3,2},{4,5},{5,4},{6,7},{7,6},{8,9},{9,8},{10,11... | collective-permute-start | bytes 221192 | tf_op jit(solution)/shard_map/ppermute | solution.py:177

commit v5 on v4

--- a/solution.py
+++ b/solution.py
@@ -117,8 +117,9 @@
         return jnp.where(low, jnp.concatenate([x, got]), jnp.concatenate([got, x]))
 
     back_part, mine, hid_share = tie((back_part, mine, hid_share))
+    mine, hid_pair = tie((mine, double(hid_share, 2)))
     other = swap(mine)
-    hid_row = double(double(hid_share, 2), 4)
+    hid_row = double(hid_pair, 4)
     near_sum = scatter_sum(back_part, both, near_groups).astype(BF16)
     near_sum, other, hid_row = tie((near_sum, other, hid_row))
     gate_other, up_other = split(other)
@@ -138,11 +139,12 @@
     sent = jnp.concatenate([wgrad(p, 1 - seq).astype(BF16) for p in (gate_pairs, up_pairs)])
     received = lax.ppermute(sent, "seq", seq_swap)
     hid_row, _ = tie((hid_row, sent))
-    hid_all = double(double(hid_row, 8), 1)
+    hid_chips, received = tie((double(hid_row, 8), received))
+    hid_all = double(hid_chips, 1)
 
     group_sums = gather(near_sum, far, both, far_groups)
     far_sum = jnp.sum(group_sums.astype(F32), axis=0)
-    far_sum, received, hid_all = tie((far_sum, received, hid_all))
+    far_sum, hid_all = tie((far_sum, hid_all))
     out_piece = lax.dynamic_index_in_dim(pair_blocks(out_mine, out_far), spot, 0, False)
     resid_piece = (out_piece.astype(F32) + far_sum).astype(BF16)
     down_pairs = ((out_grad, hid_all),)
@@ -163,7 +165,8 @@
     mix_part = (heads_by_tokens(w_out, resid_mine) + heads_by_tokens(w_out_far, resid_far)).astype(BF16)
     mix_part, resid_far = tie((mix_part, resid_far))
     mix_share = scatter_sum(mix_part.reshape(chips, -1, half), "row", chip_groups)
-    mix_all = gather(mix_share.astype(BF16), rows, "row", None)
+    mix_share, down_wgrad = tie((mix_share.astype(BF16), down_wgrad))
+    mix_all = gather(mix_share, rows, "row", None)
     attn_grad = mix_all.reshape(chips, 2, -1, half).transpose(1, 3, 0, 2).reshape(tokens, -1)
 
     resid_other = swap(resid_far)

time: 186 us -> 187 us (level)
  starting transfers between devices: 114 us -> 116 us
    ppermute x1, waiting for transfers between devices: 7.49 us -> 0.01 us  [per_device(): received = lax.ppermute(sent, 'seq', seq_swap)]
    ppermute x4, waiting for transfers between devices: 10.5 us -> 17.1 us  [double(): got = lax.ppermute(x, 'row', [(i, i ^ bit) for i in range(rows)])]
  transfers between devices with their start and end apart: 20 -> 20, of which waited for: 11 -> 10; matrix products, arithmetic and copies ran while one was open for 5% -> 5% of each run, Pallas kernels for 0% -> 0%
where the time goes in v5:
time: 187 us; the launch traced here: 186 us
  starting transfers between devices  116 us (62%)
  waiting for transfers between devices  31.8 us (17%)
  matrix products  13.4 us (7%)
  blocking collectives  11.6 us (6%)
  local copies, waits for them, and re-layouts  8.1 us (4%)
  other arithmetic  3.5 us (2%)
    ppermute x7, starting transfers between devices, swap(): return lax.ppermute(x, 'row', core_swap)  38.6 us
    all_to_all x3, starting transfers between devices, gather(): lax.all_to_all(copies, axis, 0, 0, tiled=True, axis_index_groups=groups)  37.5 us
    ppermute x4, waiting for transfers between devices, double(): got = lax.ppermute(x, 'row', [(i, i ^ bit) for i in range(rows)])  17.1 us
    all_to_all x3, starting transfers between devices, scatter_sum(): lax.all_to_all(parts, axis, 0, 0, tiled=True, axis_index_groups=groups)  17 us
    all_to_all x1, blocking collectives, gather(): lax.all_to_all(copies, axis, 0, 0, tiled=True, axis_index_groups=groups)  11.6 us
    all_to_all x3, waiting for transfers between devices, scatter_sum(): lax.all_to_all(parts, axis, 0, 0, tiled=True, axis_index_groups=groups)  9.21 us
    ppermute x4, starting transfers between devices, double(): got = lax.ppermute(x, 'row', [(i, i ^ bit) for i in range(rows)])  8.92 us
    dot_general x12, matrix products, contract_rows(): lax.dot_general(first, second, (((0,), (0,)), ((), ())), preferred_elemen...  5.32 us
  transfers between devices with their start and end apart: 20, of which 10 were waited for; matrix products, arithmetic and copies ran while one was open for 5% of the time, Pallas kernels for 0%

profile of v5, /device:TPU:1, one launch (start us, length us, event | category | flops | bytes accessed | tf_op | source)
XLA Modules:
  0.0 185.6 jit_solution(2360066257823145734)
XLA Ops:
  0.7 1.0 copy-done
  1.6 1.3 convolution_convert_fusion.2
  3.0 0.3 convolution_convert_fusion.1
  3.4 0.6 copy-done.5
  4.0 0.3 convolution_convert_fusion
  4.4 16.2 %collective-permute-start = (bf16[8,96,512]{2,1,0:T(8,128)(2,1)S(1)}, bf16[8,96,512]{2,1,0:T(8,128)(2,1)S(1)}, u32[]{:S(2)}, u32[]{:S(2)}) collective-permute-start(bf16[8,96,512]{2,1,0:T(8,128)(2,1)S(1)} %pad_maximum_fusion), channel_id=1, source_target_pairs={{0,64},{64,0},{128,192},{192,128},{256,320},{320,256},{384,448},{4... | collective-permute-start | bytes 2359304 | tf_op jit(solution)/shard_map/ppermute | solution.py:61
  20.6 0.3 convolution_convert_fusion.5
  20.9 0.3 convolution_convert_fusion.4
  21.2 0.3 convolution_convert_fusion.3
  21.5 1.0 collective-permute-done
  22.5 1.1 add_convert_fusion
  23.6 3.5 %all-to-all-start = ((bf16[8,96,512]{2,1,0:T(8,128)(2,1)}), bf16[8,96,512]{2,1,0:T(8,128)(2,1)S(1)}, u32[]{:S(2)}, u32[]{:S(2)}) async-start(bf16[8,96,512]{2,1,0:T(8,128)(2,1)} %add_convert_fusion), calls=%async_computation | async-start | bytes 1572864 | tf_op jit(solution)/shard_map/all_to_all | solution.py:37
  27.1 2.3 %collective-permute-start.1 = (bf16[384,512]{1,0:T(8,128)(2,1)S(1)}, bf16[384,512]{1,0:T(8,128)(2,1)}, u32[]{:S(2)}, u32[]{:S(2)}) collective-permute-start(bf16[384,512]{1,0:T(8,128)(2,1)S(1)} %copy-done.2), channel_id=1, source_target_pairs={{0,64},{64,0},{128,192},{192,128},{256,320},{320,256},{384,448},{4... | collective-permute-start | bytes 1179656 | tf_op jit(solution)/shard_map/ppermute | solution.py:61
  29.4 2.0 %collective-permute-start.2 = (bf16[384,512]{1,0:T(8,128)(2,1)S(1)}, bf16[384,512]{1,0:T(8,128)(2,1)}, u32[]{:S(2)}, u32[]{:S(2)}) collective-permute-start(bf16[384,512]{1,0:T(8,128)(2,1)S(1)} %copy-done.1), channel_id=1, source_target_pairs={{0,64},{64,0},{128,192},{192,128},{256,320},{320,256},{384,448},{4... | collective-permute-start | bytes 1179656 | tf_op jit(solution)/shard_map/ppermute | solution.py:61
  31.5 2.3 %collective-permute-start.4 = (bf16[256,384]{1,0:T(8,128)(2,1)S(1)}, bf16[256,384]{1,0:T(8,128)(2,1)S(1)}, u32[]{:S(2)}, u32[]{:S(2)}) collective-permute-start(bf16[256,384]{1,0:T(8,128)(2,1)S(1)} %get-tuple-element.41), channel_id=1, source_target_pairs={{0,64},{64,0},{128,192},{192,128},{256,320},{320,256},{384,448},{4... | collective-permute-start | bytes 589832 | tf_op jit(solution)/shard_map/ppermute | solution.py:61
  33.8 2.0 %collective-permute-start.3 = (bf16[384,192]{0,1:T(8,128)(2,1)}, bf16[384,192]{0,1:T(8,128)(2,1)S(1)}, u32[]{:S(2)}, u32[]{:S(2)}) collective-permute-start(bf16[384,192]{0,1:T(8,128)(2,1)} %param.13), channel_id=1, source_target_pairs={{0,64},{64,0},{128,192},{192,128},{256,320},{320,256},{384,448},{4... | collective-permute-start | bytes 442376 | tf_op jit(solution)/shard_map/ppermute | solution.py:61
  35.8 4.3 %all-to-all-done = bf16[8,96,512]{2,1,0:T(8,128)(2,1)S(1)} async-done(((bf16[8,96,512]{2,1,0:T(8,128)(2,1)}), bf16[8,96,512]{2,1,0:T(8,128)(2,1)S(1)}, u32[]{:S(2)}, u32[]{:S(2)}) %all-to-all-start) | async-done | bytes 786464 | tf_op jit(solution)/shard_map/all_to_all | solution.py:37
  40.4 0.6 copy-done.14
  41.1 11.6 %all_to_all.35 = bf16[8,64,512]{2,1,0:T(8,128)(2,1)S(1)} all-to-all(bf16[8,64,512]{2,1,0:T(8,128)(2,1)S(1)} %broadcast_in_dim.8), channel_id=1, replica_groups={{0,128,256,384,512,640,768,896},{64,192,320,448,576,704,832,960},{1,129..., dimensions={0} | all-to-all | bytes 1048576 | tf_op jit(solution)/shard_map/all_to_all | solution.py:43
  52.7 0.3 fusion.66
  53.0 0.3 fusion.5
  53.4 1.3 fusion.67
  54.7 1.3 fusion.6
  56.0 0.8 pad_maximum_fusion.1
  56.8 10.1 %all-to-all-start.2 = ((bf16[8,64,384]{2,1,0:T(8,128)(2,1)}), bf16[8,64,384]{2,1,0:T(8,128)(2,1)S(1)}, u32[]{:S(2)}, u32[]{:S(2)}) async-start(bf16[8,64,384]{2,1,0:T(8,128)(2,1)} %pad_maximum_fusion.1), calls=%async_computation.2 | async-start | bytes 786432 | tf_op jit(solution)/shard_map/all_to_all | solution.py:37
  66.9 2.5 %collective-permute-start.5 = (bf16[32,512]{1,0:T(8,128)(2,1)S(1)}, bf16[32,512]{1,0:T(8,128)(2,1)S(1)}, u32[]{:S(2)}, u32[]{:S(2)}) collective-permute-start(bf16[32,512]{1,0:T(8,128)(2,1)S(1)} %get-tuple-element.48), channel_id=1, source_target_pairs={{0,128},{64,192},{128,0},{192,64},{256,384},{320,448},{384,256},{4... | collective-permute-start | bytes 98312 | tf_op jit(solution)/shard_map/ppermute | solution.py:115
  69.4 2.4 %collective-permute-done.5 = bf16[32,512]{1,0:T(8,128)(2,1)S(1)} collective-permute-done((bf16[32,512]{1,0:T(8,128)(2,1)S(1)}, bf16[32,512]{1,0:T(8,128)(2,1)S(1)}, u32[]{:S(2)}, u32[]{:S(2)}) %collective-permute-start.5) | collective-permute-done | bytes 32800 | tf_op jit(solution)/shard_map/ppermute | solution.py:115
  71.8 1.9 %collective-permute-start.6 = (bf16[8,64,512]{2,1,0:T(8,128)(2,1)S(1)}, bf16[8,64,512]{2,1,0:T(8,128)(2,1)}, u32[]{:S(2)}, u32[]{:S(2)}) collective-permute-start(bf16[8,64,512]{2,1,0:T(8,128)(2,1)S(1)} %all_to_all.35), channel_id=1, source_target_pairs={{0,64},{64,0},{128,192},{192,128},{256,320},{320,256},{384,448},{4... | collective-permute-start | bytes 1572872 | tf_op jit(solution)/shard_map/ppermute | solution.py:61
  73.8 0.3 fusion.28
  74.0 2.4 %collective-permute-start.7 = (bf16[64,512]{1,0:T(8,128)(2,1)S(1)}, bf16[64,512]{1,0:T(8,128)(2,1)S(1)}, u32[]{:S(2)}, u32[]{:S(2)}) collective-permute-start(bf16[64,512]{1,0:T(8,128)(2,1)S(1)} %maximum_select_fusion.4), channel_id=1, source_target_pairs={{0,256},{64,320},{128,384},{192,448},{256,0},{320,64},{384,128},{4... | collective-permute-start | bytes 196616 | tf_op jit(solution)/shard_map/ppermute | solution.py:115
  76.5 0.3 fusion.25
  76.7 4.1 %collective-permute-done.7 = bf16[64,512]{1,0:T(8,128)(2,1)S(1)} collective-permute-done((bf16[64,512]{1,0:T(8,128)(2,1)S(1)}, bf16[64,512]{1,0:T(8,128)(2,1)S(1)}, u32[]{:S(2)}, u32[]{:S(2)}) %collective-permute-start.7) | collective-permute-done | bytes 65568 | tf_op jit(solution)/shard_map/ppermute | solution.py:115
  80.9 1.1 fusion.63
  82.1 0.7 broadcast_in_dim.9
  82.8 18.8 %all-to-all-start.3 = ((bf16[4,64,384]{2,1,0:T(8,128)(2,1)}), bf16[4,64,384]{2,1,0:T(8,128)(2,1)S(1)}, u32[]{:S(2)}, u32[]{:S(2)}) async-start(bf16[4,64,384]{2,1,0:T(8,128)(2,1)} %broadcast_in_dim.9), calls=%async_computation.3 | async-start | bytes 393216 | tf_op jit(solution)/shard_map/all_to_all | solution.py:43
  101.9 0.3 fusion.8
  102.2 4.5 %collective-permute-start.9 = (bf16[768,256]{1,0:T(8,128)(2,1)S(1)}, bf16[768,256]{1,0:T(8,128)(2,1)S(1)}, u32[]{:S(2)}, u32[]{:S(2)}) collective-permute-start(bf16[768,256]{1,0:T(8,128)(2,1)S(1)} %pad_maximum_fusion.2), channel_id=1, source_target_pairs={{0,1},{1,0},{2,3},{3,2},{4,5},{5,4},{6,7},{7,6},{8,9},{9,8},{10,11... | collective-permute-start | bytes 1179656 | tf_op jit(solution)/shard_map/ppermute | solution.py:140
  106.7 1.9 %collective-permute-start.8 = (bf16[128,512]{1,0:T(8,128)(2,1)S(1)}, bf16[128,512]{1,0:T(8,128)(2,1)S(1)}, u32[]{:S(2)}, u32[]{:S(2)}) collective-permute-start(bf16[128,512]{1,0:T(8,128)(2,1)S(1)} %maximum_select_fusion.3), channel_id=1, source_target_pairs={{0,512},{64,576},{128,640},{192,704},{256,768},{320,832},{384,896}... | collective-permute-start | bytes 393224 | tf_op jit(solution)/shard_map/ppermute | solution.py:115
  108.6 9.1 %collective-permute-done.8 = bf16[128,512]{1,0:T(8,128)(2,1)S(1)} collective-permute-done((bf16[128,512]{1,0:T(8,128)(2,1)S(1)}, bf16[128,512]{1,0:T(8,128)(2,1)S(1)}, u32[]{:S(2)}, u32[]{:S(2)}) %collective-permute-start.8) | collective-permute-done | bytes 131104 | tf_op jit(solution)/shard_map/ppermute | solution.py:115
  117.9 2.1 %collective-permute-start.10 = (bf16[256,512]{1,0:T(8,128)(2,1)S(1)}, bf16[256,512]{1,0:T(8,128)(2,1)S(1)}, u32[]{:S(2)}, u32[]{:S(2)}) collective-permute-start(bf16[256,512]{1,0:T(8,128)(2,1)S(1)} %maximum_select_fusion.2), channel_id=1, source_target_pairs={{0,64},{64,0},{128,192},{192,128},{256,320},{320,256},{384,448},{4... | collective-permute-start | bytes 786440 | tf_op jit(solution)/shard_map/ppermute | solution.py:115
  119.9 1.5 collective-permute-done.10
  121.4 1.0 maximum_select_fusion
  122.5 0.8 broadcast_in_dim.10
  123.3 14.2 %all-to-all-start.4 = ((bf16[8,64,384]{2,1,0:T(8,128)(2,1)}), bf16[8,64,384]{2,1,0:T(8,128)(2,1)S(1)}, u32[]{:S(2)}, u32[]{:S(2)}) async-start(bf16[8,64,384]{2,1,0:T(8,128)(2,1)} %broadcast_in_dim.10), calls=%async_computation.4 | async-start | bytes 786432 | tf_op jit(solution)/shard_map/all_to_all | solution.py:43
  138.0 0.4 copy-done.10
  138.6 1.0 convert_add_fusion.1
  139.6 0.3 fusion.10
  140.0 4.5 %collective-permute-start.11 = (bf16[384,256]{0,1:T(8,128)(2,1)S(1)}, bf16[384,256]{0,1:T(8,128)(2,1)S(1)}, u32[]{:S(2)}, u32[]{:S(2)}) collective-permute-start(bf16[384,256]{0,1:T(8,128)(2,1)S(1)} %fusion.10), channel_id=1, source_target_pairs={{0,1},{1,0},{2,3},{3,2},{4,5},{5,4},{6,7},{7,6},{8,9},{9,8},{10,11... | collective-permute-start | bytes 589832 | tf_op jit(solution)/shard_map/ppermute | solution.py:151
  144.5 1.0 convert_add_fusion.2
  145.5 2.4 %collective-permute-done.11 = bf16[384,256]{0,1:T(8,128)(2,1)S(1)} collective-permute-done((bf16[384,256]{0,1:T(8,128)(2,1)S(1)}, bf16[384,256]{0,1:T(8,128)(2,1)S(1)}, u32[]{:S(2)}, u32[]{:S(2)}) %collective-permute-start.11) | collective-permute-done | bytes 196640 | tf_op jit(solution)/shard_map/ppermute | solution.py:151
  147.9 1.1 convolution_bitcast_fusion
  149.1 0.9 fusion.12
  150.0 11.9 %collective-permute-start.12 = (bf16[256,384]{1,0:T(8,128)(2,1)S(1)}, bf16[256,384]{1,0:T(8,128)(2,1)S(1)}, u32[]{:S(2)}, u32[]{:S(2)}) collective-permute-start(bf16[256,384]{1,0:T(8,128)(2,1)S(1)} %bitcast.88), channel_id=1, source_target_pairs={{0,64},{64,0},{128,192},{192,128},{256,320},{320,256},{384,448},{4... | collective-permute-start | bytes 589832 | tf_op jit(solution)/shard_map/ppermute | solution.py:61
  161.9 3.4 %all-to-all-start.5 = ((bf16[8,24,256]{2,1,0:T(8,128)(2,1)}), bf16[8,24,256]{2,1,0:T(8,128)(2,1)S(1)}, u32[]{:S(2)}, u32[]{:S(2)}) async-start(bf16[8,24,256]{2,1,0:T(8,128)(2,1)} %bitcast.20), calls=%async_computation.5 | async-start | bytes 196608 | tf_op jit(solution)/shard_map/all_to_all | solution.py:37
  165.2 0.3 convert_add_fusion
  165.6 4.9 %all-to-all-done.5 = bf16[8,24,256]{2,1,0:T(8,128)(2,1)S(1)} async-done(((bf16[8,24,256]{2,1,0:T(8,128)(2,1)}), bf16[8,24,256]{2,1,0:T(8,128)(2,1)S(1)}, u32[]{:S(2)}, u32[]{:S(2)}) %all-to-all-start.5) | async-done | bytes 98336 | tf_op jit(solution)/shard_map/all_to_all | solution.py:37
  170.5 0.7 broadcast_in_dim.11
  171.2 4.5 %all-to-all-start.6 = ((bf16[16,24,256]{2,1,0:T(8,128)(2,1)}), bf16[16,24,256]{2,1,0:T(8,128)(2,1)S(1)}, u32[]{:S(2)}, u32[]{:S(2)}) async-start(bf16[16,24,256]{2,1,0:T(8,128)(2,1)} %broadcast_in_dim.11), calls=%async_computation.6 | async-start | bytes 393216 | tf_op jit(solution)/shard_map/all_to_all | solution.py:43
  176.1 4.6 %collective-permute-start.13 = (bf16[384,96]{0,1:T(8,128)(2,1)S(1)}, bf16[384,96]{0,1:T(8,128)(2,1)S(1)}, u32[]{:S(2)}, u32[]{:S(2)}) collective-permute-start(bf16[384,96]{0,1:T(8,128)(2,1)S(1)} %fusion.13), channel_id=1, source_target_pairs={{0,1},{1,0},{2,3},{3,2},{4,5},{5,4},{6,7},{7,6},{8,9},{9,8},{10,11... | collective-permute-start | bytes 221192 | tf_op jit(solution)/shard_map/ppermute | solution.py:180
  180.7 0.9 copy.18
  181.7 0.8 all-to-all-done.6
  182.6 0.7 copy.19
  183.3 1.4 collective-permute-done.13
  184.7 0.9 fusion.11
  (64 shorter events, 2.1 us)
Async XLA Ops:
  0.6 1.0 copy-start
  0.6 2.3 %copy-start.1 = (bf16[384,512]{1,0:T(8,128)(2,1)S(1)}, bf16[384,512]{1,0:T(8,128)(2,1)}, u32[]{:S(2)}) copy-start(bf16[384,512]{1,0:T(8,128)(2,1)} %param.11) | copy-start | bytes 1179652
  1.6 1.7 copy-start.4
  3.0 1.0 copy-start.5
  4.3 16.3 %copy-start.2 = (bf16[384,512]{1,0:T(8,128)(2,1)S(1)}, bf16[384,512]{1,0:T(8,128)(2,1)}, u32[]{:S(2)}) copy-start(bf16[384,512]{1,0:T(8,128)(2,1)} %param.10) | copy-start | bytes 1179652
  4.4 18.1 %collective-permute-start = (bf16[8,96,512]{2,1,0:T(8,128)(2,1)S(1)}, bf16[8,96,512]{2,1,0:T(8,128)(2,1)S(1)}, u32[]{:S(2)}, u32[]{:S(2)}) collective-permute-start(bf16[8,96,512]{2,1,0:T(8,128)(2,1)S(1)} %pad_maximum_fusion), channel_id=1, source_target_pairs={{0,64},{64,0},{128,192},{192,128},{256,320},{320,256},{384,448},{4... | collective-permute-start | bytes 2359304 | tf_op jit(solution)/shard_map/ppermute | solution.py:61
  23.6 16.6 %all-to-all-start = ((bf16[8,96,512]{2,1,0:T(8,128)(2,1)}), bf16[8,96,512]{2,1,0:T(8,128)(2,1)S(1)}, u32[]{:S(2)}, u32[]{:S(2)}) async-start(bf16[8,96,512]{2,1,0:T(8,128)(2,1)} %add_convert_fusion), calls=%async_computation | async-start | bytes 1572864 | tf_op jit(solution)/shard_map/all_to_all | solution.py:37
  27.1 13.2 %collective-permute-start.1 = (bf16[384,512]{1,0:T(8,128)(2,1)S(1)}, bf16[384,512]{1,0:T(8,128)(2,1)}, u32[]{:S(2)}, u32[]{:S(2)}) collective-permute-start(bf16[384,512]{1,0:T(8,128)(2,1)S(1)} %copy-done.2), channel_id=1, source_target_pairs={{0,64},{64,0},{128,192},{192,128},{256,320},{320,256},{384,448},{4... | collective-permute-start | bytes 1179656 | tf_op jit(solution)/shard_map/ppermute | solution.py:61
  29.4 10.9 %collective-permute-start.2 = (bf16[384,512]{1,0:T(8,128)(2,1)S(1)}, bf16[384,512]{1,0:T(8,128)(2,1)}, u32[]{:S(2)}, u32[]{:S(2)}) collective-permute-start(bf16[384,512]{1,0:T(8,128)(2,1)S(1)} %copy-done.1), channel_id=1, source_target_pairs={{0,64},{64,0},{128,192},{192,128},{256,320},{320,256},{384,448},{4... | collective-permute-start | bytes 1179656 | tf_op jit(solution)/shard_map/ppermute | solution.py:61
  31.5 8.8 %collective-permute-start.4 = (bf16[256,384]{1,0:T(8,128)(2,1)S(1)}, bf16[256,384]{1,0:T(8,128)(2,1)S(1)}, u32[]{:S(2)}, u32[]{:S(2)}) collective-permute-start(bf16[256,384]{1,0:T(8,128)(2,1)S(1)} %get-tuple-element.41), channel_id=1, source_target_pairs={{0,64},{64,0},{128,192},{192,128},{256,320},{320,256},{384,448},{4... | collective-permute-start | bytes 589832 | tf_op jit(solution)/shard_map/ppermute | solution.py:61
  33.8 6.5 %collective-permute-start.3 = (bf16[384,192]{0,1:T(8,128)(2,1)}, bf16[384,192]{0,1:T(8,128)(2,1)S(1)}, u32[]{:S(2)}, u32[]{:S(2)}) collective-permute-start(bf16[384,192]{0,1:T(8,128)(2,1)} %param.13), channel_id=1, source_target_pairs={{0,64},{64,0},{128,192},{192,128},{256,320},{320,256},{384,448},{4... | collective-permute-start | bytes 442376 | tf_op jit(solution)/shard_map/ppermute | solution.py:61
  40.3 13.1 %copy-start.16 = (bf16[384,192]{0,1:T(8,128)(2,1)}, bf16[384,192]{0,1:T(8,128)(2,1)S(1)}, u32[]{:S(2)}) copy-start(bf16[384,192]{0,1:T(8,128)(2,1)S(1)} %collective-permute-done.3) | copy-start | bytes 442372
  40.3 0.7 copy-start.14
  56.8 24.1 %all-to-all-start.2 = ((bf16[8,64,384]{2,1,0:T(8,128)(2,1)}), bf16[8,64,384]{2,1,0:T(8,128)(2,1)S(1)}, u32[]{:S(2)}, u32[]{:S(2)}) async-start(bf16[8,64,384]{2,1,0:T(8,128)(2,1)} %pad_maximum_fusion.1), calls=%async_computation.2 | async-start | bytes 786432 | tf_op jit(solution)/shard_map/all_to_all | solution.py:37
  66.9 4.9 %collective-permute-start.5 = (bf16[32,512]{1,0:T(8,128)(2,1)S(1)}, bf16[32,512]{1,0:T(8,128)(2,1)S(1)}, u32[]{:S(2)}, u32[]{:S(2)}) collective-permute-start(bf16[32,512]{1,0:T(8,128)(2,1)S(1)} %get-tuple-element.48), channel_id=1, source_target_pairs={{0,128},{64,192},{128,0},{192,64},{256,384},{320,448},{384,256},{4... | collective-permute-start | bytes 98312 | tf_op jit(solution)/shard_map/ppermute | solution.py:115
  71.8 9.1 %collective-permute-start.6 = (bf16[8,64,512]{2,1,0:T(8,128)(2,1)S(1)}, bf16[8,64,512]{2,1,0:T(8,128)(2,1)}, u32[]{:S(2)}, u32[]{:S(2)}) collective-permute-start(bf16[8,64,512]{2,1,0:T(8,128)(2,1)S(1)} %all_to_all.35), channel_id=1, source_target_pairs={{0,64},{64,0},{128,192},{192,128},{256,320},{320,256},{384,448},{4... | collective-permute-start | bytes 1572872 | tf_op jit(solution)/shard_map/ppermute | solution.py:61
  74.0 6.8 %collective-permute-start.7 = (bf16[64,512]{1,0:T(8,128)(2,1)S(1)}, bf16[64,512]{1,0:T(8,128)(2,1)S(1)}, u32[]{:S(2)}, u32[]{:S(2)}) collective-permute-start(bf16[64,512]{1,0:T(8,128)(2,1)S(1)} %maximum_select_fusion.4), channel_id=1, source_target_pairs={{0,256},{64,320},{128,384},{192,448},{256,0},{320,64},{384,128},{4... | collective-permute-start | bytes 196616 | tf_op jit(solution)/shard_map/ppermute | solution.py:115
  82.0 20.1 %copy-start.7 = (bf16[8,32,512]{2,1,0:T(8,128)(2,1)}, bf16[8,32,512]{2,1,0:T(8,128)(2,1)S(1)}, u32[]{:S(2)}) copy-start(bf16[8,32,512]{2,1,0:T(8,128)(2,1)S(1)} %get-tuple-element.92) | copy-start | bytes 786436
  82.0 20.1 %copy-start.9 = (bf16[8,32,512]{2,1,0:T(8,128)(2,1)}, bf16[8,32,512]{2,1,0:T(8,128)(2,1)S(1)}, u32[]{:S(2)}) copy-start(bf16[8,32,512]{2,1,0:T(8,128)(2,1)S(1)} %get-tuple-element.93) | copy-start | bytes 786436
  82.8 39.6 %all-to-all-start.3 = ((bf16[4,64,384]{2,1,0:T(8,128)(2,1)}), bf16[4,64,384]{2,1,0:T(8,128)(2,1)S(1)}, u32[]{:S(2)}, u32[]{:S(2)}) async-start(bf16[4,64,384]{2,1,0:T(8,128)(2,1)} %broadcast_in_dim.9), calls=%async_computation.3 | async-start | bytes 393216 | tf_op jit(solution)/shard_map/all_to_all | solution.py:43
  102.2 15.7 %collective-permute-start.9 = (bf16[768,256]{1,0:T(8,128)(2,1)S(1)}, bf16[768,256]{1,0:T(8,128)(2,1)S(1)}, u32[]{:S(2)}, u32[]{:S(2)}) collective-permute-start(bf16[768,256]{1,0:T(8,128)(2,1)S(1)} %pad_maximum_fusion.2), channel_id=1, source_target_pairs={{0,1},{1,0},{2,3},{3,2},{4,5},{5,4},{6,7},{7,6},{8,9},{9,8},{10,11... | collective-permute-start | bytes 1179656 | tf_op jit(solution)/shard_map/ppermute | solution.py:140
  106.7 11.1 %collective-permute-start.8 = (bf16[128,512]{1,0:T(8,128)(2,1)S(1)}, bf16[128,512]{1,0:T(8,128)(2,1)S(1)}, u32[]{:S(2)}, u32[]{:S(2)}) collective-permute-start(bf16[128,512]{1,0:T(8,128)(2,1)S(1)} %maximum_select_fusion.3), channel_id=1, source_target_pairs={{0,512},{64,576},{128,640},{192,704},{256,768},{320,832},{384,896}... | collective-permute-start | bytes 393224 | tf_op jit(solution)/shard_map/ppermute | solution.py:115
  117.8 4.6 %copy-start.15 = (bf16[256,384]{1,0:T(8,128)(2,1)S(1)}, bf16[256,384]{1,0:T(8,128)(2,1)}, u32[]{:S(2)}) copy-start(bf16[256,384]{1,0:T(8,128)(2,1)} %copy-done.14) | copy-start | bytes 589828
  117.8 5.4 %copy-start.11 = (bf16[768,256]{1,0:T(8,128)(2,1)}, bf16[768,256]{1,0:T(8,128)(2,1)S(1)}, u32[]{:S(2)}) copy-start(bf16[768,256]{1,0:T(8,128)(2,1)S(1)} %collective-permute-done.9) | copy-start | bytes 1179652
  117.9 3.6 %collective-permute-start.10 = (bf16[256,512]{1,0:T(8,128)(2,1)S(1)}, bf16[256,512]{1,0:T(8,128)(2,1)S(1)}, u32[]{:S(2)}, u32[]{:S(2)}) collective-permute-start(bf16[256,512]{1,0:T(8,128)(2,1)S(1)} %maximum_select_fusion.2), channel_id=1, source_target_pairs={{0,64},{64,0},{128,192},{192,128},{256,320},{320,256},{384,448},{4... | collective-permute-start | bytes 786440 | tf_op jit(solution)/shard_map/ppermute | solution.py:115
  123.3 24.6 %all-to-all-start.4 = ((bf16[8,64,384]{2,1,0:T(8,128)(2,1)}), bf16[8,64,384]{2,1,0:T(8,128)(2,1)S(1)}, u32[]{:S(2)}, u32[]{:S(2)}) async-start(bf16[8,64,384]{2,1,0:T(8,128)(2,1)} %broadcast_in_dim.10), calls=%async_computation.4 | async-start | bytes 786432 | tf_op jit(solution)/shard_map/all_to_all | solution.py:43
  137.5 0.9 copy-start.10
  137.5 1.1 copy-start.12
  138.6 1.0 copy-start.6
  138.6 5.9 %copy-start.8 = (bf16[8,32,512]{2,1,0:T(8,128)(2,1)S(1)}, bf16[8,32,512]{2,1,0:T(8,128)(2,1)}, u32[]{:S(2)}) copy-start(bf16[8,32,512]{2,1,0:T(8,128)(2,1)} %copy-done.7) | copy-start | bytes 786436
  140.0 7.9 %collective-permute-start.11 = (bf16[384,256]{0,1:T(8,128)(2,1)S(1)}, bf16[384,256]{0,1:T(8,128)(2,1)S(1)}, u32[]{:S(2)}, u32[]{:S(2)}) collective-permute-start(bf16[384,256]{0,1:T(8,128)(2,1)S(1)} %fusion.10), channel_id=1, source_target_pairs={{0,1},{1,0},{2,3},{3,2},{4,5},{5,4},{6,7},{7,6},{8,9},{9,8},{10,11... | collective-permute-start | bytes 589832 | tf_op jit(solution)/shard_map/ppermute | solution.py:151
  145.5 3.6 %copy-start.17 = (bf16[384,192]{0,1:T(8,128)(2,1)S(1)}, bf16[384,192]{0,1:T(8,128)(2,1)}, u32[]{:S(2)}) copy-start(bf16[384,192]{0,1:T(8,128)(2,1)} %copy-done.16) | copy-start | bytes 442372
  150.0 25.7 %collective-permute-start.12 = (bf16[256,384]{1,0:T(8,128)(2,1)S(1)}, bf16[256,384]{1,0:T(8,128)(2,1)S(1)}, u32[]{:S(2)}, u32[]{:S(2)}) collective-permute-start(bf16[256,384]{1,0:T(8,128)(2,1)S(1)} %bitcast.88), channel_id=1, source_target_pairs={{0,64},{64,0},{128,192},{192,128},{256,320},{320,256},{384,448},{4... | collective-permute-start | bytes 589832 | tf_op jit(solution)/shard_map/ppermute | solution.py:61
  161.9 8.6 %all-to-all-start.5 = ((bf16[8,24,256]{2,1,0:T(8,128)(2,1)}), bf16[8,24,256]{2,1,0:T(8,128)(2,1)S(1)}, u32[]{:S(2)}, u32[]{:S(2)}) async-start(bf16[8,24,256]{2,1,0:T(8,128)(2,1)} %bitcast.20), calls=%async_computation.5 | async-start | bytes 196608 | tf_op jit(solution)/shard_map/all_to_all | solution.py:37
  165.6 10.3 %copy-start.13 = (bf16[512,192]{0,1:T(8,128)(2,1)S(1)}, bf16[512,192]{0,1:T(8,128)(2,1)}, u32[]{:S(2)}) copy-start(bf16[512,192]{0,1:T(8,128)(2,1)} %param.8) | copy-start | bytes 589828
  171.2 11.2 %all-to-all-start.6 = ((bf16[16,24,256]{2,1,0:T(8,128)(2,1)}), bf16[16,24,256]{2,1,0:T(8,128)(2,1)S(1)}, u32[]{:S(2)}, u32[]{:S(2)}) async-start(bf16[16,24,256]{2,1,0:T(8,128)(2,1)} %broadcast_in_dim.11), calls=%async_computation.6 | async-start | bytes 393216 | tf_op jit(solution)/shard_map/all_to_all | solution.py:43
  175.8 8.8 %copy-start.3 = (bf16[512,384]{1,0:T(8,128)(2,1)}, bf16[512,384]{1,0:T(8,128)(2,1)S(1)}, u32[]{:S(2)}) copy-start(bf16[512,384]{1,0:T(8,128)(2,1)S(1)} %maximum_select_fusion.1) | copy-start | bytes 1179652
  176.1 8.6 %collective-permute-start.13 = (bf16[384,96]{0,1:T(8,128)(2,1)S(1)}, bf16[384,96]{0,1:T(8,128)(2,1)S(1)}, u32[]{:S(2)}, u32[]{:S(2)}) collective-permute-start(bf16[384,96]{0,1:T(8,128)(2,1)S(1)} %fusion.13), channel_id=1, source_target_pairs={{0,1},{1,0},{2,3},{3,2},{4,5},{5,4},{6,7},{7,6},{8,9},{9,8},{10,11... | collective-permute-start | bytes 221192 | tf_op jit(solution)/shard_map/ppermute | solution.py:180

commit v6 on v5

--- a/solution.py
+++ b/solution.py
@@ -77,21 +77,20 @@
 
     away = swap(products(in_other, out_other))
     parts = (products(in_mine, out_mine).astype(F32) + away.astype(F32)).astype(BF16)
-    parts, *to_swap = tie((parts, w_gate, w_up, w_out, out_other))
+    parts, w_gate, w_up, *to_swap = tie((parts, w_gate, w_up, w_out, out_other))
+    w_both = jnp.concatenate([w_gate, w_up], axis=1)
+    to_swap = [w_both, *to_swap]
     total = scatter_sum(parts, "row", chip_groups)
-    total, gate_far, up_far, w_out_far, out_far = tie((total, *(swap(x) for x in to_swap)))
+    w_both_far, w_out_far, out_far = (swap(x) for x in to_swap)
+    w_pair = jnp.concatenate([w_both, w_both_far])
+    w_out_pair = jnp.concatenate([w_out, w_out_far])
+    out_pair = jnp.concatenate([out_mine, out_far], axis=1)
+    total, w_pair, w_out_pair, out_pair = tie((total, w_pair, w_out_pair, out_pair))
     gate_share, up_share, hid_share = swiglu_grads(
         total[:share], total[share : 2 * share], total[2 * share :]
     )
-    mine = gather(jnp.concatenate([gate_share, up_share]), chips, "row", chip_groups)
-
-    def split(x):
-        return [
-            x[:, i * share : (i + 1) * share].reshape(half, hidden_width)
-            for i in range(2)
-        ]
-
-    gate_mine, up_mine = split(mine)
+    mine = gather(jnp.concatenate([gate_share, up_share], axis=1), chips, "row", chip_groups)
+    mine = mine.reshape(half, 2 * hidden_width)
 
     near, far = 8, cols // 8
 
@@ -102,67 +101,59 @@
     far_groups = [[place(r, k, j) for k in range(far)] for r in range(rows) for j in range(near)]
     both = ("row", "col")
     spot = (lax.axis_index("col") + cols - 4 * core) % near
-    piece = tokens // near
 
-    def pair_blocks(own, away):
-        return jnp.concatenate([x.reshape(near, half // near, width) for x in (own, away)], axis=1)
-
-    def back(wg, wu):
-        return (contract_cols(gate_mine, wg) + contract_cols(up_mine, wu)).astype(BF16)
-
-    back_part = pair_blocks(back(w_gate, w_up), back(gate_far, up_far))
-    def double(x, bit):
+    back_part = contract_cols(mine, w_pair).astype(BF16).reshape(near, half // near, 2 * width)
+    def double(x, bit, runs=1):
         got = lax.ppermute(x, "row", [(i, i ^ bit) for i in range(rows)])
         low = (lax.axis_index("row") & bit) == 0
-        return jnp.where(low, jnp.concatenate([x, got]), jnp.concatenate([got, x]))
+        x, got = (a.reshape(runs, -1, hidden_width) for a in (x, got))
+        pair = jnp.where(low, jnp.concatenate([x, got], axis=1), jnp.concatenate([got, x], axis=1))
+        return pair.reshape(-1, hidden_width)
 
-    back_part, mine, hid_share = tie((back_part, mine, hid_share))
-    mine, hid_pair = tie((mine, double(hid_share, 2)))
-    other = swap(mine)
-    hid_row = double(hid_pair, 4)
+    back_part, sent_mine, hid_share = tie((back_part, mine, hid_share))
+    sent_mine, hid_pair = tie((sent_mine, double(hid_share, 2)))
+    other = swap(sent_mine)
+    hid_row = double(hid_pair, 8)
     near_sum = scatter_sum(back_part, both, near_groups).astype(BF16)
     near_sum, other, hid_row = tie((near_sum, other, hid_row))
-    gate_other, up_other = split(other)
 
     norm_factor = (tokens * lax.axis_size("seq")) ** (-0.5)
 
-    def wgrad(pairs, which):
-        size = pairs[0][1].shape[1] // 2
+    def wgrad(pairs, which, start=0, size=hidden_width // 2):
         terms = [
-            contract_rows(a, lax.dynamic_slice_in_dim(b, which * size, size, 1))
+            contract_rows(a, lax.dynamic_slice_in_dim(b, start + which * size, size, 1))
             for a, b in pairs
         ]
         return sum(terms) * norm_factor
 
-    gate_pairs = ((in_mine, gate_mine), (in_other, gate_other))
-    up_pairs = ((in_mine, up_mine), (in_other, up_other))
-    sent = jnp.concatenate([wgrad(p, 1 - seq).astype(BF16) for p in (gate_pairs, up_pairs)])
+    both_pairs = ((in_mine, mine), (in_other, other))
+    sent = jnp.concatenate([wgrad(both_pairs, 1 - seq, n).astype(BF16) for n in (0, hidden_width)])
     received = lax.ppermute(sent, "seq", seq_swap)
     hid_row, _ = tie((hid_row, sent))
-    hid_chips, received = tie((double(hid_row, 8), received))
+    hid_chips, received = tie((double(hid_row, 4, 2), received))
     hid_all = double(hid_chips, 1)
 
     group_sums = gather(near_sum, far, both, far_groups)
     far_sum = jnp.sum(group_sums.astype(F32), axis=0)
     far_sum, hid_all = tie((far_sum, hid_all))
-    out_piece = lax.dynamic_index_in_dim(pair_blocks(out_mine, out_far), spot, 0, False)
+    out_piece = lax.dynamic_index_in_dim(out_pair.reshape(back_part.shape), spot, 0, False)
     resid_piece = (out_piece.astype(F32) + far_sum).astype(BF16)
     down_pairs = ((out_grad, hid_all),)
     down_received = lax.ppermute(wgrad(down_pairs, 1 - seq).astype(BF16), "seq", seq_swap)
-    gate_wgrad = wgrad(gate_pairs, seq) + received[:width].astype(F32)
-    up_wgrad = wgrad(up_pairs, seq) + received[width:].astype(F32)
+    gate_wgrad = wgrad(both_pairs, seq) + received[:width].astype(F32)
+    up_wgrad = wgrad(both_pairs, seq, hidden_width) + received[width:].astype(F32)
     resid_all = gather(resid_piece, near, both, near_groups)
     resid_all, down_received, gate_wgrad, up_wgrad = tie(
         (resid_all, down_received, gate_wgrad, up_wgrad)
     )
     down_wgrad = wgrad(down_pairs, seq) + down_received.astype(F32)
-    resid_all = resid_all.reshape(near, 2, half // near, width)
-    resid_mine, resid_far = (resid_all[:, i].reshape(half, width) for i in range(2))
+    resid_all = resid_all.reshape(half, 2 * width)
+    resid_mine, resid_far = resid_all[:, :width], resid_all[:, width:]
 
     def heads_by_tokens(w, x):
         return lax.dot_general(w, x, (((0,), (1,)), ((), ())), preferred_element_type=F32)
 
-    mix_part = (heads_by_tokens(w_out, resid_mine) + heads_by_tokens(w_out_far, resid_far)).astype(BF16)
+    mix_part = heads_by_tokens(w_out_pair, resid_all).astype(BF16)
     mix_part, resid_far = tie((mix_part, resid_far))
     mix_share = scatter_sum(mix_part.reshape(chips, -1, half), "row", chip_groups)
     mix_share, down_wgrad = tie((mix_share.astype(BF16), down_wgrad))
@@ -176,8 +167,9 @@
         jnp.concatenate([resid_other, resid_mine]),
     )
     out_pairs = ((resid_grad, attn_mix),)
-    out_sent = wgrad(out_pairs, 1 - seq).astype(BF16)
-    out_wgrad = wgrad(out_pairs, seq) + lax.ppermute(out_sent, "seq", seq_swap).astype(F32)
+    heads = attn_mix.shape[1] // 2
+    out_sent = wgrad(out_pairs, 1 - seq, 0, heads).astype(BF16)
+    out_wgrad = wgrad(out_pairs, seq, 0, heads) + lax.ppermute(out_sent, "seq", seq_swap).astype(F32)
     return (resid_grad, attn_grad, gate_wgrad, up_wgrad, down_wgrad, out_wgrad)
 
 

time: 187 us -> 182 us (0.973)
  waiting for transfers between devices: 31.8 us -> 28.1 us
  local copies, waits for them, and re-layouts: 8.1 us -> 5.19 us
    ppermute x4, waiting for transfers between devices: 17.1 us -> 13 us  [double(): got = lax.ppermute(x, 'row', [(i, i ^ bit) for i in range(rows)])]
    all_to_all x3, starting transfers between devices: 37.5 us -> 39.8 us  [gather(): lax.all_to_all(copies, axis, 0, 0, tiled=True, axis_index_groups=groups)]
    dot_general x12, matrix products: 5.32 us -> 7.3 us  [contract_rows(): lax.dot_general(first, second, (((0,), (0,)), ((), ())), preferred_elemen...]
    dot_general x4 -> x1, matrix products: 3.25 us -> 1.37 us  [contract_cols(): lax.dot_general(first, second, (((1,), (1,)), ((), ())), preferred_elemen...]
    unnamed x38 -> x23, local copies, waits for them, and re-layouts: 4.48 us -> 2.65 us
    ppermute x7 -> x6, starting transfers between devices: 38.6 us -> 37.1 us  [swap(): return lax.ppermute(x, 'row', core_swap)]
  transfers between devices with their start and end apart: 20 -> 19, of which waited for: 10 -> 12; matrix products, arithmetic and copies ran while one was open for 5% -> 7% of each run, Pallas kernels for 0% -> 0%
where the time goes in v6:
time: 182 us; the launch traced here: 181 us
  starting transfers between devices  117 us (64%)
  waiting for transfers between devices  28.1 us (15%)
  matrix products  13.4 us (7%)
  blocking collectives  11.6 us (6%)
  local copies, waits for them, and re-layouts  5.19 us (3%)
  other arithmetic  4.35 us (2%)
    all_to_all x3, starting transfers between devices, gather(): lax.all_to_all(copies, axis, 0, 0, tiled=True, axis_index_groups=groups)  39.8 us
    ppermute x6, starting transfers between devices, swap(): return lax.ppermute(x, 'row', core_swap)  37.1 us
    all_to_all x3, starting transfers between devices, scatter_sum(): lax.all_to_all(parts, axis, 0, 0, tiled=True, axis_index_groups=groups)  17 us
    ppermute x4, waiting for transfers between devices, double(): got = lax.ppermute(x, 'row', [(i, i ^ bit) for i in range(rows)])  13 us
    all_to_all x1, blocking collectives, gather(): lax.all_to_all(copies, axis, 0, 0, tiled=True, axis_index_groups=groups)  11.6 us
    all_to_all x3, waiting for transfers between devices, scatter_sum(): lax.all_to_all(parts, axis, 0, 0, tiled=True, axis_index_groups=groups)  9.32 us
    ppermute x4, starting transfers between devices, double(): got = lax.ppermute(x, 'row', [(i, i ^ bit) for i in range(rows)])  9.2 us
    dot_general x12, matrix products, contract_rows(): lax.dot_general(first, second, (((0,), (0,)), ((), ())), preferred_elemen...  7.3 us
  transfers between devices with their start and end apart: 19, of which 12 were waited for; matrix products, arithmetic and copies ran while one was open for 7% of the time, Pallas kernels for 0%

profile of v6, /device:TPU:1, one launch (start us, length us, event | category | flops | bytes accessed | tf_op | source)
XLA Modules:
  0.0 180.6 jit_solution(12562660558914392524)
XLA Ops:
  0.7 0.9 copy-done
  1.6 1.3 convolution_convert_fusion.2
  2.9 1.3 convolution_convert_fusion.3
  4.3 0.3 convolution_convert_fusion.1
  4.7 16.1 %collective-permute-start = (bf16[8,96,512]{2,1,0:T(8,128)(2,1)S(1)}, bf16[8,96,512]{2,1,0:T(8,128)(2,1)S(1)}, u32[]{:S(2)}, u32[]{:S(2)}) collective-permute-start(bf16[8,96,512]{2,1,0:T(8,128)(2,1)S(1)} %pad_maximum_fusion.1), channel_id=1, source_target_pairs={{0,64},{64,0},{128,192},{192,128},{256,320},{320,256},{384,448},{4... | collective-permute-start | bytes 2359304 | tf_op jit(solution)/shard_map/ppermute | solution.py:61
  20.8 0.3 convolution_convert_fusion.5
  21.1 0.3 convolution_convert_fusion.6
  21.4 0.3 convolution_convert_fusion.4
  21.7 1.0 collective-permute-done
  22.7 1.1 add_convert_fusion
  23.8 3.5 %all-to-all-start = ((bf16[8,96,512]{2,1,0:T(8,128)(2,1)}), bf16[8,96,512]{2,1,0:T(8,128)(2,1)S(1)}, u32[]{:S(2)}, u32[]{:S(2)}) async-start(bf16[8,96,512]{2,1,0:T(8,128)(2,1)} %add_convert_fusion), calls=%async_computation | async-start | bytes 1572864 | tf_op jit(solution)/shard_map/all_to_all | solution.py:37
  27.5 2.3 %collective-permute-start.1 = (bf16[384,1024]{1,0:T(8,128)(2,1)S(1)}, bf16[384,1024]{1,0:T(8,128)(2,1)S(1)}, u32[]{:S(2)}, u32[]{:S(2)}) collective-permute-start(bf16[384,1024]{1,0:T(8,128)(2,1)S(1)} %constant_dynamic-update-slice_fusion), channel_id=1, source_target_pairs={{0,64},{64,0},{128,192},{192,128},{256,320},{320,256},{384,448},{4... | collective-permute-start | bytes 2359304 | tf_op jit(solution)/shard_map/ppermute | solution.py:61
  29.8 2.0 %collective-permute-start.2 = (bf16[384,192]{0,1:T(8,128)(2,1)S(1)}, bf16[384,192]{0,1:T(8,128)(2,1)S(1)}, u32[]{:S(2)}, u32[]{:S(2)}) collective-permute-start(bf16[384,192]{0,1:T(8,128)(2,1)S(1)} %copy-done.9), channel_id=1, source_target_pairs={{0,64},{64,0},{128,192},{192,128},{256,320},{320,256},{384,448},{4... | collective-permute-start | bytes 442376 | tf_op jit(solution)/shard_map/ppermute | solution.py:61
  31.8 2.3 %collective-permute-start.3 = (bf16[256,384]{1,0:T(8,128)(2,1)S(1)}, bf16[256,384]{1,0:T(8,128)(2,1)S(1)}, u32[]{:S(2)}, u32[]{:S(2)}) collective-permute-start(bf16[256,384]{1,0:T(8,128)(2,1)S(1)} %get-tuple-element.40), channel_id=1, source_target_pairs={{0,64},{64,0},{128,192},{192,128},{256,320},{320,256},{384,448},{4... | collective-permute-start | bytes 589832 | tf_op jit(solution)/shard_map/ppermute | solution.py:61
  34.1 0.7 pad_maximum_fusion.4
  34.8 0.3 collective-permute-done.3
  35.1 0.8 pad_maximum_fusion.2
  35.9 4.4 %all-to-all-done = bf16[8,96,512]{2,1,0:T(8,128)(2,1)S(1)} async-done(((bf16[8,96,512]{2,1,0:T(8,128)(2,1)}), bf16[8,96,512]{2,1,0:T(8,128)(2,1)S(1)}, u32[]{:S(2)}, u32[]{:S(2)}) %all-to-all-start) | async-done | bytes 786464 | tf_op jit(solution)/shard_map/all_to_all | solution.py:37
  40.7 11.6 %all_to_all.35 = bf16[8,32,1024]{2,1,0:T(8,128)(2,1)S(1)} all-to-all(bf16[8,32,1024]{2,1,0:T(8,128)(2,1)S(1)} %broadcast_in_dim.8), channel_id=1, replica_groups={{0,128,256,384,512,640,768,896},{64,192,320,448,576,704,832,960},{1,129..., dimensions={0} | all-to-all | bytes 1048576 | tf_op jit(solution)/shard_map/all_to_all | solution.py:43
  52.4 1.4 convolution_convert_fusion
  53.7 10.1 %all-to-all-start.2 = ((bf16[8,32,768]{2,1,0:T(8,128)(2,1)}), bf16[8,32,768]{2,1,0:T(8,128)(2,1)S(1)}, u32[]{:S(2)}, u32[]{:S(2)}) async-start(bf16[8,32,768]{2,1,0:T(8,128)(2,1)} %bitcast.9), calls=%async_computation.2 | async-start | bytes 786432 | tf_op jit(solution)/shard_map/all_to_all | solution.py:37
  63.8 2.5 %collective-permute-start.4 = (bf16[32,512]{1,0:T(8,128)(2,1)S(1)}, bf16[32,512]{1,0:T(8,128)(2,1)S(1)}, u32[]{:S(2)}, u32[]{:S(2)}) collective-permute-start(bf16[32,512]{1,0:T(8,128)(2,1)S(1)} %get-tuple-element.46), channel_id=1, source_target_pairs={{0,128},{64,192},{128,0},{192,64},{256,384},{320,448},{384,256},{4... | collective-permute-start | bytes 98312 | tf_op jit(solution)/shard_map/ppermute | solution.py:107
  66.3 2.4 %collective-permute-done.4 = bf16[32,512]{1,0:T(8,128)(2,1)S(1)} collective-permute-done((bf16[32,512]{1,0:T(8,128)(2,1)S(1)}, bf16[32,512]{1,0:T(8,128)(2,1)S(1)}, u32[]{:S(2)}, u32[]{:S(2)}) %collective-permute-start.4) | collective-permute-done | bytes 32800 | tf_op jit(solution)/shard_map/ppermute | solution.py:107
  68.7 1.9 %collective-permute-start.5 = (bf16[256,1024]{1,0:T(8,128)(2,1)S(1)}, bf16[256,1024]{1,0:T(8,128)(2,1)S(1)}, u32[]{:S(2)}, u32[]{:S(2)}) collective-permute-start(bf16[256,1024]{1,0:T(8,128)(2,1)S(1)} %bitcast.50), channel_id=1, source_target_pairs={{0,64},{64,0},{128,192},{192,128},{256,320},{320,256},{384,448},{4... | collective-permute-start | bytes 1572872 | tf_op jit(solution)/shard_map/ppermute | solution.py:61
  70.7 0.3 fusion.24
  70.9 2.2 %collective-permute-start.6 = (bf16[64,512]{1,0:T(8,128)(2,1)S(1)}, bf16[64,512]{1,0:T(8,128)(2,1)S(1)}, u32[]{:S(2)}, u32[]{:S(2)}) collective-permute-start(bf16[64,512]{1,0:T(8,128)(2,1)S(1)} %maximum_select_fusion.4), channel_id=1, source_target_pairs={{0,512},{64,576},{128,640},{192,704},{256,768},{320,832},{384,896}... | collective-permute-start | bytes 196616 | tf_op jit(solution)/shard_map/ppermute | solution.py:107
  73.1 0.3 fusion.27
  73.4 2.9 %collective-permute-done.6 = bf16[64,512]{1,0:T(8,128)(2,1)S(1)} collective-permute-done((bf16[64,512]{1,0:T(8,128)(2,1)S(1)}, bf16[64,512]{1,0:T(8,128)(2,1)S(1)}, u32[]{:S(2)}, u32[]{:S(2)}) %collective-permute-start.6) | collective-permute-done | bytes 65568 | tf_op jit(solution)/shard_map/ppermute | solution.py:107
  76.4 0.7 broadcast_in_dim.9
  77.1 19.3 %all-to-all-start.3 = ((bf16[4,32,768]{2,1,0:T(8,128)(2,1)}), bf16[4,32,768]{2,1,0:T(8,128)(2,1)S(1)}, u32[]{:S(2)}, u32[]{:S(2)}) async-start(bf16[4,32,768]{2,1,0:T(8,128)(2,1)} %broadcast_in_dim.9), calls=%async_computation.3 | async-start | bytes 393216 | tf_op jit(solution)/shard_map/all_to_all | solution.py:43
  96.4 0.3 fusion.8
  96.7 0.3 fusion.9
  97.0 4.6 %collective-permute-start.8 = (bf16[768,256]{1,0:T(8,128)(2,1)S(1)}, bf16[768,256]{1,0:T(8,128)(2,1)}, u32[]{:S(2)}, u32[]{:S(2)}) collective-permute-start(bf16[768,256]{1,0:T(8,128)(2,1)S(1)} %pad_maximum_fusion.3), channel_id=1, source_target_pairs={{0,1},{1,0},{2,3},{3,2},{4,5},{5,4},{6,7},{7,6},{8,9},{9,8},{10,11... | collective-permute-start | bytes 1179656 | tf_op jit(solution)/shard_map/ppermute | solution.py:131
  101.6 2.5 %collective-permute-start.7 = (bf16[128,512]{1,0:T(8,128)(2,1)S(1)}, bf16[128,512]{1,0:T(8,128)(2,1)S(1)}, u32[]{:S(2)}, u32[]{:S(2)}) collective-permute-start(bf16[128,512]{1,0:T(8,128)(2,1)S(1)} %maximum_select_fusion.3), channel_id=1, source_target_pairs={{0,256},{64,320},{128,384},{192,448},{256,0},{320,64},{384,128},{4... | collective-permute-start | bytes 393224 | tf_op jit(solution)/shard_map/ppermute | solution.py:107
  104.1 6.4 %collective-permute-done.7 = bf16[128,512]{1,0:T(8,128)(2,1)S(1)} collective-permute-done((bf16[128,512]{1,0:T(8,128)(2,1)S(1)}, bf16[128,512]{1,0:T(8,128)(2,1)S(1)}, u32[]{:S(2)}, u32[]{:S(2)}) %collective-permute-start.7) | collective-permute-done | bytes 131104 | tf_op jit(solution)/shard_map/ppermute | solution.py:107
  110.6 0.6 collective-permute-done.8
  111.2 2.1 %collective-permute-start.9 = (bf16[256,512]{1,0:T(8,128)(2,1)S(1)}, bf16[256,512]{1,0:T(8,128)(2,1)S(1)}, u32[]{:S(2)}, u32[]{:S(2)}) collective-permute-start(bf16[256,512]{1,0:T(8,128)(2,1)S(1)} %bitcast.60), channel_id=1, source_target_pairs={{0,64},{64,0},{128,192},{192,128},{256,320},{320,256},{384,448},{4... | collective-permute-start | bytes 786440 | tf_op jit(solution)/shard_map/ppermute | solution.py:107
  113.3 1.3 collective-permute-done.9
  114.6 0.2 maximum_select_fusion
  114.9 0.8 fusion.29
  115.7 0.8 broadcast_in_dim.10
  116.5 15.9 %all-to-all-start.4 = ((bf16[8,32,768]{2,1,0:T(8,128)(2,1)}), bf16[8,32,768]{2,1,0:T(8,128)(2,1)S(1)}, u32[]{:S(2)}, u32[]{:S(2)}) async-start(bf16[8,32,768]{2,1,0:T(8,128)(2,1)} %broadcast_in_dim.10), calls=%async_computation.4 | async-start | bytes 786432 | tf_op jit(solution)/shard_map/all_to_all | solution.py:43
  132.4 0.2 fusion.21
  132.6 0.3 fusion.18
  132.9 2.0 %fusion.6 = f32[384,256]{1,0:T(8,128)} fusion(f32[384,256]{1,0:T(8,128)S(1)} %fusion.21, bf16[768,256]{1,0:T(8,128)(2,1)} %collective-permute-done.8, bf16[256,1024]{1,0:T(8,128)(2,1)} %copy-done.7, s32[]{:T(128)S(6)} %select_n.122, bf16[512,384]{1,0:T(8,128)(2,1)S(1)} %copy-done, s32[]{:T(128)S(6)} %select_n.107), kind=kOutput, calls=%fused_computation.22 | convolution fusion | flops 50724864 | bytes 1310728 | tf_op jit(solution)/shard_map/dot_general | solution.py:25
  134.9 0.3 fusion.10
  135.2 4.7 %collective-permute-start.10 = (bf16[384,256]{0,1:T(8,128)(2,1)S(1)}, bf16[384,256]{0,1:T(8,128)(2,1)S(1)}, u32[]{:S(2)}, u32[]{:S(2)}) collective-permute-start(bf16[384,256]{0,1:T(8,128)(2,1)S(1)} %fusion.10), channel_id=1, source_target_pairs={{0,1},{1,0},{2,3},{3,2},{4,5},{5,4},{6,7},{7,6},{8,9},{9,8},{10,11... | collective-permute-start | bytes 589832 | tf_op jit(solution)/shard_map/ppermute | solution.py:142
  140.0 2.0 %fusion.5 = f32[384,256]{1,0:T(8,128)} fusion(f32[384,256]{1,0:T(8,128)S(1)} %fusion.18, bf16[768,256]{1,0:T(8,128)(2,1)} %collective-permute-done.8, bf16[256,1024]{1,0:T(8,128)(2,1)} %copy-done.7, s32[]{:T(128)S(6)} %select_n.123, bf16[512,384]{1,0:T(8,128)(2,1)S(1)} %copy-done, s32[]{:T(128)S(6)} %select_n.107), kind=kOutput, calls=%fused_computation.21 | convolution fusion | flops 50724864 | bytes 1310728 | tf_op jit(solution)/shard_map/dot_general | solution.py:25
  142.0 1.4 collective-permute-done.10
  143.5 0.9 convolution_convert_fusion.7
  144.4 12.5 %collective-permute-start.11 = (bf16[256,384]{1,0:T(8,128)(2,1)S(1)}, bf16[256,384]{1,0:T(8,128)(2,1)S(1)}, u32[]{:S(2)}, u32[]{:S(2)}) collective-permute-start(bf16[256,384]{1,0:T(8,128)(2,1)S(1)} %get-tuple-element.59), channel_id=1, source_target_pairs={{0,64},{64,0},{128,192},{192,128},{256,320},{320,256},{384,448},{4... | collective-permute-start | bytes 589832 | tf_op jit(solution)/shard_map/ppermute | solution.py:61
  157.0 3.4 %all-to-all-start.5 = ((bf16[8,24,256]{2,1,0:T(8,128)(2,1)}), bf16[8,24,256]{2,1,0:T(8,128)(2,1)S(1)}, u32[]{:S(2)}, u32[]{:S(2)}) async-start(bf16[8,24,256]{2,1,0:T(8,128)(2,1)} %bitcast.15), calls=%async_computation.5 | async-start | bytes 196608 | tf_op jit(solution)/shard_map/all_to_all | solution.py:37
  160.4 0.3 convert_add_fusion
  160.7 4.9 %all-to-all-done.5 = bf16[8,24,256]{2,1,0:T(8,128)(2,1)S(1)} async-done(((bf16[8,24,256]{2,1,0:T(8,128)(2,1)}), bf16[8,24,256]{2,1,0:T(8,128)(2,1)S(1)}, u32[]{:S(2)}, u32[]{:S(2)}) %all-to-all-start.5) | async-done | bytes 98336 | tf_op jit(solution)/shard_map/all_to_all | solution.py:37
  165.6 0.7 broadcast_in_dim.11
  166.3 4.5 %all-to-all-start.6 = ((bf16[16,24,256]{2,1,0:T(8,128)(2,1)}), bf16[16,24,256]{2,1,0:T(8,128)(2,1)S(1)}, u32[]{:S(2)}, u32[]{:S(2)}) async-start(bf16[16,24,256]{2,1,0:T(8,128)(2,1)} %broadcast_in_dim.11), calls=%async_computation.6 | async-start | bytes 393216 | tf_op jit(solution)/shard_map/all_to_all | solution.py:43
  171.0 0.2 fusion.12
  171.2 4.3 %collective-permute-start.12 = (bf16[384,96]{0,1:T(8,128)(2,1)S(1)}, bf16[384,96]{0,1:T(8,128)(2,1)S(1)}, u32[]{:S(2)}, u32[]{:S(2)}) collective-permute-start(bf16[384,96]{0,1:T(8,128)(2,1)S(1)} %fusion.12), channel_id=1, source_target_pairs={{0,1},{1,0},{2,3},{3,2},{4,5},{5,4},{6,7},{7,6},{8,9},{9,8},{10,11... | collective-permute-start | bytes 221192 | tf_op jit(solution)/shard_map/ppermute | solution.py:172
  175.6 0.9 copy.18
  176.5 1.1 all-to-all-done.6
  177.6 0.2 copy.17
  177.7 0.7 copy.19
  178.4 1.3 collective-permute-done.12
  179.7 0.9 fusion.11
  (44 shorter events, 1.0 us)
Async XLA Ops:
  0.6 1.0 copy-start
  0.6 3.6 %copy-start.4 = (bf16[512,384]{1,0:T(8,128)(2,1)S(1)}, bf16[512,384]{1,0:T(8,128)(2,1)}, u32[]{:S(2)}) copy-start(bf16[512,384]{1,0:T(8,128)(2,1)} %param.9) | copy-start | bytes 1179652
  0.7 3.7 %copy-start.5 = (bf16[384,512]{1,0:T(8,128)(2,1)S(1)}, bf16[384,512]{1,0:T(8,128)(2,1)}, u32[]{:S(2)}) copy-start(bf16[384,512]{1,0:T(8,128)(2,1)} %param.12) | copy-start | bytes 1179652
  4.3 16.5 %copy-start.2 = (bf16[384,512]{1,0:T(8,128)(2,1)S(1)}, bf16[384,512]{1,0:T(8,128)(2,1)}, u32[]{:S(2)}) copy-start(bf16[384,512]{1,0:T(8,128)(2,1)} %param.11) | copy-start | bytes 1179652
  4.3 16.8 %copy-start.1 = (bf16[384,512]{1,0:T(8,128)(2,1)S(1)}, bf16[384,512]{1,0:T(8,128)(2,1)}, u32[]{:S(2)}) copy-start(bf16[384,512]{1,0:T(8,128)(2,1)} %param.10) | copy-start | bytes 1179652
  4.7 18.0 %collective-permute-start = (bf16[8,96,512]{2,1,0:T(8,128)(2,1)S(1)}, bf16[8,96,512]{2,1,0:T(8,128)(2,1)S(1)}, u32[]{:S(2)}, u32[]{:S(2)}) collective-permute-start(bf16[8,96,512]{2,1,0:T(8,128)(2,1)S(1)} %pad_maximum_fusion.1), channel_id=1, source_target_pairs={{0,64},{64,0},{128,192},{192,128},{256,320},{320,256},{384,448},{4... | collective-permute-start | bytes 2359304 | tf_op jit(solution)/shard_map/ppermute | solution.py:61
  23.8 16.6 %all-to-all-start = ((bf16[8,96,512]{2,1,0:T(8,128)(2,1)}), bf16[8,96,512]{2,1,0:T(8,128)(2,1)S(1)}, u32[]{:S(2)}, u32[]{:S(2)}) async-start(bf16[8,96,512]{2,1,0:T(8,128)(2,1)} %add_convert_fusion), calls=%async_computation | async-start | bytes 1572864 | tf_op jit(solution)/shard_map/all_to_all | solution.py:37
  27.3 2.4 %copy-start.9 = (bf16[384,192]{0,1:T(8,128)(2,1)S(1)}, bf16[384,192]{0,1:T(8,128)(2,1)}, u32[]{:S(2)}) copy-start(bf16[384,192]{0,1:T(8,128)(2,1)} %param.13) | copy-start | bytes 442372
  27.5 13.0 %collective-permute-start.1 = (bf16[384,1024]{1,0:T(8,128)(2,1)S(1)}, bf16[384,1024]{1,0:T(8,128)(2,1)S(1)}, u32[]{:S(2)}, u32[]{:S(2)}) collective-permute-start(bf16[384,1024]{1,0:T(8,128)(2,1)S(1)} %constant_dynamic-update-slice_fusion), channel_id=1, source_target_pairs={{0,64},{64,0},{128,192},{192,128},{256,320},{320,256},{384,448},{4... | collective-permute-start | bytes 2359304 | tf_op jit(solution)/shard_map/ppermute | solution.py:61
  29.8 4.3 %collective-permute-start.2 = (bf16[384,192]{0,1:T(8,128)(2,1)S(1)}, bf16[384,192]{0,1:T(8,128)(2,1)S(1)}, u32[]{:S(2)}, u32[]{:S(2)}) collective-permute-start(bf16[384,192]{0,1:T(8,128)(2,1)S(1)} %copy-done.9), channel_id=1, source_target_pairs={{0,64},{64,0},{128,192},{192,128},{256,320},{320,256},{384,448},{4... | collective-permute-start | bytes 442376 | tf_op jit(solution)/shard_map/ppermute | solution.py:61
  31.8 3.3 %collective-permute-start.3 = (bf16[256,384]{1,0:T(8,128)(2,1)S(1)}, bf16[256,384]{1,0:T(8,128)(2,1)S(1)}, u32[]{:S(2)}, u32[]{:S(2)}) collective-permute-start(bf16[256,384]{1,0:T(8,128)(2,1)S(1)} %get-tuple-element.40), channel_id=1, source_target_pairs={{0,64},{64,0},{128,192},{192,128},{256,320},{320,256},{384,448},{4... | collective-permute-start | bytes 589832 | tf_op jit(solution)/shard_map/ppermute | solution.py:61
  53.7 22.6 %all-to-all-start.2 = ((bf16[8,32,768]{2,1,0:T(8,128)(2,1)}), bf16[8,32,768]{2,1,0:T(8,128)(2,1)S(1)}, u32[]{:S(2)}, u32[]{:S(2)}) async-start(bf16[8,32,768]{2,1,0:T(8,128)(2,1)} %bitcast.9), calls=%async_computation.2 | async-start | bytes 786432 | tf_op jit(solution)/shard_map/all_to_all | solution.py:37
  63.8 4.9 %collective-permute-start.4 = (bf16[32,512]{1,0:T(8,128)(2,1)S(1)}, bf16[32,512]{1,0:T(8,128)(2,1)S(1)}, u32[]{:S(2)}, u32[]{:S(2)}) collective-permute-start(bf16[32,512]{1,0:T(8,128)(2,1)S(1)} %get-tuple-element.46), channel_id=1, source_target_pairs={{0,128},{64,192},{128,0},{192,64},{256,384},{320,448},{384,256},{4... | collective-permute-start | bytes 98312 | tf_op jit(solution)/shard_map/ppermute | solution.py:107
  68.7 7.6 %collective-permute-start.5 = (bf16[256,1024]{1,0:T(8,128)(2,1)S(1)}, bf16[256,1024]{1,0:T(8,128)(2,1)S(1)}, u32[]{:S(2)}, u32[]{:S(2)}) collective-permute-start(bf16[256,1024]{1,0:T(8,128)(2,1)S(1)} %bitcast.50), channel_id=1, source_target_pairs={{0,64},{64,0},{128,192},{192,128},{256,320},{320,256},{384,448},{4... | collective-permute-start | bytes 1572872 | tf_op jit(solution)/shard_map/ppermute | solution.py:61
  70.9 5.3 %collective-permute-start.6 = (bf16[64,512]{1,0:T(8,128)(2,1)S(1)}, bf16[64,512]{1,0:T(8,128)(2,1)S(1)}, u32[]{:S(2)}, u32[]{:S(2)}) collective-permute-start(bf16[64,512]{1,0:T(8,128)(2,1)S(1)} %maximum_select_fusion.4), channel_id=1, source_target_pairs={{0,512},{64,576},{128,640},{192,704},{256,768},{320,832},{384,896}... | collective-permute-start | bytes 196616 | tf_op jit(solution)/shard_map/ppermute | solution.py:107
  76.4 34.1 %copy-start.7 = (bf16[256,1024]{1,0:T(8,128)(2,1)}, bf16[256,1024]{1,0:T(8,128)(2,1)S(1)}, u32[]{:S(2)}) copy-start(bf16[256,1024]{1,0:T(8,128)(2,1)S(1)} %collective-permute-done.5) | copy-start | bytes 1572868
  77.1 37.7 %all-to-all-start.3 = ((bf16[4,32,768]{2,1,0:T(8,128)(2,1)}), bf16[4,32,768]{2,1,0:T(8,128)(2,1)S(1)}, u32[]{:S(2)}, u32[]{:S(2)}) async-start(bf16[4,32,768]{2,1,0:T(8,128)(2,1)} %broadcast_in_dim.9), calls=%async_computation.3 | async-start | bytes 393216 | tf_op jit(solution)/shard_map/all_to_all | solution.py:43
  97.0 14.2 %collective-permute-start.8 = (bf16[768,256]{1,0:T(8,128)(2,1)S(1)}, bf16[768,256]{1,0:T(8,128)(2,1)}, u32[]{:S(2)}, u32[]{:S(2)}) collective-permute-start(bf16[768,256]{1,0:T(8,128)(2,1)S(1)} %pad_maximum_fusion.3), channel_id=1, source_target_pairs={{0,1},{1,0},{2,3},{3,2},{4,5},{5,4},{6,7},{7,6},{8,9},{9,8},{10,11... | collective-permute-start | bytes 1179656 | tf_op jit(solution)/shard_map/ppermute | solution.py:131
  101.6 8.9 %collective-permute-start.7 = (bf16[128,512]{1,0:T(8,128)(2,1)S(1)}, bf16[128,512]{1,0:T(8,128)(2,1)S(1)}, u32[]{:S(2)}, u32[]{:S(2)}) collective-permute-start(bf16[128,512]{1,0:T(8,128)(2,1)S(1)} %maximum_select_fusion.3), channel_id=1, source_target_pairs={{0,256},{64,320},{128,384},{192,448},{256,0},{320,64},{384,128},{4... | collective-permute-start | bytes 393224 | tf_op jit(solution)/shard_map/ppermute | solution.py:107
  111.2 3.4 %collective-permute-start.9 = (bf16[256,512]{1,0:T(8,128)(2,1)S(1)}, bf16[256,512]{1,0:T(8,128)(2,1)S(1)}, u32[]{:S(2)}, u32[]{:S(2)}) collective-permute-start(bf16[256,512]{1,0:T(8,128)(2,1)S(1)} %bitcast.60), channel_id=1, source_target_pairs={{0,64},{64,0},{128,192},{192,128},{256,320},{320,256},{384,448},{4... | collective-permute-start | bytes 786440 | tf_op jit(solution)/shard_map/ppermute | solution.py:107
  116.5 27.0 %all-to-all-start.4 = ((bf16[8,32,768]{2,1,0:T(8,128)(2,1)}), bf16[8,32,768]{2,1,0:T(8,128)(2,1)S(1)}, u32[]{:S(2)}, u32[]{:S(2)}) async-start(bf16[8,32,768]{2,1,0:T(8,128)(2,1)} %broadcast_in_dim.10), calls=%async_computation.4 | async-start | bytes 786432 | tf_op jit(solution)/shard_map/all_to_all | solution.py:43
  134.9 8.6 %copy-start.6 = (bf16[768,192]{0,1:T(8,128)(2,1)S(1)}, bf16[768,192]{0,1:T(8,128)(2,1)}, u32[]{:S(2)}) copy-start(bf16[768,192]{0,1:T(8,128)(2,1)} %pad_maximum_fusion.4) | copy-start | bytes 884740
  135.2 8.2 %collective-permute-start.10 = (bf16[384,256]{0,1:T(8,128)(2,1)S(1)}, bf16[384,256]{0,1:T(8,128)(2,1)S(1)}, u32[]{:S(2)}, u32[]{:S(2)}) collective-permute-start(bf16[384,256]{0,1:T(8,128)(2,1)S(1)} %fusion.10), channel_id=1, source_target_pairs={{0,1},{1,0},{2,3},{3,2},{4,5},{5,4},{6,7},{7,6},{8,9},{9,8},{10,11... | collective-permute-start | bytes 589832 | tf_op jit(solution)/shard_map/ppermute | solution.py:142
  144.4 26.5 %copy-start.8 = (bf16[512,192]{0,1:T(8,128)(2,1)S(1)}, bf16[512,192]{0,1:T(8,128)(2,1)}, u32[]{:S(2)}) copy-start(bf16[512,192]{0,1:T(8,128)(2,1)} %param.8) | copy-start | bytes 589828
  144.4 26.4 %collective-permute-start.11 = (bf16[256,384]{1,0:T(8,128)(2,1)S(1)}, bf16[256,384]{1,0:T(8,128)(2,1)S(1)}, u32[]{:S(2)}, u32[]{:S(2)}) collective-permute-start(bf16[256,384]{1,0:T(8,128)(2,1)S(1)} %get-tuple-element.59), channel_id=1, source_target_pairs={{0,64},{64,0},{128,192},{192,128},{256,320},{320,256},{384,448},{4... | collective-permute-start | bytes 589832 | tf_op jit(solution)/shard_map/ppermute | solution.py:61
  157.0 8.6 %all-to-all-start.5 = ((bf16[8,24,256]{2,1,0:T(8,128)(2,1)}), bf16[8,24,256]{2,1,0:T(8,128)(2,1)S(1)}, u32[]{:S(2)}, u32[]{:S(2)}) async-start(bf16[8,24,256]{2,1,0:T(8,128)(2,1)} %bitcast.15), calls=%async_computation.5 | async-start | bytes 196608 | tf_op jit(solution)/shard_map/all_to_all | solution.py:37
  166.3 11.3 %all-to-all-start.6 = ((bf16[16,24,256]{2,1,0:T(8,128)(2,1)}), bf16[16,24,256]{2,1,0:T(8,128)(2,1)S(1)}, u32[]{:S(2)}, u32[]{:S(2)}) async-start(bf16[16,24,256]{2,1,0:T(8,128)(2,1)} %broadcast_in_dim.11), calls=%async_computation.6 | async-start | bytes 393216 | tf_op jit(solution)/shard_map/all_to_all | solution.py:43
  171.0 9.6 %copy-start.3 = (bf16[512,384]{1,0:T(8,128)(2,1)}, bf16[512,384]{1,0:T(8,128)(2,1)S(1)}, u32[]{:S(2)}) copy-start(bf16[512,384]{1,0:T(8,128)(2,1)S(1)} %maximum_select_fusion.1) | copy-start | bytes 1179652
  171.2 8.5 %collective-permute-start.12 = (bf16[384,96]{0,1:T(8,128)(2,1)S(1)}, bf16[384,96]{0,1:T(8,128)(2,1)S(1)}, u32[]{:S(2)}, u32[]{:S(2)}) collective-permute-start(bf16[384,96]{0,1:T(8,128)(2,1)S(1)} %fusion.12), channel_id=1, source_target_pairs={{0,1},{1,0},{2,3},{3,2},{4,5},{5,4},{6,7},{7,6},{8,9},{9,8},{10,11... | collective-permute-start | bytes 221192 | tf_op jit(solution)/shard_map/ppermute | solution.py:172

commit v7 on v6

--- a/solution.py
+++ b/solution.py
@@ -89,8 +89,15 @@
     gate_share, up_share, hid_share = swiglu_grads(
         total[:share], total[share : 2 * share], total[2 * share :]
     )
+    def double(x, bit, runs=1):
+        got = lax.ppermute(x, "row", [(i, i ^ bit) for i in range(rows)])
+        low = (lax.axis_index("row") & bit) == 0
+        x, got = (a.reshape(runs, -1, hidden_width) for a in (x, got))
+        pair = jnp.where(low, jnp.concatenate([x, got], axis=1), jnp.concatenate([got, x], axis=1))
+        return pair.reshape(-1, hidden_width)
+
     mine = gather(jnp.concatenate([gate_share, up_share], axis=1), chips, "row", chip_groups)
-    mine = mine.reshape(half, 2 * hidden_width)
+    mine, hid_pair = tie((mine.reshape(half, 2 * hidden_width), double(hid_share, 2)))
 
     near, far = 8, cols // 8
 
@@ -103,15 +110,7 @@
     spot = (lax.axis_index("col") + cols - 4 * core) % near
 
     back_part = contract_cols(mine, w_pair).astype(BF16).reshape(near, half // near, 2 * width)
-    def double(x, bit, runs=1):
-        got = lax.ppermute(x, "row", [(i, i ^ bit) for i in range(rows)])
-        low = (lax.axis_index("row") & bit) == 0
-        x, got = (a.reshape(runs, -1, hidden_width) for a in (x, got))
-        pair = jnp.where(low, jnp.concatenate([x, got], axis=1), jnp.concatenate([got, x], axis=1))
-        return pair.reshape(-1, hidden_width)
-
-    back_part, sent_mine, hid_share = tie((back_part, mine, hid_share))
-    sent_mine, hid_pair = tie((sent_mine, double(hid_share, 2)))
+    back_part, sent_mine, hid_pair = tie((back_part, mine, hid_pair))
     other = swap(sent_mine)
     hid_row = double(hid_pair, 8)
     near_sum = scatter_sum(back_part, both, near_groups).astype(BF16)
@@ -135,17 +134,17 @@
 
     group_sums = gather(near_sum, far, both, far_groups)
     far_sum = jnp.sum(group_sums.astype(F32), axis=0)
-    far_sum, hid_all = tie((far_sum, hid_all))
+    gate_wgrad = wgrad(both_pairs, seq) + received[:width].astype(F32)
+    up_wgrad = wgrad(both_pairs, seq, hidden_width) + received[width:].astype(F32)
     out_piece = lax.dynamic_index_in_dim(out_pair.reshape(back_part.shape), spot, 0, False)
+    far_sum, hid_all, gate_wgrad, up_wgrad, out_piece = tie(
+        (far_sum, hid_all, gate_wgrad, up_wgrad, out_piece)
+    )
     resid_piece = (out_piece.astype(F32) + far_sum).astype(BF16)
     down_pairs = ((out_grad, hid_all),)
     down_received = lax.ppermute(wgrad(down_pairs, 1 - seq).astype(BF16), "seq", seq_swap)
-    gate_wgrad = wgrad(both_pairs, seq) + received[:width].astype(F32)
-    up_wgrad = wgrad(both_pairs, seq, hidden_width) + received[width:].astype(F32)
     resid_all = gather(resid_piece, near, both, near_groups)
-    resid_all, down_received, gate_wgrad, up_wgrad = tie(
-        (resid_all, down_received, gate_wgrad, up_wgrad)
-    )
+    resid_all, down_received = tie((resid_all, down_received))
     down_wgrad = wgrad(down_pairs, seq) + down_received.astype(F32)
     resid_all = resid_all.reshape(half, 2 * width)
     resid_mine, resid_far = resid_all[:, :width], resid_all[:, width:]

time: 182 us -> 183 us (level)
  blocking collectives: 11.6 us -> 0 us
  waiting for transfers between devices: 28.1 us -> 34.5 us
  starting transfers between devices: 117 us -> 123 us
  matrix products: 13.4 us -> 11.4 us
    all_to_all x1 -> x0, blocking collectives: 11.6 us -> none  [gather(): lax.all_to_all(copies, axis, 0, 0, tiled=True, axis_index_groups=groups)]
    all_to_all x3 -> x4, waiting for transfers between devices: 1.1 us -> 5.43 us  [gather(): lax.all_to_all(copies, axis, 0, 0, tiled=True, axis_index_groups=groups)]
    ppermute x6, starting transfers between devices: 37.1 us -> 40.4 us  [swap(): return lax.ppermute(x, 'row', core_swap)]
    ppermute x1, waiting for transfers between devices: 1.45 us -> 4 us  [per_device(): lax.ppermute(wgrad(down_pairs, 1 - seq).astype(BF16), 'seq', seq_swap)]
    all_to_all x3, starting transfers between devices: 17 us -> 19.4 us  [scatter_sum(): lax.all_to_all(parts, axis, 0, 0, tiled=True, axis_index_groups=groups)]
    ppermute x4, starting transfers between devices: 9.2 us -> 11.5 us  [double(): got = lax.ppermute(x, 'row', [(i, i ^ bit) for i in range(rows)])]
    all_to_all x3, waiting for transfers between devices: 9.32 us -> 11.5 us  [scatter_sum(): lax.all_to_all(parts, axis, 0, 0, tiled=True, axis_index_groups=groups)]
    ppermute x1, starting transfers between devices: 4.32 us -> 2.25 us  [per_device(): lax.ppermute(out_sent, 'seq', seq_swap).astype(F32)]
  transfers between devices with their start and end apart: 19 -> 20, of which waited for: 12 -> 12; matrix products, arithmetic and copies ran while one was open for 7% -> 6% of each run, Pallas kernels for 0% -> 0%
where the time goes in v7:
time: 183 us; the launch traced here: 182 us
  starting transfers between devices  123 us (67%)
  waiting for transfers between devices  34.5 us (19%)
  matrix products  11.4 us (6%)
  local copies, waits for them, and re-layouts  6.76 us (4%)
  other arithmetic  4.73 us (3%)
    all_to_all x4, starting transfers between devices, gather(): lax.all_to_all(copies, axis, 0, 0, tiled=True, axis_index_groups=groups)  41.7 us
    ppermute x6, starting transfers between devices, swap(): return lax.ppermute(x, 'row', core_swap)  40.4 us
    all_to_all x3, starting transfers between devices, scatter_sum(): lax.all_to_all(parts, axis, 0, 0, tiled=True, axis_index_groups=groups)  19.4 us
    all_to_all x3, waiting for transfers between devices, scatter_sum(): lax.all_to_all(parts, axis, 0, 0, tiled=True, axis_index_groups=groups)  11.5 us
    ppermute x4, starting transfers between devices, double(): got = lax.ppermute(x, 'row', [(i, i ^ bit) for i in range(rows)])  11.5 us
    ppermute x4, waiting for transfers between devices, double(): got = lax.ppermute(x, 'row', [(i, i ^ bit) for i in range(rows)])  11.1 us
    all_to_all x4, waiting for transfers between devices, gather(): lax.all_to_all(copies, axis, 0, 0, tiled=True, axis_index_groups=groups)  5.43 us
    dot_general x12, matrix products, contract_rows(): lax.dot_general(first, second, (((0,), (0,)), ((), ())), preferred_elemen...  5.32 us
  transfers between devices with their start and end apart: 20, of which 12 were waited for; matrix products, arithmetic and copies ran while one was open for 6% of the time, Pallas kernels for 0%

profile of v7, /device:TPU:1, one launch (start us, length us, event | category | flops | bytes accessed | tf_op | source)
XLA Modules:
  0.0 182.1 jit_solution(15734146231602353438)
XLA Ops:
  0.7 0.9 copy-done
  1.6 1.3 convolution_convert_fusion.2
  2.9 1.3 convolution_convert_fusion.3
  4.3 0.3 convolution_convert_fusion.1
  4.7 16.1 %collective-permute-start = (bf16[8,96,512]{2,1,0:T(8,128)(2,1)S(1)}, bf16[8,96,512]{2,1,0:T(8,128)(2,1)S(1)}, u32[]{:S(2)}, u32[]{:S(2)}) collective-permute-start(bf16[8,96,512]{2,1,0:T(8,128)(2,1)S(1)} %pad_maximum_fusion.1), channel_id=1, source_target_pairs={{0,64},{64,0},{128,192},{192,128},{256,320},{320,256},{384,448},{4... | collective-permute-start | bytes 2359304 | tf_op jit(solution)/shard_map/ppermute | solution.py:61
  20.8 0.3 convolution_convert_fusion.5
  21.1 0.3 convolution_convert_fusion.6
  21.4 0.3 convolution_convert_fusion.4
  21.7 1.0 collective-permute-done
  22.7 1.1 add_convert_fusion
  23.8 3.5 %all-to-all-start = ((bf16[8,96,512]{2,1,0:T(8,128)(2,1)}), bf16[8,96,512]{2,1,0:T(8,128)(2,1)S(1)}, u32[]{:S(2)}, u32[]{:S(2)}) async-start(bf16[8,96,512]{2,1,0:T(8,128)(2,1)} %add_convert_fusion), calls=%async_computation | async-start | bytes 1572864 | tf_op jit(solution)/shard_map/all_to_all | solution.py:37
  27.5 2.3 %collective-permute-start.1 = (bf16[384,1024]{1,0:T(8,128)(2,1)S(1)}, bf16[384,1024]{1,0:T(8,128)(2,1)S(1)}, u32[]{:S(2)}, u32[]{:S(2)}) collective-permute-start(bf16[384,1024]{1,0:T(8,128)(2,1)S(1)} %constant_dynamic-update-slice_fusion), channel_id=1, source_target_pairs={{0,64},{64,0},{128,192},{192,128},{256,320},{320,256},{384,448},{4... | collective-permute-start | bytes 2359304 | tf_op jit(solution)/shard_map/ppermute | solution.py:61
  29.8 2.0 %collective-permute-start.2 = (bf16[384,192]{0,1:T(8,128)(2,1)S(1)}, bf16[384,192]{0,1:T(8,128)(2,1)S(1)}, u32[]{:S(2)}, u32[]{:S(2)}) collective-permute-start(bf16[384,192]{0,1:T(8,128)(2,1)S(1)} %copy-done.9), channel_id=1, source_target_pairs={{0,64},{64,0},{128,192},{192,128},{256,320},{320,256},{384,448},{4... | collective-permute-start | bytes 442376 | tf_op jit(solution)/shard_map/ppermute | solution.py:61
  31.8 2.3 %collective-permute-start.3 = (bf16[256,384]{1,0:T(8,128)(2,1)S(1)}, bf16[256,384]{1,0:T(8,128)(2,1)S(1)}, u32[]{:S(2)}, u32[]{:S(2)}) collective-permute-start(bf16[256,384]{1,0:T(8,128)(2,1)S(1)} %get-tuple-element.41), channel_id=1, source_target_pairs={{0,64},{64,0},{128,192},{192,128},{256,320},{320,256},{384,448},{4... | collective-permute-start | bytes 589832 | tf_op jit(solution)/shard_map/ppermute | solution.py:61
  34.1 0.7 pad_maximum_fusion.4
  34.9 0.3 collective-permute-done.3
  35.2 0.8 pad_maximum_fusion.2
  35.9 4.4 %all-to-all-done = bf16[8,96,512]{2,1,0:T(8,128)(2,1)S(1)} async-done(((bf16[8,96,512]{2,1,0:T(8,128)(2,1)}), bf16[8,96,512]{2,1,0:T(8,128)(2,1)S(1)}, u32[]{:S(2)}, u32[]{:S(2)}) %all-to-all-start) | async-done | bytes 786464 | tf_op jit(solution)/shard_map/all_to_all | solution.py:37
  40.5 1.3 pad_maximum_fusion
  41.9 0.8 broadcast_in_dim.8
  42.7 3.5 %all-to-all-start.1 = ((bf16[8,32,1024]{2,1,0:T(8,128)(2,1)}), bf16[8,32,1024]{2,1,0:T(8,128)(2,1)S(1)}, u32[]{:S(2)}, u32[]{:S(2)}) async-start(bf16[8,32,1024]{2,1,0:T(8,128)(2,1)} %broadcast_in_dim.8), calls=%async_computation.1 | async-start | bytes 1048576 | tf_op jit(solution)/shard_map/all_to_all | solution.py:43
  46.2 3.3 %collective-permute-start.4 = (bf16[32,512]{1,0:T(8,128)(2,1)S(1)}, bf16[32,512]{1,0:T(8,128)(2,1)S(1)}, u32[]{:S(2)}, u32[]{:S(2)}) collective-permute-start(bf16[32,512]{1,0:T(8,128)(2,1)S(1)} %get-tuple-element.96), channel_id=1, source_target_pairs={{0,128},{64,192},{128,0},{192,64},{256,384},{320,448},{384,256},{4... | collective-permute-start | bytes 98312 | tf_op jit(solution)/shard_map/ppermute | solution.py:93
  49.5 4.6 %collective-permute-done.4 = bf16[32,512]{1,0:T(8,128)(2,1)S(1)} collective-permute-done((bf16[32,512]{1,0:T(8,128)(2,1)S(1)}, bf16[32,512]{1,0:T(8,128)(2,1)S(1)}, u32[]{:S(2)}, u32[]{:S(2)}) %collective-permute-start.4) | collective-permute-done | bytes 32800 | tf_op jit(solution)/shard_map/ppermute | solution.py:93
  54.1 2.3 %all-to-all-done.1 = bf16[8,32,1024]{2,1,0:T(8,128)(2,1)S(1)} async-done(((bf16[8,32,1024]{2,1,0:T(8,128)(2,1)}), bf16[8,32,1024]{2,1,0:T(8,128)(2,1)S(1)}, u32[]{:S(2)}, u32[]{:S(2)}) %all-to-all-start.1) | async-done | bytes 524320 | tf_op jit(solution)/shard_map/all_to_all | solution.py:43
  56.4 1.4 convolution_convert_fusion
  57.7 10.0 %all-to-all-start.2 = ((bf16[8,32,768]{2,1,0:T(8,128)(2,1)}), bf16[8,32,768]{2,1,0:T(8,128)(2,1)S(1)}, u32[]{:S(2)}, u32[]{:S(2)}) async-start(bf16[8,32,768]{2,1,0:T(8,128)(2,1)} %bitcast.7), calls=%async_computation.2 | async-start | bytes 786432 | tf_op jit(solution)/shard_map/all_to_all | solution.py:37
  67.8 1.9 %collective-permute-start.5 = (bf16[256,1024]{1,0:T(8,128)(2,1)S(1)}, bf16[256,1024]{1,0:T(8,128)(2,1)S(1)}, u32[]{:S(2)}, u32[]{:S(2)}) collective-permute-start(bf16[256,1024]{1,0:T(8,128)(2,1)S(1)} %bitcast.49), channel_id=1, source_target_pairs={{0,64},{64,0},{128,192},{192,128},{256,320},{320,256},{384,448},{4... | collective-permute-start | bytes 1572872 | tf_op jit(solution)/shard_map/ppermute | solution.py:61
  69.7 2.2 %collective-permute-start.6 = (bf16[64,512]{1,0:T(8,128)(2,1)S(1)}, bf16[64,512]{1,0:T(8,128)(2,1)S(1)}, u32[]{:S(2)}, u32[]{:S(2)}) collective-permute-start(bf16[64,512]{1,0:T(8,128)(2,1)S(1)} %maximum_select_fusion.4), channel_id=1, source_target_pairs={{0,512},{64,576},{128,640},{192,704},{256,768},{320,832},{384,896}... | collective-permute-start | bytes 196616 | tf_op jit(solution)/shard_map/ppermute | solution.py:93
  71.9 0.3 fusion.24
  72.2 0.3 fusion.27
  72.4 2.6 %collective-permute-done.6 = bf16[64,512]{1,0:T(8,128)(2,1)S(1)} collective-permute-done((bf16[64,512]{1,0:T(8,128)(2,1)S(1)}, bf16[64,512]{1,0:T(8,128)(2,1)S(1)}, u32[]{:S(2)}, u32[]{:S(2)}) %collective-permute-start.6) | collective-permute-done | bytes 65568 | tf_op jit(solution)/shard_map/ppermute | solution.py:93
  75.1 2.1 %all-to-all-done.2 = bf16[8,32,768]{2,1,0:T(8,128)(2,1)S(1)} async-done(((bf16[8,32,768]{2,1,0:T(8,128)(2,1)}), bf16[8,32,768]{2,1,0:T(8,128)(2,1)S(1)}, u32[]{:S(2)}, u32[]{:S(2)}) %all-to-all-start.2) | async-done | bytes 393248 | tf_op jit(solution)/shard_map/all_to_all | solution.py:37
  77.3 0.7 broadcast_in_dim.9
  78.0 21.2 %all-to-all-start.3 = ((bf16[4,32,768]{2,1,0:T(8,128)(2,1)}), bf16[4,32,768]{2,1,0:T(8,128)(2,1)S(1)}, u32[]{:S(2)}, u32[]{:S(2)}) async-start(bf16[4,32,768]{2,1,0:T(8,128)(2,1)} %broadcast_in_dim.9), calls=%async_computation.3 | async-start | bytes 393216 | tf_op jit(solution)/shard_map/all_to_all | solution.py:43
  99.2 0.3 fusion.8
  99.4 0.3 fusion.9
  99.7 4.3 %collective-permute-start.8 = (bf16[768,256]{1,0:T(8,128)(2,1)S(1)}, bf16[768,256]{1,0:T(8,128)(2,1)S(1)}, u32[]{:S(2)}, u32[]{:S(2)}) collective-permute-start(bf16[768,256]{1,0:T(8,128)(2,1)S(1)} %pad_maximum_fusion.3), channel_id=1, source_target_pairs={{0,1},{1,0},{2,3},{3,2},{4,5},{5,4},{6,7},{7,6},{8,9},{9,8},{10,11... | collective-permute-start | bytes 1179656 | tf_op jit(solution)/shard_map/ppermute | solution.py:130
  104.0 0.8 dynamic-slice_bitcast_fusion
  104.8 3.1 %collective-permute-start.7 = (bf16[128,512]{1,0:T(8,128)(2,1)S(1)}, bf16[128,512]{1,0:T(8,128)(2,1)S(1)}, u32[]{:S(2)}, u32[]{:S(2)}) collective-permute-start(bf16[128,512]{1,0:T(8,128)(2,1)S(1)} %maximum_select_fusion.3), channel_id=1, source_target_pairs={{0,256},{64,320},{128,384},{192,448},{256,0},{320,64},{384,128},{4... | collective-permute-start | bytes 393224 | tf_op jit(solution)/shard_map/ppermute | solution.py:93
  107.9 0.3 fusion.21
  108.2 0.3 fusion.18
  108.5 3.9 %collective-permute-done.7 = bf16[128,512]{1,0:T(8,128)(2,1)S(1)} collective-permute-done((bf16[128,512]{1,0:T(8,128)(2,1)S(1)}, bf16[128,512]{1,0:T(8,128)(2,1)S(1)}, u32[]{:S(2)}, u32[]{:S(2)}) %collective-permute-start.7) | collective-permute-done | bytes 131104 | tf_op jit(solution)/shard_map/ppermute | solution.py:93
  112.4 1.2 collective-permute-done.8
  113.6 3.0 %collective-permute-start.9 = (bf16[256,512]{1,0:T(8,128)(2,1)S(1)}, bf16[256,512]{1,0:T(8,128)(2,1)S(1)}, u32[]{:S(2)}, u32[]{:S(2)}) collective-permute-start(bf16[256,512]{1,0:T(8,128)(2,1)S(1)} %bitcast.59), channel_id=1, source_target_pairs={{0,64},{64,0},{128,192},{192,128},{256,320},{320,256},{384,448},{4... | collective-permute-start | bytes 786440 | tf_op jit(solution)/shard_map/ppermute | solution.py:93
  116.6 1.0 fusion.6
  117.6 1.0 fusion.5
  118.9 0.8 broadcast_in_dim.10
  119.7 12.2 %all-to-all-start.4 = ((bf16[8,32,768]{2,1,0:T(8,128)(2,1)}), bf16[8,32,768]{2,1,0:T(8,128)(2,1)S(1)}, u32[]{:S(2)}, u32[]{:S(2)}) async-start(bf16[8,32,768]{2,1,0:T(8,128)(2,1)} %broadcast_in_dim.10), calls=%async_computation.4 | async-start | bytes 786432 | tf_op jit(solution)/shard_map/all_to_all | solution.py:43
  131.9 0.3 fusion.10
  132.2 3.9 %collective-permute-start.10 = (bf16[384,256]{0,1:T(8,128)(2,1)S(1)}, bf16[384,256]{0,1:T(8,128)(2,1)S(1)}, u32[]{:S(2)}, u32[]{:S(2)}) collective-permute-start(bf16[384,256]{0,1:T(8,128)(2,1)S(1)} %fusion.10), channel_id=1, source_target_pairs={{0,1},{1,0},{2,3},{3,2},{4,5},{5,4},{6,7},{7,6},{8,9},{9,8},{10,11... | collective-permute-start | bytes 589832 | tf_op jit(solution)/shard_map/ppermute | solution.py:145
  136.2 4.0 %collective-permute-done.10 = bf16[384,256]{0,1:T(8,128)(2,1)S(1)} collective-permute-done((bf16[384,256]{0,1:T(8,128)(2,1)S(1)}, bf16[384,256]{0,1:T(8,128)(2,1)S(1)}, u32[]{:S(2)}, u32[]{:S(2)}) %collective-permute-start.10) | collective-permute-done | bytes 196640 | tf_op jit(solution)/shard_map/ppermute | solution.py:145
  140.2 0.9 convolution_convert_fusion.7
  141.2 15.9 %collective-permute-start.11 = (bf16[256,384]{1,0:T(8,128)(2,1)S(1)}, bf16[256,384]{1,0:T(8,128)(2,1)S(1)}, u32[]{:S(2)}, u32[]{:S(2)}) collective-permute-start(bf16[256,384]{1,0:T(8,128)(2,1)S(1)} %get-tuple-element.61), channel_id=1, source_target_pairs={{0,64},{64,0},{128,192},{192,128},{256,320},{320,256},{384,448},{4... | collective-permute-start | bytes 589832 | tf_op jit(solution)/shard_map/ppermute | solution.py:61
  157.0 5.8 %all-to-all-start.5 = ((bf16[8,24,256]{2,1,0:T(8,128)(2,1)}), bf16[8,24,256]{2,1,0:T(8,128)(2,1)S(1)}, u32[]{:S(2)}, u32[]{:S(2)}) async-start(bf16[8,24,256]{2,1,0:T(8,128)(2,1)} %bitcast.15), calls=%async_computation.5 | async-start | bytes 196608 | tf_op jit(solution)/shard_map/all_to_all | solution.py:37
  162.8 0.3 convert_add_fusion
  163.2 5.0 %all-to-all-done.5 = bf16[8,24,256]{2,1,0:T(8,128)(2,1)S(1)} async-done(((bf16[8,24,256]{2,1,0:T(8,128)(2,1)}), bf16[8,24,256]{2,1,0:T(8,128)(2,1)S(1)}, u32[]{:S(2)}, u32[]{:S(2)}) %all-to-all-start.5) | async-done | bytes 98336 | tf_op jit(solution)/shard_map/all_to_all | solution.py:37
  168.2 0.7 broadcast_in_dim.11
  168.8 4.7 %all-to-all-start.6 = ((bf16[16,24,256]{2,1,0:T(8,128)(2,1)}), bf16[16,24,256]{2,1,0:T(8,128)(2,1)S(1)}, u32[]{:S(2)}, u32[]{:S(2)}) async-start(bf16[16,24,256]{2,1,0:T(8,128)(2,1)} %broadcast_in_dim.11), calls=%async_computation.6 | async-start | bytes 393216 | tf_op jit(solution)/shard_map/all_to_all | solution.py:43
  173.8 0.2 fusion.12
  174.0 2.3 %collective-permute-start.12 = (bf16[384,96]{0,1:T(8,128)(2,1)S(1)}, bf16[384,96]{0,1:T(8,128)(2,1)S(1)}, u32[]{:S(2)}, u32[]{:S(2)}) collective-permute-start(bf16[384,96]{0,1:T(8,128)(2,1)S(1)} %fusion.12), channel_id=1, source_target_pairs={{0,1},{1,0},{2,3},{3,2},{4,5},{5,4},{6,7},{7,6},{8,9},{9,8},{10,11... | collective-permute-start | bytes 221192 | tf_op jit(solution)/shard_map/ppermute | solution.py:171
  176.2 0.9 copy.18
  177.2 3.2 %all-to-all-done.6 = bf16[16,24,256]{2,1,0:T(8,128)(2,1)S(1)} async-done(((bf16[16,24,256]{2,1,0:T(8,128)(2,1)}), bf16[16,24,256]{2,1,0:T(8,128)(2,1)S(1)}, u32[]{:S(2)}, u32[]{:S(2)}) %all-to-all-start.6) | async-done | bytes 196640 | tf_op jit(solution)/shard_map/all_to_all | solution.py:43
  180.5 0.7 copy.19
  181.2 0.9 fusion.11
  (46 shorter events, 1.2 us)
Async XLA Ops:
  0.6 1.0 copy-start
  0.6 3.6 %copy-start.5 = (bf16[512,384]{1,0:T(8,128)(2,1)S(1)}, bf16[512,384]{1,0:T(8,128)(2,1)}, u32[]{:S(2)}) copy-start(bf16[512,384]{1,0:T(8,128)(2,1)} %param.9) | copy-start | bytes 1179652
  0.7 3.7 %copy-start.6 = (bf16[384,512]{1,0:T(8,128)(2,1)S(1)}, bf16[384,512]{1,0:T(8,128)(2,1)}, u32[]{:S(2)}) copy-start(bf16[384,512]{1,0:T(8,128)(2,1)} %param.12) | copy-start | bytes 1179652
  4.3 16.5 %copy-start.2 = (bf16[384,512]{1,0:T(8,128)(2,1)S(1)}, bf16[384,512]{1,0:T(8,128)(2,1)}, u32[]{:S(2)}) copy-start(bf16[384,512]{1,0:T(8,128)(2,1)} %param.11) | copy-start | bytes 1179652
  4.3 16.8 %copy-start.1 = (bf16[384,512]{1,0:T(8,128)(2,1)S(1)}, bf16[384,512]{1,0:T(8,128)(2,1)}, u32[]{:S(2)}) copy-start(bf16[384,512]{1,0:T(8,128)(2,1)} %param.10) | copy-start | bytes 1179652
  4.7 18.0 %collective-permute-start = (bf16[8,96,512]{2,1,0:T(8,128)(2,1)S(1)}, bf16[8,96,512]{2,1,0:T(8,128)(2,1)S(1)}, u32[]{:S(2)}, u32[]{:S(2)}) collective-permute-start(bf16[8,96,512]{2,1,0:T(8,128)(2,1)S(1)} %pad_maximum_fusion.1), channel_id=1, source_target_pairs={{0,64},{64,0},{128,192},{192,128},{256,320},{320,256},{384,448},{4... | collective-permute-start | bytes 2359304 | tf_op jit(solution)/shard_map/ppermute | solution.py:61
  23.8 16.6 %all-to-all-start = ((bf16[8,96,512]{2,1,0:T(8,128)(2,1)}), bf16[8,96,512]{2,1,0:T(8,128)(2,1)S(1)}, u32[]{:S(2)}, u32[]{:S(2)}) async-start(bf16[8,96,512]{2,1,0:T(8,128)(2,1)} %add_convert_fusion), calls=%async_computation | async-start | bytes 1572864 | tf_op jit(solution)/shard_map/all_to_all | solution.py:37
  27.3 2.4 %copy-start.9 = (bf16[384,192]{0,1:T(8,128)(2,1)S(1)}, bf16[384,192]{0,1:T(8,128)(2,1)}, u32[]{:S(2)}) copy-start(bf16[384,192]{0,1:T(8,128)(2,1)} %param.13) | copy-start | bytes 442372
  27.5 13.0 %collective-permute-start.1 = (bf16[384,1024]{1,0:T(8,128)(2,1)S(1)}, bf16[384,1024]{1,0:T(8,128)(2,1)S(1)}, u32[]{:S(2)}, u32[]{:S(2)}) collective-permute-start(bf16[384,1024]{1,0:T(8,128)(2,1)S(1)} %constant_dynamic-update-slice_fusion), channel_id=1, source_target_pairs={{0,64},{64,0},{128,192},{192,128},{256,320},{320,256},{384,448},{4... | collective-permute-start | bytes 2359304 | tf_op jit(solution)/shard_map/ppermute | solution.py:61
  29.8 4.3 %collective-permute-start.2 = (bf16[384,192]{0,1:T(8,128)(2,1)S(1)}, bf16[384,192]{0,1:T(8,128)(2,1)S(1)}, u32[]{:S(2)}, u32[]{:S(2)}) collective-permute-start(bf16[384,192]{0,1:T(8,128)(2,1)S(1)} %copy-done.9), channel_id=1, source_target_pairs={{0,64},{64,0},{128,192},{192,128},{256,320},{320,256},{384,448},{4... | collective-permute-start | bytes 442376 | tf_op jit(solution)/shard_map/ppermute | solution.py:61
  31.8 3.3 %collective-permute-start.3 = (bf16[256,384]{1,0:T(8,128)(2,1)S(1)}, bf16[256,384]{1,0:T(8,128)(2,1)S(1)}, u32[]{:S(2)}, u32[]{:S(2)}) collective-permute-start(bf16[256,384]{1,0:T(8,128)(2,1)S(1)} %get-tuple-element.41), channel_id=1, source_target_pairs={{0,64},{64,0},{128,192},{192,128},{256,320},{320,256},{384,448},{4... | collective-permute-start | bytes 589832 | tf_op jit(solution)/shard_map/ppermute | solution.py:61
  41.8 14.6 %copy-start.4 = (bf16[768,1024]{1,0:T(8,128)(2,1)S(1)}, bf16[768,1024]{1,0:T(8,128)(2,1)}, u32[]{:S(2)}) copy-start(bf16[768,1024]{1,0:T(8,128)(2,1)} %pad_maximum_fusion) | copy-start | bytes 4718596
  42.7 13.7 %all-to-all-start.1 = ((bf16[8,32,1024]{2,1,0:T(8,128)(2,1)}), bf16[8,32,1024]{2,1,0:T(8,128)(2,1)S(1)}, u32[]{:S(2)}, u32[]{:S(2)}) async-start(bf16[8,32,1024]{2,1,0:T(8,128)(2,1)} %broadcast_in_dim.8), calls=%async_computation.1 | async-start | bytes 1048576 | tf_op jit(solution)/shard_map/all_to_all | solution.py:43
  46.2 7.9 %collective-permute-start.4 = (bf16[32,512]{1,0:T(8,128)(2,1)S(1)}, bf16[32,512]{1,0:T(8,128)(2,1)S(1)}, u32[]{:S(2)}, u32[]{:S(2)}) collective-permute-start(bf16[32,512]{1,0:T(8,128)(2,1)S(1)} %get-tuple-element.96), channel_id=1, source_target_pairs={{0,128},{64,192},{128,0},{192,64},{256,384},{320,448},{384,256},{4... | collective-permute-start | bytes 98312 | tf_op jit(solution)/shard_map/ppermute | solution.py:93
  57.7 19.5 %all-to-all-start.2 = ((bf16[8,32,768]{2,1,0:T(8,128)(2,1)}), bf16[8,32,768]{2,1,0:T(8,128)(2,1)S(1)}, u32[]{:S(2)}, u32[]{:S(2)}) async-start(bf16[8,32,768]{2,1,0:T(8,128)(2,1)} %bitcast.7), calls=%async_computation.2 | async-start | bytes 786432 | tf_op jit(solution)/shard_map/all_to_all | solution.py:37
  67.8 9.5 %collective-permute-start.5 = (bf16[256,1024]{1,0:T(8,128)(2,1)S(1)}, bf16[256,1024]{1,0:T(8,128)(2,1)S(1)}, u32[]{:S(2)}, u32[]{:S(2)}) collective-permute-start(bf16[256,1024]{1,0:T(8,128)(2,1)S(1)} %bitcast.49), channel_id=1, source_target_pairs={{0,64},{64,0},{128,192},{192,128},{256,320},{320,256},{384,448},{4... | collective-permute-start | bytes 1572872 | tf_op jit(solution)/shard_map/ppermute | solution.py:61
  69.7 5.3 %collective-permute-start.6 = (bf16[64,512]{1,0:T(8,128)(2,1)S(1)}, bf16[64,512]{1,0:T(8,128)(2,1)S(1)}, u32[]{:S(2)}, u32[]{:S(2)}) collective-permute-start(bf16[64,512]{1,0:T(8,128)(2,1)S(1)} %maximum_select_fusion.4), channel_id=1, source_target_pairs={{0,512},{64,576},{128,640},{192,704},{256,768},{320,832},{384,896}... | collective-permute-start | bytes 196616 | tf_op jit(solution)/shard_map/ppermute | solution.py:93
  78.0 40.9 %all-to-all-start.3 = ((bf16[4,32,768]{2,1,0:T(8,128)(2,1)}), bf16[4,32,768]{2,1,0:T(8,128)(2,1)S(1)}, u32[]{:S(2)}, u32[]{:S(2)}) async-start(bf16[4,32,768]{2,1,0:T(8,128)(2,1)} %broadcast_in_dim.9), calls=%async_computation.3 | async-start | bytes 393216 | tf_op jit(solution)/shard_map/all_to_all | solution.py:43
  99.7 13.8 %collective-permute-start.8 = (bf16[768,256]{1,0:T(8,128)(2,1)S(1)}, bf16[768,256]{1,0:T(8,128)(2,1)S(1)}, u32[]{:S(2)}, u32[]{:S(2)}) collective-permute-start(bf16[768,256]{1,0:T(8,128)(2,1)S(1)} %pad_maximum_fusion.3), channel_id=1, source_target_pairs={{0,1},{1,0},{2,3},{3,2},{4,5},{5,4},{6,7},{7,6},{8,9},{9,8},{10,11... | collective-permute-start | bytes 1179656 | tf_op jit(solution)/shard_map/ppermute | solution.py:130
  104.8 7.5 %collective-permute-start.7 = (bf16[128,512]{1,0:T(8,128)(2,1)S(1)}, bf16[128,512]{1,0:T(8,128)(2,1)S(1)}, u32[]{:S(2)}, u32[]{:S(2)}) collective-permute-start(bf16[128,512]{1,0:T(8,128)(2,1)S(1)} %maximum_select_fusion.3), channel_id=1, source_target_pairs={{0,256},{64,320},{128,384},{192,448},{256,0},{320,64},{384,128},{4... | collective-permute-start | bytes 393224 | tf_op jit(solution)/shard_map/ppermute | solution.py:93
  113.6 5.0 %collective-permute-start.9 = (bf16[256,512]{1,0:T(8,128)(2,1)S(1)}, bf16[256,512]{1,0:T(8,128)(2,1)S(1)}, u32[]{:S(2)}, u32[]{:S(2)}) collective-permute-start(bf16[256,512]{1,0:T(8,128)(2,1)S(1)} %bitcast.59), channel_id=1, source_target_pairs={{0,64},{64,0},{128,192},{192,128},{256,320},{320,256},{384,448},{4... | collective-permute-start | bytes 786440 | tf_op jit(solution)/shard_map/ppermute | solution.py:93
  118.9 21.3 %copy-start.7 = (bf16[768,192]{0,1:T(8,128)(2,1)S(1)}, bf16[768,192]{0,1:T(8,128)(2,1)}, u32[]{:S(2)}) copy-start(bf16[768,192]{0,1:T(8,128)(2,1)} %pad_maximum_fusion.4) | copy-start | bytes 884740
  119.7 20.5 %all-to-all-start.4 = ((bf16[8,32,768]{2,1,0:T(8,128)(2,1)}), bf16[8,32,768]{2,1,0:T(8,128)(2,1)S(1)}, u32[]{:S(2)}, u32[]{:S(2)}) async-start(bf16[8,32,768]{2,1,0:T(8,128)(2,1)} %broadcast_in_dim.10), calls=%async_computation.4 | async-start | bytes 786432 | tf_op jit(solution)/shard_map/all_to_all | solution.py:43
  132.2 7.9 %collective-permute-start.10 = (bf16[384,256]{0,1:T(8,128)(2,1)S(1)}, bf16[384,256]{0,1:T(8,128)(2,1)S(1)}, u32[]{:S(2)}, u32[]{:S(2)}) collective-permute-start(bf16[384,256]{0,1:T(8,128)(2,1)S(1)} %fusion.10), channel_id=1, source_target_pairs={{0,1},{1,0},{2,3},{3,2},{4,5},{5,4},{6,7},{7,6},{8,9},{9,8},{10,11... | collective-permute-start | bytes 589832 | tf_op jit(solution)/shard_map/ppermute | solution.py:145
  141.2 32.6 %copy-start.8 = (bf16[512,192]{0,1:T(8,128)(2,1)S(1)}, bf16[512,192]{0,1:T(8,128)(2,1)}, u32[]{:S(2)}) copy-start(bf16[512,192]{0,1:T(8,128)(2,1)} %param.8) | copy-start | bytes 589828
  141.2 32.4 %collective-permute-start.11 = (bf16[256,384]{1,0:T(8,128)(2,1)S(1)}, bf16[256,384]{1,0:T(8,128)(2,1)S(1)}, u32[]{:S(2)}, u32[]{:S(2)}) collective-permute-start(bf16[256,384]{1,0:T(8,128)(2,1)S(1)} %get-tuple-element.61), channel_id=1, source_target_pairs={{0,64},{64,0},{128,192},{192,128},{256,320},{320,256},{384,448},{4... | collective-permute-start | bytes 589832 | tf_op jit(solution)/shard_map/ppermute | solution.py:61
  157.0 11.1 %all-to-all-start.5 = ((bf16[8,24,256]{2,1,0:T(8,128)(2,1)}), bf16[8,24,256]{2,1,0:T(8,128)(2,1)S(1)}, u32[]{:S(2)}, u32[]{:S(2)}) async-start(bf16[8,24,256]{2,1,0:T(8,128)(2,1)} %bitcast.15), calls=%async_computation.5 | async-start | bytes 196608 | tf_op jit(solution)/shard_map/all_to_all | solution.py:37
  168.8 11.5 %all-to-all-start.6 = ((bf16[16,24,256]{2,1,0:T(8,128)(2,1)}), bf16[16,24,256]{2,1,0:T(8,128)(2,1)S(1)}, u32[]{:S(2)}, u32[]{:S(2)}) async-start(bf16[16,24,256]{2,1,0:T(8,128)(2,1)} %broadcast_in_dim.11), calls=%async_computation.6 | async-start | bytes 393216 | tf_op jit(solution)/shard_map/all_to_all | solution.py:43
  173.7 8.3 %copy-start.3 = (bf16[512,384]{1,0:T(8,128)(2,1)}, bf16[512,384]{1,0:T(8,128)(2,1)S(1)}, u32[]{:S(2)}) copy-start(bf16[512,384]{1,0:T(8,128)(2,1)S(1)} %maximum_select_fusion.1) | copy-start | bytes 1179652
  174.0 7.2 %collective-permute-start.12 = (bf16[384,96]{0,1:T(8,128)(2,1)S(1)}, bf16[384,96]{0,1:T(8,128)(2,1)S(1)}, u32[]{:S(2)}, u32[]{:S(2)}) collective-permute-start(bf16[384,96]{0,1:T(8,128)(2,1)S(1)} %fusion.12), channel_id=1, source_target_pairs={{0,1},{1,0},{2,3},{3,2},{4,5},{5,4},{6,7},{7,6},{8,9},{9,8},{10,11... | collective-permute-start | bytes 221192 | tf_op jit(solution)/shard_map/ppermute | solution.py:171

commit v8 on v7

--- a/solution.py
+++ b/solution.py
@@ -56,6 +56,7 @@
     seq_swap = [(0, 1), (1, 0)]
     chip_groups = [list(range(c, rows, 2)) for c in range(2)]
     tie = lax.optimization_barrier
+    near, far = 8, cols // 8
 
     def swap(x):
         return lax.ppermute(x, "row", core_swap)
@@ -85,7 +86,9 @@
     w_pair = jnp.concatenate([w_both, w_both_far])
     w_out_pair = jnp.concatenate([w_out, w_out_far])
     out_pair = jnp.concatenate([out_mine, out_far], axis=1)
-    total, w_pair, w_out_pair, out_pair = tie((total, w_pair, w_out_pair, out_pair))
+    spot = (lax.axis_index("col") + cols - 4 * core) % near
+    out_piece = lax.dynamic_index_in_dim(out_pair.reshape(near, half // near, 2 * width), spot, 0, False)
+    total, w_out_pair, out_piece = tie((total, w_out_pair, out_piece))
     gate_share, up_share, hid_share = swiglu_grads(
         total[:share], total[share : 2 * share], total[2 * share :]
     )
@@ -97,9 +100,9 @@
         return pair.reshape(-1, hidden_width)
 
     mine = gather(jnp.concatenate([gate_share, up_share], axis=1), chips, "row", chip_groups)
-    mine, hid_pair = tie((mine.reshape(half, 2 * hidden_width), double(hid_share, 2)))
-
-    near, far = 8, cols // 8
+    mine, hid_pair, w_pair = tie(
+        (mine.reshape(half, 2 * hidden_width), double(hid_share, 2), w_pair)
+    )
 
     def place(r, k, j):
         return r * cols + (k * near + j + 4 * (r % 2)) % cols
@@ -107,7 +110,6 @@
     near_groups = [[place(r, k, j) for j in range(near)] for r in range(rows) for k in range(far)]
     far_groups = [[place(r, k, j) for k in range(far)] for r in range(rows) for j in range(near)]
     both = ("row", "col")
-    spot = (lax.axis_index("col") + cols - 4 * core) % near
 
     back_part = contract_cols(mine, w_pair).astype(BF16).reshape(near, half // near, 2 * width)
     back_part, sent_mine, hid_pair = tie((back_part, mine, hid_pair))
@@ -136,15 +138,12 @@
     far_sum = jnp.sum(group_sums.astype(F32), axis=0)
     gate_wgrad = wgrad(both_pairs, seq) + received[:width].astype(F32)
     up_wgrad = wgrad(both_pairs, seq, hidden_width) + received[width:].astype(F32)
-    out_piece = lax.dynamic_index_in_dim(out_pair.reshape(back_part.shape), spot, 0, False)
-    far_sum, hid_all, gate_wgrad, up_wgrad, out_piece = tie(
-        (far_sum, hid_all, gate_wgrad, up_wgrad, out_piece)
-    )
+    far_sum, hid_all, gate_wgrad = tie((far_sum, hid_all, gate_wgrad))
     resid_piece = (out_piece.astype(F32) + far_sum).astype(BF16)
     down_pairs = ((out_grad, hid_all),)
     down_received = lax.ppermute(wgrad(down_pairs, 1 - seq).astype(BF16), "seq", seq_swap)
     resid_all = gather(resid_piece, near, both, near_groups)
-    resid_all, down_received = tie((resid_all, down_received))
+    resid_all, down_received, up_wgrad = tie((resid_all, down_received, up_wgrad))
     down_wgrad = wgrad(down_pairs, seq) + down_received.astype(F32)
     resid_all = resid_all.reshape(half, 2 * width)
     resid_mine, resid_far = resid_all[:, :width], resid_all[:, width:]

time: 183 us -> 185 us (1.011)
  waiting for transfers between devices: 34.5 us -> 28.8 us
  starting transfers between devices: 123 us -> 128 us
    all_to_all x4, waiting for transfers between devices: 5.43 us -> 1 us  [gather(): lax.all_to_all(copies, axis, 0, 0, tiled=True, axis_index_groups=groups)]
    ppermute x1, starting transfers between devices: 2.25 us -> 4.43 us  [per_device(): lax.ppermute(out_sent, 'seq', seq_swap).astype(F32)]
    ppermute x1, waiting for transfers between devices: 4 us -> 2.02 us  [per_device(): lax.ppermute(wgrad(down_pairs, 1 - seq).astype(BF16), 'seq', seq_swap)]
  transfers between devices with their start and end apart: 20 -> 20, of which waited for: 12 -> 11; matrix products, arithmetic and copies ran while one was open for 6% -> 8% of each run, Pallas kernels for 0% -> 0%
where the time goes in v8:
time: 185 us; the launch traced here: 183 us
  starting transfers between devices  128 us (69%)
  waiting for transfers between devices  28.8 us (16%)
  matrix products  12.8 us (7%)
  local copies, waits for them, and re-layouts  6.59 us (4%)
  other arithmetic  6.04 us (3%)
    all_to_all x4, starting transfers between devices, gather(): lax.all_to_all(copies, axis, 0, 0, tiled=True, axis_index_groups=groups)  42.2 us
    ppermute x6, starting transfers between devices, swap(): return lax.ppermute(x, 'row', core_swap)  40.6 us
    all_to_all x3, starting transfers between devices, scatter_sum(): lax.all_to_all(parts, axis, 0, 0, tiled=True, axis_index_groups=groups)  18.2 us
    ppermute x4, starting transfers between devices, double(): got = lax.ppermute(x, 'row', [(i, i ^ bit) for i in range(rows)])  13 us
    all_to_all x3, waiting for transfers between devices, scatter_sum(): lax.all_to_all(parts, axis, 0, 0, tiled=True, axis_index_groups=groups)  11.6 us
    ppermute x4, waiting for transfers between devices, double(): got = lax.ppermute(x, 'row', [(i, i ^ bit) for i in range(rows)])  10.7 us
    dot_general x12, matrix products, contract_rows(): lax.dot_general(first, second, (((0,), (0,)), ((), ())), preferred_elemen...  5.32 us
    ppermute x1, starting transfers between devices, per_device(): lax.ppermute(wgrad(down_pairs, 1 - seq).astype(BF16), 'seq', seq_swap)  4.88 us
  transfers between devices with their start and end apart: 20, of which 11 were waited for; matrix products, arithmetic and copies ran while one was open for 8% of the time, Pallas kernels for 0%

profile of v8, /device:TPU:1, one launch (start us, length us, event | category | flops | bytes accessed | tf_op | source)
XLA Modules:
  0.0 183.3 jit_solution(13370859958025140439)
XLA Ops:
  0.7 0.9 copy-done
  1.6 1.3 convolution_convert_fusion.2
  2.9 1.3 convolution_convert_fusion.3
  4.3 0.3 convolution_convert_fusion.1
  4.7 16.1 %collective-permute-start = (bf16[8,96,512]{2,1,0:T(8,128)(2,1)S(1)}, bf16[8,96,512]{2,1,0:T(8,128)(2,1)S(1)}, u32[]{:S(2)}, u32[]{:S(2)}) collective-permute-start(bf16[8,96,512]{2,1,0:T(8,128)(2,1)S(1)} %pad_maximum_fusion.1), channel_id=1, source_target_pairs={{0,64},{64,0},{128,192},{192,128},{256,320},{320,256},{384,448},{4... | collective-permute-start | bytes 2359304 | tf_op jit(solution)/shard_map/ppermute | solution.py:62
  20.8 0.3 convolution_convert_fusion.5
  21.1 0.3 convolution_convert_fusion.6
  21.4 0.3 convolution_convert_fusion.4
  21.7 1.0 collective-permute-done
  22.7 1.1 add_convert_fusion
  23.8 3.5 %all-to-all-start = ((bf16[8,96,512]{2,1,0:T(8,128)(2,1)}), bf16[8,96,512]{2,1,0:T(8,128)(2,1)S(1)}, u32[]{:S(2)}, u32[]{:S(2)}) async-start(bf16[8,96,512]{2,1,0:T(8,128)(2,1)} %add_convert_fusion), calls=%async_computation | async-start | bytes 1572864 | tf_op jit(solution)/shard_map/all_to_all | solution.py:37
  27.4 2.3 %collective-permute-start.1 = (bf16[384,192]{0,1:T(8,128)(2,1)}, bf16[384,192]{0,1:T(8,128)(2,1)S(1)}, u32[]{:S(2)}, u32[]{:S(2)}) collective-permute-start(bf16[384,192]{0,1:T(8,128)(2,1)} %param.13), channel_id=1, source_target_pairs={{0,64},{64,0},{128,192},{192,128},{256,320},{320,256},{384,448},{4... | collective-permute-start | bytes 442376 | tf_op jit(solution)/shard_map/ppermute | solution.py:62
  29.7 2.0 %collective-permute-start.2 = (bf16[256,384]{1,0:T(8,128)(2,1)S(1)}, bf16[256,384]{1,0:T(8,128)(2,1)S(1)}, u32[]{:S(2)}, u32[]{:S(2)}) collective-permute-start(bf16[256,384]{1,0:T(8,128)(2,1)S(1)} %get-tuple-element.38), channel_id=1, source_target_pairs={{0,64},{64,0},{128,192},{192,128},{256,320},{320,256},{384,448},{4... | collective-permute-start | bytes 589832 | tf_op jit(solution)/shard_map/ppermute | solution.py:62
  31.8 2.3 %collective-permute-start.4 = (bf16[384,1024]{1,0:T(8,128)(2,1)S(1)}, bf16[384,1024]{1,0:T(8,128)(2,1)}, u32[]{:S(2)}, u32[]{:S(2)}) collective-permute-start(bf16[384,1024]{1,0:T(8,128)(2,1)S(1)} %constant_dynamic-update-slice_fusion), channel_id=1, source_target_pairs={{0,64},{64,0},{128,192},{192,128},{256,320},{320,256},{384,448},{4... | collective-permute-start | bytes 2359304 | tf_op jit(solution)/shard_map/ppermute | solution.py:62
  34.1 1.6 pad_maximum_fusion.4
  35.8 0.6 dynamic-slice_bitcast_fusion
  36.4 3.9 %all-to-all-done = bf16[8,96,512]{2,1,0:T(8,128)(2,1)S(1)} async-done(((bf16[8,96,512]{2,1,0:T(8,128)(2,1)}), bf16[8,96,512]{2,1,0:T(8,128)(2,1)S(1)}, u32[]{:S(2)}, u32[]{:S(2)}) %all-to-all-start) | async-done | bytes 786464 | tf_op jit(solution)/shard_map/all_to_all | solution.py:37
  40.6 0.9 broadcast_in_dim.8
  41.4 3.5 %all-to-all-start.1 = ((bf16[8,32,1024]{2,1,0:T(8,128)(2,1)}), bf16[8,32,1024]{2,1,0:T(8,128)(2,1)S(1)}, u32[]{:S(2)}, u32[]{:S(2)}) async-start(bf16[8,32,1024]{2,1,0:T(8,128)(2,1)} %broadcast_in_dim.8), calls=%async_computation.1 | async-start | bytes 1048576 | tf_op jit(solution)/shard_map/all_to_all | solution.py:43
  44.9 3.3 %collective-permute-start.3 = (bf16[32,512]{1,0:T(8,128)(2,1)S(1)}, bf16[32,512]{1,0:T(8,128)(2,1)S(1)}, u32[]{:S(2)}, u32[]{:S(2)}) collective-permute-start(bf16[32,512]{1,0:T(8,128)(2,1)S(1)} %get-tuple-element.94), channel_id=1, source_target_pairs={{0,128},{64,192},{128,0},{192,64},{256,384},{320,448},{384,256},{4... | collective-permute-start | bytes 98312 | tf_op jit(solution)/shard_map/ppermute | solution.py:96
  48.2 4.6 %collective-permute-done.3 = bf16[32,512]{1,0:T(8,128)(2,1)S(1)} collective-permute-done((bf16[32,512]{1,0:T(8,128)(2,1)S(1)}, bf16[32,512]{1,0:T(8,128)(2,1)S(1)}, u32[]{:S(2)}, u32[]{:S(2)}) %collective-permute-start.3) | collective-permute-done | bytes 32800 | tf_op jit(solution)/shard_map/ppermute | solution.py:96
  52.8 2.4 %pad_maximum_fusion = bf16[768,1024]{1,0:T(8,128)(2,1)} fusion(bf16[384,1024]{1,0:T(8,128)(2,1)} %collective-permute-done.4, bf16[384,1024]{1,0:T(8,128)(2,1)S(1)} %constant_dynamic-update-slice_fusion), kind=kLoop, calls=%fused_computation | loop fusion | flops 3145728 | bytes 3145728 | tf_op jit(solution)/shard_map/concatenate | solution.py:86
  55.3 2.8 %convolution_convert_fusion = bf16[256,768]{1,0:T(8,128)(2,1)} fusion(bf16[256,1024]{1,0:T(8,128)(2,1)S(1)} %bitcast.48, bf16[768,1024]{1,0:T(8,128)(2,1)} %pad_maximum_fusion), kind=kOutput, calls=%fused_computation.3 | convolution fusion | flops 402849792 | bytes 2490368 | tf_op jit(solution)/shard_map/dot_general | solution.py:31
  58.0 10.0 %all-to-all-start.2 = ((bf16[8,32,768]{2,1,0:T(8,128)(2,1)}), bf16[8,32,768]{2,1,0:T(8,128)(2,1)S(1)}, u32[]{:S(2)}, u32[]{:S(2)}) async-start(bf16[8,32,768]{2,1,0:T(8,128)(2,1)} %bitcast.9), calls=%async_computation.2 | async-start | bytes 786432 | tf_op jit(solution)/shard_map/all_to_all | solution.py:37
  68.0 1.9 %collective-permute-start.5 = (bf16[256,1024]{1,0:T(8,128)(2,1)S(1)}, bf16[256,1024]{1,0:T(8,128)(2,1)S(1)}, u32[]{:S(2)}, u32[]{:S(2)}) collective-permute-start(bf16[256,1024]{1,0:T(8,128)(2,1)S(1)} %bitcast.49), channel_id=1, source_target_pairs={{0,64},{64,0},{128,192},{192,128},{256,320},{320,256},{384,448},{4... | collective-permute-start | bytes 1572872 | tf_op jit(solution)/shard_map/ppermute | solution.py:62
  70.0 3.1 %collective-permute-start.6 = (bf16[64,512]{1,0:T(8,128)(2,1)S(1)}, bf16[64,512]{1,0:T(8,128)(2,1)S(1)}, u32[]{:S(2)}, u32[]{:S(2)}) collective-permute-start(bf16[64,512]{1,0:T(8,128)(2,1)S(1)} %maximum_select_fusion.4), channel_id=1, source_target_pairs={{0,512},{64,576},{128,640},{192,704},{256,768},{320,832},{384,896}... | collective-permute-start | bytes 196616 | tf_op jit(solution)/shard_map/ppermute | solution.py:96
  73.1 0.3 fusion.24
  73.3 0.3 fusion.27
  73.6 1.7 collective-permute-done.6
  75.3 2.8 %all-to-all-done.2 = bf16[8,32,768]{2,1,0:T(8,128)(2,1)S(1)} async-done(((bf16[8,32,768]{2,1,0:T(8,128)(2,1)}), bf16[8,32,768]{2,1,0:T(8,128)(2,1)S(1)}, u32[]{:S(2)}, u32[]{:S(2)}) %all-to-all-start.2) | async-done | bytes 393248 | tf_op jit(solution)/shard_map/all_to_all | solution.py:37
  78.1 0.7 broadcast_in_dim.9
  78.8 21.6 %all-to-all-start.3 = ((bf16[4,32,768]{2,1,0:T(8,128)(2,1)}), bf16[4,32,768]{2,1,0:T(8,128)(2,1)S(1)}, u32[]{:S(2)}, u32[]{:S(2)}) async-start(bf16[4,32,768]{2,1,0:T(8,128)(2,1)} %broadcast_in_dim.9), calls=%async_computation.3 | async-start | bytes 393216 | tf_op jit(solution)/shard_map/all_to_all | solution.py:43
  100.4 0.3 fusion.8
  100.7 0.3 fusion.9
  101.0 4.6 %collective-permute-start.8 = (bf16[768,256]{1,0:T(8,128)(2,1)S(1)}, bf16[768,256]{1,0:T(8,128)(2,1)S(1)}, u32[]{:S(2)}, u32[]{:S(2)}) collective-permute-start(bf16[768,256]{1,0:T(8,128)(2,1)S(1)} %pad_maximum_fusion.3), channel_id=1, source_target_pairs={{0,1},{1,0},{2,3},{3,2},{4,5},{5,4},{6,7},{7,6},{8,9},{9,8},{10,11... | collective-permute-start | bytes 1179656 | tf_op jit(solution)/shard_map/ppermute | solution.py:132
  105.6 4.3 %collective-permute-start.7 = (bf16[128,512]{1,0:T(8,128)(2,1)S(1)}, bf16[128,512]{1,0:T(8,128)(2,1)S(1)}, u32[]{:S(2)}, u32[]{:S(2)}) collective-permute-start(bf16[128,512]{1,0:T(8,128)(2,1)S(1)} %maximum_select_fusion.3), channel_id=1, source_target_pairs={{0,256},{64,320},{128,384},{192,448},{256,0},{320,64},{384,128},{4... | collective-permute-start | bytes 393224 | tf_op jit(solution)/shard_map/ppermute | solution.py:96
  109.9 4.4 %collective-permute-done.7 = bf16[128,512]{1,0:T(8,128)(2,1)S(1)} collective-permute-done((bf16[128,512]{1,0:T(8,128)(2,1)S(1)}, bf16[128,512]{1,0:T(8,128)(2,1)S(1)}, u32[]{:S(2)}, u32[]{:S(2)}) %collective-permute-start.7) | collective-permute-done | bytes 131104 | tf_op jit(solution)/shard_map/ppermute | solution.py:96
  114.4 1.1 collective-permute-done.8
  115.5 2.3 %collective-permute-start.9 = (bf16[256,512]{1,0:T(8,128)(2,1)S(1)}, bf16[256,512]{1,0:T(8,128)(2,1)S(1)}, u32[]{:S(2)}, u32[]{:S(2)}) collective-permute-start(bf16[256,512]{1,0:T(8,128)(2,1)S(1)} %bitcast.59), channel_id=1, source_target_pairs={{0,64},{64,0},{128,192},{192,128},{256,320},{320,256},{384,448},{4... | collective-permute-start | bytes 786440 | tf_op jit(solution)/shard_map/ppermute | solution.py:96
  117.8 0.3 fusion.21
  118.1 1.0 fusion.6
  119.1 0.2 maximum_select_fusion
  119.4 0.8 broadcast_in_dim.10
  120.2 12.3 %all-to-all-start.4 = ((bf16[8,32,768]{2,1,0:T(8,128)(2,1)}), bf16[8,32,768]{2,1,0:T(8,128)(2,1)S(1)}, u32[]{:S(2)}, u32[]{:S(2)}) async-start(bf16[8,32,768]{2,1,0:T(8,128)(2,1)} %broadcast_in_dim.10), calls=%async_computation.4 | async-start | bytes 786432 | tf_op jit(solution)/shard_map/all_to_all | solution.py:43
  132.5 0.2 fusion.18
  132.8 0.3 fusion.10
  133.1 4.9 %collective-permute-start.10 = (bf16[384,256]{0,1:T(8,128)(2,1)S(1)}, bf16[384,256]{0,1:T(8,128)(2,1)S(1)}, u32[]{:S(2)}, u32[]{:S(2)}) collective-permute-start(bf16[384,256]{0,1:T(8,128)(2,1)S(1)} %fusion.10), channel_id=1, source_target_pairs={{0,1},{1,0},{2,3},{3,2},{4,5},{5,4},{6,7},{7,6},{8,9},{9,8},{10,11... | collective-permute-start | bytes 589832 | tf_op jit(solution)/shard_map/ppermute | solution.py:144
  138.0 1.0 fusion.5
  139.0 2.0 %collective-permute-done.10 = bf16[384,256]{0,1:T(8,128)(2,1)S(1)} collective-permute-done((bf16[384,256]{0,1:T(8,128)(2,1)S(1)}, bf16[384,256]{0,1:T(8,128)(2,1)S(1)}, u32[]{:S(2)}, u32[]{:S(2)}) %collective-permute-start.10) | collective-permute-done | bytes 196640 | tf_op jit(solution)/shard_map/ppermute | solution.py:144
  141.1 0.9 convolution_convert_fusion.7
  142.0 16.0 %collective-permute-start.11 = (bf16[256,384]{1,0:T(8,128)(2,1)S(1)}, bf16[256,384]{1,0:T(8,128)(2,1)S(1)}, u32[]{:S(2)}, u32[]{:S(2)}) collective-permute-start(bf16[256,384]{1,0:T(8,128)(2,1)S(1)} %get-tuple-element.59), channel_id=1, source_target_pairs={{0,64},{64,0},{128,192},{192,128},{256,320},{320,256},{384,448},{4... | collective-permute-start | bytes 589832 | tf_op jit(solution)/shard_map/ppermute | solution.py:62
  158.0 4.6 %all-to-all-start.5 = ((bf16[8,24,256]{2,1,0:T(8,128)(2,1)}), bf16[8,24,256]{2,1,0:T(8,128)(2,1)S(1)}, u32[]{:S(2)}, u32[]{:S(2)}) async-start(bf16[8,24,256]{2,1,0:T(8,128)(2,1)} %bitcast.15), calls=%async_computation.5 | async-start | bytes 196608 | tf_op jit(solution)/shard_map/all_to_all | solution.py:37
  162.6 0.3 convert_add_fusion
  163.0 5.0 %all-to-all-done.5 = bf16[8,24,256]{2,1,0:T(8,128)(2,1)S(1)} async-done(((bf16[8,24,256]{2,1,0:T(8,128)(2,1)}), bf16[8,24,256]{2,1,0:T(8,128)(2,1)S(1)}, u32[]{:S(2)}, u32[]{:S(2)}) %all-to-all-start.5) | async-done | bytes 98336 | tf_op jit(solution)/shard_map/all_to_all | solution.py:37
  168.0 0.7 broadcast_in_dim.11
  168.6 4.7 %all-to-all-start.6 = ((bf16[16,24,256]{2,1,0:T(8,128)(2,1)}), bf16[16,24,256]{2,1,0:T(8,128)(2,1)S(1)}, u32[]{:S(2)}, u32[]{:S(2)}) async-start(bf16[16,24,256]{2,1,0:T(8,128)(2,1)} %broadcast_in_dim.11), calls=%async_computation.6 | async-start | bytes 393216 | tf_op jit(solution)/shard_map/all_to_all | solution.py:43
  173.6 0.2 fusion.12
  173.8 4.4 %collective-permute-start.12 = (bf16[384,96]{0,1:T(8,128)(2,1)S(1)}, bf16[384,96]{0,1:T(8,128)(2,1)S(1)}, u32[]{:S(2)}, u32[]{:S(2)}) collective-permute-start(bf16[384,96]{0,1:T(8,128)(2,1)S(1)} %fusion.12), channel_id=1, source_target_pairs={{0,1},{1,0},{2,3},{3,2},{4,5},{5,4},{6,7},{7,6},{8,9},{9,8},{10,11... | collective-permute-start | bytes 221192 | tf_op jit(solution)/shard_map/ppermute | solution.py:170
  178.2 0.9 copy.18
  179.1 1.0 all-to-all-done.6
  180.1 0.2 copy.17
  180.3 0.7 copy.19
  181.0 1.4 collective-permute-done.12
  182.4 0.9 fusion.11
  (44 shorter events, 0.9 us)
Async XLA Ops:
  0.6 1.0 copy-start
  0.6 3.6 %copy-start.4 = (bf16[512,384]{1,0:T(8,128)(2,1)S(1)}, bf16[512,384]{1,0:T(8,128)(2,1)}, u32[]{:S(2)}) copy-start(bf16[512,384]{1,0:T(8,128)(2,1)} %param.9) | copy-start | bytes 1179652
  0.7 3.7 %copy-start.5 = (bf16[384,512]{1,0:T(8,128)(2,1)S(1)}, bf16[384,512]{1,0:T(8,128)(2,1)}, u32[]{:S(2)}) copy-start(bf16[384,512]{1,0:T(8,128)(2,1)} %param.12) | copy-start | bytes 1179652
  4.3 16.5 %copy-start.2 = (bf16[384,512]{1,0:T(8,128)(2,1)S(1)}, bf16[384,512]{1,0:T(8,128)(2,1)}, u32[]{:S(2)}) copy-start(bf16[384,512]{1,0:T(8,128)(2,1)} %param.11) | copy-start | bytes 1179652
  4.3 16.8 %copy-start.1 = (bf16[384,512]{1,0:T(8,128)(2,1)S(1)}, bf16[384,512]{1,0:T(8,128)(2,1)}, u32[]{:S(2)}) copy-start(bf16[384,512]{1,0:T(8,128)(2,1)} %param.10) | copy-start | bytes 1179652
  4.7 18.0 %collective-permute-start = (bf16[8,96,512]{2,1,0:T(8,128)(2,1)S(1)}, bf16[8,96,512]{2,1,0:T(8,128)(2,1)S(1)}, u32[]{:S(2)}, u32[]{:S(2)}) collective-permute-start(bf16[8,96,512]{2,1,0:T(8,128)(2,1)S(1)} %pad_maximum_fusion.1), channel_id=1, source_target_pairs={{0,64},{64,0},{128,192},{192,128},{256,320},{320,256},{384,448},{4... | collective-permute-start | bytes 2359304 | tf_op jit(solution)/shard_map/ppermute | solution.py:62
  23.8 16.6 %all-to-all-start = ((bf16[8,96,512]{2,1,0:T(8,128)(2,1)}), bf16[8,96,512]{2,1,0:T(8,128)(2,1)S(1)}, u32[]{:S(2)}, u32[]{:S(2)}) async-start(bf16[8,96,512]{2,1,0:T(8,128)(2,1)} %add_convert_fusion), calls=%async_computation | async-start | bytes 1572864 | tf_op jit(solution)/shard_map/all_to_all | solution.py:37
  27.4 6.7 %collective-permute-start.1 = (bf16[384,192]{0,1:T(8,128)(2,1)}, bf16[384,192]{0,1:T(8,128)(2,1)S(1)}, u32[]{:S(2)}, u32[]{:S(2)}) collective-permute-start(bf16[384,192]{0,1:T(8,128)(2,1)} %param.13), channel_id=1, source_target_pairs={{0,64},{64,0},{128,192},{192,128},{256,320},{320,256},{384,448},{4... | collective-permute-start | bytes 442376 | tf_op jit(solution)/shard_map/ppermute | solution.py:62
  29.7 6.1 %collective-permute-start.2 = (bf16[256,384]{1,0:T(8,128)(2,1)S(1)}, bf16[256,384]{1,0:T(8,128)(2,1)S(1)}, u32[]{:S(2)}, u32[]{:S(2)}) collective-permute-start(bf16[256,384]{1,0:T(8,128)(2,1)S(1)} %get-tuple-element.38), channel_id=1, source_target_pairs={{0,64},{64,0},{128,192},{192,128},{256,320},{320,256},{384,448},{4... | collective-permute-start | bytes 589832 | tf_op jit(solution)/shard_map/ppermute | solution.py:62
  31.8 21.0 %collective-permute-start.4 = (bf16[384,1024]{1,0:T(8,128)(2,1)S(1)}, bf16[384,1024]{1,0:T(8,128)(2,1)}, u32[]{:S(2)}, u32[]{:S(2)}) collective-permute-start(bf16[384,1024]{1,0:T(8,128)(2,1)S(1)} %constant_dynamic-update-slice_fusion), channel_id=1, source_target_pairs={{0,64},{64,0},{128,192},{192,128},{256,320},{320,256},{384,448},{4... | collective-permute-start | bytes 2359304 | tf_op jit(solution)/shard_map/ppermute | solution.py:62
  41.4 13.8 %all-to-all-start.1 = ((bf16[8,32,1024]{2,1,0:T(8,128)(2,1)}), bf16[8,32,1024]{2,1,0:T(8,128)(2,1)S(1)}, u32[]{:S(2)}, u32[]{:S(2)}) async-start(bf16[8,32,1024]{2,1,0:T(8,128)(2,1)} %broadcast_in_dim.8), calls=%async_computation.1 | async-start | bytes 1048576 | tf_op jit(solution)/shard_map/all_to_all | solution.py:43
  44.9 7.9 %collective-permute-start.3 = (bf16[32,512]{1,0:T(8,128)(2,1)S(1)}, bf16[32,512]{1,0:T(8,128)(2,1)S(1)}, u32[]{:S(2)}, u32[]{:S(2)}) collective-permute-start(bf16[32,512]{1,0:T(8,128)(2,1)S(1)} %get-tuple-element.94), channel_id=1, source_target_pairs={{0,128},{64,192},{128,0},{192,64},{256,384},{320,448},{384,256},{4... | collective-permute-start | bytes 98312 | tf_op jit(solution)/shard_map/ppermute | solution.py:96
  58.0 20.0 %all-to-all-start.2 = ((bf16[8,32,768]{2,1,0:T(8,128)(2,1)}), bf16[8,32,768]{2,1,0:T(8,128)(2,1)S(1)}, u32[]{:S(2)}, u32[]{:S(2)}) async-start(bf16[8,32,768]{2,1,0:T(8,128)(2,1)} %bitcast.9), calls=%async_computation.2 | async-start | bytes 786432 | tf_op jit(solution)/shard_map/all_to_all | solution.py:37
  68.0 10.1 %collective-permute-start.5 = (bf16[256,1024]{1,0:T(8,128)(2,1)S(1)}, bf16[256,1024]{1,0:T(8,128)(2,1)S(1)}, u32[]{:S(2)}, u32[]{:S(2)}) collective-permute-start(bf16[256,1024]{1,0:T(8,128)(2,1)S(1)} %bitcast.49), channel_id=1, source_target_pairs={{0,64},{64,0},{128,192},{192,128},{256,320},{320,256},{384,448},{4... | collective-permute-start | bytes 1572872 | tf_op jit(solution)/shard_map/ppermute | solution.py:62
  70.0 5.3 %collective-permute-start.6 = (bf16[64,512]{1,0:T(8,128)(2,1)S(1)}, bf16[64,512]{1,0:T(8,128)(2,1)S(1)}, u32[]{:S(2)}, u32[]{:S(2)}) collective-permute-start(bf16[64,512]{1,0:T(8,128)(2,1)S(1)} %maximum_select_fusion.4), channel_id=1, source_target_pairs={{0,512},{64,576},{128,640},{192,704},{256,768},{320,832},{384,896}... | collective-permute-start | bytes 196616 | tf_op jit(solution)/shard_map/ppermute | solution.py:96
  78.8 40.5 %all-to-all-start.3 = ((bf16[4,32,768]{2,1,0:T(8,128)(2,1)}), bf16[4,32,768]{2,1,0:T(8,128)(2,1)S(1)}, u32[]{:S(2)}, u32[]{:S(2)}) async-start(bf16[4,32,768]{2,1,0:T(8,128)(2,1)} %broadcast_in_dim.9), calls=%async_computation.3 | async-start | bytes 393216 | tf_op jit(solution)/shard_map/all_to_all | solution.py:43
  101.0 14.5 %collective-permute-start.8 = (bf16[768,256]{1,0:T(8,128)(2,1)S(1)}, bf16[768,256]{1,0:T(8,128)(2,1)S(1)}, u32[]{:S(2)}, u32[]{:S(2)}) collective-permute-start(bf16[768,256]{1,0:T(8,128)(2,1)S(1)} %pad_maximum_fusion.3), channel_id=1, source_target_pairs={{0,1},{1,0},{2,3},{3,2},{4,5},{5,4},{6,7},{7,6},{8,9},{9,8},{10,11... | collective-permute-start | bytes 1179656 | tf_op jit(solution)/shard_map/ppermute | solution.py:132
  105.6 8.8 %collective-permute-start.7 = (bf16[128,512]{1,0:T(8,128)(2,1)S(1)}, bf16[128,512]{1,0:T(8,128)(2,1)S(1)}, u32[]{:S(2)}, u32[]{:S(2)}) collective-permute-start(bf16[128,512]{1,0:T(8,128)(2,1)S(1)} %maximum_select_fusion.3), channel_id=1, source_target_pairs={{0,256},{64,320},{128,384},{192,448},{256,0},{320,64},{384,128},{4... | collective-permute-start | bytes 393224 | tf_op jit(solution)/shard_map/ppermute | solution.py:96
  115.5 3.9 %copy-start.8 = (bf16[32,768]{1,0:T(8,128)(2,1)S(1)}, bf16[32,768]{1,0:T(8,128)(2,1)}, u32[]{:S(2)}) copy-start(bf16[32,768]{1,0:T(8,128)(2,1)} %dynamic-slice_bitcast_fusion) | copy-start | bytes 147460
  115.5 3.6 %collective-permute-start.9 = (bf16[256,512]{1,0:T(8,128)(2,1)S(1)}, bf16[256,512]{1,0:T(8,128)(2,1)S(1)}, u32[]{:S(2)}, u32[]{:S(2)}) collective-permute-start(bf16[256,512]{1,0:T(8,128)(2,1)S(1)} %bitcast.59), channel_id=1, source_target_pairs={{0,64},{64,0},{128,192},{192,128},{256,320},{320,256},{384,448},{4... | collective-permute-start | bytes 786440 | tf_op jit(solution)/shard_map/ppermute | solution.py:96
  120.2 20.9 %all-to-all-start.4 = ((bf16[8,32,768]{2,1,0:T(8,128)(2,1)}), bf16[8,32,768]{2,1,0:T(8,128)(2,1)S(1)}, u32[]{:S(2)}, u32[]{:S(2)}) async-start(bf16[8,32,768]{2,1,0:T(8,128)(2,1)} %broadcast_in_dim.10), calls=%async_computation.4 | async-start | bytes 786432 | tf_op jit(solution)/shard_map/all_to_all | solution.py:43
  132.7 8.3 %copy-start.6 = (bf16[768,192]{0,1:T(8,128)(2,1)S(1)}, bf16[768,192]{0,1:T(8,128)(2,1)}, u32[]{:S(2)}) copy-start(bf16[768,192]{0,1:T(8,128)(2,1)} %pad_maximum_fusion.4) | copy-start | bytes 884740
  133.1 7.9 %collective-permute-start.10 = (bf16[384,256]{0,1:T(8,128)(2,1)S(1)}, bf16[384,256]{0,1:T(8,128)(2,1)S(1)}, u32[]{:S(2)}, u32[]{:S(2)}) collective-permute-start(bf16[384,256]{0,1:T(8,128)(2,1)S(1)} %fusion.10), channel_id=1, source_target_pairs={{0,1},{1,0},{2,3},{3,2},{4,5},{5,4},{6,7},{7,6},{8,9},{9,8},{10,11... | collective-permute-start | bytes 589832 | tf_op jit(solution)/shard_map/ppermute | solution.py:144
  142.0 31.5 %copy-start.7 = (bf16[512,192]{0,1:T(8,128)(2,1)S(1)}, bf16[512,192]{0,1:T(8,128)(2,1)}, u32[]{:S(2)}) copy-start(bf16[512,192]{0,1:T(8,128)(2,1)} %param.8) | copy-start | bytes 589828
  142.0 31.4 %collective-permute-start.11 = (bf16[256,384]{1,0:T(8,128)(2,1)S(1)}, bf16[256,384]{1,0:T(8,128)(2,1)S(1)}, u32[]{:S(2)}, u32[]{:S(2)}) collective-permute-start(bf16[256,384]{1,0:T(8,128)(2,1)S(1)} %get-tuple-element.59), channel_id=1, source_target_pairs={{0,64},{64,0},{128,192},{192,128},{256,320},{320,256},{384,448},{4... | collective-permute-start | bytes 589832 | tf_op jit(solution)/shard_map/ppermute | solution.py:62
  158.0 9.9 %all-to-all-start.5 = ((bf16[8,24,256]{2,1,0:T(8,128)(2,1)}), bf16[8,24,256]{2,1,0:T(8,128)(2,1)S(1)}, u32[]{:S(2)}, u32[]{:S(2)}) async-start(bf16[8,24,256]{2,1,0:T(8,128)(2,1)} %bitcast.15), calls=%async_computation.5 | async-start | bytes 196608 | tf_op jit(solution)/shard_map/all_to_all | solution.py:37
  168.6 11.5 %all-to-all-start.6 = ((bf16[16,24,256]{2,1,0:T(8,128)(2,1)}), bf16[16,24,256]{2,1,0:T(8,128)(2,1)S(1)}, u32[]{:S(2)}, u32[]{:S(2)}) async-start(bf16[16,24,256]{2,1,0:T(8,128)(2,1)} %broadcast_in_dim.11), calls=%async_computation.6 | async-start | bytes 393216 | tf_op jit(solution)/shard_map/all_to_all | solution.py:43
  173.6 9.7 %copy-start.3 = (bf16[512,384]{1,0:T(8,128)(2,1)}, bf16[512,384]{1,0:T(8,128)(2,1)S(1)}, u32[]{:S(2)}) copy-start(bf16[512,384]{1,0:T(8,128)(2,1)S(1)} %maximum_select_fusion.1) | copy-start | bytes 1179652
  173.8 8.6 %collective-permute-start.12 = (bf16[384,96]{0,1:T(8,128)(2,1)S(1)}, bf16[384,96]{0,1:T(8,128)(2,1)S(1)}, u32[]{:S(2)}, u32[]{:S(2)}) collective-permute-start(bf16[384,96]{0,1:T(8,128)(2,1)S(1)} %fusion.12), channel_id=1, source_target_pairs={{0,1},{1,0},{2,3},{3,2},{4,5},{5,4},{6,7},{7,6},{8,9},{9,8},{10,11... | collective-permute-start | bytes 221192 | tf_op jit(solution)/shard_map/ppermute | solution.py:170

commit v9 on v8

--- a/solution.py
+++ b/solution.py
@@ -83,12 +83,11 @@
     to_swap = [w_both, *to_swap]
     total = scatter_sum(parts, "row", chip_groups)
     w_both_far, w_out_far, out_far = (swap(x) for x in to_swap)
-    w_pair = jnp.concatenate([w_both, w_both_far])
     w_out_pair = jnp.concatenate([w_out, w_out_far])
     out_pair = jnp.concatenate([out_mine, out_far], axis=1)
     spot = (lax.axis_index("col") + cols - 4 * core) % near
     out_piece = lax.dynamic_index_in_dim(out_pair.reshape(near, half // near, 2 * width), spot, 0, False)
-    total, w_out_pair, out_piece = tie((total, w_out_pair, out_piece))
+    total, w_both_far, w_out_pair, out_piece = tie((total, w_both_far, w_out_pair, out_piece))
     gate_share, up_share, hid_share = swiglu_grads(
         total[:share], total[share : 2 * share], total[2 * share :]
     )
@@ -100,9 +99,7 @@
         return pair.reshape(-1, hidden_width)
 
     mine = gather(jnp.concatenate([gate_share, up_share], axis=1), chips, "row", chip_groups)
-    mine, hid_pair, w_pair = tie(
-        (mine.reshape(half, 2 * hidden_width), double(hid_share, 2), w_pair)
-    )
+    mine, hid_pair = tie((mine.reshape(half, 2 * hidden_width), double(hid_share, 2)))
 
     def place(r, k, j):
         return r * cols + (k * near + j + 4 * (r % 2)) % cols
@@ -111,7 +108,8 @@
     far_groups = [[place(r, k, j) for k in range(far)] for r in range(rows) for j in range(near)]
     both = ("row", "col")
 
-    back_part = contract_cols(mine, w_pair).astype(BF16).reshape(near, half // near, 2 * width)
+    back_part = jnp.concatenate([contract_cols(mine, w).astype(BF16) for w in (w_both, w_both_far)], axis=1)
+    back_part = back_part.reshape(near, half // near, 2 * width)
     back_part, sent_mine, hid_pair = tie((back_part, mine, hid_pair))
     other = swap(sent_mine)
     hid_row = double(hid_pair, 8)
@@ -138,12 +136,14 @@
     far_sum = jnp.sum(group_sums.astype(F32), axis=0)
     gate_wgrad = wgrad(both_pairs, seq) + received[:width].astype(F32)
     up_wgrad = wgrad(both_pairs, seq, hidden_width) + received[width:].astype(F32)
-    far_sum, hid_all, gate_wgrad = tie((far_sum, hid_all, gate_wgrad))
+    far_sum, hid_all = tie((far_sum, hid_all))
     resid_piece = (out_piece.astype(F32) + far_sum).astype(BF16)
     down_pairs = ((out_grad, hid_all),)
     down_received = lax.ppermute(wgrad(down_pairs, 1 - seq).astype(BF16), "seq", seq_swap)
     resid_all = gather(resid_piece, near, both, near_groups)
-    resid_all, down_received, up_wgrad = tie((resid_all, down_received, up_wgrad))
+    resid_all, down_received, gate_wgrad, up_wgrad = tie(
+        (resid_all, down_received, gate_wgrad, up_wgrad)
+    )
     down_wgrad = wgrad(down_pairs, seq) + down_received.astype(F32)
     resid_all = resid_all.reshape(half, 2 * width)
     resid_mine, resid_far = resid_all[:, :width], resid_all[:, width:]

time: 185 us -> 180 us (0.973)
  starting transfers between devices: 128 us -> 125 us
    all_to_all x3, waiting for transfers between devices: 11.6 us -> 5.71 us  [scatter_sum(): lax.all_to_all(parts, axis, 0, 0, tiled=True, axis_index_groups=groups)]
    all_to_all x4, starting transfers between devices: 42.2 us -> 45.3 us  [gather(): lax.all_to_all(copies, axis, 0, 0, tiled=True, axis_index_groups=groups)]
    ppermute x6, starting transfers between devices: 40.6 us -> 37.7 us  [swap(): return lax.ppermute(x, 'row', core_swap)]
    all_to_all x4, waiting for transfers between devices: 1 us -> 3.25 us  [gather(): lax.all_to_all(copies, axis, 0, 0, tiled=True, axis_index_groups=groups)]
    dot_general x1 -> x2, matrix products: 2.77 us -> 0.91 us  [contract_cols(): lax.dot_general(first, second, (((1,), (1,)), ((), ())), preferred_elemen...]
    unnamed x21 -> x29, local copies, waits for them, and re-layouts: 2.65 us -> 3.76 us
  transfers between devices with their start and end apart: 20 -> 20, of which waited for: 11 -> 12; matrix products, arithmetic and copies ran while one was open for 8% -> 7% of each run, Pallas kernels for 0% -> 0%
where the time goes in v9:
time: 180 us; the launch traced here: 178 us
  starting transfers between devices  125 us (69%)
  waiting for transfers between devices  27.6 us (15%)
  matrix products  11.8 us (7%)
  local copies, waits for them, and re-layouts  7.28 us (4%)
  other arithmetic  5.38 us (3%)
    all_to_all x4, starting transfers between devices, gather(): lax.all_to_all(copies, axis, 0, 0, tiled=True, axis_index_groups=groups)  45.3 us
    ppermute x6, starting transfers between devices, swap(): return lax.ppermute(x, 'row', core_swap)  37.7 us
    all_to_all x3, starting transfers between devices, scatter_sum(): lax.all_to_all(parts, axis, 0, 0, tiled=True, axis_index_groups=groups)  16.9 us
    ppermute x4, starting transfers between devices, double(): got = lax.ppermute(x, 'row', [(i, i ^ bit) for i in range(rows)])  12.4 us
    ppermute x4, waiting for transfers between devices, double(): got = lax.ppermute(x, 'row', [(i, i ^ bit) for i in range(rows)])  11.9 us
    dot_general x12, matrix products, contract_rows(): lax.dot_general(first, second, (((0,), (0,)), ((), ())), preferred_elemen...  7.12 us
    all_to_all x3, waiting for transfers between devices, scatter_sum(): lax.all_to_all(parts, axis, 0, 0, tiled=True, axis_index_groups=groups)  5.71 us
    ppermute x1, starting transfers between devices, per_device(): lax.ppermute(out_sent, 'seq', seq_swap).astype(F32)  4.42 us
  transfers between devices with their start and end apart: 20, of which 12 were waited for; matrix products, arithmetic and copies ran while one was open for 7% of the time, Pallas kernels for 0%

profile of v9, /device:TPU:1, one launch (start us, length us, event | category | flops | bytes accessed | tf_op | source)
XLA Modules:
  0.0 178.4 jit_solution(18430013099836031826)
XLA Ops:
  0.7 1.0 copy-done
  1.6 1.3 convolution_convert_fusion.2
  3.0 0.3 convolution_convert_fusion.1
  3.4 0.6 copy-done.5
  4.0 0.3 convolution_convert_fusion
  4.4 16.2 %collective-permute-start = (bf16[8,96,512]{2,1,0:T(8,128)(2,1)S(1)}, bf16[8,96,512]{2,1,0:T(8,128)(2,1)S(1)}, u32[]{:S(2)}, u32[]{:S(2)}) collective-permute-start(bf16[8,96,512]{2,1,0:T(8,128)(2,1)S(1)} %pad_maximum_fusion), channel_id=1, source_target_pairs={{0,64},{64,0},{128,192},{192,128},{256,320},{320,256},{384,448},{4... | collective-permute-start | bytes 2359304 | tf_op jit(solution)/shard_map/ppermute | solution.py:62
  20.6 0.3 convolution_convert_fusion.5
  20.9 0.3 convolution_convert_fusion.4
  21.2 0.3 convolution_convert_fusion.3
  21.5 1.0 collective-permute-done
  22.5 1.1 add_convert_fusion
  23.6 3.5 %all-to-all-start = ((bf16[8,96,512]{2,1,0:T(8,128)(2,1)}), bf16[8,96,512]{2,1,0:T(8,128)(2,1)S(1)}, u32[]{:S(2)}, u32[]{:S(2)}) async-start(bf16[8,96,512]{2,1,0:T(8,128)(2,1)} %add_convert_fusion), calls=%async_computation | async-start | bytes 1572864 | tf_op jit(solution)/shard_map/all_to_all | solution.py:37
  27.2 2.3 %collective-permute-start.1 = (bf16[384,1024]{1,0:T(8,128)(2,1)S(1)}, bf16[384,1024]{1,0:T(8,128)(2,1)S(1)}, u32[]{:S(2)}, u32[]{:S(2)}) collective-permute-start(bf16[384,1024]{1,0:T(8,128)(2,1)S(1)} %constant_dynamic-update-slice_fusion), channel_id=1, source_target_pairs={{0,64},{64,0},{128,192},{192,128},{256,320},{320,256},{384,448},{4... | collective-permute-start | bytes 2359304 | tf_op jit(solution)/shard_map/ppermute | solution.py:62
  29.5 2.0 %collective-permute-start.2 = (bf16[384,192]{0,1:T(8,128)(2,1)}, bf16[384,192]{0,1:T(8,128)(2,1)}, u32[]{:S(2)}, u32[]{:S(2)}) collective-permute-start(bf16[384,192]{0,1:T(8,128)(2,1)} %param.13), channel_id=1, source_target_pairs={{0,64},{64,0},{128,192},{192,128},{256,320},{320,256},{384,448},{4... | collective-permute-start | bytes 442376 | tf_op jit(solution)/shard_map/ppermute | solution.py:62
  31.6 2.3 %collective-permute-start.3 = (bf16[256,384]{1,0:T(8,128)(2,1)S(1)}, bf16[256,384]{1,0:T(8,128)(2,1)}, u32[]{:S(2)}, u32[]{:S(2)}) collective-permute-start(bf16[256,384]{1,0:T(8,128)(2,1)S(1)} %get-tuple-element.40), channel_id=1, source_target_pairs={{0,64},{64,0},{128,192},{192,128},{256,320},{320,256},{384,448},{4... | collective-permute-start | bytes 589832 | tf_op jit(solution)/shard_map/ppermute | solution.py:62
  33.9 1.7 pad_maximum_fusion.4
  35.6 1.0 pad_maximum_fusion.1
  36.6 3.5 %all-to-all-done = bf16[8,96,512]{2,1,0:T(8,128)(2,1)S(1)} async-done(((bf16[8,96,512]{2,1,0:T(8,128)(2,1)}), bf16[8,96,512]{2,1,0:T(8,128)(2,1)S(1)}, u32[]{:S(2)}, u32[]{:S(2)}) %all-to-all-start) | async-done | bytes 786464 | tf_op jit(solution)/shard_map/all_to_all | solution.py:37
  40.4 1.0 broadcast_in_dim.8
  41.4 3.5 %all-to-all-start.1 = ((bf16[8,32,1024]{2,1,0:T(8,128)(2,1)}), bf16[8,32,1024]{2,1,0:T(8,128)(2,1)S(1)}, u32[]{:S(2)}, u32[]{:S(2)}) async-start(bf16[8,32,1024]{2,1,0:T(8,128)(2,1)} %broadcast_in_dim.8), calls=%async_computation.1 | async-start | bytes 1048576 | tf_op jit(solution)/shard_map/all_to_all | solution.py:43
  44.9 3.3 %collective-permute-start.4 = (bf16[32,512]{1,0:T(8,128)(2,1)S(1)}, bf16[32,512]{1,0:T(8,128)(2,1)S(1)}, u32[]{:S(2)}, u32[]{:S(2)}) collective-permute-start(bf16[32,512]{1,0:T(8,128)(2,1)S(1)} %get-tuple-element.94), channel_id=1, source_target_pairs={{0,128},{64,192},{128,0},{192,64},{256,384},{320,448},{384,256},{4... | collective-permute-start | bytes 98312 | tf_op jit(solution)/shard_map/ppermute | solution.py:95
  48.1 4.6 %collective-permute-done.4 = bf16[32,512]{1,0:T(8,128)(2,1)S(1)} collective-permute-done((bf16[32,512]{1,0:T(8,128)(2,1)S(1)}, bf16[32,512]{1,0:T(8,128)(2,1)S(1)}, u32[]{:S(2)}, u32[]{:S(2)}) %collective-permute-start.4) | collective-permute-done | bytes 32800 | tf_op jit(solution)/shard_map/ppermute | solution.py:95
  52.8 2.3 %all-to-all-done.1 = bf16[8,32,1024]{2,1,0:T(8,128)(2,1)S(1)} async-done(((bf16[8,32,1024]{2,1,0:T(8,128)(2,1)}), bf16[8,32,1024]{2,1,0:T(8,128)(2,1)S(1)}, u32[]{:S(2)}, u32[]{:S(2)}) %all-to-all-start.1) | async-done | bytes 524320 | tf_op jit(solution)/shard_map/all_to_all | solution.py:43
  55.0 0.5 convolution_convert_fusion.7
  55.5 0.5 convolution_convert_fusion.6
  56.0 0.8 pad_maximum_fusion.2
  56.8 10.0 %all-to-all-start.2 = ((bf16[8,32,768]{2,1,0:T(8,128)(2,1)}), bf16[8,32,768]{2,1,0:T(8,128)(2,1)S(1)}, u32[]{:S(2)}, u32[]{:S(2)}) async-start(bf16[8,32,768]{2,1,0:T(8,128)(2,1)} %bitcast.9), calls=%async_computation.2 | async-start | bytes 786432 | tf_op jit(solution)/shard_map/all_to_all | solution.py:37
  66.8 1.9 %collective-permute-start.5 = (bf16[256,1024]{1,0:T(8,128)(2,1)S(1)}, bf16[256,1024]{1,0:T(8,128)(2,1)S(1)}, u32[]{:S(2)}, u32[]{:S(2)}) collective-permute-start(bf16[256,1024]{1,0:T(8,128)(2,1)S(1)} %bitcast.50), channel_id=1, source_target_pairs={{0,64},{64,0},{128,192},{192,128},{256,320},{320,256},{384,448},{4... | collective-permute-start | bytes 1572872 | tf_op jit(solution)/shard_map/ppermute | solution.py:62
  68.7 2.2 %collective-permute-start.6 = (bf16[64,512]{1,0:T(8,128)(2,1)S(1)}, bf16[64,512]{1,0:T(8,128)(2,1)S(1)}, u32[]{:S(2)}, u32[]{:S(2)}) collective-permute-start(bf16[64,512]{1,0:T(8,128)(2,1)S(1)} %maximum_select_fusion.4), channel_id=1, source_target_pairs={{0,512},{64,576},{128,640},{192,704},{256,768},{320,832},{384,896}... | collective-permute-start | bytes 196616 | tf_op jit(solution)/shard_map/ppermute | solution.py:95
  70.9 0.3 fusion.24
  71.2 0.3 fusion.27
  71.4 2.6 %collective-permute-done.6 = bf16[64,512]{1,0:T(8,128)(2,1)S(1)} collective-permute-done((bf16[64,512]{1,0:T(8,128)(2,1)S(1)}, bf16[64,512]{1,0:T(8,128)(2,1)S(1)}, u32[]{:S(2)}, u32[]{:S(2)}) %collective-permute-start.6) | collective-permute-done | bytes 65568 | tf_op jit(solution)/shard_map/ppermute | solution.py:95
  74.1 2.2 %all-to-all-done.2 = bf16[8,32,768]{2,1,0:T(8,128)(2,1)S(1)} async-done(((bf16[8,32,768]{2,1,0:T(8,128)(2,1)}), bf16[8,32,768]{2,1,0:T(8,128)(2,1)S(1)}, u32[]{:S(2)}, u32[]{:S(2)}) %all-to-all-start.2) | async-done | bytes 393248 | tf_op jit(solution)/shard_map/all_to_all | solution.py:37
  76.3 0.7 broadcast_in_dim.9
  77.0 21.2 %all-to-all-start.3 = ((bf16[4,32,768]{2,1,0:T(8,128)(2,1)}), bf16[4,32,768]{2,1,0:T(8,128)(2,1)S(1)}, u32[]{:S(2)}, u32[]{:S(2)}) async-start(bf16[4,32,768]{2,1,0:T(8,128)(2,1)} %broadcast_in_dim.9), calls=%async_computation.3 | async-start | bytes 393216 | tf_op jit(solution)/shard_map/all_to_all | solution.py:43
  98.3 0.3 fusion.8
  98.5 0.3 fusion.9
  98.8 4.3 %collective-permute-start.8 = (bf16[768,256]{1,0:T(8,128)(2,1)S(1)}, bf16[768,256]{1,0:T(8,128)(2,1)S(1)}, u32[]{:S(2)}, u32[]{:S(2)}) collective-permute-start(bf16[768,256]{1,0:T(8,128)(2,1)S(1)} %pad_maximum_fusion.3), channel_id=1, source_target_pairs={{0,1},{1,0},{2,3},{3,2},{4,5},{5,4},{6,7},{7,6},{8,9},{9,8},{10,11... | collective-permute-start | bytes 1179656 | tf_op jit(solution)/shard_map/ppermute | solution.py:130
  103.1 4.0 %collective-permute-start.7 = (bf16[128,512]{1,0:T(8,128)(2,1)S(1)}, bf16[128,512]{1,0:T(8,128)(2,1)S(1)}, u32[]{:S(2)}, u32[]{:S(2)}) collective-permute-start(bf16[128,512]{1,0:T(8,128)(2,1)S(1)} %maximum_select_fusion.3), channel_id=1, source_target_pairs={{0,256},{64,320},{128,384},{192,448},{256,0},{320,64},{384,128},{4... | collective-permute-start | bytes 393224 | tf_op jit(solution)/shard_map/ppermute | solution.py:95
  107.1 3.5 %collective-permute-done.7 = bf16[128,512]{1,0:T(8,128)(2,1)S(1)} collective-permute-done((bf16[128,512]{1,0:T(8,128)(2,1)S(1)}, bf16[128,512]{1,0:T(8,128)(2,1)S(1)}, u32[]{:S(2)}, u32[]{:S(2)}) %collective-permute-start.7) | collective-permute-done | bytes 131104 | tf_op jit(solution)/shard_map/ppermute | solution.py:95
  110.7 2.0 %collective-permute-done.8 = bf16[768,256]{1,0:T(8,128)(2,1)S(1)} collective-permute-done((bf16[768,256]{1,0:T(8,128)(2,1)S(1)}, bf16[768,256]{1,0:T(8,128)(2,1)S(1)}, u32[]{:S(2)}, u32[]{:S(2)}) %collective-permute-start.8) | collective-permute-done | bytes 393248 | tf_op jit(solution)/shard_map/ppermute | solution.py:130
  112.7 3.0 %collective-permute-start.9 = (bf16[256,512]{1,0:T(8,128)(2,1)S(1)}, bf16[256,512]{1,0:T(8,128)(2,1)S(1)}, u32[]{:S(2)}, u32[]{:S(2)}) collective-permute-start(bf16[256,512]{1,0:T(8,128)(2,1)S(1)} %bitcast.62), channel_id=1, source_target_pairs={{0,64},{64,0},{128,192},{192,128},{256,320},{320,256},{384,448},{4... | collective-permute-start | bytes 786440 | tf_op jit(solution)/shard_map/ppermute | solution.py:95
  115.7 1.1 collective-permute-done.9
  117.1 0.8 broadcast_in_dim.10
  117.9 13.1 %all-to-all-start.4 = ((bf16[8,32,768]{2,1,0:T(8,128)(2,1)}), bf16[8,32,768]{2,1,0:T(8,128)(2,1)S(1)}, u32[]{:S(2)}, u32[]{:S(2)}) async-start(bf16[8,32,768]{2,1,0:T(8,128)(2,1)} %broadcast_in_dim.10), calls=%async_computation.4 | async-start | bytes 786432 | tf_op jit(solution)/shard_map/all_to_all | solution.py:43
  131.2 0.3 fusion.21
  131.5 0.5 copy-done.11
  132.0 1.9 %fusion.5 = f32[384,256]{1,0:T(8,128)} fusion(f32[384,256]{1,0:T(8,128)S(1)} %fusion.18, bf16[768,256]{1,0:T(8,128)(2,1)S(1)} %copy-done.11, bf16[256,1024]{1,0:T(8,128)(2,1)} %copy-done.9, s32[]{:T(128)S(6)} %select_n.123, bf16[512,384]{1,0:T(8,128)(2,1)S(1)} %copy-done, s32[]{:T(128)S(6)} %select_n.107), kind=kOutput, calls=%fused_computation.19 | convolution fusion | flops 50724864 | bytes 1310728 | tf_op jit(solution)/shard_map/dot_general | solution.py:25
  133.9 0.3 fusion.10
  134.2 4.0 %collective-permute-start.10 = (bf16[384,256]{0,1:T(8,128)(2,1)S(1)}, bf16[384,256]{0,1:T(8,128)(2,1)S(1)}, u32[]{:S(2)}, u32[]{:S(2)}) collective-permute-start(bf16[384,256]{0,1:T(8,128)(2,1)S(1)} %fusion.10), channel_id=1, source_target_pairs={{0,1},{1,0},{2,3},{3,2},{4,5},{5,4},{6,7},{7,6},{8,9},{9,8},{10,11... | collective-permute-start | bytes 589832 | tf_op jit(solution)/shard_map/ppermute | solution.py:142
  138.3 1.9 %fusion.6 = f32[384,256]{1,0:T(8,128)} fusion(f32[384,256]{1,0:T(8,128)S(1)} %fusion.21, bf16[768,256]{1,0:T(8,128)(2,1)S(1)} %copy-done.11, bf16[256,1024]{1,0:T(8,128)(2,1)} %copy-done.9, s32[]{:T(128)S(6)} %select_n.122, bf16[512,384]{1,0:T(8,128)(2,1)S(1)} %copy-done, s32[]{:T(128)S(6)} %select_n.107), kind=kOutput, calls=%fused_computation.20 | convolution fusion | flops 50724864 | bytes 1310728 | tf_op jit(solution)/shard_map/dot_general | solution.py:25
  140.2 2.4 %collective-permute-done.10 = bf16[384,256]{0,1:T(8,128)(2,1)S(1)} collective-permute-done((bf16[384,256]{0,1:T(8,128)(2,1)S(1)}, bf16[384,256]{0,1:T(8,128)(2,1)S(1)}, u32[]{:S(2)}, u32[]{:S(2)}) %collective-permute-start.10) | collective-permute-done | bytes 196640 | tf_op jit(solution)/shard_map/ppermute | solution.py:142
  142.6 0.9 convolution_convert_fusion.8
  143.6 3.4 %all-to-all-start.5 = ((bf16[8,24,256]{2,1,0:T(8,128)(2,1)}), bf16[8,24,256]{2,1,0:T(8,128)(2,1)S(1)}, u32[]{:S(2)}, u32[]{:S(2)}) async-start(bf16[8,24,256]{2,1,0:T(8,128)(2,1)} %bitcast.15), calls=%async_computation.5 | async-start | bytes 196608 | tf_op jit(solution)/shard_map/all_to_all | solution.py:37
  146.9 13.0 %collective-permute-start.11 = (bf16[256,384]{1,0:T(8,128)(2,1)S(1)}, bf16[256,384]{1,0:T(8,128)(2,1)S(1)}, u32[]{:S(2)}, u32[]{:S(2)}) collective-permute-start(bf16[256,384]{1,0:T(8,128)(2,1)S(1)} %get-tuple-element.59), channel_id=1, source_target_pairs={{0,64},{64,0},{128,192},{192,128},{256,320},{320,256},{384,448},{4... | collective-permute-start | bytes 589832 | tf_op jit(solution)/shard_map/ppermute | solution.py:62
  159.9 0.3 convert_add_fusion
  160.3 0.7 broadcast_in_dim.11
  161.0 7.5 %all-to-all-start.6 = ((bf16[16,24,256]{2,1,0:T(8,128)(2,1)}), bf16[16,24,256]{2,1,0:T(8,128)(2,1)S(1)}, u32[]{:S(2)}, u32[]{:S(2)}) async-start(bf16[16,24,256]{2,1,0:T(8,128)(2,1)} %broadcast_in_dim.11), calls=%async_computation.6 | async-start | bytes 393216 | tf_op jit(solution)/shard_map/all_to_all | solution.py:43
  168.9 4.4 %collective-permute-start.12 = (bf16[384,96]{0,1:T(8,128)(2,1)S(1)}, bf16[384,96]{0,1:T(8,128)(2,1)S(1)}, u32[]{:S(2)}, u32[]{:S(2)}) collective-permute-start(bf16[384,96]{0,1:T(8,128)(2,1)S(1)} %fusion.12), channel_id=1, source_target_pairs={{0,1},{1,0},{2,3},{3,2},{4,5},{5,4},{6,7},{7,6},{8,9},{9,8},{10,11... | collective-permute-start | bytes 221192 | tf_op jit(solution)/shard_map/ppermute | solution.py:170
  173.3 0.9 copy.18
  174.2 1.0 all-to-all-done.6
  175.4 0.7 copy.19
  176.1 1.4 collective-permute-done.12
  177.5 0.9 fusion.11
  (53 shorter events, 1.7 us)
Async XLA Ops:
  0.6 1.0 copy-start
  0.6 2.3 %copy-start.2 = (bf16[384,512]{1,0:T(8,128)(2,1)S(1)}, bf16[384,512]{1,0:T(8,128)(2,1)}, u32[]{:S(2)}) copy-start(bf16[384,512]{1,0:T(8,128)(2,1)} %param.11) | copy-start | bytes 1179652
  1.6 1.7 copy-start.4
  3.0 1.0 copy-start.5
  4.3 16.3 %copy-start.1 = (bf16[384,512]{1,0:T(8,128)(2,1)S(1)}, bf16[384,512]{1,0:T(8,128)(2,1)}, u32[]{:S(2)}) copy-start(bf16[384,512]{1,0:T(8,128)(2,1)} %param.10) | copy-start | bytes 1179652
  4.4 18.1 %collective-permute-start = (bf16[8,96,512]{2,1,0:T(8,128)(2,1)S(1)}, bf16[8,96,512]{2,1,0:T(8,128)(2,1)S(1)}, u32[]{:S(2)}, u32[]{:S(2)}) collective-permute-start(bf16[8,96,512]{2,1,0:T(8,128)(2,1)S(1)} %pad_maximum_fusion), channel_id=1, source_target_pairs={{0,64},{64,0},{128,192},{192,128},{256,320},{320,256},{384,448},{4... | collective-permute-start | bytes 2359304 | tf_op jit(solution)/shard_map/ppermute | solution.py:62
  23.6 16.6 %all-to-all-start = ((bf16[8,96,512]{2,1,0:T(8,128)(2,1)}), bf16[8,96,512]{2,1,0:T(8,128)(2,1)S(1)}, u32[]{:S(2)}, u32[]{:S(2)}) async-start(bf16[8,96,512]{2,1,0:T(8,128)(2,1)} %add_convert_fusion), calls=%async_computation | async-start | bytes 1572864 | tf_op jit(solution)/shard_map/all_to_all | solution.py:37
  27.2 13.0 %collective-permute-start.1 = (bf16[384,1024]{1,0:T(8,128)(2,1)S(1)}, bf16[384,1024]{1,0:T(8,128)(2,1)S(1)}, u32[]{:S(2)}, u32[]{:S(2)}) collective-permute-start(bf16[384,1024]{1,0:T(8,128)(2,1)S(1)} %constant_dynamic-update-slice_fusion), channel_id=1, source_target_pairs={{0,64},{64,0},{128,192},{192,128},{256,320},{320,256},{384,448},{4... | collective-permute-start | bytes 2359304 | tf_op jit(solution)/shard_map/ppermute | solution.py:62
  29.5 4.4 %collective-permute-start.2 = (bf16[384,192]{0,1:T(8,128)(2,1)}, bf16[384,192]{0,1:T(8,128)(2,1)}, u32[]{:S(2)}, u32[]{:S(2)}) collective-permute-start(bf16[384,192]{0,1:T(8,128)(2,1)} %param.13), channel_id=1, source_target_pairs={{0,64},{64,0},{128,192},{192,128},{256,320},{320,256},{384,448},{4... | collective-permute-start | bytes 442376 | tf_op jit(solution)/shard_map/ppermute | solution.py:62
  31.6 4.0 %collective-permute-start.3 = (bf16[256,384]{1,0:T(8,128)(2,1)S(1)}, bf16[256,384]{1,0:T(8,128)(2,1)}, u32[]{:S(2)}, u32[]{:S(2)}) collective-permute-start(bf16[256,384]{1,0:T(8,128)(2,1)S(1)} %get-tuple-element.40), channel_id=1, source_target_pairs={{0,64},{64,0},{128,192},{192,128},{256,320},{320,256},{384,448},{4... | collective-permute-start | bytes 589832 | tf_op jit(solution)/shard_map/ppermute | solution.py:62
  40.3 1.1 copy-start.7
  41.4 13.7 %all-to-all-start.1 = ((bf16[8,32,1024]{2,1,0:T(8,128)(2,1)}), bf16[8,32,1024]{2,1,0:T(8,128)(2,1)S(1)}, u32[]{:S(2)}, u32[]{:S(2)}) async-start(bf16[8,32,1024]{2,1,0:T(8,128)(2,1)} %broadcast_in_dim.8), calls=%async_computation.1 | async-start | bytes 1048576 | tf_op jit(solution)/shard_map/all_to_all | solution.py:43
  44.9 7.9 %collective-permute-start.4 = (bf16[32,512]{1,0:T(8,128)(2,1)S(1)}, bf16[32,512]{1,0:T(8,128)(2,1)S(1)}, u32[]{:S(2)}, u32[]{:S(2)}) collective-permute-start(bf16[32,512]{1,0:T(8,128)(2,1)S(1)} %get-tuple-element.94), channel_id=1, source_target_pairs={{0,128},{64,192},{128,0},{192,64},{256,384},{320,448},{384,256},{4... | collective-permute-start | bytes 98312 | tf_op jit(solution)/shard_map/ppermute | solution.py:95
  52.8 2.7 %copy-start.8 = (bf16[384,1024]{1,0:T(8,128)(2,1)S(1)}, bf16[384,1024]{1,0:T(8,128)(2,1)}, u32[]{:S(2)}) copy-start(bf16[384,1024]{1,0:T(8,128)(2,1)} %copy-done.7) | copy-start | bytes 2359300
  56.8 19.5 %all-to-all-start.2 = ((bf16[8,32,768]{2,1,0:T(8,128)(2,1)}), bf16[8,32,768]{2,1,0:T(8,128)(2,1)S(1)}, u32[]{:S(2)}, u32[]{:S(2)}) async-start(bf16[8,32,768]{2,1,0:T(8,128)(2,1)} %bitcast.9), calls=%async_computation.2 | async-start | bytes 786432 | tf_op jit(solution)/shard_map/all_to_all | solution.py:37
  66.8 9.5 %collective-permute-start.5 = (bf16[256,1024]{1,0:T(8,128)(2,1)S(1)}, bf16[256,1024]{1,0:T(8,128)(2,1)S(1)}, u32[]{:S(2)}, u32[]{:S(2)}) collective-permute-start(bf16[256,1024]{1,0:T(8,128)(2,1)S(1)} %bitcast.50), channel_id=1, source_target_pairs={{0,64},{64,0},{128,192},{192,128},{256,320},{320,256},{384,448},{4... | collective-permute-start | bytes 1572872 | tf_op jit(solution)/shard_map/ppermute | solution.py:62
  68.7 5.3 %collective-permute-start.6 = (bf16[64,512]{1,0:T(8,128)(2,1)S(1)}, bf16[64,512]{1,0:T(8,128)(2,1)S(1)}, u32[]{:S(2)}, u32[]{:S(2)}) collective-permute-start(bf16[64,512]{1,0:T(8,128)(2,1)S(1)} %maximum_select_fusion.4), channel_id=1, source_target_pairs={{0,512},{64,576},{128,640},{192,704},{256,768},{320,832},{384,896}... | collective-permute-start | bytes 196616 | tf_op jit(solution)/shard_map/ppermute | solution.py:95
  76.3 34.3 %copy-start.9 = (bf16[256,1024]{1,0:T(8,128)(2,1)}, bf16[256,1024]{1,0:T(8,128)(2,1)S(1)}, u32[]{:S(2)}) copy-start(bf16[256,1024]{1,0:T(8,128)(2,1)S(1)} %collective-permute-done.5) | copy-start | bytes 1572868
  77.0 40.0 %all-to-all-start.3 = ((bf16[4,32,768]{2,1,0:T(8,128)(2,1)}), bf16[4,32,768]{2,1,0:T(8,128)(2,1)S(1)}, u32[]{:S(2)}, u32[]{:S(2)}) async-start(bf16[4,32,768]{2,1,0:T(8,128)(2,1)} %broadcast_in_dim.9), calls=%async_computation.3 | async-start | bytes 393216 | tf_op jit(solution)/shard_map/all_to_all | solution.py:43
  98.8 13.8 %collective-permute-start.8 = (bf16[768,256]{1,0:T(8,128)(2,1)S(1)}, bf16[768,256]{1,0:T(8,128)(2,1)S(1)}, u32[]{:S(2)}, u32[]{:S(2)}) collective-permute-start(bf16[768,256]{1,0:T(8,128)(2,1)S(1)} %pad_maximum_fusion.3), channel_id=1, source_target_pairs={{0,1},{1,0},{2,3},{3,2},{4,5},{5,4},{6,7},{7,6},{8,9},{9,8},{10,11... | collective-permute-start | bytes 1179656 | tf_op jit(solution)/shard_map/ppermute | solution.py:130
  103.1 7.5 %collective-permute-start.7 = (bf16[128,512]{1,0:T(8,128)(2,1)S(1)}, bf16[128,512]{1,0:T(8,128)(2,1)S(1)}, u32[]{:S(2)}, u32[]{:S(2)}) collective-permute-start(bf16[128,512]{1,0:T(8,128)(2,1)S(1)} %maximum_select_fusion.3), channel_id=1, source_target_pairs={{0,256},{64,320},{128,384},{192,448},{256,0},{320,64},{384,128},{4... | collective-permute-start | bytes 393224 | tf_op jit(solution)/shard_map/ppermute | solution.py:95
  112.7 5.2 %copy-start.10 = (bf16[768,256]{1,0:T(8,128)(2,1)}, bf16[768,256]{1,0:T(8,128)(2,1)S(1)}, u32[]{:S(2)}) copy-start(bf16[768,256]{1,0:T(8,128)(2,1)S(1)} %collective-permute-done.8) | copy-start | bytes 1179652
  112.7 4.1 %collective-permute-start.9 = (bf16[256,512]{1,0:T(8,128)(2,1)S(1)}, bf16[256,512]{1,0:T(8,128)(2,1)S(1)}, u32[]{:S(2)}, u32[]{:S(2)}) collective-permute-start(bf16[256,512]{1,0:T(8,128)(2,1)S(1)} %bitcast.62), channel_id=1, source_target_pairs={{0,64},{64,0},{128,192},{192,128},{256,320},{320,256},{384,448},{4... | collective-permute-start | bytes 786440 | tf_op jit(solution)/shard_map/ppermute | solution.py:95
  117.9 24.7 %all-to-all-start.4 = ((bf16[8,32,768]{2,1,0:T(8,128)(2,1)}), bf16[8,32,768]{2,1,0:T(8,128)(2,1)S(1)}, u32[]{:S(2)}, u32[]{:S(2)}) async-start(bf16[8,32,768]{2,1,0:T(8,128)(2,1)} %broadcast_in_dim.10), calls=%async_computation.4 | async-start | bytes 786432 | tf_op jit(solution)/shard_map/all_to_all | solution.py:43
  131.0 1.0 copy-start.11
  134.2 8.4 %copy-start.6 = (bf16[768,192]{0,1:T(8,128)(2,1)S(1)}, bf16[768,192]{0,1:T(8,128)(2,1)}, u32[]{:S(2)}) copy-start(bf16[768,192]{0,1:T(8,128)(2,1)} %pad_maximum_fusion.4) | copy-start | bytes 884740
  134.2 8.3 %collective-permute-start.10 = (bf16[384,256]{0,1:T(8,128)(2,1)S(1)}, bf16[384,256]{0,1:T(8,128)(2,1)S(1)}, u32[]{:S(2)}, u32[]{:S(2)}) collective-permute-start(bf16[384,256]{0,1:T(8,128)(2,1)S(1)} %fusion.10), channel_id=1, source_target_pairs={{0,1},{1,0},{2,3},{3,2},{4,5},{5,4},{6,7},{7,6},{8,9},{9,8},{10,11... | collective-permute-start | bytes 589832 | tf_op jit(solution)/shard_map/ppermute | solution.py:142
  143.6 16.7 %all-to-all-start.5 = ((bf16[8,24,256]{2,1,0:T(8,128)(2,1)}), bf16[8,24,256]{2,1,0:T(8,128)(2,1)S(1)}, u32[]{:S(2)}, u32[]{:S(2)}) async-start(bf16[8,24,256]{2,1,0:T(8,128)(2,1)} %bitcast.15), calls=%async_computation.5 | async-start | bytes 196608 | tf_op jit(solution)/shard_map/all_to_all | solution.py:37
  146.9 21.6 %collective-permute-start.11 = (bf16[256,384]{1,0:T(8,128)(2,1)S(1)}, bf16[256,384]{1,0:T(8,128)(2,1)S(1)}, u32[]{:S(2)}, u32[]{:S(2)}) collective-permute-start(bf16[256,384]{1,0:T(8,128)(2,1)S(1)} %get-tuple-element.59), channel_id=1, source_target_pairs={{0,64},{64,0},{128,192},{192,128},{256,320},{320,256},{384,448},{4... | collective-permute-start | bytes 589832 | tf_op jit(solution)/shard_map/ppermute | solution.py:62
  160.3 8.4 %copy-start.12 = (bf16[512,192]{0,1:T(8,128)(2,1)S(1)}, bf16[512,192]{0,1:T(8,128)(2,1)}, u32[]{:S(2)}) copy-start(bf16[512,192]{0,1:T(8,128)(2,1)} %param.8) | copy-start | bytes 589828
  161.0 14.2 %all-to-all-start.6 = ((bf16[16,24,256]{2,1,0:T(8,128)(2,1)}), bf16[16,24,256]{2,1,0:T(8,128)(2,1)S(1)}, u32[]{:S(2)}, u32[]{:S(2)}) async-start(bf16[16,24,256]{2,1,0:T(8,128)(2,1)} %broadcast_in_dim.11), calls=%async_computation.6 | async-start | bytes 393216 | tf_op jit(solution)/shard_map/all_to_all | solution.py:43
  168.7 8.8 %copy-start.3 = (bf16[512,384]{1,0:T(8,128)(2,1)}, bf16[512,384]{1,0:T(8,128)(2,1)S(1)}, u32[]{:S(2)}) copy-start(bf16[512,384]{1,0:T(8,128)(2,1)S(1)} %maximum_select_fusion.1) | copy-start | bytes 1179652
  168.9 8.6 %collective-permute-start.12 = (bf16[384,96]{0,1:T(8,128)(2,1)S(1)}, bf16[384,96]{0,1:T(8,128)(2,1)S(1)}, u32[]{:S(2)}, u32[]{:S(2)}) collective-permute-start(bf16[384,96]{0,1:T(8,128)(2,1)S(1)} %fusion.12), channel_id=1, source_target_pairs={{0,1},{1,0},{2,3},{3,2},{4,5},{5,4},{6,7},{7,6},{8,9},{9,8},{10,11... | collective-permute-start | bytes 221192 | tf_op jit(solution)/shard_map/ppermute | solution.py:170

commit v10 on v9

--- a/solution.py
+++ b/solution.py
@@ -68,6 +68,7 @@
 
     in_mine, in_other = halves(ffn_input)
     out_mine, out_other = halves(out_grad)
+    in_order = jnp.concatenate([in_mine, in_other])
 
     def products(x, g):
         blocks = [
@@ -87,7 +88,9 @@
     out_pair = jnp.concatenate([out_mine, out_far], axis=1)
     spot = (lax.axis_index("col") + cols - 4 * core) % near
     out_piece = lax.dynamic_index_in_dim(out_pair.reshape(near, half // near, 2 * width), spot, 0, False)
-    total, w_both_far, w_out_pair, out_piece = tie((total, w_both_far, w_out_pair, out_piece))
+    total, w_both_far, w_out_pair, out_piece, in_order = tie(
+        (total, w_both_far, w_out_pair, out_piece, in_order)
+    )
     gate_share, up_share, hid_share = swiglu_grads(
         total[:share], total[share : 2 * share], total[2 * share :]
     )
@@ -125,7 +128,7 @@
         ]
         return sum(terms) * norm_factor
 
-    both_pairs = ((in_mine, mine), (in_other, other))
+    both_pairs = ((in_order, jnp.concatenate([mine, other])),)
     sent = jnp.concatenate([wgrad(both_pairs, 1 - seq, n).astype(BF16) for n in (0, hidden_width)])
     received = lax.ppermute(sent, "seq", seq_swap)
     hid_row, _ = tie((hid_row, sent))

time: 180 us -> 182 us (1.011)
  waiting for transfers between devices: 27.6 us -> 37.3 us
  starting transfers between devices: 125 us -> 120 us
    all_to_all x3, waiting for transfers between devices: 5.71 us -> 12.3 us  [scatter_sum(): lax.all_to_all(parts, axis, 0, 0, tiled=True, axis_index_groups=groups)]
    all_to_all x4, starting transfers between devices: 45.3 us -> 40.7 us  [gather(): lax.all_to_all(copies, axis, 0, 0, tiled=True, axis_index_groups=groups)]
    all_to_all x3, starting transfers between devices: 16.9 us -> 19.3 us  [scatter_sum(): lax.all_to_all(parts, axis, 0, 0, tiled=True, axis_index_groups=groups)]
    all_to_all x4, waiting for transfers between devices: 3.25 us -> 5.42 us  [gather(): lax.all_to_all(copies, axis, 0, 0, tiled=True, axis_index_groups=groups)]
    ppermute x1, starting transfers between devices: 4.42 us -> 2.26 us  [per_device(): lax.ppermute(out_sent, 'seq', seq_swap).astype(F32)]
    unnamed x29 -> x28, local copies, waits for them, and re-layouts: 3.76 us -> 1.75 us
    dot_general x12 -> x8, matrix products: 7.12 us -> 6.52 us  [contract_rows(): lax.dot_general(first, second, (((0,), (0,)), ((), ())), preferred_elemen...]
  transfers between devices with their start and end apart: 20 -> 20, of which waited for: 12 -> 13; matrix products, arithmetic and copies ran while one was open for 7% -> 6% of each run, Pallas kernels for 0% -> 0%
where the time goes in v10:
time: 182 us; the launch traced here: 181 us
  starting transfers between devices  120 us (66%)
  waiting for transfers between devices  37.3 us (20%)
  matrix products  11.3 us (6%)
  local copies, waits for them, and re-layouts  7.51 us (4%)
  other arithmetic  3.59 us (2%)
    all_to_all x4, starting transfers between devices, gather(): lax.all_to_all(copies, axis, 0, 0, tiled=True, axis_index_groups=groups)  40.7 us
    ppermute x6, starting transfers between devices, swap(): return lax.ppermute(x, 'row', core_swap)  38.2 us
    all_to_all x3, starting transfers between devices, scatter_sum(): lax.all_to_all(parts, axis, 0, 0, tiled=True, axis_index_groups=groups)  19.3 us
    ppermute x4, waiting for transfers between devices, double(): got = lax.ppermute(x, 'row', [(i, i ^ bit) for i in range(rows)])  13.2 us
    all_to_all x3, waiting for transfers between devices, scatter_sum(): lax.all_to_all(parts, axis, 0, 0, tiled=True, axis_index_groups=groups)  12.3 us
    ppermute x4, starting transfers between devices, double(): got = lax.ppermute(x, 'row', [(i, i ^ bit) for i in range(rows)])  11.5 us
    dot_general x8, matrix products, contract_rows(): lax.dot_general(first, second, (((0,), (0,)), ((), ())), preferred_elemen...  6.52 us
    all_to_all x4, waiting for transfers between devices, gather(): lax.all_to_all(copies, axis, 0, 0, tiled=True, axis_index_groups=groups)  5.42 us
  transfers between devices with their start and end apart: 20, of which 13 were waited for; matrix products, arithmetic and copies ran while one was open for 6% of the time, Pallas kernels for 0%

profile of v10, /device:TPU:1, one launch (start us, length us, event | category | flops | bytes accessed | tf_op | source)
XLA Modules:
  0.0 180.9 jit_solution(6266779514959381947)
XLA Ops:
  0.7 1.4 constant_dynamic-slice_fusion.2
  2.1 0.3 convolution_convert_fusion.2
  2.4 0.3 convolution_convert_fusion.1
  2.7 0.3 convolution_convert_fusion
  3.1 16.1 %collective-permute-start = (bf16[8,96,512]{2,1,0:T(8,128)(2,1)S(1)}, bf16[8,96,512]{2,1,0:T(8,128)(2,1)S(1)}, u32[]{:S(2)}, u32[]{:S(2)}) collective-permute-start(bf16[8,96,512]{2,1,0:T(8,128)(2,1)S(1)} %pad_maximum_fusion), channel_id=1, source_target_pairs={{0,64},{64,0},{128,192},{192,128},{256,320},{320,256},{384,448},{4... | collective-permute-start | bytes 2359304 | tf_op jit(solution)/shard_map/ppermute | solution.py:62
  19.2 0.3 convolution_convert_fusion.5
  19.5 0.3 convolution_convert_fusion.4
  19.8 0.3 convolution_convert_fusion.3
  20.1 1.0 collective-permute-done
  21.1 1.2 add_convert_fusion
  22.3 3.7 %all-to-all-start = ((bf16[8,96,512]{2,1,0:T(8,128)(2,1)}), bf16[8,96,512]{2,1,0:T(8,128)(2,1)S(1)}, u32[]{:S(2)}, u32[]{:S(2)}) async-start(bf16[8,96,512]{2,1,0:T(8,128)(2,1)} %add_convert_fusion), calls=%async_computation | async-start | bytes 1572864 | tf_op jit(solution)/shard_map/all_to_all | solution.py:37
  26.0 2.3 %collective-permute-start.1 = (bf16[384,1024]{1,0:T(8,128)(2,1)S(1)}, bf16[384,1024]{1,0:T(8,128)(2,1)}, u32[]{:S(2)}, u32[]{:S(2)}) collective-permute-start(bf16[384,1024]{1,0:T(8,128)(2,1)S(1)} %constant_dynamic-update-slice_fusion), channel_id=1, source_target_pairs={{0,64},{64,0},{128,192},{192,128},{256,320},{320,256},{384,448},{4... | collective-permute-start | bytes 2359304 | tf_op jit(solution)/shard_map/ppermute | solution.py:62
  28.3 2.0 %collective-permute-start.2 = (bf16[384,192]{0,1:T(8,128)(2,1)S(1)}, bf16[384,192]{0,1:T(8,128)(2,1)S(1)}, u32[]{:S(2)}, u32[]{:S(2)}) collective-permute-start(bf16[384,192]{0,1:T(8,128)(2,1)S(1)} %copy-done.11), channel_id=1, source_target_pairs={{0,64},{64,0},{128,192},{192,128},{256,320},{320,256},{384,448},{4... | collective-permute-start | bytes 442376 | tf_op jit(solution)/shard_map/ppermute | solution.py:62
  30.4 2.3 %collective-permute-start.3 = (bf16[256,384]{1,0:T(8,128)(2,1)S(1)}, bf16[256,384]{1,0:T(8,128)(2,1)S(1)}, u32[]{:S(2)}, u32[]{:S(2)}) collective-permute-start(bf16[256,384]{1,0:T(8,128)(2,1)S(1)} %copy-done.7), channel_id=1, source_target_pairs={{0,64},{64,0},{128,192},{192,128},{256,320},{320,256},{384,448},{4... | collective-permute-start | bytes 589832 | tf_op jit(solution)/shard_map/ppermute | solution.py:62
  32.8 1.0 collective-permute-done.3
  33.8 5.2 %all-to-all-done = bf16[8,96,512]{2,1,0:T(8,128)(2,1)S(1)} async-done(((bf16[8,96,512]{2,1,0:T(8,128)(2,1)}), bf16[8,96,512]{2,1,0:T(8,128)(2,1)S(1)}, u32[]{:S(2)}, u32[]{:S(2)}) %all-to-all-start) | async-done | bytes 786464 | tf_op jit(solution)/shard_map/all_to_all | solution.py:37
  39.2 0.9 broadcast_in_dim.8
  40.1 3.5 %all-to-all-start.1 = ((bf16[8,32,1024]{2,1,0:T(8,128)(2,1)}), bf16[8,32,1024]{2,1,0:T(8,128)(2,1)S(1)}, u32[]{:S(2)}, u32[]{:S(2)}) async-start(bf16[8,32,1024]{2,1,0:T(8,128)(2,1)} %broadcast_in_dim.8), calls=%async_computation.1 | async-start | bytes 1048576 | tf_op jit(solution)/shard_map/all_to_all | solution.py:43
  43.6 3.3 %collective-permute-start.4 = (bf16[32,512]{1,0:T(8,128)(2,1)S(1)}, bf16[32,512]{1,0:T(8,128)(2,1)S(1)}, u32[]{:S(2)}, u32[]{:S(2)}) collective-permute-start(bf16[32,512]{1,0:T(8,128)(2,1)S(1)} %get-tuple-element.98), channel_id=1, source_target_pairs={{0,128},{64,192},{128,0},{192,64},{256,384},{320,448},{384,256},{4... | collective-permute-start | bytes 98312 | tf_op jit(solution)/shard_map/ppermute | solution.py:98
  46.9 4.6 %collective-permute-done.4 = bf16[32,512]{1,0:T(8,128)(2,1)S(1)} collective-permute-done((bf16[32,512]{1,0:T(8,128)(2,1)S(1)}, bf16[32,512]{1,0:T(8,128)(2,1)S(1)}, u32[]{:S(2)}, u32[]{:S(2)}) %collective-permute-start.4) | collective-permute-done | bytes 32800 | tf_op jit(solution)/shard_map/ppermute | solution.py:98
  51.5 2.3 %all-to-all-done.1 = bf16[8,32,1024]{2,1,0:T(8,128)(2,1)S(1)} async-done(((bf16[8,32,1024]{2,1,0:T(8,128)(2,1)}), bf16[8,32,1024]{2,1,0:T(8,128)(2,1)S(1)}, u32[]{:S(2)}, u32[]{:S(2)}) %all-to-all-start.1) | async-done | bytes 524320 | tf_op jit(solution)/shard_map/all_to_all | solution.py:43
  53.8 0.5 convolution_convert_fusion.7
  54.2 1.6 convolution_convert_fusion.6
  55.8 0.8 pad_maximum_fusion.3
  56.6 10.0 %all-to-all-start.2 = ((bf16[8,32,768]{2,1,0:T(8,128)(2,1)}), bf16[8,32,768]{2,1,0:T(8,128)(2,1)S(1)}, u32[]{:S(2)}, u32[]{:S(2)}) async-start(bf16[8,32,768]{2,1,0:T(8,128)(2,1)} %bitcast.9), calls=%async_computation.2 | async-start | bytes 786432 | tf_op jit(solution)/shard_map/all_to_all | solution.py:37
  66.6 1.9 %collective-permute-start.5 = (bf16[256,1024]{1,0:T(8,128)(2,1)S(1)}, bf16[256,1024]{1,0:T(8,128)(2,1)}, u32[]{:S(2)}, u32[]{:S(2)}) collective-permute-start(bf16[256,1024]{1,0:T(8,128)(2,1)S(1)} %bitcast.58), channel_id=1, source_target_pairs={{0,64},{64,0},{128,192},{192,128},{256,320},{320,256},{384,448},{4... | collective-permute-start | bytes 1572872 | tf_op jit(solution)/shard_map/ppermute | solution.py:62
  68.6 2.2 %collective-permute-start.6 = (bf16[64,512]{1,0:T(8,128)(2,1)S(1)}, bf16[64,512]{1,0:T(8,128)(2,1)S(1)}, u32[]{:S(2)}, u32[]{:S(2)}) collective-permute-start(bf16[64,512]{1,0:T(8,128)(2,1)S(1)} %maximum_select_fusion.4), channel_id=1, source_target_pairs={{0,512},{64,576},{128,640},{192,704},{256,768},{320,832},{384,896}... | collective-permute-start | bytes 196616 | tf_op jit(solution)/shard_map/ppermute | solution.py:98
  70.8 3.1 %collective-permute-done.6 = bf16[64,512]{1,0:T(8,128)(2,1)S(1)} collective-permute-done((bf16[64,512]{1,0:T(8,128)(2,1)S(1)}, bf16[64,512]{1,0:T(8,128)(2,1)S(1)}, u32[]{:S(2)}, u32[]{:S(2)}) %collective-permute-start.6) | collective-permute-done | bytes 65568 | tf_op jit(solution)/shard_map/ppermute | solution.py:98
  73.9 2.2 %all-to-all-done.2 = bf16[8,32,768]{2,1,0:T(8,128)(2,1)S(1)} async-done(((bf16[8,32,768]{2,1,0:T(8,128)(2,1)}), bf16[8,32,768]{2,1,0:T(8,128)(2,1)S(1)}, u32[]{:S(2)}, u32[]{:S(2)}) %all-to-all-start.2) | async-done | bytes 393248 | tf_op jit(solution)/shard_map/all_to_all | solution.py:37
  76.1 0.7 broadcast_in_dim.9
  76.8 21.2 %all-to-all-start.3 = ((bf16[4,32,768]{2,1,0:T(8,128)(2,1)}), bf16[4,32,768]{2,1,0:T(8,128)(2,1)S(1)}, u32[]{:S(2)}, u32[]{:S(2)}) async-start(bf16[4,32,768]{2,1,0:T(8,128)(2,1)} %broadcast_in_dim.9), calls=%async_computation.3 | async-start | bytes 393216 | tf_op jit(solution)/shard_map/all_to_all | solution.py:43
  98.1 1.1 constant_dynamic-update-slice_fusion.2
  99.1 0.3 fusion.3
  99.5 0.3 fusion.4
  99.8 0.8 pad_maximum_fusion.4
  100.6 4.2 %collective-permute-start.8 = (bf16[768,256]{1,0:T(8,128)(2,1)}, bf16[768,256]{1,0:T(8,128)(2,1)S(1)}, u32[]{:S(2)}, u32[]{:S(2)}) collective-permute-start(bf16[768,256]{1,0:T(8,128)(2,1)} %pad_maximum_fusion.4), channel_id=1, source_target_pairs={{0,1},{1,0},{2,3},{3,2},{4,5},{5,4},{6,7},{7,6},{8,9},{9,8},{10,11... | collective-permute-start | bytes 1179656 | tf_op jit(solution)/shard_map/ppermute | solution.py:133
  104.8 3.1 %collective-permute-start.7 = (bf16[128,512]{1,0:T(8,128)(2,1)S(1)}, bf16[128,512]{1,0:T(8,128)(2,1)S(1)}, u32[]{:S(2)}, u32[]{:S(2)}) collective-permute-start(bf16[128,512]{1,0:T(8,128)(2,1)S(1)} %maximum_select_fusion.3), channel_id=1, source_target_pairs={{0,256},{64,320},{128,384},{192,448},{256,0},{320,64},{384,128},{4... | collective-permute-start | bytes 393224 | tf_op jit(solution)/shard_map/ppermute | solution.py:98
  107.9 4.4 %collective-permute-done.7 = bf16[128,512]{1,0:T(8,128)(2,1)S(1)} collective-permute-done((bf16[128,512]{1,0:T(8,128)(2,1)S(1)}, bf16[128,512]{1,0:T(8,128)(2,1)S(1)}, u32[]{:S(2)}, u32[]{:S(2)}) %collective-permute-start.7) | collective-permute-done | bytes 131104 | tf_op jit(solution)/shard_map/ppermute | solution.py:98
  112.4 2.2 %collective-permute-done.8 = bf16[768,256]{1,0:T(8,128)(2,1)S(1)} collective-permute-done((bf16[768,256]{1,0:T(8,128)(2,1)}, bf16[768,256]{1,0:T(8,128)(2,1)S(1)}, u32[]{:S(2)}, u32[]{:S(2)}) %collective-permute-start.8) | collective-permute-done | bytes 393248 | tf_op jit(solution)/shard_map/ppermute | solution.py:133
  114.6 3.0 %collective-permute-start.9 = (bf16[256,512]{1,0:T(8,128)(2,1)S(1)}, bf16[256,512]{1,0:T(8,128)(2,1)S(1)}, u32[]{:S(2)}, u32[]{:S(2)}) collective-permute-start(bf16[256,512]{1,0:T(8,128)(2,1)S(1)} %bitcast.65), channel_id=1, source_target_pairs={{0,64},{64,0},{128,192},{192,128},{256,320},{320,256},{384,448},{4... | collective-permute-start | bytes 786440 | tf_op jit(solution)/shard_map/ppermute | solution.py:98
  117.6 1.1 collective-permute-done.9
  118.7 0.2 maximum_select_fusion
  119.0 0.8 broadcast_in_dim.10
  119.8 11.2 %all-to-all-start.4 = ((bf16[8,32,768]{2,1,0:T(8,128)(2,1)}), bf16[8,32,768]{2,1,0:T(8,128)(2,1)S(1)}, u32[]{:S(2)}, u32[]{:S(2)}) async-start(bf16[8,32,768]{2,1,0:T(8,128)(2,1)} %broadcast_in_dim.10), calls=%async_computation.4 | async-start | bytes 786432 | tf_op jit(solution)/shard_map/all_to_all | solution.py:43
  131.0 2.1 %fusion.2 = f32[384,256]{1,0:T(8,128)} fusion(bf16[512,384]{1,0:T(8,128)(2,1)S(1)} %pad_maximum_fusion.2, bf16[512,1024]{1,0:T(8,128)(2,1)} %copy-done.5, s32[]{:T(128)S(6)} %select_n.119, bf16[768,256]{1,0:T(8,128)(2,1)} %copy-done.8), kind=kOutput, calls=%fused_computation.16 | convolution fusion | flops 100958208 | bytes 1245188 | tf_op jit(solution)/shard_map/dot_general | solution.py:25
  133.1 0.3 fusion.6
  133.5 3.8 %collective-permute-start.10 = (bf16[384,256]{0,1:T(8,128)(2,1)S(1)}, bf16[384,256]{0,1:T(8,128)(2,1)S(1)}, u32[]{:S(2)}, u32[]{:S(2)}) collective-permute-start(bf16[384,256]{0,1:T(8,128)(2,1)S(1)} %fusion.6), channel_id=1, source_target_pairs={{0,1},{1,0},{2,3},{3,2},{4,5},{5,4},{6,7},{7,6},{8,9},{9,8},{10,11... | collective-permute-start | bytes 589832 | tf_op jit(solution)/shard_map/ppermute | solution.py:145
  137.3 2.0 %fusion.1 = f32[384,256]{1,0:T(8,128)} fusion(bf16[512,384]{1,0:T(8,128)(2,1)S(1)} %pad_maximum_fusion.2, bf16[512,1024]{1,0:T(8,128)(2,1)} %copy-done.5, s32[]{:T(128)S(6)} %select_n.118, bf16[768,256]{1,0:T(8,128)(2,1)S(1)} %copy-done.9), kind=kOutput, calls=%fused_computation.15 | convolution fusion | flops 100958208 | bytes 1245188 | tf_op jit(solution)/shard_map/dot_general | solution.py:25
  139.3 2.1 %collective-permute-done.10 = bf16[384,256]{0,1:T(8,128)(2,1)S(1)} collective-permute-done((bf16[384,256]{0,1:T(8,128)(2,1)S(1)}, bf16[384,256]{0,1:T(8,128)(2,1)S(1)}, u32[]{:S(2)}, u32[]{:S(2)}) %collective-permute-start.10) | collective-permute-done | bytes 196640 | tf_op jit(solution)/shard_map/ppermute | solution.py:145
  141.5 0.9 convolution_convert_fusion.8
  142.4 13.6 %collective-permute-start.11 = (bf16[256,384]{1,0:T(8,128)(2,1)S(1)}, bf16[256,384]{1,0:T(8,128)(2,1)S(1)}, u32[]{:S(2)}, u32[]{:S(2)}) collective-permute-start(bf16[256,384]{1,0:T(8,128)(2,1)S(1)} %get-tuple-element.61), channel_id=1, source_target_pairs={{0,64},{64,0},{128,192},{192,128},{256,320},{320,256},{384,448},{4... | collective-permute-start | bytes 589832 | tf_op jit(solution)/shard_map/ppermute | solution.py:62
  156.0 5.6 %all-to-all-start.5 = ((bf16[8,24,256]{2,1,0:T(8,128)(2,1)}), bf16[8,24,256]{2,1,0:T(8,128)(2,1)S(1)}, u32[]{:S(2)}, u32[]{:S(2)}) async-start(bf16[8,24,256]{2,1,0:T(8,128)(2,1)} %bitcast.15), calls=%async_computation.5 | async-start | bytes 196608 | tf_op jit(solution)/shard_map/all_to_all | solution.py:37
  161.6 0.3 convert_add_fusion
  162.0 4.9 %all-to-all-done.5 = bf16[8,24,256]{2,1,0:T(8,128)(2,1)S(1)} async-done(((bf16[8,24,256]{2,1,0:T(8,128)(2,1)}), bf16[8,24,256]{2,1,0:T(8,128)(2,1)S(1)}, u32[]{:S(2)}, u32[]{:S(2)}) %all-to-all-start.5) | async-done | bytes 98336 | tf_op jit(solution)/shard_map/all_to_all | solution.py:37
  166.9 0.7 broadcast_in_dim.11
  167.6 4.7 %all-to-all-start.6 = ((bf16[16,24,256]{2,1,0:T(8,128)(2,1)}), bf16[16,24,256]{2,1,0:T(8,128)(2,1)S(1)}, u32[]{:S(2)}, u32[]{:S(2)}) async-start(bf16[16,24,256]{2,1,0:T(8,128)(2,1)} %broadcast_in_dim.11), calls=%async_computation.6 | async-start | bytes 393216 | tf_op jit(solution)/shard_map/all_to_all | solution.py:43
  172.4 0.1 maximum_select_fusion.1
  172.5 0.2 fusion.8
  172.8 2.3 %collective-permute-start.12 = (bf16[384,96]{0,1:T(8,128)(2,1)S(1)}, bf16[384,96]{0,1:T(8,128)(2,1)S(1)}, u32[]{:S(2)}, u32[]{:S(2)}) collective-permute-start(bf16[384,96]{0,1:T(8,128)(2,1)S(1)} %fusion.8), channel_id=1, source_target_pairs={{0,1},{1,0},{2,3},{3,2},{4,5},{5,4},{6,7},{7,6},{8,9},{9,8},{10,11... | collective-permute-start | bytes 221192 | tf_op jit(solution)/shard_map/ppermute | solution.py:173
  175.0 0.9 copy.18
  176.0 3.2 %all-to-all-done.6 = bf16[16,24,256]{2,1,0:T(8,128)(2,1)S(1)} async-done(((bf16[16,24,256]{2,1,0:T(8,128)(2,1)}), bf16[16,24,256]{2,1,0:T(8,128)(2,1)S(1)}, u32[]{:S(2)}, u32[]{:S(2)}) %all-to-all-start.6) | async-done | bytes 196640 | tf_op jit(solution)/shard_map/all_to_all | solution.py:43
  179.1 0.2 copy.17
  179.3 0.7 copy.19
  180.0 0.9 fusion.7
  (50 shorter events, 0.8 us)
Async XLA Ops:
  0.6 2.1 %copy-start = (bf16[384,512]{1,0:T(8,128)(2,1)S(1)}, bf16[384,512]{1,0:T(8,128)(2,1)}, u32[]{:S(2)}) copy-start(bf16[384,512]{1,0:T(8,128)(2,1)} %param.12) | copy-start | bytes 1179652
  0.6 1.4 copy-start.2
  0.7 1.7 copy-start.3
  2.1 0.9 copy-start.6
  3.1 18.0 %collective-permute-start = (bf16[8,96,512]{2,1,0:T(8,128)(2,1)S(1)}, bf16[8,96,512]{2,1,0:T(8,128)(2,1)S(1)}, u32[]{:S(2)}, u32[]{:S(2)}) collective-permute-start(bf16[8,96,512]{2,1,0:T(8,128)(2,1)S(1)} %pad_maximum_fusion), channel_id=1, source_target_pairs={{0,64},{64,0},{128,192},{192,128},{256,320},{320,256},{384,448},{4... | collective-permute-start | bytes 2359304 | tf_op jit(solution)/shard_map/ppermute | solution.py:62
  22.3 6.1 %copy-start.11 = (bf16[384,192]{0,1:T(8,128)(2,1)S(1)}, bf16[384,192]{0,1:T(8,128)(2,1)}, u32[]{:S(2)}) copy-start(bf16[384,192]{0,1:T(8,128)(2,1)} %param.13) | copy-start | bytes 442372
  22.3 8.1 %copy-start.7 = (bf16[256,384]{1,0:T(8,128)(2,1)S(1)}, bf16[256,384]{1,0:T(8,128)(2,1)}, u32[]{:S(2)}) copy-start(bf16[256,384]{1,0:T(8,128)(2,1)} %copy-done.6) | copy-start | bytes 589828
  22.3 16.7 %all-to-all-start = ((bf16[8,96,512]{2,1,0:T(8,128)(2,1)}), bf16[8,96,512]{2,1,0:T(8,128)(2,1)S(1)}, u32[]{:S(2)}, u32[]{:S(2)}) async-start(bf16[8,96,512]{2,1,0:T(8,128)(2,1)} %add_convert_fusion), calls=%async_computation | async-start | bytes 1572864 | tf_op jit(solution)/shard_map/all_to_all | solution.py:37
  26.0 13.1 %collective-permute-start.1 = (bf16[384,1024]{1,0:T(8,128)(2,1)S(1)}, bf16[384,1024]{1,0:T(8,128)(2,1)}, u32[]{:S(2)}, u32[]{:S(2)}) collective-permute-start(bf16[384,1024]{1,0:T(8,128)(2,1)S(1)} %constant_dynamic-update-slice_fusion), channel_id=1, source_target_pairs={{0,64},{64,0},{128,192},{192,128},{256,320},{320,256},{384,448},{4... | collective-permute-start | bytes 2359304 | tf_op jit(solution)/shard_map/ppermute | solution.py:62
  28.3 4.4 %collective-permute-start.2 = (bf16[384,192]{0,1:T(8,128)(2,1)S(1)}, bf16[384,192]{0,1:T(8,128)(2,1)S(1)}, u32[]{:S(2)}, u32[]{:S(2)}) collective-permute-start(bf16[384,192]{0,1:T(8,128)(2,1)S(1)} %copy-done.11), channel_id=1, source_target_pairs={{0,64},{64,0},{128,192},{192,128},{256,320},{320,256},{384,448},{4... | collective-permute-start | bytes 442376 | tf_op jit(solution)/shard_map/ppermute | solution.py:62
  30.4 3.3 %collective-permute-start.3 = (bf16[256,384]{1,0:T(8,128)(2,1)S(1)}, bf16[256,384]{1,0:T(8,128)(2,1)S(1)}, u32[]{:S(2)}, u32[]{:S(2)}) collective-permute-start(bf16[256,384]{1,0:T(8,128)(2,1)S(1)} %copy-done.7), channel_id=1, source_target_pairs={{0,64},{64,0},{128,192},{192,128},{256,320},{320,256},{384,448},{4... | collective-permute-start | bytes 589832 | tf_op jit(solution)/shard_map/ppermute | solution.py:62
  40.1 13.7 %all-to-all-start.1 = ((bf16[8,32,1024]{2,1,0:T(8,128)(2,1)}), bf16[8,32,1024]{2,1,0:T(8,128)(2,1)S(1)}, u32[]{:S(2)}, u32[]{:S(2)}) async-start(bf16[8,32,1024]{2,1,0:T(8,128)(2,1)} %broadcast_in_dim.8), calls=%async_computation.1 | async-start | bytes 1048576 | tf_op jit(solution)/shard_map/all_to_all | solution.py:43
  43.6 7.9 %collective-permute-start.4 = (bf16[32,512]{1,0:T(8,128)(2,1)S(1)}, bf16[32,512]{1,0:T(8,128)(2,1)S(1)}, u32[]{:S(2)}, u32[]{:S(2)}) collective-permute-start(bf16[32,512]{1,0:T(8,128)(2,1)S(1)} %get-tuple-element.98), channel_id=1, source_target_pairs={{0,128},{64,192},{128,0},{192,64},{256,384},{320,448},{384,256},{4... | collective-permute-start | bytes 98312 | tf_op jit(solution)/shard_map/ppermute | solution.py:98
  56.6 19.5 %all-to-all-start.2 = ((bf16[8,32,768]{2,1,0:T(8,128)(2,1)}), bf16[8,32,768]{2,1,0:T(8,128)(2,1)S(1)}, u32[]{:S(2)}, u32[]{:S(2)}) async-start(bf16[8,32,768]{2,1,0:T(8,128)(2,1)} %bitcast.9), calls=%async_computation.2 | async-start | bytes 786432 | tf_op jit(solution)/shard_map/all_to_all | solution.py:37
  66.6 9.5 %collective-permute-start.5 = (bf16[256,1024]{1,0:T(8,128)(2,1)S(1)}, bf16[256,1024]{1,0:T(8,128)(2,1)}, u32[]{:S(2)}, u32[]{:S(2)}) collective-permute-start(bf16[256,1024]{1,0:T(8,128)(2,1)S(1)} %bitcast.58), channel_id=1, source_target_pairs={{0,64},{64,0},{128,192},{192,128},{256,320},{320,256},{384,448},{4... | collective-permute-start | bytes 1572872 | tf_op jit(solution)/shard_map/ppermute | solution.py:62
  68.6 5.3 %collective-permute-start.6 = (bf16[64,512]{1,0:T(8,128)(2,1)S(1)}, bf16[64,512]{1,0:T(8,128)(2,1)S(1)}, u32[]{:S(2)}, u32[]{:S(2)}) collective-permute-start(bf16[64,512]{1,0:T(8,128)(2,1)S(1)} %maximum_select_fusion.4), channel_id=1, source_target_pairs={{0,512},{64,576},{128,640},{192,704},{256,768},{320,832},{384,896}... | collective-permute-start | bytes 196616 | tf_op jit(solution)/shard_map/ppermute | solution.py:98
  76.8 42.1 %all-to-all-start.3 = ((bf16[4,32,768]{2,1,0:T(8,128)(2,1)}), bf16[4,32,768]{2,1,0:T(8,128)(2,1)S(1)}, u32[]{:S(2)}, u32[]{:S(2)}) async-start(bf16[4,32,768]{2,1,0:T(8,128)(2,1)} %broadcast_in_dim.9), calls=%async_computation.3 | async-start | bytes 393216 | tf_op jit(solution)/shard_map/all_to_all | solution.py:43
  99.1 18.5 %copy-start.5 = (bf16[512,1024]{1,0:T(8,128)(2,1)}, bf16[512,1024]{1,0:T(8,128)(2,1)S(1)}, u32[]{:S(2)}) copy-start(bf16[512,1024]{1,0:T(8,128)(2,1)S(1)} %constant_dynamic-update-slice_fusion.2) | copy-start | bytes 3145732
  100.6 14.0 %collective-permute-start.8 = (bf16[768,256]{1,0:T(8,128)(2,1)}, bf16[768,256]{1,0:T(8,128)(2,1)S(1)}, u32[]{:S(2)}, u32[]{:S(2)}) collective-permute-start(bf16[768,256]{1,0:T(8,128)(2,1)} %pad_maximum_fusion.4), channel_id=1, source_target_pairs={{0,1},{1,0},{2,3},{3,2},{4,5},{5,4},{6,7},{7,6},{8,9},{9,8},{10,11... | collective-permute-start | bytes 1179656 | tf_op jit(solution)/shard_map/ppermute | solution.py:133
  104.8 7.5 %collective-permute-start.7 = (bf16[128,512]{1,0:T(8,128)(2,1)S(1)}, bf16[128,512]{1,0:T(8,128)(2,1)S(1)}, u32[]{:S(2)}, u32[]{:S(2)}) collective-permute-start(bf16[128,512]{1,0:T(8,128)(2,1)S(1)} %maximum_select_fusion.3), channel_id=1, source_target_pairs={{0,256},{64,320},{128,384},{192,448},{256,0},{320,64},{384,128},{4... | collective-permute-start | bytes 393224 | tf_op jit(solution)/shard_map/ppermute | solution.py:98
  114.6 4.4 %copy-start.8 = (bf16[768,256]{1,0:T(8,128)(2,1)}, bf16[768,256]{1,0:T(8,128)(2,1)S(1)}, u32[]{:S(2)}) copy-start(bf16[768,256]{1,0:T(8,128)(2,1)S(1)} %collective-permute-done.8) | copy-start | bytes 1179652
  114.6 4.1 %collective-permute-start.9 = (bf16[256,512]{1,0:T(8,128)(2,1)S(1)}, bf16[256,512]{1,0:T(8,128)(2,1)S(1)}, u32[]{:S(2)}, u32[]{:S(2)}) collective-permute-start(bf16[256,512]{1,0:T(8,128)(2,1)S(1)} %bitcast.65), channel_id=1, source_target_pairs={{0,64},{64,0},{128,192},{192,128},{256,320},{320,256},{384,448},{4... | collective-permute-start | bytes 786440 | tf_op jit(solution)/shard_map/ppermute | solution.py:98
  119.8 13.3 %copy-start.4 = (bf16[512,384]{1,0:T(8,128)(2,1)S(1)}, bf16[512,384]{1,0:T(8,128)(2,1)}, u32[]{:S(2)}) copy-start(bf16[512,384]{1,0:T(8,128)(2,1)} %param.9) | copy-start | bytes 1179652
  119.8 21.6 %all-to-all-start.4 = ((bf16[8,32,768]{2,1,0:T(8,128)(2,1)}), bf16[8,32,768]{2,1,0:T(8,128)(2,1)S(1)}, u32[]{:S(2)}, u32[]{:S(2)}) async-start(bf16[8,32,768]{2,1,0:T(8,128)(2,1)} %broadcast_in_dim.10), calls=%async_computation.4 | async-start | bytes 786432 | tf_op jit(solution)/shard_map/all_to_all | solution.py:43
  131.0 6.2 %copy-start.9 = (bf16[768,256]{1,0:T(8,128)(2,1)S(1)}, bf16[768,256]{1,0:T(8,128)(2,1)}, u32[]{:S(2)}) copy-start(bf16[768,256]{1,0:T(8,128)(2,1)} %copy-done.8) | copy-start | bytes 1179652
  133.5 7.9 %collective-permute-start.10 = (bf16[384,256]{0,1:T(8,128)(2,1)S(1)}, bf16[384,256]{0,1:T(8,128)(2,1)S(1)}, u32[]{:S(2)}, u32[]{:S(2)}) collective-permute-start(bf16[384,256]{0,1:T(8,128)(2,1)S(1)} %fusion.6), channel_id=1, source_target_pairs={{0,1},{1,0},{2,3},{3,2},{4,5},{5,4},{6,7},{7,6},{8,9},{9,8},{10,11... | collective-permute-start | bytes 589832 | tf_op jit(solution)/shard_map/ppermute | solution.py:145
  142.4 30.0 %collective-permute-start.11 = (bf16[256,384]{1,0:T(8,128)(2,1)S(1)}, bf16[256,384]{1,0:T(8,128)(2,1)S(1)}, u32[]{:S(2)}, u32[]{:S(2)}) collective-permute-start(bf16[256,384]{1,0:T(8,128)(2,1)S(1)} %get-tuple-element.61), channel_id=1, source_target_pairs={{0,64},{64,0},{128,192},{192,128},{256,320},{320,256},{384,448},{4... | collective-permute-start | bytes 589832 | tf_op jit(solution)/shard_map/ppermute | solution.py:62
  156.0 10.9 %all-to-all-start.5 = ((bf16[8,24,256]{2,1,0:T(8,128)(2,1)}), bf16[8,24,256]{2,1,0:T(8,128)(2,1)S(1)}, u32[]{:S(2)}, u32[]{:S(2)}) async-start(bf16[8,24,256]{2,1,0:T(8,128)(2,1)} %bitcast.15), calls=%async_computation.5 | async-start | bytes 196608 | tf_op jit(solution)/shard_map/all_to_all | solution.py:37
  162.0 10.6 %copy-start.10 = (bf16[512,192]{0,1:T(8,128)(2,1)S(1)}, bf16[512,192]{0,1:T(8,128)(2,1)}, u32[]{:S(2)}) copy-start(bf16[512,192]{0,1:T(8,128)(2,1)} %param.8) | copy-start | bytes 589828
  167.6 11.5 %all-to-all-start.6 = ((bf16[16,24,256]{2,1,0:T(8,128)(2,1)}), bf16[16,24,256]{2,1,0:T(8,128)(2,1)S(1)}, u32[]{:S(2)}, u32[]{:S(2)}) async-start(bf16[16,24,256]{2,1,0:T(8,128)(2,1)} %broadcast_in_dim.11), calls=%async_computation.6 | async-start | bytes 393216 | tf_op jit(solution)/shard_map/all_to_all | solution.py:43
  172.5 7.4 %copy-start.1 = (bf16[512,384]{1,0:T(8,128)(2,1)}, bf16[512,384]{1,0:T(8,128)(2,1)S(1)}, u32[]{:S(2)}) copy-start(bf16[512,384]{1,0:T(8,128)(2,1)S(1)} %maximum_select_fusion.1) | copy-start | bytes 1179652
  172.8 7.2 %collective-permute-start.12 = (bf16[384,96]{0,1:T(8,128)(2,1)S(1)}, bf16[384,96]{0,1:T(8,128)(2,1)S(1)}, u32[]{:S(2)}, u32[]{:S(2)}) collective-permute-start(bf16[384,96]{0,1:T(8,128)(2,1)S(1)} %fusion.8), channel_id=1, source_target_pairs={{0,1},{1,0},{2,3},{3,2},{4,5},{5,4},{6,7},{7,6},{8,9},{9,8},{10,11... | collective-permute-start | bytes 221192 | tf_op jit(solution)/shard_map/ppermute | solution.py:173
